TPU v7x, 512 devices: a whole 4x8x8 slice. The times are simulated.
512 devices in a mesh: row: 8 (over y), col: 16 (over z, core), rep: 4 (over x).
Axes of the slice: x: 4, y: 8, z: 8, core: 2. Of those that a mesh axis runs over, the one named last changes fastest.
Arguments:
- tokens: bfloat16 [2048, 6144], P(('rep', 'row'), 'col'), may hold values from -6 to 6
- up_weight: bfloat16 [6144, 12288], P('col', 'row'), may hold values from -0.078125 to 0.078125
- down_weight: bfloat16 [12288, 6144], P('row', 'col'), may hold values from -0.0546875 to 0.0546875
- out_grads: bfloat16 [2048, 6144], P(('rep', 'row'), 'col'), may hold values from -6 to 6
Outputs:
- block_out: bfloat16 [2048, 6144], P(('rep', 'row'), 'col')
- token_grads: bfloat16 [2048, 6144], P(('rep', 'row'), 'col')
- up_grads: bfloat16 [6144, 12288], P('col', 'row')
- down_grads: bfloat16 [12288, 6144], P('row', 'col')
All inputs are finite; a program needn't handle non-finite values.
Results may differ from a plain program's by a relative error of at most 0.033.
Values may be sent and summed in bfloat16 or wider, within the bound.
No kernel may reach another device: no remote copies, remote signals or barrier semaphores. Data moves between devices by JAX's collectives and lax.ppermute only.
A program may use at most 64 MiB of HBM per device.

v0:
```python
import jax
import jax.numpy as jnp
from jax import lax
from jax.sharding import PartitionSpec as P


def gelu_pullback(hidden, upstream):
    _, pullback = jax.vjp(jax.nn.gelu, hidden)
    return pullback(upstream)[0]


def contract_rows(left, right):
    return lax.dot_general(
        left, right, (((0,), (0,)), ((), ())), preferred_element_type=jnp.float32
    )


def contract_columns(left, right):
    return lax.dot_general(
        left, right, (((1,), (1,)), ((), ())), preferred_element_type=jnp.float32
    )


def per_device(tokens, up_weight, down_weight, out_grads):
    gathered = lax.all_gather(tokens, "row", axis=0, tiled=True)
    part = gathered
    hidden = lax.psum_scatter(
        jnp.dot(part, up_weight, preferred_element_type=jnp.float32).astype(jnp.bfloat16),
        "col",
        scatter_dimension=0,
        tiled=True,
    ).astype(jnp.float32)
    activated = jax.nn.gelu(hidden).astype(jnp.bfloat16)
    act_rows = lax.all_gather(activated, "col", axis=0, tiled=True)
    part = act_rows
    block_out = lax.psum_scatter(
        jnp.dot(part, down_weight, preferred_element_type=jnp.float32).astype(jnp.bfloat16),
        "row",
        scatter_dimension=0,
        tiled=True,
    )
    grads_rows = lax.all_gather(out_grads, "row", axis=0, tiled=True)
    part = grads_rows
    activated_grads = lax.psum_scatter(
        contract_columns(part, down_weight).astype(jnp.bfloat16),
        "col",
        scatter_dimension=0,
        tiled=True,
    ).astype(jnp.float32)
    hidden_grads = gelu_pullback(hidden, activated_grads).astype(jnp.bfloat16)
    hidden_rows = lax.all_gather(hidden_grads, "col", axis=0, tiled=True)
    part = hidden_rows
    token_grads = lax.psum_scatter(
        contract_columns(part, up_weight).astype(jnp.bfloat16),
        "row",
        scatter_dimension=0,
        tiled=True,
    )
    down_local = contract_rows(act_rows, grads_rows)
    down_grads = lax.psum(down_local.astype(jnp.bfloat16), "rep")
    up_local = contract_rows(gathered, hidden_rows)
    up_grads = lax.psum(up_local.astype(jnp.bfloat16), "rep")
    return (block_out, token_grads, up_grads, down_grads)


def solution(mesh):
    in_specs = (
        P(("rep", "row"), "col"),
        P("col", "row"),
        P("row", "col"),
        P(("rep", "row"), "col"),
    )
    out_specs = (
        P(("rep", "row"), "col"),
        P(("rep", "row"), "col"),
        P("col", "row"),
        P("row", "col"),
    )
    return jax.shard_map(
        per_device, mesh=mesh, in_specs=in_specs, out_specs=out_specs, check_vma=False
    )
```

profile of v0, /device:TPU:1, one launch (start us, length us, event | category | flops | bytes accessed | tf_op | source)
XLA Modules:
  0.0 414.1 jit_solution(13490258118989839903)
XLA Ops:
  7.2 0.0 copy-start
  7.2 0.0 reduce-scatter.9.cloned.1.call-start
  7.2 21.7 %all_gather.14 = bf16[512,384]{1,0:T(8,128)(2,1)S(1)} all-gather(bf16[64,384]{1,0:T(8,128)(2,1)} %param.7), channel_id=1, replica_groups=mesh['row'=8,'col'=16,'rep'=4] {'row'}, dimensions={0}, use_global_device_ids=true | all-gather | bytes 442368 | tf_op jit(solution)/shard_map/all_gather | solution.py:42
  29.0 0.0 copy-done
  29.0 2.2 convolution_convert_fusion
  31.1 0.0 copy-start.3
  31.1 0.0 copy-start.1
  31.1 0.0 reduce-scatter.9.cloned.1.call-update
  31.2 0.0 reduce-scatter.5.cloned.1.call-start
  31.2 0.7 copy-done.3
  31.9 19.4 %all_gather.12 = bf16[512,384]{1,0:T(8,128)(2,1)S(1)} all-gather(bf16[64,384]{1,0:T(8,128)(2,1)S(1)} %copy-done.3), channel_id=1, replica_groups=mesh['row'=8,'col'=16,'rep'=4] {'row'}, dimensions={0}, use_global_device_ids=true | all-gather | bytes 442368 | tf_op jit(solution)/shard_map/all_gather | solution.py:25
  51.3 0.0 copy-done.1
  51.3 2.1 convolution_convert_fusion.1
  53.4 0.0 reduce-scatter.5.cloned.1.call-update
  53.4 0.0 all-gather.5.cloned.1.call-start
  53.5 46.2 %reduce-scatter.9.cloned.1.call-done = bf16[32,1536]{1,0:T(8,128)(2,1)} async-done(((bf16[512,1536]{1,0:T(8,128)(2,1)}), bf16[32,1536]{1,0:T(8,128)(2,1)}) %reduce-scatter.9.cloned.1.call-update) | async-done | bytes 98320 | tf_op jit(solution)/shard_map/reduce_scatter | solution.py:44
  99.6 62.4 %reduce-scatter.5.cloned.1.call-done = bf16[32,1536]{1,0:T(8,128)(2,1)} async-done(((bf16[512,1536]{1,0:T(8,128)(2,1)}), bf16[32,1536]{1,0:T(8,128)(2,1)}) %reduce-scatter.5.cloned.1.call-update) | async-done | bytes 98320 | tf_op jit(solution)/shard_map/reduce_scatter | solution.py:27
  162.0 1.8 fusion.4
  163.8 0.0 all-gather.5.cloned.1.call-update
  163.8 0.0 all-gather.3.cloned.1.call-start
  163.9 0.5 all-gather.3.cloned.1.call-update
  164.4 0.0 all-reduce.3.cloned.1.call-start
  164.4 44.0 %all-gather.5.cloned.1.call-done = bf16[512,1536]{1,0:T(8,128)(2,1)} async-done(((bf16[32,1536]{1,0:T(8,128)(2,1)}), bf16[512,1536]{1,0:T(8,128)(2,1)}) %all-gather.5.cloned.1.call-update) | async-done | bytes 1572880 | tf_op jit(solution)/shard_map/all_gather | solution.py:51
  208.4 3.4 fusion
  211.9 39.7 %all-gather.3.cloned.1.call-done = bf16[512,1536]{1,0:T(8,128)(2,1)} async-done(((bf16[32,1536]{1,0:T(8,128)(2,1)}), bf16[512,1536]{1,0:T(8,128)(2,1)}) %all-gather.3.cloned.1.call-update) | async-done | bytes 1572880 | tf_op jit(solution)/shard_map/all_gather | solution.py:34
  251.6 3.4 convolution_convert_fusion.2
  255.0 0.0 all-reduce.3.cloned.1.call-update
  255.1 0.0 reduce-scatter.7.cloned.1.call-start
  255.1 3.1 convolution_convert_fusion.5
  258.2 0.0 reduce-scatter.7.cloned.1.call-update
  258.3 0.0 reduce-scatter.11.cloned.1.call-start
  258.3 3.1 convolution_convert_fusion.4
  261.5 0.0 reduce-scatter.11.cloned.1.call-update
  261.5 65.2 %all-reduce.3.cloned.1.call-done = (bf16[384,1536]{0,1:T(8,128)(2,1)}, bf16[1536,384]{1,0:T(8,128)(2,1)}) async-done(((bf16[384,1536]{0,1:T(8,128)(2,1)}, bf16[1536,384]{1,0:T(8,128)(2,1)}), (bf16[384,1536]{0,1:T(8,128)(2,1)}, bf16[1536,384]{1,0:T(8,128)(2,1)})) %all-reduce.3.cloned.1.call-update) | async-done | bytes 2359312 | tf_op jit(solution)/shard_map/psum | solution.py:62
  326.7 0.0 copy-start.2
  326.7 2.5 copy.8
  329.1 35.1 %reduce-scatter.7.cloned.1.call-done = bf16[64,384]{1,0:T(8,128)(2,1)} async-done(((bf16[512,384]{1,0:T(8,128)(2,1)}), bf16[64,384]{1,0:T(8,128)(2,1)}) %reduce-scatter.7.cloned.1.call-update) | async-done | bytes 49168 | tf_op jit(solution)/shard_map/reduce_scatter | solution.py:36
  364.2 42.0 %reduce-scatter.11.cloned.1.call-done = bf16[64,384]{1,0:T(8,128)(2,1)} async-done(((bf16[512,384]{1,0:T(8,128)(2,1)}), bf16[64,384]{1,0:T(8,128)(2,1)}) %reduce-scatter.11.cloned.1.call-update) | async-done | bytes 49168 | tf_op jit(solution)/shard_map/reduce_scatter | solution.py:53
  406.2 0.0 copy-done.2
  406.2 1.0 copy.11
Async XLA Ops:
  7.2 21.8 %copy-start = (bf16[1536,384]{1,0:T(8,128)(2,1)S(1)}, bf16[1536,384]{1,0:T(8,128)(2,1)}, u32[]{:S(2)}) copy-start(bf16[1536,384]{1,0:T(8,128)(2,1)} %param.6) | copy-start | bytes 3538948
  7.2 92.5 %reduce-scatter.9.cloned.1.call-start = ((), (), s32[]{:S(2)}) async-start(), calls=%async_computation.7 | async-start | bytes 1671168 | tf_op jit(solution)/shard_map/reduce_scatter | solution.py:44
  31.1 0.8 copy-start.3
  31.1 20.2 %copy-start.1 = (bf16[384,1536]{1,0:T(8,128)(2,1)S(1)}, bf16[384,1536]{1,0:T(8,128)(2,1)}, u32[]{:S(2)}) copy-start(bf16[384,1536]{1,0:T(8,128)(2,1)} %param.5) | copy-start | bytes 3538948
  31.2 130.9 %reduce-scatter.5.cloned.1.call-start = ((), (), s32[]{:S(2)}) async-start(), calls=%async_computation.4 | async-start | bytes 1671168 | tf_op jit(solution)/shard_map/reduce_scatter | solution.py:27
  53.4 155.0 %all-gather.5.cloned.1.call-start = ((), (), s32[]{:S(2)}) async-start(), calls=%async_computation.8 | async-start | bytes 1671168 | tf_op jit(solution)/shard_map/all_gather | solution.py:51
  163.8 87.8 %all-gather.3.cloned.1.call-start = ((), (), s32[]{:S(2)}) async-start(), calls=%async_computation.5 | async-start | bytes 1671168 | tf_op jit(solution)/shard_map/all_gather | solution.py:34
  164.4 162.3 %all-reduce.3.cloned.1.call-start = ((), (), s32[]{:S(2)}) async-start(), calls=%async_computation.10 | async-start | bytes 4718592 | tf_op jit(solution)/shard_map/psum | solution.py:62
  255.1 109.2 %reduce-scatter.7.cloned.1.call-start = ((), (), s32[]{:S(2)}) async-start(), calls=%async_computation.6 | async-start | bytes 442368 | tf_op jit(solution)/shard_map/reduce_scatter | solution.py:36
  258.3 147.9 %reduce-scatter.11.cloned.1.call-start = ((), (), s32[]{:S(2)}) async-start(), calls=%async_computation.9 | async-start | bytes 442368 | tf_op jit(solution)/shard_map/reduce_scatter | solution.py:53
  326.7 79.5 %copy-start.2 = (bf16[1536,384]{1,0:T(8,128)(2,1)S(1)}, bf16[1536,384]{1,0:T(8,128)(2,1)}, u32[]{:S(2)}) copy-start(bf16[1536,384]{1,0:T(8,128)(2,1)} %get-tuple-element.15) | copy-start | bytes 3538948
Sparse Core Ops, SparseCore 0:
  31.3 68.3 reduce-scatter.8
  102.7 59.2 reduce-scatter.4
  164.7 43.6 all-gather.4
  211.0 40.5 all-gather.2
  255.2 71.4 all-reduce.2
  329.9 34.2 reduce-scatter.6
  367.8 38.3 reduce-scatter.10
where the time goes:
time: 418 us; the launch traced here: 414 us
  waiting for transfers between devices  335 us (80%)
  blocking collectives  41.1 us (10%)
  matrix products  17.4 us (4%)
  between operations  14.1 us (3%)
  local copies, waits for them, and re-layouts  4.22 us (1%)
    psum x1, waiting for transfers between devices, per_device(): up_grads = lax.psum(up_local.astype(jnp.bfloat16), 'rep')  65.2 us
    reduce_scatter x1, waiting for transfers between devices, per_device(): lax.psum_scatter(jnp.dot(part, up_weight, preferred_element_type=jnp.floa...  62.4 us
    reduce_scatter x1, waiting for transfers between devices, per_device(): lax.psum_scatter(contract_columns(part, down_weight).astype(jnp.bfloat16)...  46.2 us
    all_gather x1, waiting for transfers between devices, per_device(): hidden_rows = lax.all_gather(hidden_grads, 'col', axis=0, tiled=True)  44 us
    reduce_scatter x1, waiting for transfers between devices, per_device(): lax.psum_scatter(contract_columns(part, up_weight).astype(jnp.bfloat16),...  42 us
    all_gather x1, waiting for transfers between devices, per_device(): act_rows = lax.all_gather(activated, 'col', axis=0, tiled=True)  39.7 us
    reduce_scatter x1, waiting for transfers between devices, per_device(): lax.psum_scatter(jnp.dot(part, down_weight, preferred_element_type=jnp.fl...  35.1 us
    all_gather x1, blocking collectives, per_device(): grads_rows = lax.all_gather(out_grads, 'row', axis=0, tiled=True)  21.7 us
  transfers between devices with their start and end apart: 7, of which 7 were waited for; matrix products, arithmetic and copies ran while one was open for 3% of the time, Pallas kernels for 0%

commit v1 on v0

v1 whole, which is shorter than its diff:
```python
import jax
import jax.numpy as jnp
from jax import lax
from jax.sharding import Mesh, PartitionSpec as P

bf16 = jnp.bfloat16
f32 = jnp.float32


def gelu_pullback(hidden, upstream):
    _, pullback = jax.vjp(jax.nn.gelu, hidden)
    return pullback(upstream)[0]


def dot(left, right, dims):
    return lax.dot_general(
        left, right, ((dims[:1], dims[1:]), ((), ())), preferred_element_type=f32
    ).astype(bf16)


def swap(x):
    return lax.ppermute(x, "core", [(0, 1), (1, 0)])


def exchange(x, axis):
    return lax.all_to_all(x, axis, 0, 0, tiled=False)


def gather(x, axis):
    n = lax.axis_size(axis)
    got = exchange(jnp.broadcast_to(x[None], (n,) + x.shape), axis)
    return got.reshape((n * x.shape[0],) + x.shape[1:])


def per_device(tokens, up_weight, down_weight, out_grads):
    core = lax.axis_index("core")
    rows, width = tokens.shape
    half = up_weight.shape[1] // 2
    n_row, n_z, n_rep = (lax.axis_size(a) for a in ("row", "z", "rep"))
    mine, theirs = core * half, (1 - core) * half

    up_own = lax.dynamic_slice_in_dim(up_weight, mine, half, 1)
    up_other = swap(lax.dynamic_slice_in_dim(up_weight, theirs, half, 1))
    down_own = lax.dynamic_slice_in_dim(down_weight, mine, half, 0)
    down_other = swap(lax.dynamic_slice_in_dim(down_weight, theirs, half, 0))
    up = jnp.concatenate([up_own, up_other], 0)
    down = jnp.concatenate([down_own, down_other], 1)

    gathered = gather(jnp.concatenate([tokens, out_grads], 1), "row")
    other = swap(gathered)
    tok = jnp.concatenate([gathered[:, :width], other[:, :width]], 1)
    og = jnp.concatenate([gathered[:, width:], other[:, width:]], 1)

    total = tok.shape[0]
    share = total // n_z
    partial = jnp.concatenate([dot(tok, up, (1, 0)), dot(og, down, (1, 1))], 1)
    terms = exchange(partial.reshape(n_z, share, 2 * half), "z")
    sums = jnp.sum(terms.astype(f32), 0)
    hidden, act_grads = sums[:, :half], sums[:, half:]
    act = jax.nn.gelu(hidden).astype(bf16)
    hid_grads = gelu_pullback(hidden, act_grads).astype(bf16)
    both = gather(jnp.concatenate([act, hid_grads], 1), "z")
    act, hid_grads = both[:, :half], both[:, half:]

    down_local = dot(act, og, (0, 0)).reshape(n_rep, half // n_rep, 2 * width)
    up_local = dot(tok, hid_grads, (0, 0)).reshape(2, n_rep, width // n_rep, half)
    up_local = jnp.swapaxes(up_local, 0, 1).reshape(n_rep, 2 * width // n_rep, half)
    local = jnp.concatenate([down_local, up_local], 1)
    grads = jnp.sum(exchange(local, "rep").astype(f32), 0).astype(bf16)
    part = half // n_rep
    piece = width // n_rep
    down_mine, down_send = grads[:part, :width], grads[:part, width:]
    up_mine, up_send = grads[part : part + piece], grads[part + piece :]
    down_got, up_got = swap(down_send), swap(up_send)
    first = core == 0
    down_pair = jnp.where(
        first, jnp.stack([down_mine, down_got]), jnp.stack([down_got, down_mine])
    )
    up_pair = jnp.where(
        first,
        jnp.concatenate([up_mine, up_got], 1),
        jnp.concatenate([up_got, up_mine], 1),
    )
    rep = lax.axis_index("rep")
    down_out = jnp.zeros((2, n_rep, part, width), bf16)
    up_out = jnp.zeros((n_rep, piece, 2 * half), bf16)
    for k in range(n_rep):
        if k:
            ring = [(i, (i + k) % n_rep) for i in range(n_rep)]
            down_k = lax.ppermute(down_pair, "rep", ring)
            up_k = lax.ppermute(up_pair, "rep", ring)
        else:
            down_k, up_k = down_pair, up_pair
        source = lax.rem(rep + n_rep - k, n_rep)
        down_out = lax.dynamic_update_slice_in_dim(down_out, down_k[:, None], source, 1)
        up_out = lax.dynamic_update_slice_in_dim(up_out, up_k[None], source, 0)
    down_grads = down_out.reshape(2 * half, width)
    up_grads = up_out.reshape(width, 2 * half)

    def halves(x):
        return x[:, :width], x[:, width:]

    block_own, block_send = halves(dot(act, down, (1, 0)))
    token_own, token_send = halves(dot(hid_grads, up, (1, 1)))
    own = jnp.concatenate([block_own, token_own], 1)
    got = swap(jnp.concatenate([block_send, token_send], 1))
    out = (own.astype(f32) + got.astype(f32)).astype(bf16)
    out = exchange(out.reshape(n_row, rows, 2 * width), "row")
    out = jnp.sum(out.astype(f32), 0).astype(bf16)
    return (out[:, :width], out[:, width:], up_grads, down_grads)


def solution(mesh):
    n_row, n_col, n_rep = mesh.devices.shape
    split = Mesh(
        mesh.devices.reshape(n_row, n_col // 2, 2, n_rep), ("row", "z", "core", "rep")
    )
    col = ("z", "core")
    acts = P(("rep", "row"), col)
    up = P(col, "row")
    down = P("row", col)
    return jax.shard_map(
        per_device,
        mesh=split,
        in_specs=(acts, up, down, acts),
        out_specs=(acts, acts, up, down),
        check_vma=False,
    )
```

time: 418 us -> 222 us (0.53)
  waiting for transfers between devices: 335 us -> 29.3 us
  blocking collectives: 41.1 us -> 121 us
  starting transfers between devices: 0.29 us -> 44.7 us
  between operations: 14.1 us -> 1.2 us
  matrix products: 17.4 us -> 6.27 us
  local copies, waits for them, and re-layouts: 4.22 us -> 12 us
  other arithmetic: 1.77 us -> 6.58 us
    reduce_scatter x4 -> x0, waiting for transfers between devices: 186 us -> none  [the longest x1 62.4 us: per_device(): lax.psum_scatter(jnp.dot(part, up_weight, preferred_element_type=jnp.floa...]
    all_to_all x0 -> x3, blocking collectives: none -> 121 us  [exchange(): return lax.all_to_all(x, axis, 0, 0, tiled=False)]
    all_gather x2 -> x0, waiting for transfers between devices: 83.7 us -> none  [the longest x1 44 us: per_device(): hidden_rows = lax.all_gather(hidden_grads, 'col', axis=0, tiled=True)]
    psum x1 -> x0, waiting for transfers between devices: 65.2 us -> none  [per_device(): up_grads = lax.psum(up_local.astype(jnp.bfloat16), 'rep')]
    all_gather x2 -> x0, blocking collectives: 41.1 us -> none  [the longest x1 21.7 us: per_device(): grads_rows = lax.all_gather(out_grads, 'row', axis=0, tiled=True)]
    ppermute x0 -> x12, starting transfers between devices: none -> 37 us  [the longest x6 18.4 us: swap(): return lax.ppermute(x, 'core', [(0, 1), (1, 0)])]
    all_to_all x0 -> x2, waiting for transfers between devices: none -> 19.3 us  [exchange(): return lax.all_to_all(x, axis, 0, 0, tiled=False)]
    dot_general x6, matrix products: 17.4 us -> 6.27 us  [dot(): lax.dot_general(left, right, ((dims[:1], dims[1:]), ((), ())), preferred_...]
  transfers between devices with their start and end apart: 7 -> 14, of which waited for: 7 -> 3; matrix products, arithmetic and copies ran while one was open for 3% -> 8% of each run, Pallas kernels for 0% -> 0%
where the time goes in v1:
time: 222 us; the launch traced here: 221 us
  blocking collectives  121 us (55%)
  starting transfers between devices  44.7 us (20%)
  waiting for transfers between devices  29.3 us (13%)
  local copies, waits for them, and re-layouts  12 us (5%)
  other arithmetic  6.58 us (3%)
  matrix products  6.27 us (3%)
    all_to_all x3, blocking collectives, exchange(): return lax.all_to_all(x, axis, 0, 0, tiled=False)  121 us
    all_to_all x2, waiting for transfers between devices, exchange(): return lax.all_to_all(x, axis, 0, 0, tiled=False)  19.3 us
    ppermute x6, starting transfers between devices, swap(): return lax.ppermute(x, 'core', [(0, 1), (1, 0)])  18.4 us
    ppermute x3, starting transfers between devices, per_device(): down_k = lax.ppermute(down_pair, 'rep', ring)  10.1 us
    ppermute x3, starting transfers between devices, per_device(): up_k = lax.ppermute(up_pair, 'rep', ring)  8.41 us
    ppermute x3, waiting for transfers between devices, per_device(): down_k = lax.ppermute(down_pair, 'rep', ring)  8.13 us
    all_to_all x2, starting transfers between devices, exchange(): return lax.all_to_all(x, axis, 0, 0, tiled=False)  7.69 us
    dot_general x6, matrix products, dot(): lax.dot_general(left, right, ((dims[:1], dims[1:]), ((), ())), preferred_...  6.27 us
  transfers between devices with their start and end apart: 14, of which 3 were waited for; matrix products, arithmetic and copies ran while one was open for 8% of the time, Pallas kernels for 0%

profile of v1, /device:TPU:1, one launch (start us, length us, event | category | flops | bytes accessed | tf_op | source)
XLA Modules:
  0.0 220.9 jit_solution(6759376753188146846)
XLA Ops:
  0.6 0.9 pad_maximum_fusion.16
  1.6 0.1 broadcast_in_dim.38
  1.6 27.8 %all_to_all.25 = bf16[8,64,768]{2,1,0:T(8,128)(2,1)S(1)} all-to-all(bf16[8,64,768]{2,1,0:T(8,128)(2,1)S(1)} %broadcast_in_dim.38), channel_id=1, replica_groups=mesh['row'=8,'z'=8,'core'=2,'rep'=4] {'row'}, dimensions={0} | all-to-all | bytes 1572864 | tf_op jit(solution)/shard_map/all_to_all | solution.py:26
  29.4 5.7 %collective-permute-start = (bf16[512,768]{1,0:T(8,128)(2,1)S(1)}, bf16[512,768]{1,0:T(8,128)(2,1)}, u32[]{:S(2)}, u32[]{:S(2)}) collective-permute-start(bf16[512,768]{1,0:T(8,128)(2,1)S(1)} %bitcast.38), channel_id=1, source_target_pairs={{0,4},{4,0},{1,5},{5,1},{2,6},{6,2},{3,7},{7,3},{8,12},{12,8},{9,1... | collective-permute-start | bytes 2359304 | tf_op jit(solution)/shard_map/ppermute | solution.py:22
  35.2 0.1 constant_dynamic-slice_fusion.1
  35.3 0.0 copy-start.6
  35.4 1.9 collective-permute-start.2
  37.3 0.1 constant_dynamic-slice_fusion.3
  37.4 2.4 %collective-permute-start.1 = (bf16[384,768]{1,0:T(8,128)(2,1)S(1)}, bf16[384,768]{1,0:T(8,128)(2,1)S(1)}, u32[]{:S(2)}, u32[]{:S(2)}) collective-permute-start(bf16[384,768]{1,0:T(8,128)(2,1)S(1)} %get-tuple-element.7), channel_id=1, source_target_pairs={{0,4},{4,0},{1,5},{5,1},{2,6},{6,2},{3,7},{7,3},{8,12},{12,8},{9,1... | collective-permute-start | bytes 1769480 | tf_op jit(solution)/shard_map/ppermute | solution.py:22
  39.8 0.1 fusion.21
  39.9 1.2 fusion.22
  41.1 0.0 copy-start.10
  41.1 0.8 convolution_convert_fusion.4
  42.0 0.8 copy-done.11
  42.8 0.8 convolution_convert_fusion.5
  43.6 0.1 pad_maximum_fusion.1
  43.7 50.3 %all_to_all.26 = bf16[8,64,1536]{2,1,0:T(8,128)(2,1)S(1)} all-to-all(bf16[8,64,1536]{2,1,0:T(8,128)(2,1)S(1)} %bitcast.36), channel_id=1, replica_groups=mesh['row'=8,'z'=8,'core'=2,'rep'=4] {'z'}, dimensions={0} | all-to-all | bytes 3145728 | tf_op jit(solution)/shard_map/all_to_all | solution.py:26
  94.0 0.2 convert_reduce_fusion
  94.2 0.1 multiply_convert_fusion
  94.4 0.1 broadcast_in_dim.39
  94.5 42.8 %all_to_all.27 = bf16[8,64,1536]{2,1,0:T(8,128)(2,1)S(1)} all-to-all(bf16[8,64,1536]{2,1,0:T(8,128)(2,1)S(1)} %broadcast_in_dim.39), channel_id=1, replica_groups=mesh['row'=8,'z'=8,'core'=2,'rep'=4] {'z'}, dimensions={0} | all-to-all | bytes 3145728 | tf_op jit(solution)/shard_map/all_to_all | solution.py:26
  137.3 0.8 convolution_convert_fusion
  138.1 0.3 copy-done
  138.4 0.8 convolution_convert_fusion.1
  139.3 0.1 copy.8
  139.4 1.6 pad_maximum_fusion
  140.9 4.1 %all-to-all-start.4 = ((bf16[4,384,768]{2,1,0:T(8,128)(2,1)}), bf16[4,384,768]{2,1,0:T(8,128)(2,1)S(1)}, u32[]{:S(2)}, u32[]{:S(2)}) async-start(bf16[4,384,768]{2,1,0:T(8,128)(2,1)} %pad_maximum_fusion), calls=%async_computation.4 | async-start | bytes 4718592 | tf_op jit(solution)/shard_map/all_to_all | solution.py:26
  145.1 2.2 %convolution_convert_fusion.3 = bf16[512,768]{1,0:T(8,128)(2,1)S(1)} fusion(bf16[768,384]{1,0:T(8,128)(2,1)} %copy-done.10, bf16[768,384]{1,0:T(8,128)(2,1)S(1)} %copy-done.7, bf16[512,1536]{1,0:T(8,128)(2,1)} %bitcast.43), kind=kOutput, calls=%fused_computation.7 | convolution fusion | flops 606732288 | bytes 2752512 | tf_op jit(solution)/shard_map/dot_general | solution.py:16
  147.4 0.8 convolution_convert_fusion.2
  148.2 0.2 fusion.19
  148.4 0.1 pad_maximum_fusion.6
  148.4 2.8 %collective-permute-start.3 = (bf16[512,768]{1,0:T(8,128)(2,1)S(1)}, bf16[512,768]{1,0:T(8,128)(2,1)S(1)}, u32[]{:S(2)}, u32[]{:S(2)}) collective-permute-start(bf16[512,768]{1,0:T(8,128)(2,1)S(1)} %pad_maximum_fusion.6), channel_id=1, source_target_pairs={{0,4},{4,0},{1,5},{5,1},{2,6},{6,2},{3,7},{7,3},{8,12},{12,8},{9,1... | collective-permute-start | bytes 2359304 | tf_op jit(solution)/shard_map/ppermute | solution.py:22
  151.2 1.9 collective-permute-done.3
  153.1 1.1 add_convert_fusion
  154.2 19.3 %all-to-all-done.4 = bf16[4,384,768]{2,1,0:T(8,128)(2,1)S(1)} async-done(((bf16[4,384,768]{2,1,0:T(8,128)(2,1)}), bf16[4,384,768]{2,1,0:T(8,128)(2,1)S(1)}, u32[]{:S(2)}, u32[]{:S(2)}) %all-to-all-start.4) | async-done | bytes 2359328 | tf_op jit(solution)/shard_map/all_to_all | solution.py:26
  173.4 3.5 %all-to-all-start.3 = ((bf16[8,64,768]{2,1,0:T(8,128)(2,1)}), bf16[8,64,768]{2,1,0:T(8,128)(2,1)S(1)}, u32[]{:S(2)}, u32[]{:S(2)}) async-start(bf16[8,64,768]{2,1,0:T(8,128)(2,1)} %bitcast.40), calls=%async_computation.3 | async-start | bytes 1572864 | tf_op jit(solution)/shard_map/all_to_all | solution.py:26
  177.0 1.3 reduce_sum.35
  178.3 1.0 fusion.23
  179.3 3.7 %collective-permute-start.4 = (bf16[96,768]{1,0:T(8,128)(2,1)S(1)}, bf16[96,768]{1,0:T(8,128)(2,1)S(1)}, u32[]{:S(2)}, u32[]{:S(2)}) collective-permute-start(bf16[96,768]{1,0:T(8,128)(2,1)S(1)} %get-tuple-element.21), channel_id=1, source_target_pairs={{0,4},{4,0},{1,5},{5,1},{2,6},{6,2},{3,7},{7,3},{8,12},{12,8},{9,1... | collective-permute-start | bytes 442376 | tf_op jit(solution)/shard_map/ppermute | solution.py:22
  183.0 1.0 slice_bitcast_fusion
  184.0 1.9 collective-permute-start.8
  186.0 0.8 maximum_select_fusion.1
  186.8 2.2 collective-permute-start.5
  189.0 3.7 %collective-permute-start.6 = (bf16[96,1536]{1,0:T(8,128)(2,1)}, bf16[96,1536]{1,0:T(8,128)(2,1)}, u32[]{:S(2)}, u32[]{:S(2)}) collective-permute-start(bf16[96,1536]{1,0:T(8,128)(2,1)} %maximum_select_fusion.1), channel_id=1, source_target_pairs={{0,2},{1,3},{2,0},{3,1},{4,6},{5,7},{6,4},{7,5},{8,10},{9,11},{10,... | collective-permute-start | bytes 884744 | tf_op jit(solution)/shard_map/ppermute | solution.py:91
  192.7 2.5 %collective-permute-start.7 = (bf16[96,1536]{1,0:T(8,128)(2,1)}, bf16[96,1536]{1,0:T(8,128)(2,1)}, u32[]{:S(2)}, u32[]{:S(2)}) collective-permute-start(bf16[96,1536]{1,0:T(8,128)(2,1)} %maximum_select_fusion.1), channel_id=1, source_target_pairs={{0,3},{1,0},{2,1},{3,2},{4,7},{5,4},{6,5},{7,6},{8,11},{9,8},{10,9... | collective-permute-start | bytes 884744 | tf_op jit(solution)/shard_map/ppermute | solution.py:91
  195.3 2.8 %collective-permute-start.9 = (bf16[2,192,384]{2,1,0:T(8,128)(2,1)S(1)}, bf16[2,192,384]{2,1,0:T(8,128)(2,1)}, u32[]{:S(2)}, u32[]{:S(2)}) collective-permute-start(bf16[2,192,384]{2,1,0:T(8,128)(2,1)S(1)} %maximum_select_fusion.3), channel_id=1, source_target_pairs={{0,1},{1,2},{2,3},{3,0},{4,5},{5,6},{6,7},{7,4},{8,9},{9,10},{10,1... | collective-permute-start | bytes 884744 | tf_op jit(solution)/shard_map/ppermute | solution.py:90
  198.0 3.4 %collective-permute-start.10 = (bf16[2,192,384]{2,1,0:T(8,128)(2,1)S(1)}, bf16[2,192,384]{2,1,0:T(8,128)(2,1)}, u32[]{:S(2)}, u32[]{:S(2)}) collective-permute-start(bf16[2,192,384]{2,1,0:T(8,128)(2,1)S(1)} %maximum_select_fusion.3), channel_id=1, source_target_pairs={{0,2},{1,3},{2,0},{3,1},{4,6},{5,7},{6,4},{7,5},{8,10},{9,11},{10,... | collective-permute-start | bytes 884744 | tf_op jit(solution)/shard_map/ppermute | solution.py:90
  201.5 0.1 broadcast_in_dim.40
  201.6 0.1 fusion.4
  201.7 0.1 broadcast_in_dim.44
  201.8 0.1 fusion.5
  201.9 0.1 reduce_sum.34
  202.0 0.6 fusion.24
  202.6 4.0 %collective-permute-start.11 = (bf16[2,192,384]{2,1,0:T(8,128)(2,1)S(1)}, bf16[2,192,384]{2,1,0:T(8,128)(2,1)S(1)}, u32[]{:S(2)}, u32[]{:S(2)}) collective-permute-start(bf16[2,192,384]{2,1,0:T(8,128)(2,1)S(1)} %maximum_select_fusion.3), channel_id=1, source_target_pairs={{0,3},{1,0},{2,1},{3,2},{4,7},{5,4},{6,5},{7,6},{8,11},{9,8},{10,9... | collective-permute-start | bytes 884744 | tf_op jit(solution)/shard_map/ppermute | solution.py:90
  206.6 1.0 bitcast_dynamic-update-slice_fusion.5
  207.6 1.0 bitcast_dynamic-update-slice_fusion.4
  208.6 1.0 bitcast_dynamic-update-slice_fusion.3
  209.6 0.0 copy-start.5
  209.6 8.1 %collective-permute-done.9 = bf16[2,192,384]{2,1,0:T(8,128)(2,1)} collective-permute-done((bf16[2,192,384]{2,1,0:T(8,128)(2,1)S(1)}, bf16[2,192,384]{2,1,0:T(8,128)(2,1)}, u32[]{:S(2)}, u32[]{:S(2)}) %collective-permute-start.9) | collective-permute-done | bytes 294944 | tf_op jit(solution)/shard_map/ppermute | solution.py:90
  217.7 1.0 bitcast_dynamic-update-slice_fusion.1
  218.8 1.0 bitcast_dynamic-update-slice_fusion
  219.8 0.1 bitcast_dynamic-update-slice_fusion.2
  219.8 0.0 copy-start.4
  219.9 1.0 copy-done.4
  (32 shorter events, 0.1 us)
Async XLA Ops:
  0.6 34.6 %copy-start.2 = (bf16[1536,384]{1,0:T(8,128)(2,1)S(1)}, bf16[1536,384]{1,0:T(8,128)(2,1)}, u32[]{:S(2)}) copy-start(bf16[1536,384]{1,0:T(8,128)(2,1)} %param.6) | copy-start | bytes 3538948
  29.4 7.9 %copy-start.3 = (bf16[384,1536]{1,0:T(8,128)(2,1)S(1)}, bf16[384,1536]{1,0:T(8,128)(2,1)}, u32[]{:S(2)}) copy-start(bf16[384,1536]{1,0:T(8,128)(2,1)} %param.5) | copy-start | bytes 3538948
  29.4 10.5 %collective-permute-start = (bf16[512,768]{1,0:T(8,128)(2,1)S(1)}, bf16[512,768]{1,0:T(8,128)(2,1)}, u32[]{:S(2)}, u32[]{:S(2)}) collective-permute-start(bf16[512,768]{1,0:T(8,128)(2,1)S(1)} %bitcast.38), channel_id=1, source_target_pairs={{0,4},{4,0},{1,5},{5,1},{2,6},{6,2},{3,7},{7,3},{8,12},{12,8},{9,1... | collective-permute-start | bytes 2359304 | tf_op jit(solution)/shard_map/ppermute | solution.py:22
  35.3 5.8 %copy-start.6 = (bf16[768,384]{1,0:T(8,128)(2,1)}, bf16[768,384]{1,0:T(8,128)(2,1)S(1)}, u32[]{:S(2)}) copy-start(bf16[768,384]{1,0:T(8,128)(2,1)S(1)} %get-tuple-element.4) | copy-start | bytes 1769476
  35.4 5.8 %collective-permute-start.2 = (bf16[768,384]{1,0:T(8,128)(2,1)S(1)}, bf16[768,384]{1,0:T(8,128)(2,1)S(1)}, u32[]{:S(2)}, u32[]{:S(2)}) collective-permute-start(bf16[768,384]{1,0:T(8,128)(2,1)S(1)} %get-tuple-element.5), channel_id=1, source_target_pairs={{0,4},{4,0},{1,5},{5,1},{2,6},{6,2},{3,7},{7,3},{8,12},{12,8},{9,1... | collective-permute-start | bytes 1769480 | tf_op jit(solution)/shard_map/ppermute | solution.py:22
  37.4 4.6 %copy-start.8 = (bf16[384,768]{1,0:T(8,128)(2,1)}, bf16[384,768]{1,0:T(8,128)(2,1)S(1)}, u32[]{:S(2)}) copy-start(bf16[384,768]{1,0:T(8,128)(2,1)S(1)} %get-tuple-element.6) | copy-start | bytes 1769476
  37.4 4.6 %collective-permute-start.1 = (bf16[384,768]{1,0:T(8,128)(2,1)S(1)}, bf16[384,768]{1,0:T(8,128)(2,1)S(1)}, u32[]{:S(2)}, u32[]{:S(2)}) collective-permute-start(bf16[384,768]{1,0:T(8,128)(2,1)S(1)} %get-tuple-element.7), channel_id=1, source_target_pairs={{0,4},{4,0},{1,5},{5,1},{2,6},{6,2},{3,7},{7,3},{8,12},{12,8},{9,1... | collective-permute-start | bytes 1769480 | tf_op jit(solution)/shard_map/ppermute | solution.py:22
  41.1 0.8 copy-start.10
  42.0 0.8 copy-start.11
  137.3 1.2 copy-start
  140.9 4.1 %copy-start.7 = (bf16[768,384]{1,0:T(8,128)(2,1)S(1)}, bf16[768,384]{1,0:T(8,128)(2,1)}, u32[]{:S(2)}) copy-start(bf16[768,384]{1,0:T(8,128)(2,1)} %copy-done.6) | copy-start | bytes 1769476
  140.9 32.5 %all-to-all-start.4 = ((bf16[4,384,768]{2,1,0:T(8,128)(2,1)}), bf16[4,384,768]{2,1,0:T(8,128)(2,1)S(1)}, u32[]{:S(2)}, u32[]{:S(2)}) async-start(bf16[4,384,768]{2,1,0:T(8,128)(2,1)} %pad_maximum_fusion), calls=%async_computation.4 | async-start | bytes 4718592 | tf_op jit(solution)/shard_map/all_to_all | solution.py:26
  145.1 2.3 %copy-start.1 = (bf16[8,64,1536]{2,1,0:T(8,128)(2,1)S(1)}, bf16[8,64,1536]{2,1,0:T(8,128)(2,1)}, u32[]{:S(2)}) copy-start(bf16[8,64,1536]{2,1,0:T(8,128)(2,1)} %copy-done) | copy-start | bytes 4718596
  145.1 2.3 %copy-start.9 = (bf16[384,768]{1,0:T(8,128)(2,1)S(1)}, bf16[384,768]{1,0:T(8,128)(2,1)}, u32[]{:S(2)}) copy-start(bf16[384,768]{1,0:T(8,128)(2,1)} %copy-done.8) | copy-start | bytes 1769476
  145.1 2.3 %copy-start.12 = (bf16[384,768]{1,0:T(8,128)(2,1)S(1)}, bf16[384,768]{1,0:T(8,128)(2,1)}, u32[]{:S(2)}) copy-start(bf16[384,768]{1,0:T(8,128)(2,1)} %copy-done.11) | copy-start | bytes 1769476
  148.4 4.7 %collective-permute-start.3 = (bf16[512,768]{1,0:T(8,128)(2,1)S(1)}, bf16[512,768]{1,0:T(8,128)(2,1)S(1)}, u32[]{:S(2)}, u32[]{:S(2)}) collective-permute-start(bf16[512,768]{1,0:T(8,128)(2,1)S(1)} %pad_maximum_fusion.6), channel_id=1, source_target_pairs={{0,4},{4,0},{1,5},{5,1},{2,6},{6,2},{3,7},{7,3},{8,12},{12,8},{9,1... | collective-permute-start | bytes 2359304 | tf_op jit(solution)/shard_map/ppermute | solution.py:22
  173.4 28.4 %all-to-all-start.3 = ((bf16[8,64,768]{2,1,0:T(8,128)(2,1)}), bf16[8,64,768]{2,1,0:T(8,128)(2,1)S(1)}, u32[]{:S(2)}, u32[]{:S(2)}) async-start(bf16[8,64,768]{2,1,0:T(8,128)(2,1)} %bitcast.40), calls=%async_computation.3 | async-start | bytes 1572864 | tf_op jit(solution)/shard_map/all_to_all | solution.py:26
  179.3 6.6 %collective-permute-start.4 = (bf16[96,768]{1,0:T(8,128)(2,1)S(1)}, bf16[96,768]{1,0:T(8,128)(2,1)S(1)}, u32[]{:S(2)}, u32[]{:S(2)}) collective-permute-start(bf16[96,768]{1,0:T(8,128)(2,1)S(1)} %get-tuple-element.21), channel_id=1, source_target_pairs={{0,4},{4,0},{1,5},{5,1},{2,6},{6,2},{3,7},{7,3},{8,12},{12,8},{9,1... | collective-permute-start | bytes 442376 | tf_op jit(solution)/shard_map/ppermute | solution.py:22
  184.0 11.2 %collective-permute-start.8 = (bf16[192,384]{1,0:T(8,128)(2,1)S(1)}, bf16[192,384]{1,0:T(8,128)(2,1)S(1)}, u32[]{:S(2)}, u32[]{:S(2)}) collective-permute-start(bf16[192,384]{1,0:T(8,128)(2,1)S(1)} %get-tuple-element.17), channel_id=1, source_target_pairs={{0,4},{4,0},{1,5},{5,1},{2,6},{6,2},{3,7},{7,3},{8,12},{12,8},{9,1... | collective-permute-start | bytes 442376 | tf_op jit(solution)/shard_map/ppermute | solution.py:22
  186.8 15.9 %collective-permute-start.5 = (bf16[96,1536]{1,0:T(8,128)(2,1)}, bf16[96,1536]{1,0:T(8,128)(2,1)}, u32[]{:S(2)}, u32[]{:S(2)}) collective-permute-start(bf16[96,1536]{1,0:T(8,128)(2,1)} %maximum_select_fusion.1), channel_id=1, source_target_pairs={{0,1},{1,2},{2,3},{3,0},{4,5},{5,6},{6,7},{7,4},{8,9},{9,10},{10,1... | collective-permute-start | bytes 884744 | tf_op jit(solution)/shard_map/ppermute | solution.py:91
  189.0 18.6 %collective-permute-start.6 = (bf16[96,1536]{1,0:T(8,128)(2,1)}, bf16[96,1536]{1,0:T(8,128)(2,1)}, u32[]{:S(2)}, u32[]{:S(2)}) collective-permute-start(bf16[96,1536]{1,0:T(8,128)(2,1)} %maximum_select_fusion.1), channel_id=1, source_target_pairs={{0,2},{1,3},{2,0},{3,1},{4,6},{5,7},{6,4},{7,5},{8,10},{9,11},{10,... | collective-permute-start | bytes 884744 | tf_op jit(solution)/shard_map/ppermute | solution.py:91
  192.7 15.9 %collective-permute-start.7 = (bf16[96,1536]{1,0:T(8,128)(2,1)}, bf16[96,1536]{1,0:T(8,128)(2,1)}, u32[]{:S(2)}, u32[]{:S(2)}) collective-permute-start(bf16[96,1536]{1,0:T(8,128)(2,1)} %maximum_select_fusion.1), channel_id=1, source_target_pairs={{0,3},{1,0},{2,1},{3,2},{4,7},{5,4},{6,5},{7,6},{8,11},{9,8},{10,9... | collective-permute-start | bytes 884744 | tf_op jit(solution)/shard_map/ppermute | solution.py:91
  195.3 22.5 %collective-permute-start.9 = (bf16[2,192,384]{2,1,0:T(8,128)(2,1)S(1)}, bf16[2,192,384]{2,1,0:T(8,128)(2,1)}, u32[]{:S(2)}, u32[]{:S(2)}) collective-permute-start(bf16[2,192,384]{2,1,0:T(8,128)(2,1)S(1)} %maximum_select_fusion.3), channel_id=1, source_target_pairs={{0,1},{1,2},{2,3},{3,0},{4,5},{5,6},{6,7},{7,4},{8,9},{9,10},{10,1... | collective-permute-start | bytes 884744 | tf_op jit(solution)/shard_map/ppermute | solution.py:90
  198.0 20.7 %collective-permute-start.10 = (bf16[2,192,384]{2,1,0:T(8,128)(2,1)S(1)}, bf16[2,192,384]{2,1,0:T(8,128)(2,1)}, u32[]{:S(2)}, u32[]{:S(2)}) collective-permute-start(bf16[2,192,384]{2,1,0:T(8,128)(2,1)S(1)} %maximum_select_fusion.3), channel_id=1, source_target_pairs={{0,2},{1,3},{2,0},{3,1},{4,6},{5,7},{6,4},{7,5},{8,10},{9,11},{10,... | collective-permute-start | bytes 884744 | tf_op jit(solution)/shard_map/ppermute | solution.py:90
  202.6 17.1 %collective-permute-start.11 = (bf16[2,192,384]{2,1,0:T(8,128)(2,1)S(1)}, bf16[2,192,384]{2,1,0:T(8,128)(2,1)S(1)}, u32[]{:S(2)}, u32[]{:S(2)}) collective-permute-start(bf16[2,192,384]{2,1,0:T(8,128)(2,1)S(1)} %maximum_select_fusion.3), channel_id=1, source_target_pairs={{0,3},{1,0},{2,1},{3,2},{4,7},{5,4},{6,5},{7,6},{8,11},{9,8},{10,9... | collective-permute-start | bytes 884744 | tf_op jit(solution)/shard_map/ppermute | solution.py:90
  209.6 10.3 %copy-start.5 = (bf16[4,96,1536]{2,1,0:T(8,128)(2,1)}, bf16[4,96,1536]{2,1,0:T(8,128)(2,1)S(1)}, u32[]{:S(2)}) copy-start(bf16[4,96,1536]{2,1,0:T(8,128)(2,1)S(1)} %bitcast_dynamic-update-slice_fusion.3) | copy-start | bytes 3538948
  219.8 1.0 copy-start.4

commit v2 on v1

v2 whole, which is shorter than its diff:
```python
import jax
import jax.numpy as jnp
from jax import lax
from jax.sharding import Mesh, PartitionSpec as P

bf16 = jnp.bfloat16
f32 = jnp.float32
barrier = lax.optimization_barrier


def gelu_pullback(hidden, upstream):
    _, pullback = jax.vjp(jax.nn.gelu, hidden)
    return pullback(upstream)[0]


def dot(left, right, dims):
    return lax.dot_general(
        left, right, ((dims[:1], dims[1:]), ((), ())), preferred_element_type=f32
    ).astype(bf16)


def swap(x):
    return lax.ppermute(x, "core", [(0, 1), (1, 0)])


def exchange(x, axis):
    return lax.all_to_all(x, axis, 0, 0, tiled=False)


def total_of(x):
    parts = [x[i].astype(f32) for i in range(x.shape[0])]
    while len(parts) > 1:
        parts = [a + b for a, b in zip(parts[::2], parts[1::2])]
    return parts[0]


def gather(x, axis):
    n = lax.axis_size(axis)
    got = exchange(jnp.broadcast_to(x[None], (n,) + x.shape), axis)
    return got.reshape((n * x.shape[0],) + x.shape[1:])


def per_device(tokens, up_weight, down_weight, out_grads):
    core = lax.axis_index("core")
    first = core == 0
    rows, width = tokens.shape
    half = up_weight.shape[1] // 2
    n_row, n_z, n_rep = (lax.axis_size(a) for a in ("row", "z", "rep"))
    mine, theirs = core * half, (1 - core) * half

    def in_order(own, other, axis):
        return jnp.where(
            first,
            jnp.concatenate([own, other], axis),
            jnp.concatenate([other, own], axis),
        )

    up_own = lax.dynamic_slice_in_dim(up_weight, mine, half, 1)
    up_other = swap(lax.dynamic_slice_in_dim(up_weight, theirs, half, 1))
    down_keep = lax.dynamic_slice_in_dim(down_weight, mine, half, 0)
    down_other = swap(lax.dynamic_slice_in_dim(down_weight, theirs, half, 0))
    up = jnp.concatenate([up_own, up_other], 0)
    down = jnp.concatenate([down_keep, down_other], 1)

    tok_own = gather(tokens, "row")
    tok = jnp.concatenate([tok_own, swap(tok_own)], 1)
    total = tok.shape[0]
    share = total // n_z
    hid_part = dot(tok, up, (1, 0)).reshape(n_z, share, half)
    hid_part, out_grads = barrier((hid_part, out_grads))
    hid_terms = exchange(hid_part, "z")
    og_own = lax.all_gather(out_grads, "row", axis=0, tiled=True)
    og = jnp.concatenate([og_own, swap(og_own)], 1)
    ag_part = dot(og, down, (1, 1)).reshape(n_z, share, half)

    hidden = total_of(hid_terms)
    act = jax.nn.gelu(hidden).astype(bf16)
    padded = jnp.pad(act, ((0, share // 2), (0, 0)))
    padded, ag_part = barrier((padded, ag_part))
    act_all = lax.all_gather(padded, "z", axis=0, tiled=False)
    act_all = act_all[:, :share].reshape(total, half)
    act_grads = total_of(exchange(ag_part, "z"))
    hid_grads = gelu_pullback(hidden, act_grads).astype(bf16)
    hg = gather(hid_grads, "z")

    rep = lax.axis_index("rep")
    quarter = half // n_rep

    def shifted(x, k):
        return lax.ppermute(x, "rep", [(i, (i + k) % n_rep) for i in range(n_rep)])

    down_local = dot(act_all, og, (0, 0)).reshape(n_rep, quarter, 2 * width)
    terms = []
    for k in range(n_rep):
        block = lax.dynamic_index_in_dim(down_local, lax.rem(rep + k, n_rep), 0, False)
        terms.append(shifted(block, k) if k else block)
    terms, hg = barrier((terms, hg))
    down_sum = total_of(jnp.stack(terms)).astype(bf16)
    down_own, down_got = down_sum[:, :width], swap(down_sum[:, width:])
    down_pair = in_order(down_own[None], down_got[None], 0)
    down_grads = jnp.zeros((2, n_rep, quarter, width), bf16)
    for k in range(n_rep):
        got = shifted(down_pair, k) if k else down_pair
        source = lax.rem(rep + n_rep - k, n_rep)
        down_grads = lax.dynamic_update_slice_in_dim(down_grads, got[:, None], source, 1)
    down_grads = down_grads.reshape(2 * half, width)

    piece = width // n_rep
    up_local = dot(tok, hg, (0, 0)).reshape(2, n_rep, piece, half)
    up_sum = total_of(exchange(jnp.swapaxes(up_local, 0, 1), "rep")).astype(bf16)
    up_sum = jnp.where(first, up_sum, up_sum[::-1])
    up_send = jnp.broadcast_to(up_sum[:, None], (2, n_rep, piece, half))
    up_all = exchange(up_send.reshape(2 * n_rep, piece, half), ("core", "rep"))
    up_all = up_all.reshape(2, width, half)
    up_grads = jnp.concatenate([up_all[0], up_all[1]], 1)

    def output(left, weight, dims):
        part = dot(left, weight, dims)
        own, other = part[:, :width], swap(part[:, width:])
        return (own.astype(f32) + other.astype(f32)).astype(bf16)

    out = jnp.concatenate([output(act_all, down, (1, 0)), output(hg, up, (1, 1))], 1)
    out = lax.psum_scatter(out, "row", scatter_dimension=0, tiled=True)
    return (out[:, :width], out[:, width:], up_grads, down_grads)


def solution(mesh):
    n_row, n_col, n_rep = mesh.devices.shape
    split = Mesh(
        mesh.devices.reshape(n_row, n_col // 2, 2, n_rep), ("row", "z", "core", "rep")
    )
    col = ("z", "core")
    acts = P(("rep", "row"), col)
    up = P(col, "row")
    down = P("row", col)
    return jax.shard_map(
        per_device,
        mesh=split,
        in_specs=(acts, up, down, acts),
        out_specs=(acts, acts, up, down),
        check_vma=False,
    )
```

time: 222 us -> 230 us (1.036)
  blocking collectives: 121 us -> 54.3 us
  starting transfers between devices: 44.7 us -> 84.9 us
  waiting for transfers between devices: 29.3 us -> 48.7 us
  between operations: 1.2 us -> 14.5 us
  matrix products: 6.27 us -> 9.93 us
    all_to_all x3 -> x1, blocking collectives: 121 us -> 34.2 us  [exchange(): return lax.all_to_all(x, axis, 0, 0, tiled=False)]
    all_to_all x2 -> x5, starting transfers between devices: 7.69 us -> 30.8 us  [exchange(): return lax.all_to_all(x, axis, 0, 0, tiled=False)]
    all_gather x0 -> x1, blocking collectives: none -> 20 us  [per_device(): og_own = lax.all_gather(out_grads, 'row', axis=0, tiled=True)]
    ppermute x6, waiting for transfers between devices: 8.13 us -> 27.7 us  [shifted(): return lax.ppermute(x, 'rep', [(i, (i + k) % n_rep) for i in range(n_rep)])]
    ppermute x6 -> x7, starting transfers between devices: 18.4 us -> 33.4 us  [swap(): return lax.ppermute(x, 'core', [(0, 1), (1, 0)])]
    all_to_all x2 -> x5, waiting for transfers between devices: 19.3 us -> 13.8 us  [exchange(): return lax.all_to_all(x, axis, 0, 0, tiled=False)]
    dynamic_update_slice x6 -> x3, local copies, waits for them, and re-layouts: 5.04 us -> 0.15 us  [per_device(): lax.dynamic_update_slice_in_dim(down_grads, got[:, None], source, 1)]
    all_gather x0 -> x1, waiting for transfers between devices: none -> 4.64 us  [per_device(): act_all = lax.all_gather(padded, 'z', axis=0, tiled=False)]
  transfers between devices with their start and end apart: 14 -> 20, of which waited for: 3 -> 9; matrix products, arithmetic and copies ran while one was open for 8% -> 7% of each run, Pallas kernels for 0% -> 0%
where the time goes in v2:
time: 230 us; the launch traced here: 229 us
  starting transfers between devices  84.9 us (37%)
  blocking collectives  54.3 us (24%)
  waiting for transfers between devices  48.7 us (21%)
  between operations  14.5 us (6%)
  local copies, waits for them, and re-layouts  11.7 us (5%)
  matrix products  9.93 us (4%)
  other arithmetic  5.2 us (2%)
    all_to_all x1, blocking collectives, exchange(): return lax.all_to_all(x, axis, 0, 0, tiled=False)  34.2 us
    ppermute x7, starting transfers between devices, swap(): return lax.ppermute(x, 'core', [(0, 1), (1, 0)])  33.4 us
    all_to_all x5, starting transfers between devices, exchange(): return lax.all_to_all(x, axis, 0, 0, tiled=False)  30.8 us
    ppermute x6, waiting for transfers between devices, shifted(): return lax.ppermute(x, 'rep', [(i, (i + k) % n_rep) for i in range(n_rep)])  27.7 us
    ppermute x6, starting transfers between devices, shifted(): return lax.ppermute(x, 'rep', [(i, (i + k) % n_rep) for i in range(n_rep)])  20.8 us
    all_gather x1, blocking collectives, per_device(): og_own = lax.all_gather(out_grads, 'row', axis=0, tiled=True)  20 us
    all_to_all x5, waiting for transfers between devices, exchange(): return lax.all_to_all(x, axis, 0, 0, tiled=False)  13.8 us
    dot_general x6, matrix products, dot(): lax.dot_general(left, right, ((dims[:1], dims[1:]), ((), ())), preferred_...  9.93 us
  transfers between devices with their start and end apart: 20, of which 9 were waited for; matrix products, arithmetic and copies ran while one was open for 7% of the time, Pallas kernels for 0%

profile of v2, /device:TPU:1, one launch (start us, length us, event | category | flops | bytes accessed | tf_op | source)
XLA Modules:
  0.0 229.2 jit_solution(12078744507927852584)
XLA Ops:
  7.2 1.7 broadcast_in_dim.39
  8.8 7.7 %all-to-all-start = ((bf16[8,64,384]{2,1,0:T(8,128)(2,1)}), bf16[8,64,384]{2,1,0:T(8,128)(2,1)S(1)}, u32[]{:S(2)}, u32[]{:S(2)}) async-start(bf16[8,64,384]{2,1,0:T(8,128)(2,1)} %broadcast_in_dim.39), calls=%async_computation | async-start | bytes 786432 | tf_op jit(solution)/shard_map/all_to_all | solution.py:27
  16.5 0.1 constant_dynamic-slice_fusion.3
  16.6 4.6 %collective-permute-start.1 = (bf16[384,768]{1,0:T(8,128)(2,1)S(1)}, bf16[384,768]{1,0:T(8,128)(2,1)S(1)}, u32[]{:S(2)}, u32[]{:S(2)}) collective-permute-start(bf16[384,768]{1,0:T(8,128)(2,1)S(1)} %get-tuple-element.33), channel_id=1, source_target_pairs={{0,4},{4,0},{1,5},{5,1},{2,6},{6,2},{3,7},{7,3},{8,12},{12,8},{9,1... | collective-permute-start | bytes 1769480 | tf_op jit(solution)/shard_map/ppermute | solution.py:23
  21.2 6.9 %all-to-all-done = bf16[8,64,384]{2,1,0:T(8,128)(2,1)S(1)} async-done(((bf16[8,64,384]{2,1,0:T(8,128)(2,1)}), bf16[8,64,384]{2,1,0:T(8,128)(2,1)S(1)}, u32[]{:S(2)}, u32[]{:S(2)}) %all-to-all-start) | async-done | bytes 393248 | tf_op jit(solution)/shard_map/all_to_all | solution.py:27
  28.1 5.9 %collective-permute-start = (bf16[512,384]{1,0:T(8,128)(2,1)S(1)}, bf16[512,384]{1,0:T(8,128)(2,1)S(1)}, u32[]{:S(2)}, u32[]{:S(2)}) collective-permute-start(bf16[512,384]{1,0:T(8,128)(2,1)S(1)} %bitcast.64), channel_id=1, source_target_pairs={{0,4},{4,0},{1,5},{5,1},{2,6},{6,2},{3,7},{7,3},{8,12},{12,8},{9,1... | collective-permute-start | bytes 1179656 | tf_op jit(solution)/shard_map/ppermute | solution.py:23
  34.1 1.3 collective-permute-done
  35.4 1.7 convolution_convert_fusion.5
  37.0 10.2 %all-to-all-start.1 = ((bf16[8,64,768]{2,1,0:T(8,128)(2,1)}), bf16[8,64,768]{2,1,0:T(8,128)(2,1)S(1)}, u32[]{:S(2)}, u32[]{:S(2)}) async-start(bf16[8,64,768]{2,1,0:T(8,128)(2,1)} %bitcast.1), calls=%async_computation.1 | async-start | bytes 1572864 | tf_op jit(solution)/shard_map/all_to_all | solution.py:27
  47.2 0.0 all-gather.3.cloned.1.call-start
  47.3 0.1 constant_dynamic-slice_fusion.1
  47.4 2.6 %collective-permute-start.3 = (bf16[768,384]{1,0:T(8,128)(2,1)S(1)}, bf16[768,384]{1,0:T(8,128)(2,1)}, u32[]{:S(2)}, u32[]{:S(2)}) collective-permute-start(bf16[768,384]{1,0:T(8,128)(2,1)S(1)} %get-tuple-element.31), channel_id=1, source_target_pairs={{0,4},{4,0},{1,5},{5,1},{2,6},{6,2},{3,7},{7,3},{8,12},{12,8},{9,1... | collective-permute-start | bytes 1769480 | tf_op jit(solution)/shard_map/ppermute | solution.py:23
  50.0 20.0 %all_gather.9 = bf16[512,384]{1,0:T(8,128)(2,1)S(1)} all-gather(bf16[64,384]{1,0:T(8,128)(2,1)S(1)} %copy-done.9), channel_id=1, replica_groups=mesh['row'=8,'z'=8,'core'=2,'rep'=4] {'row'}, dimensions={0}, use_global_device_ids=true | all-gather | bytes 442368 | tf_op jit(solution)/shard_map/all_gather | solution.py:72
  70.1 7.1 %collective-permute-start.2 = (bf16[512,384]{1,0:T(8,128)(2,1)S(1)}, bf16[512,384]{1,0:T(8,128)(2,1)S(1)}, u32[]{:S(2)}, u32[]{:S(2)}) collective-permute-start(bf16[512,384]{1,0:T(8,128)(2,1)S(1)} %all_gather.9), channel_id=1, source_target_pairs={{0,4},{4,0},{1,5},{5,1},{2,6},{6,2},{3,7},{7,3},{8,12},{12,8},{9,1... | collective-permute-start | bytes 1179656 | tf_op jit(solution)/shard_map/ppermute | solution.py:23
  77.2 1.3 collective-permute-done.2
  78.5 0.1 constant_dynamic-update-slice_fusion
  78.6 0.9 copy-done.7
  79.5 1.9 convolution_convert_fusion.4
  81.4 0.2 fusion.16
  81.5 0.7 pad.4
  82.2 0.0 all-gather.3.cloned.1.call-update
  82.2 34.2 %all_to_all.30 = bf16[8,64,768]{2,1,0:T(8,128)(2,1)S(1)} all-to-all(bf16[8,64,768]{2,1,0:T(8,128)(2,1)S(1)} %bitcast.58), channel_id=1, replica_groups=mesh['row'=8,'z'=8,'core'=2,'rep'=4] {'z'}, dimensions={0} | all-to-all | bytes 1572864 | tf_op jit(solution)/shard_map/all_to_all | solution.py:27
  116.4 0.2 fusion.17
  116.7 0.9 broadcast_in_dim.41
  117.6 3.5 %all-to-all-start.3 = ((bf16[8,64,768]{2,1,0:T(8,128)(2,1)}), bf16[8,64,768]{2,1,0:T(8,128)(2,1)S(1)}, u32[]{:S(2)}, u32[]{:S(2)}) async-start(bf16[8,64,768]{2,1,0:T(8,128)(2,1)} %broadcast_in_dim.41), calls=%async_computation.3 | async-start | bytes 1572864 | tf_op jit(solution)/shard_map/all_to_all | solution.py:27
  121.2 4.6 %all-gather.3.cloned.1.call-done = bf16[768,768]{1,0:T(8,128)(2,1)} async-done(((bf16[96,768]{1,0:T(8,128)(2,1)}), bf16[768,768]{1,0:T(8,128)(2,1)}) %all-gather.3.cloned.1.call-update) | async-done | bytes 1179664 | tf_op jit(solution)/shard_map/all_gather | solution.py:80
  125.9 1.2 slice.134
  127.1 1.9 convolution_convert_fusion.3
  129.0 8.6 %collective-permute-start.4 = (bf16[512,384]{1,0:T(8,128)(2,1)S(1)}, bf16[512,384]{1,0:T(8,128)(2,1)}, u32[]{:S(2)}, u32[]{:S(2)}) collective-permute-start(bf16[512,384]{1,0:T(8,128)(2,1)S(1)} %slice.136), channel_id=1, source_target_pairs={{0,4},{4,0},{1,5},{5,1},{2,6},{6,2},{3,7},{7,3},{8,12},{12,8},{9,1... | collective-permute-start | bytes 1179656 | tf_op jit(solution)/shard_map/ppermute | solution.py:23
  137.6 0.8 convolution_convert_fusion.1
  138.4 1.0 dynamic-slice_bitcast_fusion
  139.4 2.9 %collective-permute-start.5 = (bf16[192,768]{1,0:T(8,128)(2,1)}, bf16[192,768]{1,0:T(8,128)(2,1)S(1)}, u32[]{:S(2)}, u32[]{:S(2)}) collective-permute-start(bf16[192,768]{1,0:T(8,128)(2,1)} %get-tuple-element.28), channel_id=1, source_target_pairs={{0,1},{1,2},{2,3},{3,0},{4,5},{5,6},{6,7},{7,4},{8,9},{9,10},{10,1... | collective-permute-start | bytes 884744 | tf_op jit(solution)/shard_map/ppermute | solution.py:90
  142.3 3.2 %collective-permute-start.6 = (bf16[192,768]{1,0:T(8,128)(2,1)}, bf16[192,768]{1,0:T(8,128)(2,1)}, u32[]{:S(2)}, u32[]{:S(2)}) collective-permute-start(bf16[192,768]{1,0:T(8,128)(2,1)} %get-tuple-element.27), channel_id=1, source_target_pairs={{0,2},{1,3},{2,0},{3,1},{4,6},{5,7},{6,4},{7,5},{8,10},{9,11},{10,... | collective-permute-start | bytes 884744 | tf_op jit(solution)/shard_map/ppermute | solution.py:90
  145.5 4.0 %collective-permute-start.7 = (bf16[192,768]{1,0:T(8,128)(2,1)}, bf16[192,768]{1,0:T(8,128)(2,1)}, u32[]{:S(2)}, u32[]{:S(2)}) collective-permute-start(bf16[192,768]{1,0:T(8,128)(2,1)} %get-tuple-element.26), channel_id=1, source_target_pairs={{0,3},{1,0},{2,1},{3,2},{4,7},{5,4},{6,5},{7,6},{8,11},{9,8},{10,9... | collective-permute-start | bytes 884744 | tf_op jit(solution)/shard_map/ppermute | solution.py:90
  149.5 1.1 add_convert_fusion.1
  150.6 7.2 %collective-permute-done.5 = bf16[192,768]{1,0:T(8,128)(2,1)S(1)} collective-permute-done((bf16[192,768]{1,0:T(8,128)(2,1)}, bf16[192,768]{1,0:T(8,128)(2,1)S(1)}, u32[]{:S(2)}, u32[]{:S(2)}) %collective-permute-start.5) | collective-permute-done | bytes 294944 | tf_op jit(solution)/shard_map/ppermute | solution.py:90
  157.8 2.3 collective-permute-done.7
  160.1 1.8 convolution_convert_fusion
  161.9 1.1 copy.14
  163.0 4.2 %all-to-all-start.4 = ((bf16[4,2,96,768]{3,2,1,0:T(8,128)(2,1)}), bf16[4,2,96,768]{3,2,1,0:T(8,128)(2,1)S(1)}, u32[]{:S(2)}, u32[]{:S(2)}) async-start(bf16[4,2,96,768]{3,2,1,0:T(8,128)(2,1)} %bitcast.50), calls=%async_computation.5 | async-start | bytes 2359296 | tf_op jit(solution)/shard_map/all_to_all | solution.py:27
  167.3 1.9 convolution_convert_fusion.2
  169.2 2.7 %collective-permute-start.8 = (bf16[512,384]{1,0:T(8,128)(2,1)S(1)}, bf16[512,384]{1,0:T(8,128)(2,1)S(1)}, u32[]{:S(2)}, u32[]{:S(2)}) collective-permute-start(bf16[512,384]{1,0:T(8,128)(2,1)S(1)} %slice.146), channel_id=1, source_target_pairs={{0,4},{4,0},{1,5},{5,1},{2,6},{6,2},{3,7},{7,3},{8,12},{12,8},{9,1... | collective-permute-start | bytes 1179656 | tf_op jit(solution)/shard_map/ppermute | solution.py:23
  171.9 1.2 add_convert_fusion.2
  173.1 1.9 collective-permute-start.9
  175.1 0.1 add_convert_fusion
  175.2 1.0 pad_maximum_fusion.4
  176.1 0.0 reduce-scatter.2.cloned.1.call-update
  176.2 6.9 %all-to-all-done.4 = bf16[4,2,96,768]{3,2,1,0:T(8,128)(2,1)S(1)} async-done(((bf16[4,2,96,768]{3,2,1,0:T(8,128)(2,1)}), bf16[4,2,96,768]{3,2,1,0:T(8,128)(2,1)S(1)}, u32[]{:S(2)}, u32[]{:S(2)}) %all-to-all-start.4) | async-done | bytes 1179680 | tf_op jit(solution)/shard_map/all_to_all | solution.py:27
  183.0 0.1 fusion
  183.2 0.1 reverse_select_fusion
  183.3 1.1 broadcast_in_dim.42
  184.4 5.1 %all-to-all-start.5 = ((bf16[8,96,768]{2,1,0:T(8,128)(2,1)}), bf16[8,96,768]{2,1,0:T(8,128)(2,1)S(1)}, u32[]{:S(2)}, u32[]{:S(2)}) async-start(bf16[8,96,768]{2,1,0:T(8,128)(2,1)} %bitcast.16), calls=%async_computation.6 | async-start | bytes 2359296 | tf_op jit(solution)/shard_map/all_to_all | solution.py:27
  189.6 3.3 %collective-permute-start.10 = (bf16[2,192,384]{2,1,0:T(8,128)(2,1)S(1)}, bf16[2,192,384]{2,1,0:T(8,128)(2,1)S(1)}, u32[]{:S(2)}, u32[]{:S(2)}) collective-permute-start(bf16[2,192,384]{2,1,0:T(8,128)(2,1)S(1)} %maximum_select_fusion.1), channel_id=1, source_target_pairs={{0,1},{1,2},{2,3},{3,0},{4,5},{5,6},{6,7},{7,4},{8,9},{9,10},{10,1... | collective-permute-start | bytes 884744 | tf_op jit(solution)/shard_map/ppermute | solution.py:90
  192.8 4.3 %collective-permute-start.11 = (bf16[2,192,384]{2,1,0:T(8,128)(2,1)S(1)}, bf16[2,192,384]{2,1,0:T(8,128)(2,1)S(1)}, u32[]{:S(2)}, u32[]{:S(2)}) collective-permute-start(bf16[2,192,384]{2,1,0:T(8,128)(2,1)S(1)} %maximum_select_fusion.1), channel_id=1, source_target_pairs={{0,2},{1,3},{2,0},{3,1},{4,6},{5,7},{6,4},{7,5},{8,10},{9,11},{10,... | collective-permute-start | bytes 884744 | tf_op jit(solution)/shard_map/ppermute | solution.py:90
  197.2 3.1 %collective-permute-start.12 = (bf16[2,192,384]{2,1,0:T(8,128)(2,1)S(1)}, bf16[2,192,384]{2,1,0:T(8,128)(2,1)S(1)}, u32[]{:S(2)}, u32[]{:S(2)}) collective-permute-start(bf16[2,192,384]{2,1,0:T(8,128)(2,1)S(1)} %maximum_select_fusion.1), channel_id=1, source_target_pairs={{0,3},{1,0},{2,1},{3,2},{4,7},{5,4},{6,5},{7,6},{8,11},{9,8},{10,9... | collective-permute-start | bytes 884744 | tf_op jit(solution)/shard_map/ppermute | solution.py:90
  200.3 0.1 broadcast_in_dim.43
  200.4 0.1 fusion.1
  200.5 11.8 %collective-permute-done.10 = bf16[2,192,384]{2,1,0:T(8,128)(2,1)S(1)} collective-permute-done((bf16[2,192,384]{2,1,0:T(8,128)(2,1)S(1)}, bf16[2,192,384]{2,1,0:T(8,128)(2,1)S(1)}, u32[]{:S(2)}, u32[]{:S(2)}) %collective-permute-start.10) | collective-permute-done | bytes 294944 | tf_op jit(solution)/shard_map/ppermute | solution.py:90
  212.3 6.4 %collective-permute-done.11 = bf16[2,192,384]{2,1,0:T(8,128)(2,1)S(1)} collective-permute-done((bf16[2,192,384]{2,1,0:T(8,128)(2,1)S(1)}, bf16[2,192,384]{2,1,0:T(8,128)(2,1)S(1)}, u32[]{:S(2)}, u32[]{:S(2)}) %collective-permute-start.11) | collective-permute-done | bytes 294944 | tf_op jit(solution)/shard_map/ppermute | solution.py:90
  218.8 0.1 bitcast_dynamic-update-slice_fusion.2
  218.8 0.1 fusion.23
  218.9 0.9 copy-done.2
  219.8 1.1 pad_maximum_fusion.2
  220.9 1.5 fusion.24
  (41 shorter events, 0.4 us)
Async XLA Ops:
  7.2 9.3 %copy-start = (bf16[384,1536]{1,0:T(8,128)(2,1)S(1)}, bf16[384,1536]{1,0:T(8,128)(2,1)}, u32[]{:S(2)}) copy-start(bf16[384,1536]{1,0:T(8,128)(2,1)} %param.5) | copy-start | bytes 3538948
  8.8 19.3 %all-to-all-start = ((bf16[8,64,384]{2,1,0:T(8,128)(2,1)}), bf16[8,64,384]{2,1,0:T(8,128)(2,1)S(1)}, u32[]{:S(2)}, u32[]{:S(2)}) async-start(bf16[8,64,384]{2,1,0:T(8,128)(2,1)} %broadcast_in_dim.39), calls=%async_computation | async-start | bytes 786432 | tf_op jit(solution)/shard_map/all_to_all | solution.py:27
  16.6 17.5 %collective-permute-start.1 = (bf16[384,768]{1,0:T(8,128)(2,1)S(1)}, bf16[384,768]{1,0:T(8,128)(2,1)S(1)}, u32[]{:S(2)}, u32[]{:S(2)}) collective-permute-start(bf16[384,768]{1,0:T(8,128)(2,1)S(1)} %get-tuple-element.33), channel_id=1, source_target_pairs={{0,4},{4,0},{1,5},{5,1},{2,6},{6,2},{3,7},{7,3},{8,12},{12,8},{9,1... | collective-permute-start | bytes 1769480 | tf_op jit(solution)/shard_map/ppermute | solution.py:23
  28.1 7.3 %copy-start.5 = (bf16[8,64,384]{2,1,0:T(8,128)(2,1)}, bf16[8,64,384]{2,1,0:T(8,128)(2,1)S(1)}, u32[]{:S(2)}) copy-start(bf16[8,64,384]{2,1,0:T(8,128)(2,1)S(1)} %all-to-all-done) | copy-start | bytes 1179652
  28.1 7.2 %collective-permute-start = (bf16[512,384]{1,0:T(8,128)(2,1)S(1)}, bf16[512,384]{1,0:T(8,128)(2,1)S(1)}, u32[]{:S(2)}, u32[]{:S(2)}) collective-permute-start(bf16[512,384]{1,0:T(8,128)(2,1)S(1)} %bitcast.64), channel_id=1, source_target_pairs={{0,4},{4,0},{1,5},{5,1},{2,6},{6,2},{3,7},{7,3},{8,12},{12,8},{9,1... | collective-permute-start | bytes 1179656 | tf_op jit(solution)/shard_map/ppermute | solution.py:23
  34.1 3.0 %copy-start.10 = (bf16[384,768]{1,0:T(8,128)(2,1)}, bf16[384,768]{1,0:T(8,128)(2,1)S(1)}, u32[]{:S(2)}) copy-start(bf16[384,768]{1,0:T(8,128)(2,1)S(1)} %collective-permute-done.1) | copy-start | bytes 1769476
  35.4 1.7 copy-start.11
  37.0 10.2 %copy-start.1 = (bf16[1536,384]{1,0:T(8,128)(2,1)S(1)}, bf16[1536,384]{1,0:T(8,128)(2,1)}, u32[]{:S(2)}) copy-start(bf16[1536,384]{1,0:T(8,128)(2,1)} %param.6) | copy-start | bytes 3538948
  37.0 44.3 %all-to-all-start.1 = ((bf16[8,64,768]{2,1,0:T(8,128)(2,1)}), bf16[8,64,768]{2,1,0:T(8,128)(2,1)S(1)}, u32[]{:S(2)}, u32[]{:S(2)}) async-start(bf16[8,64,768]{2,1,0:T(8,128)(2,1)} %bitcast.1), calls=%async_computation.1 | async-start | bytes 1572864 | tf_op jit(solution)/shard_map/all_to_all | solution.py:27
  47.2 2.8 %copy-start.9 = (bf16[64,384]{1,0:T(8,128)(2,1)S(1)}, bf16[64,384]{1,0:T(8,128)(2,1)}, u32[]{:S(2)}) copy-start(bf16[64,384]{1,0:T(8,128)(2,1)} %param.7) | copy-start | bytes 147460
  47.2 78.6 %all-gather.3.cloned.1.call-start = ((), (), s32[]{:S(2)}) async-start(), calls=%async_computation.8 | async-start | bytes 1327104 | tf_op jit(solution)/shard_map/all_gather | solution.py:80
  47.4 33.9 %copy-start.3 = (bf16[768,384]{1,0:T(8,128)(2,1)}, bf16[768,384]{1,0:T(8,128)(2,1)S(1)}, u32[]{:S(2)}) copy-start(bf16[768,384]{1,0:T(8,128)(2,1)S(1)} %get-tuple-element.30) | copy-start | bytes 1769476
  47.4 31.2 %collective-permute-start.3 = (bf16[768,384]{1,0:T(8,128)(2,1)S(1)}, bf16[768,384]{1,0:T(8,128)(2,1)}, u32[]{:S(2)}, u32[]{:S(2)}) collective-permute-start(bf16[768,384]{1,0:T(8,128)(2,1)S(1)} %get-tuple-element.31), channel_id=1, source_target_pairs={{0,4},{4,0},{1,5},{5,1},{2,6},{6,2},{3,7},{7,3},{8,12},{12,8},{9,1... | collective-permute-start | bytes 1769480 | tf_op jit(solution)/shard_map/ppermute | solution.py:23
  70.1 8.4 %collective-permute-start.2 = (bf16[512,384]{1,0:T(8,128)(2,1)S(1)}, bf16[512,384]{1,0:T(8,128)(2,1)S(1)}, u32[]{:S(2)}, u32[]{:S(2)}) collective-permute-start(bf16[512,384]{1,0:T(8,128)(2,1)S(1)} %all_gather.9), channel_id=1, source_target_pairs={{0,4},{4,0},{1,5},{5,1},{2,6},{6,2},{3,7},{7,3},{8,12},{12,8},{9,1... | collective-permute-start | bytes 1179656 | tf_op jit(solution)/shard_map/ppermute | solution.py:23
  78.6 0.9 copy-start.7
  117.6 42.5 %all-to-all-start.3 = ((bf16[8,64,768]{2,1,0:T(8,128)(2,1)}), bf16[8,64,768]{2,1,0:T(8,128)(2,1)S(1)}, u32[]{:S(2)}, u32[]{:S(2)}) async-start(bf16[8,64,768]{2,1,0:T(8,128)(2,1)} %broadcast_in_dim.41), calls=%async_computation.3 | async-start | bytes 1572864 | tf_op jit(solution)/shard_map/all_to_all | solution.py:27
  121.2 5.9 %copy-start.4 = (bf16[768,384]{1,0:T(8,128)(2,1)S(1)}, bf16[768,384]{1,0:T(8,128)(2,1)}, u32[]{:S(2)}) copy-start(bf16[768,384]{1,0:T(8,128)(2,1)} %copy-done.3) | copy-start | bytes 1769476
  127.1 10.6 %copy-start.8 = (bf16[512,768]{1,0:T(8,128)(2,1)S(1)}, bf16[512,768]{1,0:T(8,128)(2,1)}, u32[]{:S(2)}) copy-start(bf16[512,768]{1,0:T(8,128)(2,1)} %copy-done.7) | copy-start | bytes 2359300
  129.0 20.5 %collective-permute-start.4 = (bf16[512,384]{1,0:T(8,128)(2,1)S(1)}, bf16[512,384]{1,0:T(8,128)(2,1)}, u32[]{:S(2)}, u32[]{:S(2)}) collective-permute-start(bf16[512,384]{1,0:T(8,128)(2,1)S(1)} %slice.136), channel_id=1, source_target_pairs={{0,4},{4,0},{1,5},{5,1},{2,6},{6,2},{3,7},{7,3},{8,12},{12,8},{9,1... | collective-permute-start | bytes 1179656 | tf_op jit(solution)/shard_map/ppermute | solution.py:23
  139.4 20.7 %copy-start.6 = (bf16[8,64,384]{2,1,0:T(8,128)(2,1)S(1)}, bf16[8,64,384]{2,1,0:T(8,128)(2,1)}, u32[]{:S(2)}) copy-start(bf16[8,64,384]{2,1,0:T(8,128)(2,1)} %copy-done.5) | copy-start | bytes 1179652
  139.4 18.4 %collective-permute-start.5 = (bf16[192,768]{1,0:T(8,128)(2,1)}, bf16[192,768]{1,0:T(8,128)(2,1)S(1)}, u32[]{:S(2)}, u32[]{:S(2)}) collective-permute-start(bf16[192,768]{1,0:T(8,128)(2,1)} %get-tuple-element.28), channel_id=1, source_target_pairs={{0,1},{1,2},{2,3},{3,0},{4,5},{5,6},{6,7},{7,4},{8,9},{9,10},{10,1... | collective-permute-start | bytes 884744 | tf_op jit(solution)/shard_map/ppermute | solution.py:90
  142.3 15.5 %collective-permute-start.6 = (bf16[192,768]{1,0:T(8,128)(2,1)}, bf16[192,768]{1,0:T(8,128)(2,1)}, u32[]{:S(2)}, u32[]{:S(2)}) collective-permute-start(bf16[192,768]{1,0:T(8,128)(2,1)} %get-tuple-element.27), channel_id=1, source_target_pairs={{0,2},{1,3},{2,0},{3,1},{4,6},{5,7},{6,4},{7,5},{8,10},{9,11},{10,... | collective-permute-start | bytes 884744 | tf_op jit(solution)/shard_map/ppermute | solution.py:90
  145.5 14.6 %collective-permute-start.7 = (bf16[192,768]{1,0:T(8,128)(2,1)}, bf16[192,768]{1,0:T(8,128)(2,1)}, u32[]{:S(2)}, u32[]{:S(2)}) collective-permute-start(bf16[192,768]{1,0:T(8,128)(2,1)} %get-tuple-element.26), channel_id=1, source_target_pairs={{0,3},{1,0},{2,1},{3,2},{4,7},{5,4},{6,5},{7,6},{8,11},{9,8},{10,9... | collective-permute-start | bytes 884744 | tf_op jit(solution)/shard_map/ppermute | solution.py:90
  163.0 20.0 %all-to-all-start.4 = ((bf16[4,2,96,768]{3,2,1,0:T(8,128)(2,1)}), bf16[4,2,96,768]{3,2,1,0:T(8,128)(2,1)S(1)}, u32[]{:S(2)}, u32[]{:S(2)}) async-start(bf16[4,2,96,768]{3,2,1,0:T(8,128)(2,1)} %bitcast.50), calls=%async_computation.5 | async-start | bytes 2359296 | tf_op jit(solution)/shard_map/all_to_all | solution.py:27
  167.3 53.7 %reduce-scatter.2.cloned.1.call-start = ((), (), s32[]{:S(2)}) async-start(), calls=%async_computation.7 | async-start | bytes 884736 | tf_op jit(solution)/shard_map/reduce_scatter | solution.py:123
  169.2 5.9 %collective-permute-start.8 = (bf16[512,384]{1,0:T(8,128)(2,1)S(1)}, bf16[512,384]{1,0:T(8,128)(2,1)S(1)}, u32[]{:S(2)}, u32[]{:S(2)}) collective-permute-start(bf16[512,384]{1,0:T(8,128)(2,1)S(1)} %slice.146), channel_id=1, source_target_pairs={{0,4},{4,0},{1,5},{5,1},{2,6},{6,2},{3,7},{7,3},{8,12},{12,8},{9,1... | collective-permute-start | bytes 1179656 | tf_op jit(solution)/shard_map/ppermute | solution.py:23
  173.1 16.4 %collective-permute-start.9 = (bf16[192,384]{1,0:T(8,128)(2,1)S(1)}, bf16[192,384]{1,0:T(8,128)(2,1)S(1)}, u32[]{:S(2)}, u32[]{:S(2)}) collective-permute-start(bf16[192,384]{1,0:T(8,128)(2,1)S(1)} %get-tuple-element.35), channel_id=1, source_target_pairs={{0,4},{4,0},{1,5},{5,1},{2,6},{6,2},{3,7},{7,3},{8,12},{12,8},{9,1... | collective-permute-start | bytes 442376 | tf_op jit(solution)/shard_map/ppermute | solution.py:23
  184.4 34.5 %all-to-all-start.5 = ((bf16[8,96,768]{2,1,0:T(8,128)(2,1)}), bf16[8,96,768]{2,1,0:T(8,128)(2,1)S(1)}, u32[]{:S(2)}, u32[]{:S(2)}) async-start(bf16[8,96,768]{2,1,0:T(8,128)(2,1)} %bitcast.16), calls=%async_computation.6 | async-start | bytes 2359296 | tf_op jit(solution)/shard_map/all_to_all | solution.py:27
  189.6 22.7 %collective-permute-start.10 = (bf16[2,192,384]{2,1,0:T(8,128)(2,1)S(1)}, bf16[2,192,384]{2,1,0:T(8,128)(2,1)S(1)}, u32[]{:S(2)}, u32[]{:S(2)}) collective-permute-start(bf16[2,192,384]{2,1,0:T(8,128)(2,1)S(1)} %maximum_select_fusion.1), channel_id=1, source_target_pairs={{0,1},{1,2},{2,3},{3,0},{4,5},{5,6},{6,7},{7,4},{8,9},{9,10},{10,1... | collective-permute-start | bytes 884744 | tf_op jit(solution)/shard_map/ppermute | solution.py:90
  192.8 25.8 %collective-permute-start.11 = (bf16[2,192,384]{2,1,0:T(8,128)(2,1)S(1)}, bf16[2,192,384]{2,1,0:T(8,128)(2,1)S(1)}, u32[]{:S(2)}, u32[]{:S(2)}) collective-permute-start(bf16[2,192,384]{2,1,0:T(8,128)(2,1)S(1)} %maximum_select_fusion.1), channel_id=1, source_target_pairs={{0,2},{1,3},{2,0},{3,1},{4,6},{5,7},{6,4},{7,5},{8,10},{9,11},{10,... | collective-permute-start | bytes 884744 | tf_op jit(solution)/shard_map/ppermute | solution.py:90
  197.2 21.6 %collective-permute-start.12 = (bf16[2,192,384]{2,1,0:T(8,128)(2,1)S(1)}, bf16[2,192,384]{2,1,0:T(8,128)(2,1)S(1)}, u32[]{:S(2)}, u32[]{:S(2)}) collective-permute-start(bf16[2,192,384]{2,1,0:T(8,128)(2,1)S(1)} %maximum_select_fusion.1), channel_id=1, source_target_pairs={{0,3},{1,0},{2,1},{3,2},{4,7},{5,4},{6,5},{7,6},{8,11},{9,8},{10,9... | collective-permute-start | bytes 884744 | tf_op jit(solution)/shard_map/ppermute | solution.py:90
  218.8 1.0 copy-start.2
Sparse Core Ops, SparseCore 0:
  82.4 43.4 all-gather.2
  176.3 33.1 reduce-scatter.1

commit v3 on v2

--- a/solution.py
+++ b/solution.py
@@ -62,25 +62,20 @@
     up = jnp.concatenate([up_own, up_other], 0)
     down = jnp.concatenate([down_keep, down_other], 1)
 
-    tok_own = gather(tokens, "row")
-    tok = jnp.concatenate([tok_own, swap(tok_own)], 1)
+    own = gather(jnp.concatenate([tokens, out_grads], 1), "row")
+    other = swap(own)
+    tok = jnp.concatenate([own[:, :width], other[:, :width]], 1)
+    og = jnp.concatenate([own[:, width:], other[:, width:]], 1)
     total = tok.shape[0]
     share = total // n_z
+    ag_part = dot(og, down, (1, 1))
+    act_grads = lax.psum_scatter(ag_part, "z", scatter_dimension=0, tiled=True)
     hid_part = dot(tok, up, (1, 0)).reshape(n_z, share, half)
-    hid_part, out_grads = barrier((hid_part, out_grads))
-    hid_terms = exchange(hid_part, "z")
-    og_own = lax.all_gather(out_grads, "row", axis=0, tiled=True)
-    og = jnp.concatenate([og_own, swap(og_own)], 1)
-    ag_part = dot(og, down, (1, 1)).reshape(n_z, share, half)
-
-    hidden = total_of(hid_terms)
+    hidden = total_of(exchange(hid_part, "z"))
     act = jax.nn.gelu(hidden).astype(bf16)
-    padded = jnp.pad(act, ((0, share // 2), (0, 0)))
-    padded, ag_part = barrier((padded, ag_part))
-    act_all = lax.all_gather(padded, "z", axis=0, tiled=False)
-    act_all = act_all[:, :share].reshape(total, half)
-    act_grads = total_of(exchange(ag_part, "z"))
-    hid_grads = gelu_pullback(hidden, act_grads).astype(bf16)
+    act_all = gather(act, "z")
+    act_grads, act_all = barrier((act_grads, act_all))
+    hid_grads = gelu_pullback(hidden, act_grads.astype(f32)).astype(bf16)
     hg = gather(hid_grads, "z")
 
     rep = lax.axis_index("rep")
@@ -94,7 +89,6 @@
     for k in range(n_rep):
         block = lax.dynamic_index_in_dim(down_local, lax.rem(rep + k, n_rep), 0, False)
         terms.append(shifted(block, k) if k else block)
-    terms, hg = barrier((terms, hg))
     down_sum = total_of(jnp.stack(terms)).astype(bf16)
     down_own, down_got = down_sum[:, :width], swap(down_sum[:, width:])
     down_pair = in_order(down_own[None], down_got[None], 0)

time: 230 us -> 212 us (0.922)
  blocking collectives: 54.3 us -> 27.9 us
  waiting for transfers between devices: 48.7 us -> 73.5 us
  starting transfers between devices: 84.9 us -> 67.3 us
  local copies, waits for them, and re-layouts: 11.7 us -> 9.16 us
    all_gather x1 -> x0, blocking collectives: 20 us -> none  [per_device(): og_own = lax.all_gather(out_grads, 'row', axis=0, tiled=True)]
    reduce_scatter x0 -> x1, waiting for transfers between devices: none -> 18.8 us  [per_device(): act_grads = lax.psum_scatter(ag_part, 'z', scatter_dimension=0, tiled=True)]
    all_to_all x5, waiting for transfers between devices: 13.8 us -> 27.2 us  [exchange(): return lax.all_to_all(x, axis, 0, 0, tiled=False)]
    ppermute x7 -> x6, starting transfers between devices: 33.4 us -> 20.3 us  [swap(): return lax.ppermute(x, 'core', [(0, 1), (1, 0)])]
    all_to_all x1, blocking collectives: 34.2 us -> 27.9 us  [exchange(): return lax.all_to_all(x, axis, 0, 0, tiled=False)]
    all_gather x1 -> x0, waiting for transfers between devices: 4.64 us -> none  [per_device(): act_all = lax.all_gather(padded, 'z', axis=0, tiled=False)]
    all_to_all x5, starting transfers between devices: 30.8 us -> 26.9 us  [exchange(): return lax.all_to_all(x, axis, 0, 0, tiled=False)]
    ppermute x6, waiting for transfers between devices: 27.7 us -> 24 us  [shifted(): return lax.ppermute(x, 'rep', [(i, (i + k) % n_rep) for i in range(n_rep)])]
  transfers between devices with their start and end apart: 20 -> 19, of which waited for: 9 -> 9; matrix products, arithmetic and copies ran while one was open for 7% -> 10% of each run, Pallas kernels for 0% -> 0%
where the time goes in v3:
time: 212 us; the launch traced here: 210 us
  waiting for transfers between devices  73.5 us (35%)
  starting transfers between devices  67.3 us (32%)
  blocking collectives  27.9 us (13%)
  between operations  14.5 us (7%)
  matrix products  11.1 us (5%)
  local copies, waits for them, and re-layouts  9.16 us (4%)
  other arithmetic  6.93 us (3%)
    all_to_all x1, blocking collectives, exchange(): return lax.all_to_all(x, axis, 0, 0, tiled=False)  27.9 us
    all_to_all x5, waiting for transfers between devices, exchange(): return lax.all_to_all(x, axis, 0, 0, tiled=False)  27.2 us
    all_to_all x5, starting transfers between devices, exchange(): return lax.all_to_all(x, axis, 0, 0, tiled=False)  26.9 us
    ppermute x6, waiting for transfers between devices, shifted(): return lax.ppermute(x, 'rep', [(i, (i + k) % n_rep) for i in range(n_rep)])  24 us
    ppermute x6, starting transfers between devices, swap(): return lax.ppermute(x, 'core', [(0, 1), (1, 0)])  20.3 us
    ppermute x6, starting transfers between devices, shifted(): return lax.ppermute(x, 'rep', [(i, (i + k) % n_rep) for i in range(n_rep)])  20 us
    reduce_scatter x1, waiting for transfers between devices, per_device(): act_grads = lax.psum_scatter(ag_part, 'z', scatter_dimension=0, tiled=True)  18.8 us
    dot_general x6, matrix products, dot(): lax.dot_general(left, right, ((dims[:1], dims[1:]), ((), ())), preferred_...  11.1 us
  transfers between devices with their start and end apart: 19, of which 9 were waited for; matrix products, arithmetic and copies ran while one was open for 10% of the time, Pallas kernels for 0%

profile of v3, /device:TPU:1, one launch (start us, length us, event | category | flops | bytes accessed | tf_op | source)
XLA Modules:
  0.0 210.4 jit_solution(3513453499153279796)
XLA Ops:
  7.2 0.8 pad_maximum_fusion.14
  8.0 0.0 copy-start
  8.0 0.1 broadcast_in_dim.22
  8.1 27.9 %all_to_all.30 = bf16[8,64,768]{2,1,0:T(8,128)(2,1)S(1)} all-to-all(bf16[8,64,768]{2,1,0:T(8,128)(2,1)S(1)} %broadcast_in_dim.22), channel_id=1, replica_groups=mesh['row'=8,'z'=8,'core'=2,'rep'=4] {'row'}, dimensions={0} | all-to-all | bytes 1572864 | tf_op jit(solution)/shard_map/all_to_all | solution.py:27
  36.0 5.6 %collective-permute-start = (bf16[512,768]{1,0:T(8,128)(2,1)S(1)}, bf16[512,768]{1,0:T(8,128)(2,1)S(1)}, u32[]{:S(2)}, u32[]{:S(2)}) collective-permute-start(bf16[512,768]{1,0:T(8,128)(2,1)S(1)} %bitcast.56), channel_id=1, source_target_pairs={{0,4},{4,0},{1,5},{5,1},{2,6},{6,2},{3,7},{7,3},{8,12},{12,8},{9,1... | collective-permute-start | bytes 2359304 | tf_op jit(solution)/shard_map/ppermute | solution.py:23
  41.6 0.1 constant_dynamic-slice_fusion.1
  41.7 1.9 collective-permute-start.2
  43.7 0.1 fusion.30
  43.8 0.1 fusion.31
  43.9 1.8 collective-permute-done.2
  45.7 1.7 convolution_convert_fusion.4
  47.3 10.2 %all-to-all-start.1 = ((bf16[8,64,768]{2,1,0:T(8,128)(2,1)}), bf16[8,64,768]{2,1,0:T(8,128)(2,1)S(1)}, u32[]{:S(2)}, u32[]{:S(2)}) async-start(bf16[8,64,768]{2,1,0:T(8,128)(2,1)} %bitcast.1), calls=%async_computation.2 | async-start | bytes 1572864 | tf_op jit(solution)/shard_map/all_to_all | solution.py:27
  57.5 0.0 reduce-scatter.3.cloned.1.call-start
  57.5 1.0 constant_dynamic-slice_fusion.3
  58.5 2.3 %collective-permute-start.1 = (bf16[768,384]{1,0:T(8,128)(2,1)S(1)}, bf16[768,384]{1,0:T(8,128)(2,1)S(1)}, u32[]{:S(2)}, u32[]{:S(2)}) collective-permute-start(bf16[768,384]{1,0:T(8,128)(2,1)S(1)} %get-tuple-element.18), channel_id=1, source_target_pairs={{0,4},{4,0},{1,5},{5,1},{2,6},{6,2},{3,7},{7,3},{8,12},{12,8},{9,1... | collective-permute-start | bytes 1769480 | tf_op jit(solution)/shard_map/ppermute | solution.py:23
  60.8 1.6 collective-permute-done.1
  62.5 3.0 %convolution_convert_fusion.5 = bf16[512,768]{1,0:T(8,128)(2,1)} fusion(bf16[768,384]{1,0:T(8,128)(2,1)S(1)} %collective-permute-done.1, bf16[768,384]{1,0:T(8,128)(2,1)} %get-tuple-element.17, bf16[512,384]{1,0:T(8,128)(2,1)S(1)} %get-tuple-element.22, bf16[512,384]{1,0:T(8,128)(2,1)S(1)} %get-tuple-element.20), kind=kOutput, calls=%fused_computation.5 | convolution fusion | flops 608305152 | bytes 2752512 | tf_op jit(solution)/shard_map/dot_general | solution.py:17
  65.4 0.0 reduce-scatter.3.cloned.1.call-update
  65.4 15.7 %all-to-all-done.1 = bf16[8,64,768]{2,1,0:T(8,128)(2,1)S(1)} async-done(((bf16[8,64,768]{2,1,0:T(8,128)(2,1)}), bf16[8,64,768]{2,1,0:T(8,128)(2,1)S(1)}, u32[]{:S(2)}, u32[]{:S(2)}) %all-to-all-start.1) | async-done | bytes 786464 | tf_op jit(solution)/shard_map/all_to_all | solution.py:27
  81.1 0.2 fusion.22
  81.3 0.9 broadcast_in_dim.47
  82.2 3.5 %all-to-all-start.2 = ((bf16[8,64,768]{2,1,0:T(8,128)(2,1)}), bf16[8,64,768]{2,1,0:T(8,128)(2,1)S(1)}, u32[]{:S(2)}, u32[]{:S(2)}) async-start(bf16[8,64,768]{2,1,0:T(8,128)(2,1)} %broadcast_in_dim.47), calls=%async_computation.3 | async-start | bytes 1572864 | tf_op jit(solution)/shard_map/all_to_all | solution.py:27
  85.8 18.8 %reduce-scatter.3.cloned.1.call-done = bf16[64,768]{1,0:T(8,128)(2,1)} async-done(((bf16[512,768]{1,0:T(8,128)(2,1)}), bf16[64,768]{1,0:T(8,128)(2,1)}) %reduce-scatter.3.cloned.1.call-update) | async-done | bytes 98320 | tf_op jit(solution)/shard_map/reduce_scatter | solution.py:72
  104.6 6.2 %all-to-all-done.2 = bf16[8,64,768]{2,1,0:T(8,128)(2,1)S(1)} async-done(((bf16[8,64,768]{2,1,0:T(8,128)(2,1)}), bf16[8,64,768]{2,1,0:T(8,128)(2,1)S(1)}, u32[]{:S(2)}, u32[]{:S(2)}) %all-to-all-start.2) | async-done | bytes 786464 | tf_op jit(solution)/shard_map/all_to_all | solution.py:27
  110.8 1.0 fusion.6
  111.8 0.9 broadcast_in_dim.48
  112.7 3.7 %all-to-all-start.3 = ((bf16[8,64,768]{2,1,0:T(8,128)(2,1)}), bf16[8,64,768]{2,1,0:T(8,128)(2,1)S(1)}, u32[]{:S(2)}, u32[]{:S(2)}) async-start(bf16[8,64,768]{2,1,0:T(8,128)(2,1)} %broadcast_in_dim.48), calls=%async_computation.4 | async-start | bytes 1572864 | tf_op jit(solution)/shard_map/all_to_all | solution.py:27
  116.4 1.8 convolution_convert_fusion
  118.2 1.0 dynamic-slice_bitcast_fusion.2
  119.2 4.3 %collective-permute-start.7 = (bf16[192,768]{1,0:T(8,128)(2,1)}, bf16[192,768]{1,0:T(8,128)(2,1)}, u32[]{:S(2)}, u32[]{:S(2)}) collective-permute-start(bf16[192,768]{1,0:T(8,128)(2,1)} %get-tuple-element.11), channel_id=1, source_target_pairs={{0,3},{1,0},{2,1},{3,2},{4,7},{5,4},{6,5},{7,6},{8,11},{9,8},{10,9... | collective-permute-start | bytes 884744 | tf_op jit(solution)/shard_map/ppermute | solution.py:85
  123.5 2.4 %collective-permute-start.6 = (bf16[192,768]{1,0:T(8,128)(2,1)}, bf16[192,768]{1,0:T(8,128)(2,1)}, u32[]{:S(2)}, u32[]{:S(2)}) collective-permute-start(bf16[192,768]{1,0:T(8,128)(2,1)} %get-tuple-element.12), channel_id=1, source_target_pairs={{0,2},{1,3},{2,0},{3,1},{4,6},{5,7},{6,4},{7,5},{8,10},{9,11},{10,... | collective-permute-start | bytes 884744 | tf_op jit(solution)/shard_map/ppermute | solution.py:85
  126.0 2.5 %collective-permute-start.5 = (bf16[192,768]{1,0:T(8,128)(2,1)}, bf16[192,768]{1,0:T(8,128)(2,1)}, u32[]{:S(2)}, u32[]{:S(2)}) collective-permute-start(bf16[192,768]{1,0:T(8,128)(2,1)} %get-tuple-element.10), channel_id=1, source_target_pairs={{0,1},{1,2},{2,3},{3,0},{4,5},{5,6},{6,7},{7,4},{8,9},{9,10},{10,1... | collective-permute-start | bytes 884744 | tf_op jit(solution)/shard_map/ppermute | solution.py:85
  128.5 2.0 convolution_convert_fusion.3
  130.6 5.1 %collective-permute-start.3 = (bf16[512,384]{1,0:T(8,128)(2,1)S(1)}, bf16[512,384]{1,0:T(8,128)(2,1)}, u32[]{:S(2)}, u32[]{:S(2)}) collective-permute-start(bf16[512,384]{1,0:T(8,128)(2,1)S(1)} %slice.119), channel_id=1, source_target_pairs={{0,4},{4,0},{1,5},{5,1},{2,6},{6,2},{3,7},{7,3},{8,12},{12,8},{9,1... | collective-permute-start | bytes 1179656 | tf_op jit(solution)/shard_map/ppermute | solution.py:23
  135.8 5.8 %collective-permute-done.5 = bf16[192,768]{1,0:T(8,128)(2,1)} collective-permute-done((bf16[192,768]{1,0:T(8,128)(2,1)}, bf16[192,768]{1,0:T(8,128)(2,1)}, u32[]{:S(2)}, u32[]{:S(2)}) %collective-permute-start.5) | collective-permute-done | bytes 294944 | tf_op jit(solution)/shard_map/ppermute | solution.py:85
  141.6 1.3 fusion.1
  142.9 0.8 convolution_convert_fusion.1
  143.7 1.1 copy.16
  144.8 3.7 %all-to-all-start.4 = ((bf16[4,2,96,768]{3,2,1,0:T(8,128)(2,1)}), bf16[4,2,96,768]{3,2,1,0:T(8,128)(2,1)S(1)}, u32[]{:S(2)}, u32[]{:S(2)}) async-start(bf16[4,2,96,768]{3,2,1,0:T(8,128)(2,1)} %bitcast.55), calls=%async_computation.6 | async-start | bytes 2359296 | tf_op jit(solution)/shard_map/all_to_all | solution.py:27
  148.4 0.0 reduce-scatter.5.cloned.1.call-start
  148.5 1.9 convolution_convert_fusion.2
  150.4 3.5 %collective-permute-start.4 = (bf16[512,384]{1,0:T(8,128)(2,1)S(1)}, bf16[512,384]{1,0:T(8,128)(2,1)S(1)}, u32[]{:S(2)}, u32[]{:S(2)}) collective-permute-start(bf16[512,384]{1,0:T(8,128)(2,1)S(1)} %slice.121), channel_id=1, source_target_pairs={{0,4},{4,0},{1,5},{5,1},{2,6},{6,2},{3,7},{7,3},{8,12},{12,8},{9,1... | collective-permute-start | bytes 1179656 | tf_op jit(solution)/shard_map/ppermute | solution.py:23
  153.9 1.9 collective-permute-start.8
  155.9 1.1 add_convert_fusion.1
  157.0 0.1 add_convert_fusion
  157.1 1.0 pad_maximum_fusion.5
  158.1 0.0 reduce-scatter.5.cloned.1.call-update
  158.1 5.4 %all-to-all-done.4 = bf16[4,2,96,768]{3,2,1,0:T(8,128)(2,1)S(1)} async-done(((bf16[4,2,96,768]{3,2,1,0:T(8,128)(2,1)}), bf16[4,2,96,768]{3,2,1,0:T(8,128)(2,1)S(1)}, u32[]{:S(2)}, u32[]{:S(2)}) %all-to-all-start.4) | async-done | bytes 1179680 | tf_op jit(solution)/shard_map/all_to_all | solution.py:27
  163.5 0.1 fusion.2
  163.7 0.1 reverse_select_fusion
  163.7 1.1 broadcast_in_dim.49
  164.8 5.8 %all-to-all-start.5 = ((bf16[8,96,768]{2,1,0:T(8,128)(2,1)}), bf16[8,96,768]{2,1,0:T(8,128)(2,1)S(1)}, u32[]{:S(2)}, u32[]{:S(2)}) async-start(bf16[8,96,768]{2,1,0:T(8,128)(2,1)} %bitcast.9), calls=%async_computation.7 | async-start | bytes 2359296 | tf_op jit(solution)/shard_map/all_to_all | solution.py:27
  170.7 3.3 %collective-permute-start.9 = (bf16[2,192,384]{2,1,0:T(8,128)(2,1)S(1)}, bf16[2,192,384]{2,1,0:T(8,128)(2,1)S(1)}, u32[]{:S(2)}, u32[]{:S(2)}) collective-permute-start(bf16[2,192,384]{2,1,0:T(8,128)(2,1)S(1)} %maximum_select_fusion.1), channel_id=1, source_target_pairs={{0,1},{1,2},{2,3},{3,0},{4,5},{5,6},{6,7},{7,4},{8,9},{9,10},{10,1... | collective-permute-start | bytes 884744 | tf_op jit(solution)/shard_map/ppermute | solution.py:85
  174.0 4.3 %collective-permute-start.10 = (bf16[2,192,384]{2,1,0:T(8,128)(2,1)S(1)}, bf16[2,192,384]{2,1,0:T(8,128)(2,1)S(1)}, u32[]{:S(2)}, u32[]{:S(2)}) collective-permute-start(bf16[2,192,384]{2,1,0:T(8,128)(2,1)S(1)} %maximum_select_fusion.1), channel_id=1, source_target_pairs={{0,2},{1,3},{2,0},{3,1},{4,6},{5,7},{6,4},{7,5},{8,10},{9,11},{10,... | collective-permute-start | bytes 884744 | tf_op jit(solution)/shard_map/ppermute | solution.py:85
  178.3 3.1 %collective-permute-start.11 = (bf16[2,192,384]{2,1,0:T(8,128)(2,1)S(1)}, bf16[2,192,384]{2,1,0:T(8,128)(2,1)S(1)}, u32[]{:S(2)}, u32[]{:S(2)}) collective-permute-start(bf16[2,192,384]{2,1,0:T(8,128)(2,1)S(1)} %maximum_select_fusion.1), channel_id=1, source_target_pairs={{0,3},{1,0},{2,1},{3,2},{4,7},{5,4},{6,5},{7,6},{8,11},{9,8},{10,9... | collective-permute-start | bytes 884744 | tf_op jit(solution)/shard_map/ppermute | solution.py:85
  181.4 0.1 broadcast_in_dim.50
  181.5 0.1 fusion.3
  181.6 11.7 %collective-permute-done.9 = bf16[2,192,384]{2,1,0:T(8,128)(2,1)S(1)} collective-permute-done((bf16[2,192,384]{2,1,0:T(8,128)(2,1)S(1)}, bf16[2,192,384]{2,1,0:T(8,128)(2,1)S(1)}, u32[]{:S(2)}, u32[]{:S(2)}) %collective-permute-start.9) | collective-permute-done | bytes 294944 | tf_op jit(solution)/shard_map/ppermute | solution.py:85
  193.4 6.5 %collective-permute-done.10 = bf16[2,192,384]{2,1,0:T(8,128)(2,1)S(1)} collective-permute-done((bf16[2,192,384]{2,1,0:T(8,128)(2,1)S(1)}, bf16[2,192,384]{2,1,0:T(8,128)(2,1)S(1)}, u32[]{:S(2)}, u32[]{:S(2)}) %collective-permute-start.10) | collective-permute-done | bytes 294944 | tf_op jit(solution)/shard_map/ppermute | solution.py:85
  199.9 0.1 bitcast_dynamic-update-slice_fusion
  200.0 0.1 fusion.29
  200.1 0.9 copy-done.2
  201.0 1.1 pad_maximum_fusion.2
  202.1 1.5 fusion.32
  (38 shorter events, 0.3 us)
Async XLA Ops:
  8.0 33.6 %copy-start = (bf16[384,1536]{1,0:T(8,128)(2,1)S(1)}, bf16[384,1536]{1,0:T(8,128)(2,1)}, u32[]{:S(2)}) copy-start(bf16[384,1536]{1,0:T(8,128)(2,1)} %param.5) | copy-start | bytes 3538948
  36.0 7.8 %collective-permute-start = (bf16[512,768]{1,0:T(8,128)(2,1)S(1)}, bf16[512,768]{1,0:T(8,128)(2,1)S(1)}, u32[]{:S(2)}, u32[]{:S(2)}) collective-permute-start(bf16[512,768]{1,0:T(8,128)(2,1)S(1)} %bitcast.56), channel_id=1, source_target_pairs={{0,4},{4,0},{1,5},{5,1},{2,6},{6,2},{3,7},{7,3},{8,12},{12,8},{9,1... | collective-permute-start | bytes 2359304 | tf_op jit(solution)/shard_map/ppermute | solution.py:23
  41.7 3.9 %copy-start.5 = (bf16[384,768]{1,0:T(8,128)(2,1)}, bf16[384,768]{1,0:T(8,128)(2,1)S(1)}, u32[]{:S(2)}) copy-start(bf16[384,768]{1,0:T(8,128)(2,1)S(1)} %get-tuple-element.15) | copy-start | bytes 1769476
  41.7 3.9 %collective-permute-start.2 = (bf16[384,768]{1,0:T(8,128)(2,1)S(1)}, bf16[384,768]{1,0:T(8,128)(2,1)S(1)}, u32[]{:S(2)}, u32[]{:S(2)}) collective-permute-start(bf16[384,768]{1,0:T(8,128)(2,1)S(1)} %get-tuple-element.16), channel_id=1, source_target_pairs={{0,4},{4,0},{1,5},{5,1},{2,6},{6,2},{3,7},{7,3},{8,12},{12,8},{9,1... | collective-permute-start | bytes 1769480 | tf_op jit(solution)/shard_map/ppermute | solution.py:23
  43.8 1.9 copy-start.7
  43.9 18.6 %copy-start.9 = (bf16[512,384]{1,0:T(8,128)(2,1)}, bf16[512,384]{1,0:T(8,128)(2,1)S(1)}, u32[]{:S(2)}) copy-start(bf16[512,384]{1,0:T(8,128)(2,1)S(1)} %get-tuple-element.22) | copy-start | bytes 1179652
  45.6 1.7 copy-start.10
  47.3 10.2 %copy-start.1 = (bf16[1536,384]{1,0:T(8,128)(2,1)S(1)}, bf16[1536,384]{1,0:T(8,128)(2,1)}, u32[]{:S(2)}) copy-start(bf16[1536,384]{1,0:T(8,128)(2,1)} %param.6) | copy-start | bytes 3538948
  47.3 33.8 %all-to-all-start.1 = ((bf16[8,64,768]{2,1,0:T(8,128)(2,1)}), bf16[8,64,768]{2,1,0:T(8,128)(2,1)S(1)}, u32[]{:S(2)}, u32[]{:S(2)}) async-start(bf16[8,64,768]{2,1,0:T(8,128)(2,1)} %bitcast.1), calls=%async_computation.2 | async-start | bytes 1572864 | tf_op jit(solution)/shard_map/all_to_all | solution.py:27
  57.5 47.1 %reduce-scatter.3.cloned.1.call-start = ((), (), s32[]{:S(2)}) async-start(), calls=%async_computation.8 | async-start | bytes 884736 | tf_op jit(solution)/shard_map/reduce_scatter | solution.py:72
  58.5 3.9 %collective-permute-start.1 = (bf16[768,384]{1,0:T(8,128)(2,1)S(1)}, bf16[768,384]{1,0:T(8,128)(2,1)S(1)}, u32[]{:S(2)}, u32[]{:S(2)}) collective-permute-start(bf16[768,384]{1,0:T(8,128)(2,1)S(1)} %get-tuple-element.18), channel_id=1, source_target_pairs={{0,4},{4,0},{1,5},{5,1},{2,6},{6,2},{3,7},{7,3},{8,12},{12,8},{9,1... | collective-permute-start | bytes 1769480 | tf_op jit(solution)/shard_map/ppermute | solution.py:23
  62.5 3.0 %copy-start.11 = (bf16[768,384]{1,0:T(8,128)(2,1)}, bf16[768,384]{1,0:T(8,128)(2,1)S(1)}, u32[]{:S(2)}) copy-start(bf16[768,384]{1,0:T(8,128)(2,1)S(1)} %collective-permute-done.1) | copy-start | bytes 1769476
  82.2 28.5 %all-to-all-start.2 = ((bf16[8,64,768]{2,1,0:T(8,128)(2,1)}), bf16[8,64,768]{2,1,0:T(8,128)(2,1)S(1)}, u32[]{:S(2)}, u32[]{:S(2)}) async-start(bf16[8,64,768]{2,1,0:T(8,128)(2,1)} %broadcast_in_dim.47), calls=%async_computation.3 | async-start | bytes 1572864 | tf_op jit(solution)/shard_map/all_to_all | solution.py:27
  112.7 30.1 %all-to-all-start.3 = ((bf16[8,64,768]{2,1,0:T(8,128)(2,1)}), bf16[8,64,768]{2,1,0:T(8,128)(2,1)S(1)}, u32[]{:S(2)}, u32[]{:S(2)}) async-start(bf16[8,64,768]{2,1,0:T(8,128)(2,1)} %broadcast_in_dim.48), calls=%async_computation.4 | async-start | bytes 1572864 | tf_op jit(solution)/shard_map/all_to_all | solution.py:27
  119.2 16.6 %collective-permute-start.7 = (bf16[192,768]{1,0:T(8,128)(2,1)}, bf16[192,768]{1,0:T(8,128)(2,1)}, u32[]{:S(2)}, u32[]{:S(2)}) collective-permute-start(bf16[192,768]{1,0:T(8,128)(2,1)} %get-tuple-element.11), channel_id=1, source_target_pairs={{0,3},{1,0},{2,1},{3,2},{4,7},{5,4},{6,5},{7,6},{8,11},{9,8},{10,9... | collective-permute-start | bytes 884744 | tf_op jit(solution)/shard_map/ppermute | solution.py:85
  123.5 12.2 %collective-permute-start.6 = (bf16[192,768]{1,0:T(8,128)(2,1)}, bf16[192,768]{1,0:T(8,128)(2,1)}, u32[]{:S(2)}, u32[]{:S(2)}) collective-permute-start(bf16[192,768]{1,0:T(8,128)(2,1)} %get-tuple-element.12), channel_id=1, source_target_pairs={{0,2},{1,3},{2,0},{3,1},{4,6},{5,7},{6,4},{7,5},{8,10},{9,11},{10,... | collective-permute-start | bytes 884744 | tf_op jit(solution)/shard_map/ppermute | solution.py:85
  126.0 15.6 %collective-permute-start.5 = (bf16[192,768]{1,0:T(8,128)(2,1)}, bf16[192,768]{1,0:T(8,128)(2,1)}, u32[]{:S(2)}, u32[]{:S(2)}) collective-permute-start(bf16[192,768]{1,0:T(8,128)(2,1)} %get-tuple-element.10), channel_id=1, source_target_pairs={{0,1},{1,2},{2,3},{3,0},{4,5},{5,6},{6,7},{7,4},{8,9},{9,10},{10,1... | collective-permute-start | bytes 884744 | tf_op jit(solution)/shard_map/ppermute | solution.py:85
  130.5 11.0 %copy-start.3 = (bf16[512,768]{1,0:T(8,128)(2,1)}, bf16[512,768]{1,0:T(8,128)(2,1)S(1)}, u32[]{:S(2)}) copy-start(bf16[512,768]{1,0:T(8,128)(2,1)S(1)} %convolution_convert_fusion.3) | copy-start | bytes 2359300
  130.5 12.3 %copy-start.8 = (bf16[512,384]{1,0:T(8,128)(2,1)S(1)}, bf16[512,384]{1,0:T(8,128)(2,1)}, u32[]{:S(2)}) copy-start(bf16[512,384]{1,0:T(8,128)(2,1)} %copy-done.7) | copy-start | bytes 1179652
  130.6 25.3 %collective-permute-start.3 = (bf16[512,384]{1,0:T(8,128)(2,1)S(1)}, bf16[512,384]{1,0:T(8,128)(2,1)}, u32[]{:S(2)}, u32[]{:S(2)}) collective-permute-start(bf16[512,384]{1,0:T(8,128)(2,1)S(1)} %slice.119), channel_id=1, source_target_pairs={{0,4},{4,0},{1,5},{5,1},{2,6},{6,2},{3,7},{7,3},{8,12},{12,8},{9,1... | collective-permute-start | bytes 1179656 | tf_op jit(solution)/shard_map/ppermute | solution.py:23
  144.8 3.7 %copy-start.6 = (bf16[384,768]{1,0:T(8,128)(2,1)S(1)}, bf16[384,768]{1,0:T(8,128)(2,1)}, u32[]{:S(2)}) copy-start(bf16[384,768]{1,0:T(8,128)(2,1)} %copy-done.5) | copy-start | bytes 1769476
  144.8 18.8 %all-to-all-start.4 = ((bf16[4,2,96,768]{3,2,1,0:T(8,128)(2,1)}), bf16[4,2,96,768]{3,2,1,0:T(8,128)(2,1)S(1)}, u32[]{:S(2)}, u32[]{:S(2)}) async-start(bf16[4,2,96,768]{3,2,1,0:T(8,128)(2,1)} %bitcast.55), calls=%async_computation.6 | async-start | bytes 2359296 | tf_op jit(solution)/shard_map/all_to_all | solution.py:27
  148.4 53.6 %reduce-scatter.5.cloned.1.call-start = ((), (), s32[]{:S(2)}) async-start(), calls=%async_computation.9 | async-start | bytes 884736 | tf_op jit(solution)/shard_map/reduce_scatter | solution.py:117
  150.4 5.5 %copy-start.4 = (bf16[512,768]{1,0:T(8,128)(2,1)S(1)}, bf16[512,768]{1,0:T(8,128)(2,1)}, u32[]{:S(2)}) copy-start(bf16[512,768]{1,0:T(8,128)(2,1)} %copy-done.3) | copy-start | bytes 2359300
  150.4 6.6 %collective-permute-start.4 = (bf16[512,384]{1,0:T(8,128)(2,1)S(1)}, bf16[512,384]{1,0:T(8,128)(2,1)S(1)}, u32[]{:S(2)}, u32[]{:S(2)}) collective-permute-start(bf16[512,384]{1,0:T(8,128)(2,1)S(1)} %slice.121), channel_id=1, source_target_pairs={{0,4},{4,0},{1,5},{5,1},{2,6},{6,2},{3,7},{7,3},{8,12},{12,8},{9,1... | collective-permute-start | bytes 1179656 | tf_op jit(solution)/shard_map/ppermute | solution.py:23
  153.9 16.7 %collective-permute-start.8 = (bf16[192,384]{1,0:T(8,128)(2,1)S(1)}, bf16[192,384]{1,0:T(8,128)(2,1)S(1)}, u32[]{:S(2)}, u32[]{:S(2)}) collective-permute-start(bf16[192,384]{1,0:T(8,128)(2,1)S(1)} %get-tuple-element.24), channel_id=1, source_target_pairs={{0,4},{4,0},{1,5},{5,1},{2,6},{6,2},{3,7},{7,3},{8,12},{12,8},{9,1... | collective-permute-start | bytes 442376 | tf_op jit(solution)/shard_map/ppermute | solution.py:23
  164.8 35.1 %all-to-all-start.5 = ((bf16[8,96,768]{2,1,0:T(8,128)(2,1)}), bf16[8,96,768]{2,1,0:T(8,128)(2,1)S(1)}, u32[]{:S(2)}, u32[]{:S(2)}) async-start(bf16[8,96,768]{2,1,0:T(8,128)(2,1)} %bitcast.9), calls=%async_computation.7 | async-start | bytes 2359296 | tf_op jit(solution)/shard_map/all_to_all | solution.py:27
  170.7 22.6 %collective-permute-start.9 = (bf16[2,192,384]{2,1,0:T(8,128)(2,1)S(1)}, bf16[2,192,384]{2,1,0:T(8,128)(2,1)S(1)}, u32[]{:S(2)}, u32[]{:S(2)}) collective-permute-start(bf16[2,192,384]{2,1,0:T(8,128)(2,1)S(1)} %maximum_select_fusion.1), channel_id=1, source_target_pairs={{0,1},{1,2},{2,3},{3,0},{4,5},{5,6},{6,7},{7,4},{8,9},{9,10},{10,1... | collective-permute-start | bytes 884744 | tf_op jit(solution)/shard_map/ppermute | solution.py:85
  174.0 25.8 %collective-permute-start.10 = (bf16[2,192,384]{2,1,0:T(8,128)(2,1)S(1)}, bf16[2,192,384]{2,1,0:T(8,128)(2,1)S(1)}, u32[]{:S(2)}, u32[]{:S(2)}) collective-permute-start(bf16[2,192,384]{2,1,0:T(8,128)(2,1)S(1)} %maximum_select_fusion.1), channel_id=1, source_target_pairs={{0,2},{1,3},{2,0},{3,1},{4,6},{5,7},{6,4},{7,5},{8,10},{9,11},{10,... | collective-permute-start | bytes 884744 | tf_op jit(solution)/shard_map/ppermute | solution.py:85
  178.3 21.6 %collective-permute-start.11 = (bf16[2,192,384]{2,1,0:T(8,128)(2,1)S(1)}, bf16[2,192,384]{2,1,0:T(8,128)(2,1)S(1)}, u32[]{:S(2)}, u32[]{:S(2)}) collective-permute-start(bf16[2,192,384]{2,1,0:T(8,128)(2,1)S(1)} %maximum_select_fusion.1), channel_id=1, source_target_pairs={{0,3},{1,0},{2,1},{3,2},{4,7},{5,4},{6,5},{7,6},{8,11},{9,8},{10,9... | collective-permute-start | bytes 884744 | tf_op jit(solution)/shard_map/ppermute | solution.py:85
  200.0 1.0 copy-start.2
Sparse Core Ops, SparseCore 0:
  65.6 38.9 reduce-scatter.2
  158.2 34.8 reduce-scatter.4

commit v4 on v2

--- a/solution.py
+++ b/solution.py
@@ -75,11 +75,12 @@
 
     hidden = total_of(hid_terms)
     act = jax.nn.gelu(hidden).astype(bf16)
-    padded = jnp.pad(act, ((0, share // 2), (0, 0)))
-    padded, ag_part = barrier((padded, ag_part))
-    act_all = lax.all_gather(padded, "z", axis=0, tiled=False)
-    act_all = act_all[:, :share].reshape(total, half)
-    act_grads = total_of(exchange(ag_part, "z"))
+    packed = jnp.concatenate(
+        [jnp.broadcast_to(act[None], (n_z, share, half)), ag_part], 2
+    )
+    got = exchange(packed, "z")
+    act_all = got[:, :, :half].reshape(total, half)
+    act_grads = total_of(got[:, :, half:])
     hid_grads = gelu_pullback(hidden, act_grads).astype(bf16)
     hg = gather(hid_grads, "z")
 
@@ -94,7 +95,6 @@
     for k in range(n_rep):
         block = lax.dynamic_index_in_dim(down_local, lax.rem(rep + k, n_rep), 0, False)
         terms.append(shifted(block, k) if k else block)
-    terms, hg = barrier((terms, hg))
     down_sum = total_of(jnp.stack(terms)).astype(bf16)
     down_own, down_got = down_sum[:, :width], swap(down_sum[:, width:])
     down_pair = in_order(down_own[None], down_got[None], 0)
@@ -120,7 +120,14 @@
         return (own.astype(f32) + other.astype(f32)).astype(bf16)
 
     out = jnp.concatenate([output(act_all, down, (1, 0)), output(hg, up, (1, 1))], 1)
-    out = lax.psum_scatter(out, "row", scatter_dimension=0, tiled=True)
+    out = out.reshape(n_row, rows, 2 * width)
+    row = lax.axis_index("row")
+    pieces = []
+    for k in range(n_row):
+        block = lax.dynamic_index_in_dim(out, lax.rem(row + k, n_row), 0, False)
+        ring = [(i, (i + k) % n_row) for i in range(n_row)]
+        pieces.append(lax.ppermute(block, "row", ring) if k else block)
+    out = total_of(jnp.stack(pieces)).astype(bf16)
     return (out[:, :width], out[:, width:], up_grads, down_grads)
 
 

time: 230 us -> 237 us (1.030)
  blocking collectives: 54.3 us -> 20 us
  starting transfers between devices: 84.9 us -> 112 us
  waiting for transfers between devices: 48.7 us -> 75.2 us
  between operations: 14.5 us -> 1.4 us
  matrix products: 9.93 us -> 5.66 us
  local copies, waits for them, and re-layouts: 11.7 us -> 14.1 us
    all_to_all x5 -> x6, waiting for transfers between devices: 13.8 us -> 50.2 us  [exchange(): return lax.all_to_all(x, axis, 0, 0, tiled=False)]
    all_to_all x1 -> x0, blocking collectives: 34.2 us -> none  [exchange(): return lax.all_to_all(x, axis, 0, 0, tiled=False)]
    ppermute x0 -> x7, starting transfers between devices: none -> 22.6 us  [per_device(): pieces.append(lax.ppermute(block, 'row', ring) if k else block)]
    ppermute x6, waiting for transfers between devices: 27.7 us -> 12.5 us  [shifted(): return lax.ppermute(x, 'rep', [(i, (i + k) % n_rep) for i in range(n_rep)])]
    all_to_all x5 -> x6, starting transfers between devices: 30.8 us -> 41.9 us  [exchange(): return lax.all_to_all(x, axis, 0, 0, tiled=False)]
    ppermute x0 -> x7, waiting for transfers between devices: none -> 9.85 us  [per_device(): pieces.append(lax.ppermute(block, 'row', ring) if k else block)]
    ppermute x7, starting transfers between devices: 33.4 us -> 28.3 us  [swap(): return lax.ppermute(x, 'core', [(0, 1), (1, 0)])]
    all_gather x1 -> x0, waiting for transfers between devices: 4.64 us -> none  [per_device(): act_all = lax.all_gather(padded, 'z', axis=0, tiled=False)]
  transfers between devices with their start and end apart: 20 -> 26, of which waited for: 9 -> 9; matrix products, arithmetic and copies ran while one was open for 7% -> 8% of each run, Pallas kernels for 0% -> 0%
where the time goes in v4:
time: 237 us; the launch traced here: 236 us
  starting transfers between devices  112 us (47%)
  waiting for transfers between devices  75.2 us (32%)
  blocking collectives  20 us (8%)
  local copies, waits for them, and re-layouts  14.1 us (6%)
  other arithmetic  7.53 us (3%)
  matrix products  5.66 us (2%)
    all_to_all x6, waiting for transfers between devices, exchange(): return lax.all_to_all(x, axis, 0, 0, tiled=False)  50.2 us
    all_to_all x6, starting transfers between devices, exchange(): return lax.all_to_all(x, axis, 0, 0, tiled=False)  41.9 us
    ppermute x7, starting transfers between devices, swap(): return lax.ppermute(x, 'core', [(0, 1), (1, 0)])  28.3 us
    ppermute x7, starting transfers between devices, per_device(): pieces.append(lax.ppermute(block, 'row', ring) if k else block)  22.6 us
    all_gather x1, blocking collectives, per_device(): og_own = lax.all_gather(out_grads, 'row', axis=0, tiled=True)  20 us
    ppermute x6, starting transfers between devices, shifted(): return lax.ppermute(x, 'rep', [(i, (i + k) % n_rep) for i in range(n_rep)])  18.9 us
    ppermute x6, waiting for transfers between devices, shifted(): return lax.ppermute(x, 'rep', [(i, (i + k) % n_rep) for i in range(n_rep)])  12.5 us
    ppermute x7, waiting for transfers between devices, per_device(): pieces.append(lax.ppermute(block, 'row', ring) if k else block)  9.85 us
  transfers between devices with their start and end apart: 26, of which 9 were waited for; matrix products, arithmetic and copies ran while one was open for 8% of the time, Pallas kernels for 0%

profile of v4, /device:TPU:1, one launch (start us, length us, event | category | flops | bytes accessed | tf_op | source)
XLA Modules:
  0.0 235.7 jit_solution(2828863253373475318)
XLA Ops:
  0.6 1.7 broadcast_in_dim.47
  2.3 7.7 %all-to-all-start = ((bf16[8,64,384]{2,1,0:T(8,128)(2,1)}), bf16[8,64,384]{2,1,0:T(8,128)(2,1)S(1)}, u32[]{:S(2)}, u32[]{:S(2)}) async-start(bf16[8,64,384]{2,1,0:T(8,128)(2,1)} %broadcast_in_dim.47), calls=%async_computation | async-start | bytes 786432 | tf_op jit(solution)/shard_map/all_to_all | solution.py:27
  10.1 4.6 %collective-permute-start.1 = (bf16[384,768]{1,0:T(8,128)(2,1)S(1)}, bf16[384,768]{1,0:T(8,128)(2,1)S(1)}, u32[]{:S(2)}, u32[]{:S(2)}) collective-permute-start(bf16[384,768]{1,0:T(8,128)(2,1)S(1)} %get-tuple-element.18), channel_id=1, source_target_pairs={{0,4},{4,0},{1,5},{5,1},{2,6},{6,2},{3,7},{7,3},{8,12},{12,8},{9,1... | collective-permute-start | bytes 1769480 | tf_op jit(solution)/shard_map/ppermute | solution.py:23
  14.7 6.9 %all-to-all-done = bf16[8,64,384]{2,1,0:T(8,128)(2,1)S(1)} async-done(((bf16[8,64,384]{2,1,0:T(8,128)(2,1)}), bf16[8,64,384]{2,1,0:T(8,128)(2,1)S(1)}, u32[]{:S(2)}, u32[]{:S(2)}) %all-to-all-start) | async-done | bytes 393248 | tf_op jit(solution)/shard_map/all_to_all | solution.py:27
  21.6 5.9 %collective-permute-start = (bf16[512,384]{1,0:T(8,128)(2,1)S(1)}, bf16[512,384]{1,0:T(8,128)(2,1)S(1)}, u32[]{:S(2)}, u32[]{:S(2)}) collective-permute-start(bf16[512,384]{1,0:T(8,128)(2,1)S(1)} %bitcast.86), channel_id=1, source_target_pairs={{0,4},{4,0},{1,5},{5,1},{2,6},{6,2},{3,7},{7,3},{8,12},{12,8},{9,1... | collective-permute-start | bytes 1179656 | tf_op jit(solution)/shard_map/ppermute | solution.py:23
  27.5 1.3 collective-permute-done
  28.8 1.7 convolution_convert_fusion.5
  30.5 10.2 %all-to-all-start.1 = ((bf16[8,64,768]{2,1,0:T(8,128)(2,1)}), bf16[8,64,768]{2,1,0:T(8,128)(2,1)S(1)}, u32[]{:S(2)}, u32[]{:S(2)}) async-start(bf16[8,64,768]{2,1,0:T(8,128)(2,1)} %bitcast.1), calls=%async_computation.1 | async-start | bytes 1572864 | tf_op jit(solution)/shard_map/all_to_all | solution.py:27
  40.9 2.6 %collective-permute-start.3 = (bf16[768,384]{1,0:T(8,128)(2,1)S(1)}, bf16[768,384]{1,0:T(8,128)(2,1)S(1)}, u32[]{:S(2)}, u32[]{:S(2)}) collective-permute-start(bf16[768,384]{1,0:T(8,128)(2,1)S(1)} %get-tuple-element.16), channel_id=1, source_target_pairs={{0,4},{4,0},{1,5},{5,1},{2,6},{6,2},{3,7},{7,3},{8,12},{12,8},{9,1... | collective-permute-start | bytes 1769480 | tf_op jit(solution)/shard_map/ppermute | solution.py:23
  43.4 20.0 %all_gather.3 = bf16[512,384]{1,0:T(8,128)(2,1)S(1)} all-gather(bf16[64,384]{1,0:T(8,128)(2,1)S(1)} %copy-done.17), channel_id=1, replica_groups=mesh['row'=8,'z'=8,'core'=2,'rep'=4] {'row'}, dimensions={0}, use_global_device_ids=true | all-gather | bytes 442368 | tf_op jit(solution)/shard_map/all_gather | solution.py:72
  63.5 7.1 %collective-permute-start.2 = (bf16[512,384]{1,0:T(8,128)(2,1)S(1)}, bf16[512,384]{1,0:T(8,128)(2,1)S(1)}, u32[]{:S(2)}, u32[]{:S(2)}) collective-permute-start(bf16[512,384]{1,0:T(8,128)(2,1)S(1)} %all_gather.3), channel_id=1, source_target_pairs={{0,4},{4,0},{1,5},{5,1},{2,6},{6,2},{3,7},{7,3},{8,12},{12,8},{9,1... | collective-permute-start | bytes 1179656 | tf_op jit(solution)/shard_map/ppermute | solution.py:23
  70.7 1.3 collective-permute-done.2
  72.1 0.8 copy-done.15
  72.9 0.2 copy-done.20
  73.1 0.8 convolution_convert_fusion.4
  73.9 0.2 fusion.14
  74.1 1.3 pad_maximum_fusion
  75.4 6.9 %all-to-all-start.2 = ((bf16[8,64,1536]{2,1,0:T(8,128)(2,1)}), bf16[8,64,1536]{2,1,0:T(8,128)(2,1)S(1)}, u32[]{:S(2)}, u32[]{:S(2)}) async-start(bf16[8,64,1536]{2,1,0:T(8,128)(2,1)} %pad_maximum_fusion), calls=%async_computation.2 | async-start | bytes 3145728 | tf_op jit(solution)/shard_map/all_to_all | solution.py:27
  82.4 38.3 %all-to-all-done.2 = bf16[8,64,1536]{2,1,0:T(8,128)(2,1)S(1)} async-done(((bf16[8,64,1536]{2,1,0:T(8,128)(2,1)}), bf16[8,64,1536]{2,1,0:T(8,128)(2,1)S(1)}, u32[]{:S(2)}, u32[]{:S(2)}) %all-to-all-start.2) | async-done | bytes 1572896 | tf_op jit(solution)/shard_map/all_to_all | solution.py:27
  120.6 0.2 fusion.15
  120.9 0.9 broadcast_in_dim.51
  121.8 3.5 %all-to-all-start.3 = ((bf16[8,64,768]{2,1,0:T(8,128)(2,1)}), bf16[8,64,768]{2,1,0:T(8,128)(2,1)S(1)}, u32[]{:S(2)}, u32[]{:S(2)}) async-start(bf16[8,64,768]{2,1,0:T(8,128)(2,1)} %broadcast_in_dim.51), calls=%async_computation.3 | async-start | bytes 1572864 | tf_op jit(solution)/shard_map/all_to_all | solution.py:27
  125.4 1.1 copy-done.16
  126.5 0.8 convolution_convert_fusion
  127.3 1.0 dynamic-slice_bitcast_fusion.2
  128.3 4.4 %collective-permute-start.15 = (bf16[192,768]{1,0:T(8,128)(2,1)}, bf16[192,768]{1,0:T(8,128)(2,1)}, u32[]{:S(2)}, u32[]{:S(2)}) collective-permute-start(bf16[192,768]{1,0:T(8,128)(2,1)} %get-tuple-element.11), channel_id=1, source_target_pairs={{0,3},{1,0},{2,1},{3,2},{4,7},{5,4},{6,5},{7,6},{8,11},{9,8},{10,9... | collective-permute-start | bytes 884744 | tf_op jit(solution)/shard_map/ppermute | solution.py:91
  132.7 2.4 %collective-permute-start.14 = (bf16[192,768]{1,0:T(8,128)(2,1)}, bf16[192,768]{1,0:T(8,128)(2,1)}, u32[]{:S(2)}, u32[]{:S(2)}) collective-permute-start(bf16[192,768]{1,0:T(8,128)(2,1)} %get-tuple-element.12), channel_id=1, source_target_pairs={{0,2},{1,3},{2,0},{3,1},{4,6},{5,7},{6,4},{7,5},{8,10},{9,11},{10,... | collective-permute-start | bytes 884744 | tf_op jit(solution)/shard_map/ppermute | solution.py:91
  135.1 2.5 %collective-permute-start.13 = (bf16[192,768]{1,0:T(8,128)(2,1)}, bf16[192,768]{1,0:T(8,128)(2,1)}, u32[]{:S(2)}, u32[]{:S(2)}) collective-permute-start(bf16[192,768]{1,0:T(8,128)(2,1)} %get-tuple-element.10), channel_id=1, source_target_pairs={{0,1},{1,2},{2,3},{3,0},{4,5},{5,6},{6,7},{7,4},{8,9},{9,10},{10,1... | collective-permute-start | bytes 884744 | tf_op jit(solution)/shard_map/ppermute | solution.py:91
  137.7 4.4 %collective-permute-done.14 = bf16[192,768]{1,0:T(8,128)(2,1)} collective-permute-done((bf16[192,768]{1,0:T(8,128)(2,1)}, bf16[192,768]{1,0:T(8,128)(2,1)}, u32[]{:S(2)}, u32[]{:S(2)}) %collective-permute-start.14) | collective-permute-done | bytes 294944 | tf_op jit(solution)/shard_map/ppermute | solution.py:91
  142.1 8.0 %collective-permute-done.13 = bf16[192,768]{1,0:T(8,128)(2,1)} collective-permute-done((bf16[192,768]{1,0:T(8,128)(2,1)}, bf16[192,768]{1,0:T(8,128)(2,1)}, u32[]{:S(2)}, u32[]{:S(2)}) %collective-permute-start.13) | collective-permute-done | bytes 294944 | tf_op jit(solution)/shard_map/ppermute | solution.py:91
  150.2 1.3 fusion.1
  151.5 3.8 %collective-permute-start.16 = (bf16[192,384]{1,0:T(8,128)(2,1)S(1)}, bf16[192,384]{1,0:T(8,128)(2,1)S(1)}, u32[]{:S(2)}, u32[]{:S(2)}) collective-permute-start(bf16[192,384]{1,0:T(8,128)(2,1)S(1)} %get-tuple-element.27), channel_id=1, source_target_pairs={{0,4},{4,0},{1,5},{5,1},{2,6},{6,2},{3,7},{7,3},{8,12},{12,8},{9,1... | collective-permute-start | bytes 442376 | tf_op jit(solution)/shard_map/ppermute | solution.py:23
  155.4 0.8 convolution_convert_fusion.3
  156.2 0.8 slice.145
  157.0 1.9 collective-permute-start.4
  158.9 0.8 maximum_select_fusion.1
  159.7 1.9 collective-permute-start.17
  161.7 0.8 convolution_convert_fusion.2
  162.5 0.8 slice.155
  163.5 2.4 %collective-permute-start.5 = (bf16[512,384]{1,0:T(8,128)(2,1)}, bf16[512,384]{1,0:T(8,128)(2,1)}, u32[]{:S(2)}, u32[]{:S(2)}) collective-permute-start(bf16[512,384]{1,0:T(8,128)(2,1)} %slice.155), channel_id=1, source_target_pairs={{0,4},{4,0},{1,5},{5,1},{2,6},{6,2},{3,7},{7,3},{8,12},{12,8},{9,1... | collective-permute-start | bytes 1179656 | tf_op jit(solution)/shard_map/ppermute | solution.py:23
  165.9 0.8 convolution_convert_fusion.1
  166.7 1.1 copy.16
  167.8 4.3 %all-to-all-start.4 = ((bf16[4,2,96,768]{3,2,1,0:T(8,128)(2,1)}), bf16[4,2,96,768]{3,2,1,0:T(8,128)(2,1)S(1)}, u32[]{:S(2)}, u32[]{:S(2)}) async-start(bf16[4,2,96,768]{3,2,1,0:T(8,128)(2,1)} %bitcast.70), calls=%async_computation.4 | async-start | bytes 2359296 | tf_op jit(solution)/shard_map/all_to_all | solution.py:27
  172.2 1.1 add_convert_fusion.1
  173.3 4.9 %collective-permute-start.18 = (bf16[2,192,384]{2,1,0:T(8,128)(2,1)}, bf16[2,192,384]{2,1,0:T(8,128)(2,1)}, u32[]{:S(2)}, u32[]{:S(2)}) collective-permute-start(bf16[2,192,384]{2,1,0:T(8,128)(2,1)} %maximum_select_fusion.1), channel_id=1, source_target_pairs={{0,2},{1,3},{2,0},{3,1},{4,6},{5,7},{6,4},{7,5},{8,10},{9,11},{10,... | collective-permute-start | bytes 884744 | tf_op jit(solution)/shard_map/ppermute | solution.py:91
  178.2 2.8 %collective-permute-start.19 = (bf16[2,192,384]{2,1,0:T(8,128)(2,1)}, bf16[2,192,384]{2,1,0:T(8,128)(2,1)}, u32[]{:S(2)}, u32[]{:S(2)}) collective-permute-start(bf16[2,192,384]{2,1,0:T(8,128)(2,1)} %maximum_select_fusion.1), channel_id=1, source_target_pairs={{0,3},{1,0},{2,1},{3,2},{4,7},{5,4},{6,5},{7,6},{8,11},{9,8},{10,9... | collective-permute-start | bytes 884744 | tf_op jit(solution)/shard_map/ppermute | solution.py:91
  181.2 1.0 bitcast_dynamic-update-slice_fusion.2
  182.3 1.1 add_convert_fusion
  183.5 5.1 %all-to-all-done.4 = bf16[4,2,96,768]{3,2,1,0:T(8,128)(2,1)S(1)} async-done(((bf16[4,2,96,768]{3,2,1,0:T(8,128)(2,1)}), bf16[4,2,96,768]{3,2,1,0:T(8,128)(2,1)S(1)}, u32[]{:S(2)}, u32[]{:S(2)}) %all-to-all-start.4) | async-done | bytes 1179680 | tf_op jit(solution)/shard_map/all_to_all | solution.py:27
  188.7 1.1 broadcast_in_dim.52
  189.8 9.3 %all-to-all-start.5 = ((bf16[8,96,768]{2,1,0:T(8,128)(2,1)}), bf16[8,96,768]{2,1,0:T(8,128)(2,1)S(1)}, u32[]{:S(2)}, u32[]{:S(2)}) async-start(bf16[8,96,768]{2,1,0:T(8,128)(2,1)} %bitcast.19), calls=%async_computation.5 | async-start | bytes 2359296 | tf_op jit(solution)/shard_map/all_to_all | solution.py:27
  199.1 2.0 collective-permute-start.12
  201.1 3.0 %collective-permute-start.11 = (bf16[64,768]{1,0:T(8,128)(2,1)S(1)}, bf16[64,768]{1,0:T(8,128)(2,1)S(1)}, u32[]{:S(2)}, u32[]{:S(2)}) collective-permute-start(bf16[64,768]{1,0:T(8,128)(2,1)S(1)} %get-tuple-element.21), channel_id=1, source_target_pairs={{0,384},{64,448},{128,0},{192,64},{256,128},{320,192},{384,256},{4... | collective-permute-start | bytes 294920 | tf_op jit(solution)/shard_map/ppermute | solution.py:129
  204.2 1.0 bitcast_dynamic-update-slice_fusion.1
  205.2 4.3 %collective-permute-start.10 = (bf16[64,768]{1,0:T(8,128)(2,1)S(1)}, bf16[64,768]{1,0:T(8,128)(2,1)S(1)}, u32[]{:S(2)}, u32[]{:S(2)}) collective-permute-start(bf16[64,768]{1,0:T(8,128)(2,1)S(1)} %get-tuple-element.22), channel_id=1, source_target_pairs={{0,320},{64,384},{128,448},{192,0},{256,64},{320,128},{384,192},{4... | collective-permute-start | bytes 294920 | tf_op jit(solution)/shard_map/ppermute | solution.py:129
  209.5 5.2 %collective-permute-start.9 = (bf16[64,768]{1,0:T(8,128)(2,1)S(1)}, bf16[64,768]{1,0:T(8,128)(2,1)S(1)}, u32[]{:S(2)}, u32[]{:S(2)}) collective-permute-start(bf16[64,768]{1,0:T(8,128)(2,1)S(1)} %get-tuple-element.23), channel_id=1, source_target_pairs={{0,256},{64,320},{128,384},{192,448},{256,0},{320,64},{384,128},{4... | collective-permute-start | bytes 294920 | tf_op jit(solution)/shard_map/ppermute | solution.py:129
  214.7 1.9 collective-permute-start.8
  216.6 4.0 %collective-permute-start.7 = (bf16[64,768]{1,0:T(8,128)(2,1)S(1)}, bf16[64,768]{1,0:T(8,128)(2,1)S(1)}, u32[]{:S(2)}, u32[]{:S(2)}) collective-permute-start(bf16[64,768]{1,0:T(8,128)(2,1)S(1)} %get-tuple-element.25), channel_id=1, source_target_pairs={{0,128},{64,192},{128,256},{192,320},{256,384},{320,448},{384,0},{... | collective-permute-start | bytes 294920 | tf_op jit(solution)/shard_map/ppermute | solution.py:129
  220.7 2.2 collective-permute-start.6
  222.8 1.0 bitcast_dynamic-update-slice_fusion
  223.9 5.4 %collective-permute-done.8 = bf16[64,768]{1,0:T(8,128)(2,1)S(1)} collective-permute-done((bf16[64,768]{1,0:T(8,128)(2,1)S(1)}, bf16[64,768]{1,0:T(8,128)(2,1)S(1)}, u32[]{:S(2)}, u32[]{:S(2)}) %collective-permute-start.8) | collective-permute-done | bytes 98336 | tf_op jit(solution)/shard_map/ppermute | solution.py:129
  229.3 4.4 %collective-permute-done.6 = bf16[64,768]{1,0:T(8,128)(2,1)S(1)} collective-permute-done((bf16[64,768]{1,0:T(8,128)(2,1)S(1)}, bf16[64,768]{1,0:T(8,128)(2,1)S(1)}, u32[]{:S(2)}, u32[]{:S(2)}) %collective-permute-start.6) | collective-permute-done | bytes 98336 | tf_op jit(solution)/shard_map/ppermute | solution.py:129
  233.8 0.6 fusion.22
  234.6 1.1 pad_maximum_fusion.3
  (77 shorter events, 1.4 us)
Async XLA Ops:
  0.6 9.3 %copy-start = (bf16[384,1536]{1,0:T(8,128)(2,1)S(1)}, bf16[384,1536]{1,0:T(8,128)(2,1)}, u32[]{:S(2)}) copy-start(bf16[384,1536]{1,0:T(8,128)(2,1)} %param.5) | copy-start | bytes 3538948
  2.3 19.3 %all-to-all-start = ((bf16[8,64,384]{2,1,0:T(8,128)(2,1)}), bf16[8,64,384]{2,1,0:T(8,128)(2,1)S(1)}, u32[]{:S(2)}, u32[]{:S(2)}) async-start(bf16[8,64,384]{2,1,0:T(8,128)(2,1)} %broadcast_in_dim.47), calls=%async_computation | async-start | bytes 786432 | tf_op jit(solution)/shard_map/all_to_all | solution.py:27
  10.1 18.8 %copy-start.7 = (bf16[384,768]{1,0:T(8,128)(2,1)}, bf16[384,768]{1,0:T(8,128)(2,1)S(1)}, u32[]{:S(2)}) copy-start(bf16[384,768]{1,0:T(8,128)(2,1)S(1)} %get-tuple-element.17) | copy-start | bytes 1769476
  10.1 17.4 %collective-permute-start.1 = (bf16[384,768]{1,0:T(8,128)(2,1)S(1)}, bf16[384,768]{1,0:T(8,128)(2,1)S(1)}, u32[]{:S(2)}, u32[]{:S(2)}) collective-permute-start(bf16[384,768]{1,0:T(8,128)(2,1)S(1)} %get-tuple-element.18), channel_id=1, source_target_pairs={{0,4},{4,0},{1,5},{5,1},{2,6},{6,2},{3,7},{7,3},{8,12},{12,8},{9,1... | collective-permute-start | bytes 1769480 | tf_op jit(solution)/shard_map/ppermute | solution.py:23
  21.6 8.9 %copy-start.13 = (bf16[8,64,384]{2,1,0:T(8,128)(2,1)}, bf16[8,64,384]{2,1,0:T(8,128)(2,1)S(1)}, u32[]{:S(2)}) copy-start(bf16[8,64,384]{2,1,0:T(8,128)(2,1)S(1)} %all-to-all-done) | copy-start | bytes 1179652
  21.6 7.2 %collective-permute-start = (bf16[512,384]{1,0:T(8,128)(2,1)S(1)}, bf16[512,384]{1,0:T(8,128)(2,1)S(1)}, u32[]{:S(2)}, u32[]{:S(2)}) collective-permute-start(bf16[512,384]{1,0:T(8,128)(2,1)S(1)} %bitcast.86), channel_id=1, source_target_pairs={{0,4},{4,0},{1,5},{5,1},{2,6},{6,2},{3,7},{7,3},{8,12},{12,8},{9,1... | collective-permute-start | bytes 1179656 | tf_op jit(solution)/shard_map/ppermute | solution.py:23
  27.5 3.0 %copy-start.18 = (bf16[384,768]{1,0:T(8,128)(2,1)}, bf16[384,768]{1,0:T(8,128)(2,1)S(1)}, u32[]{:S(2)}) copy-start(bf16[384,768]{1,0:T(8,128)(2,1)S(1)} %collective-permute-done.1) | copy-start | bytes 1769476
  28.8 1.7 copy-start.22
  30.5 10.2 %copy-start.1 = (bf16[1536,384]{1,0:T(8,128)(2,1)S(1)}, bf16[1536,384]{1,0:T(8,128)(2,1)}, u32[]{:S(2)}) copy-start(bf16[1536,384]{1,0:T(8,128)(2,1)} %param.6) | copy-start | bytes 3538948
  30.5 43.4 %all-to-all-start.1 = ((bf16[8,64,768]{2,1,0:T(8,128)(2,1)}), bf16[8,64,768]{2,1,0:T(8,128)(2,1)S(1)}, u32[]{:S(2)}, u32[]{:S(2)}) async-start(bf16[8,64,768]{2,1,0:T(8,128)(2,1)} %bitcast.1), calls=%async_computation.1 | async-start | bytes 1572864 | tf_op jit(solution)/shard_map/all_to_all | solution.py:27
  40.7 2.7 %copy-start.17 = (bf16[64,384]{1,0:T(8,128)(2,1)S(1)}, bf16[64,384]{1,0:T(8,128)(2,1)}, u32[]{:S(2)}) copy-start(bf16[64,384]{1,0:T(8,128)(2,1)} %param.7) | copy-start | bytes 147460
  40.9 31.2 %copy-start.9 = (bf16[768,384]{1,0:T(8,128)(2,1)}, bf16[768,384]{1,0:T(8,128)(2,1)S(1)}, u32[]{:S(2)}) copy-start(bf16[768,384]{1,0:T(8,128)(2,1)S(1)} %get-tuple-element.15) | copy-start | bytes 1769476
  40.9 31.2 %collective-permute-start.3 = (bf16[768,384]{1,0:T(8,128)(2,1)S(1)}, bf16[768,384]{1,0:T(8,128)(2,1)S(1)}, u32[]{:S(2)}, u32[]{:S(2)}) collective-permute-start(bf16[768,384]{1,0:T(8,128)(2,1)S(1)} %get-tuple-element.16), channel_id=1, source_target_pairs={{0,4},{4,0},{1,5},{5,1},{2,6},{6,2},{3,7},{7,3},{8,12},{12,8},{9,1... | collective-permute-start | bytes 1769480 | tf_op jit(solution)/shard_map/ppermute | solution.py:23
  63.5 8.4 %collective-permute-start.2 = (bf16[512,384]{1,0:T(8,128)(2,1)S(1)}, bf16[512,384]{1,0:T(8,128)(2,1)S(1)}, u32[]{:S(2)}, u32[]{:S(2)}) collective-permute-start(bf16[512,384]{1,0:T(8,128)(2,1)S(1)} %all_gather.3), channel_id=1, source_target_pairs={{0,4},{4,0},{1,5},{5,1},{2,6},{6,2},{3,7},{7,3},{8,12},{12,8},{9,1... | collective-permute-start | bytes 1179656 | tf_op jit(solution)/shard_map/ppermute | solution.py:23
  72.0 0.9 copy-start.15
  72.0 1.1 copy-start.20
  75.4 45.2 %all-to-all-start.2 = ((bf16[8,64,1536]{2,1,0:T(8,128)(2,1)}), bf16[8,64,1536]{2,1,0:T(8,128)(2,1)S(1)}, u32[]{:S(2)}, u32[]{:S(2)}) async-start(bf16[8,64,1536]{2,1,0:T(8,128)(2,1)} %pad_maximum_fusion), calls=%async_computation.2 | async-start | bytes 3145728 | tf_op jit(solution)/shard_map/all_to_all | solution.py:27
  121.8 39.8 %all-to-all-start.3 = ((bf16[8,64,768]{2,1,0:T(8,128)(2,1)}), bf16[8,64,768]{2,1,0:T(8,128)(2,1)S(1)}, u32[]{:S(2)}, u32[]{:S(2)}) async-start(bf16[8,64,768]{2,1,0:T(8,128)(2,1)} %broadcast_in_dim.51), calls=%async_computation.3 | async-start | bytes 1572864 | tf_op jit(solution)/shard_map/all_to_all | solution.py:27
  125.4 1.1 copy-start.16
  128.3 9.4 %collective-permute-start.15 = (bf16[192,768]{1,0:T(8,128)(2,1)}, bf16[192,768]{1,0:T(8,128)(2,1)}, u32[]{:S(2)}, u32[]{:S(2)}) collective-permute-start(bf16[192,768]{1,0:T(8,128)(2,1)} %get-tuple-element.11), channel_id=1, source_target_pairs={{0,3},{1,0},{2,1},{3,2},{4,7},{5,4},{6,5},{7,6},{8,11},{9,8},{10,9... | collective-permute-start | bytes 884744 | tf_op jit(solution)/shard_map/ppermute | solution.py:91
  132.7 9.5 %collective-permute-start.14 = (bf16[192,768]{1,0:T(8,128)(2,1)}, bf16[192,768]{1,0:T(8,128)(2,1)}, u32[]{:S(2)}, u32[]{:S(2)}) collective-permute-start(bf16[192,768]{1,0:T(8,128)(2,1)} %get-tuple-element.12), channel_id=1, source_target_pairs={{0,2},{1,3},{2,0},{3,1},{4,6},{5,7},{6,4},{7,5},{8,10},{9,11},{10,... | collective-permute-start | bytes 884744 | tf_op jit(solution)/shard_map/ppermute | solution.py:91
  135.1 15.1 %collective-permute-start.13 = (bf16[192,768]{1,0:T(8,128)(2,1)}, bf16[192,768]{1,0:T(8,128)(2,1)}, u32[]{:S(2)}, u32[]{:S(2)}) collective-permute-start(bf16[192,768]{1,0:T(8,128)(2,1)} %get-tuple-element.10), channel_id=1, source_target_pairs={{0,1},{1,2},{2,3},{3,0},{4,5},{5,6},{6,7},{7,4},{8,9},{9,10},{10,1... | collective-permute-start | bytes 884744 | tf_op jit(solution)/shard_map/ppermute | solution.py:91
  137.6 17.7 %copy-start.10 = (bf16[768,384]{1,0:T(8,128)(2,1)S(1)}, bf16[768,384]{1,0:T(8,128)(2,1)}, u32[]{:S(2)}) copy-start(bf16[768,384]{1,0:T(8,128)(2,1)} %copy-done.9) | copy-start | bytes 1769476
  137.7 17.7 %copy-start.21 = (bf16[768,384]{1,0:T(8,128)(2,1)S(1)}, bf16[768,384]{1,0:T(8,128)(2,1)}, u32[]{:S(2)}) copy-start(bf16[768,384]{1,0:T(8,128)(2,1)} %copy-done.20) | copy-start | bytes 1769476
  151.5 7.4 %collective-permute-start.16 = (bf16[192,384]{1,0:T(8,128)(2,1)S(1)}, bf16[192,384]{1,0:T(8,128)(2,1)S(1)}, u32[]{:S(2)}, u32[]{:S(2)}) collective-permute-start(bf16[192,384]{1,0:T(8,128)(2,1)S(1)} %get-tuple-element.27), channel_id=1, source_target_pairs={{0,4},{4,0},{1,5},{5,1},{2,6},{6,2},{3,7},{7,3},{8,12},{12,8},{9,1... | collective-permute-start | bytes 442376 | tf_op jit(solution)/shard_map/ppermute | solution.py:23
  156.2 3.5 %copy-start.5 = (bf16[512,768]{1,0:T(8,128)(2,1)}, bf16[512,768]{1,0:T(8,128)(2,1)S(1)}, u32[]{:S(2)}) copy-start(bf16[512,768]{1,0:T(8,128)(2,1)S(1)} %convolution_convert_fusion.3) | copy-start | bytes 2359300
  156.2 5.4 %copy-start.8 = (bf16[384,768]{1,0:T(8,128)(2,1)S(1)}, bf16[384,768]{1,0:T(8,128)(2,1)}, u32[]{:S(2)}) copy-start(bf16[384,768]{1,0:T(8,128)(2,1)} %copy-done.7) | copy-start | bytes 1769476
  156.2 5.4 %copy-start.19 = (bf16[384,768]{1,0:T(8,128)(2,1)S(1)}, bf16[384,768]{1,0:T(8,128)(2,1)}, u32[]{:S(2)}) copy-start(bf16[384,768]{1,0:T(8,128)(2,1)} %copy-done.18) | copy-start | bytes 1769476
  157.0 15.2 %collective-permute-start.4 = (bf16[512,384]{1,0:T(8,128)(2,1)}, bf16[512,384]{1,0:T(8,128)(2,1)}, u32[]{:S(2)}, u32[]{:S(2)}) collective-permute-start(bf16[512,384]{1,0:T(8,128)(2,1)} %slice.145), channel_id=1, source_target_pairs={{0,4},{4,0},{1,5},{5,1},{2,6},{6,2},{3,7},{7,3},{8,12},{12,8},{9,1... | collective-permute-start | bytes 1179656 | tf_op jit(solution)/shard_map/ppermute | solution.py:23
  158.9 3.6 %copy-start.11 = (bf16[192,384]{1,0:T(8,128)(2,1)}, bf16[192,384]{1,0:T(8,128)(2,1)S(1)}, u32[]{:S(2)}) copy-start(bf16[192,384]{1,0:T(8,128)(2,1)S(1)} %collective-permute-done.16) | copy-start | bytes 442372
  159.7 21.5 %collective-permute-start.17 = (bf16[2,192,384]{2,1,0:T(8,128)(2,1)}, bf16[2,192,384]{2,1,0:T(8,128)(2,1)}, u32[]{:S(2)}, u32[]{:S(2)}) collective-permute-start(bf16[2,192,384]{2,1,0:T(8,128)(2,1)} %maximum_select_fusion.1), channel_id=1, source_target_pairs={{0,1},{1,2},{2,3},{3,0},{4,5},{5,6},{6,7},{7,4},{8,9},{9,10},{10,1... | collective-permute-start | bytes 884744 | tf_op jit(solution)/shard_map/ppermute | solution.py:91
  161.6 4.3 %copy-start.14 = (bf16[8,64,384]{2,1,0:T(8,128)(2,1)S(1)}, bf16[8,64,384]{2,1,0:T(8,128)(2,1)}, u32[]{:S(2)}) copy-start(bf16[8,64,384]{2,1,0:T(8,128)(2,1)} %copy-done.13) | copy-start | bytes 1179652
  161.7 4.3 %copy-start.23 = (bf16[512,384]{1,0:T(8,128)(2,1)S(1)}, bf16[512,384]{1,0:T(8,128)(2,1)}, u32[]{:S(2)}) copy-start(bf16[512,384]{1,0:T(8,128)(2,1)} %copy-done.22) | copy-start | bytes 1179652
  162.5 1.0 copy-start.3
  163.5 18.8 %collective-permute-start.5 = (bf16[512,384]{1,0:T(8,128)(2,1)}, bf16[512,384]{1,0:T(8,128)(2,1)}, u32[]{:S(2)}, u32[]{:S(2)}) collective-permute-start(bf16[512,384]{1,0:T(8,128)(2,1)} %slice.155), channel_id=1, source_target_pairs={{0,4},{4,0},{1,5},{5,1},{2,6},{6,2},{3,7},{7,3},{8,12},{12,8},{9,1... | collective-permute-start | bytes 1179656 | tf_op jit(solution)/shard_map/ppermute | solution.py:23
  167.8 4.4 %copy-start.6 = (bf16[512,768]{1,0:T(8,128)(2,1)S(1)}, bf16[512,768]{1,0:T(8,128)(2,1)}, u32[]{:S(2)}) copy-start(bf16[512,768]{1,0:T(8,128)(2,1)} %copy-done.5) | copy-start | bytes 2359300
  167.8 20.7 %all-to-all-start.4 = ((bf16[4,2,96,768]{3,2,1,0:T(8,128)(2,1)}), bf16[4,2,96,768]{3,2,1,0:T(8,128)(2,1)S(1)}, u32[]{:S(2)}, u32[]{:S(2)}) async-start(bf16[4,2,96,768]{3,2,1,0:T(8,128)(2,1)} %bitcast.70), calls=%async_computation.4 | async-start | bytes 2359296 | tf_op jit(solution)/shard_map/all_to_all | solution.py:27
  172.2 9.0 %copy-start.12 = (bf16[192,384]{1,0:T(8,128)(2,1)S(1)}, bf16[192,384]{1,0:T(8,128)(2,1)}, u32[]{:S(2)}) copy-start(bf16[192,384]{1,0:T(8,128)(2,1)} %copy-done.11) | copy-start | bytes 442372
  173.3 30.9 %collective-permute-start.18 = (bf16[2,192,384]{2,1,0:T(8,128)(2,1)}, bf16[2,192,384]{2,1,0:T(8,128)(2,1)}, u32[]{:S(2)}, u32[]{:S(2)}) collective-permute-start(bf16[2,192,384]{2,1,0:T(8,128)(2,1)} %maximum_select_fusion.1), channel_id=1, source_target_pairs={{0,2},{1,3},{2,0},{3,1},{4,6},{5,7},{6,4},{7,5},{8,10},{9,11},{10,... | collective-permute-start | bytes 884744 | tf_op jit(solution)/shard_map/ppermute | solution.py:91
  178.2 36.5 %collective-permute-start.19 = (bf16[2,192,384]{2,1,0:T(8,128)(2,1)}, bf16[2,192,384]{2,1,0:T(8,128)(2,1)}, u32[]{:S(2)}, u32[]{:S(2)}) collective-permute-start(bf16[2,192,384]{2,1,0:T(8,128)(2,1)} %maximum_select_fusion.1), channel_id=1, source_target_pairs={{0,3},{1,0},{2,1},{3,2},{4,7},{5,4},{6,5},{7,6},{8,11},{9,8},{10,9... | collective-permute-start | bytes 884744 | tf_op jit(solution)/shard_map/ppermute | solution.py:91
  181.0 1.3 copy-start.4
  189.8 44.7 %all-to-all-start.5 = ((bf16[8,96,768]{2,1,0:T(8,128)(2,1)}), bf16[8,96,768]{2,1,0:T(8,128)(2,1)S(1)}, u32[]{:S(2)}, u32[]{:S(2)}) async-start(bf16[8,96,768]{2,1,0:T(8,128)(2,1)} %bitcast.19), calls=%async_computation.5 | async-start | bytes 2359296 | tf_op jit(solution)/shard_map/all_to_all | solution.py:27
  199.1 17.5 %collective-permute-start.12 = (bf16[64,768]{1,0:T(8,128)(2,1)S(1)}, bf16[64,768]{1,0:T(8,128)(2,1)S(1)}, u32[]{:S(2)}, u32[]{:S(2)}) collective-permute-start(bf16[64,768]{1,0:T(8,128)(2,1)S(1)} %get-tuple-element.20), channel_id=1, source_target_pairs={{0,448},{64,0},{128,64},{192,128},{256,192},{320,256},{384,320},{4... | collective-permute-start | bytes 294920 | tf_op jit(solution)/shard_map/ppermute | solution.py:129
  201.1 19.5 %collective-permute-start.11 = (bf16[64,768]{1,0:T(8,128)(2,1)S(1)}, bf16[64,768]{1,0:T(8,128)(2,1)S(1)}, u32[]{:S(2)}, u32[]{:S(2)}) collective-permute-start(bf16[64,768]{1,0:T(8,128)(2,1)S(1)} %get-tuple-element.21), channel_id=1, source_target_pairs={{0,384},{64,448},{128,0},{192,64},{256,128},{320,192},{384,256},{4... | collective-permute-start | bytes 294920 | tf_op jit(solution)/shard_map/ppermute | solution.py:129
  205.2 18.7 %collective-permute-start.10 = (bf16[64,768]{1,0:T(8,128)(2,1)S(1)}, bf16[64,768]{1,0:T(8,128)(2,1)S(1)}, u32[]{:S(2)}, u32[]{:S(2)}) collective-permute-start(bf16[64,768]{1,0:T(8,128)(2,1)S(1)} %get-tuple-element.22), channel_id=1, source_target_pairs={{0,320},{64,384},{128,448},{192,0},{256,64},{320,128},{384,192},{4... | collective-permute-start | bytes 294920 | tf_op jit(solution)/shard_map/ppermute | solution.py:129
  209.5 14.4 %collective-permute-start.9 = (bf16[64,768]{1,0:T(8,128)(2,1)S(1)}, bf16[64,768]{1,0:T(8,128)(2,1)S(1)}, u32[]{:S(2)}, u32[]{:S(2)}) collective-permute-start(bf16[64,768]{1,0:T(8,128)(2,1)S(1)} %get-tuple-element.23), channel_id=1, source_target_pairs={{0,256},{64,320},{128,384},{192,448},{256,0},{320,64},{384,128},{4... | collective-permute-start | bytes 294920 | tf_op jit(solution)/shard_map/ppermute | solution.py:129
  214.7 14.6 %collective-permute-start.8 = (bf16[64,768]{1,0:T(8,128)(2,1)S(1)}, bf16[64,768]{1,0:T(8,128)(2,1)S(1)}, u32[]{:S(2)}, u32[]{:S(2)}) collective-permute-start(bf16[64,768]{1,0:T(8,128)(2,1)S(1)} %get-tuple-element.24), channel_id=1, source_target_pairs={{0,192},{64,256},{128,320},{192,384},{256,448},{320,0},{384,64},{4... | collective-permute-start | bytes 294920 | tf_op jit(solution)/shard_map/ppermute | solution.py:129
  216.6 12.7 %collective-permute-start.7 = (bf16[64,768]{1,0:T(8,128)(2,1)S(1)}, bf16[64,768]{1,0:T(8,128)(2,1)S(1)}, u32[]{:S(2)}, u32[]{:S(2)}) collective-permute-start(bf16[64,768]{1,0:T(8,128)(2,1)S(1)} %get-tuple-element.25), channel_id=1, source_target_pairs={{0,128},{64,192},{128,256},{192,320},{256,384},{320,448},{384,0},{... | collective-permute-start | bytes 294920 | tf_op jit(solution)/shard_map/ppermute | solution.py:129
  220.7 13.1 %collective-permute-start.6 = (bf16[64,768]{1,0:T(8,128)(2,1)S(1)}, bf16[64,768]{1,0:T(8,128)(2,1)S(1)}, u32[]{:S(2)}, u32[]{:S(2)}) collective-permute-start(bf16[64,768]{1,0:T(8,128)(2,1)S(1)} %get-tuple-element.19), channel_id=1, source_target_pairs={{0,64},{64,128},{128,192},{192,256},{256,320},{320,384},{384,448},... | collective-permute-start | bytes 294920 | tf_op jit(solution)/shard_map/ppermute | solution.py:129
  223.9 10.7 %copy-start.2 = (bf16[2,4,192,384]{3,2,1,0:T(8,128)(2,1)}, bf16[2,4,192,384]{3,2,1,0:T(8,128)(2,1)S(1)}, u32[]{:S(2)}) copy-start(bf16[2,4,192,384]{3,2,1,0:T(8,128)(2,1)S(1)} %bitcast_dynamic-update-slice_fusion) | copy-start | bytes 3538948

commit v5 on v3

v5 whole, which is shorter than its diff:
```python
import jax
import jax.numpy as jnp
from jax import lax
from jax.sharding import Mesh, PartitionSpec as P

bf16 = jnp.bfloat16
f32 = jnp.float32


def gelu_pullback(hidden, upstream):
    _, pullback = jax.vjp(jax.nn.gelu, hidden)
    return pullback(upstream)[0]


def dot(left, right, dims):
    return lax.dot_general(
        left, right, ((dims[:1], dims[1:]), ((), ())), preferred_element_type=f32
    ).astype(bf16)


def swap(x):
    return lax.ppermute(x, "core", [(0, 1), (1, 0)])


def exchange(x, axis):
    return lax.all_to_all(x, axis, 0, 0, tiled=False)


def total_of(x):
    parts = [x[i].astype(f32) for i in range(x.shape[0])]
    while len(parts) > 1:
        parts = [a + b for a, b in zip(parts[::2], parts[1::2])]
    return parts[0]


def gather(x, axis):
    n = lax.axis_size(axis)
    got = exchange(jnp.broadcast_to(x[None], (n,) + x.shape), axis)
    return got.reshape((n * x.shape[0],) + x.shape[1:])


def pair(own, other, place, axis):
    return jnp.where(
        place == 0,
        jnp.concatenate([own, other], axis),
        jnp.concatenate([other, own], axis),
    )


def per_device(tokens, up_weight, down_weight, out_grads):
    core, zl, rep = (lax.axis_index(a) for a in ("core", "zl", "rep"))
    rows, width = tokens.shape
    half = up_weight.shape[1] // 2
    n_row, n_zh, n_rep = (lax.axis_size(a) for a in ("row", "zh", "rep"))
    n_z = 2 * n_zh
    mine, theirs = core * half, (1 - core) * half

    even = [(p, p ^ 1) for p in range(n_z)]
    odd = [(p, (p + 1 if p % 2 else p - 1) % n_z) for p in range(n_z)]
    near = [(r, r ^ 1) for r in range(n_rep)]
    far = [(r, n_rep - 1 - r) for r in range(n_rep)]

    def z_swap(x, pairs):
        return lax.ppermute(x, ("zh", "zl"), pairs)

    def pick(x, index):
        return lax.dynamic_index_in_dim(x, index, 0, False)

    def plus(a, b):
        return (a.astype(f32) + b.astype(f32)).astype(bf16)

    up_own = lax.dynamic_slice_in_dim(up_weight, mine, half, 1)
    up_other = swap(lax.dynamic_slice_in_dim(up_weight, theirs, half, 1))
    down_own = lax.dynamic_slice_in_dim(down_weight, mine, half, 0)
    down_other = swap(lax.dynamic_slice_in_dim(down_weight, theirs, half, 0))
    up = jnp.concatenate([up_own, up_other], 0)
    down = jnp.concatenate([down_own, down_other], 1)

    own = gather(jnp.concatenate([tokens, out_grads], 1), "row")
    other = swap(own)
    tok = jnp.concatenate([own[:, :width], other[:, :width]], 1)
    og = jnp.concatenate([own[:, width:], other[:, width:]], 1)
    total = tok.shape[0]
    share = total // n_z

    def first_sum(part, pairs):
        part = part.reshape(2, n_zh, share, half)
        return plus(pick(part, zl), z_swap(pick(part, 1 - zl), pairs))

    hid_half = first_sum(dot(tok, up, (1, 0)), even)
    ag_half = first_sum(dot(og, down, (1, 1)), odd)
    sums = total_of(exchange(jnp.concatenate([hid_half, ag_half], 2), "zh"))
    hidden, act_grads = sums[:, :half], sums[:, half:]
    act = jax.nn.gelu(hidden).astype(bf16)
    hid_grads = gelu_pullback(hidden, act_grads).astype(bf16)

    both = lax.all_gather(
        jnp.concatenate([act, hid_grads], 1), "zh", axis=0, tiled=True
    )

    def whole(part, pairs):
        return pair(part, z_swap(part, pairs), zl, 0)

    act, hg = whole(both[:, :half], even), whole(both[:, half:], odd)

    def split(x, bit):
        x = x.reshape((2, x.shape[0] // 2) + x.shape[1:])
        return pick(x, bit), pick(x, 1 - bit)

    def scatter(x, step):
        keep, send = split(x, step[0])
        return plus(keep, lax.ppermute(send, "rep", step[1]))

    def collect(x, steps, axis):
        for bit, pairs in steps[::-1]:
            x = pair(x, lax.ppermute(x, "rep", pairs), bit, axis)
        return x

    high, low = rep // 2, rep % 2
    down_steps = [((rep + 1) // 2 % 2, near), (high, far)]
    up_steps = [(high, far), (low, near)]
    piece = width // n_rep
    down_part = scatter(dot(act, og, (0, 0)), down_steps[0])
    up_part = dot(tok, hg, (0, 0)).reshape(2, n_rep, piece, half)
    up_part = scatter(jnp.swapaxes(up_part, 0, 1), up_steps[0])
    down_part, up_part, act, hg = lax.optimization_barrier(
        (down_part, up_part, act, hg)
    )
    down_part = scatter(down_part, down_steps[1])
    up_part = scatter(up_part, up_steps[1]).reshape(2, piece, half)
    down_part = pair(down_part[None, :, :width], swap(down_part[None, :, width:]), core, 0)
    up_part = pair(up_part[0], swap(up_part[1]), core, 1)
    down_grads = collect(down_part, down_steps, 1).reshape(2 * half, width)
    up_grads = collect(up_part, up_steps, 0)

    def output(left, weight, dims):
        part = dot(left, weight, dims)
        return plus(part[:, :width], swap(part[:, width:]))

    out = jnp.concatenate([output(act, down, (1, 0)), output(hg, up, (1, 1))], 1)
    out = total_of(exchange(out.reshape(n_row, rows, 2 * width), "row")).astype(bf16)
    return (out[:, :width], out[:, width:], up_grads, down_grads)


def solution(mesh):
    n_row, n_col, n_rep = mesh.devices.shape
    split = Mesh(
        mesh.devices.reshape(n_row, n_col // 4, 2, 2, n_rep),
        ("row", "zh", "zl", "core", "rep"),
    )
    col = ("zh", "zl", "core")
    acts = P(("rep", "row"), col)
    up = P(col, "row")
    down = P("row", col)
    return jax.shard_map(
        per_device,
        mesh=split,
        in_specs=(acts, up, down, acts),
        out_specs=(acts, acts, up, down),
        check_vma=False,
    )
```

time: 212 us -> 207 us (0.976)
  blocking collectives: 27.9 us -> 66.5 us
  waiting for transfers between devices: 73.5 us -> 37.3 us
  between operations: 14.5 us -> 1.44 us
  starting transfers between devices: 67.3 us -> 76.1 us
  local copies, waits for them, and re-layouts: 9.16 us -> 4.96 us
    all_to_all x5 -> x1, waiting for transfers between devices: 27.2 us -> 0.01 us  [exchange(): return lax.all_to_all(x, axis, 0, 0, tiled=False)]
    ppermute x6 -> x12, starting transfers between devices: 20 us -> 44 us  [the longest x4 20 us: z_swap(): return lax.ppermute(x, ('zh', 'zl'), pairs)]
    all_to_all x5 -> x1, starting transfers between devices: 26.9 us -> 3.55 us  [exchange(): return lax.all_to_all(x, axis, 0, 0, tiled=False)]
    all_to_all x1 -> x2, blocking collectives: 27.9 us -> 48.1 us  [exchange(): return lax.all_to_all(x, axis, 0, 0, tiled=False)]
    reduce_scatter x2 -> x0, waiting for transfers between devices: 18.8 us -> none  [the longest x1 18.8 us: per_device(): act_grads = lax.psum_scatter(ag_part, 'z', scatter_dimension=0, tiled=True)]
    all_gather x0 -> x1, blocking collectives: none -> 18.5 us  [per_device(): lax.all_gather(jnp.concatenate([act, hid_grads], 1), 'zh', axis=0, tiled=...]
    ppermute x6 -> x12, waiting for transfers between devices: 24 us -> 36.5 us  [the longest x4 13 us: collect(): x = pair(x, lax.ppermute(x, 'rep', pairs), bit, axis)]
    ppermute x6 -> x7, starting transfers between devices: 20.3 us -> 28.5 us  [swap(): return lax.ppermute(x, 'core', [(0, 1), (1, 0)])]
  transfers between devices with their start and end apart: 19 -> 20, of which waited for: 9 -> 11; matrix products, arithmetic and copies ran while one was open for 10% -> 9% of each run, Pallas kernels for 0% -> 0%
where the time goes in v5:
time: 207 us; the launch traced here: 205 us
  starting transfers between devices  76.1 us (37%)
  blocking collectives  66.5 us (32%)
  waiting for transfers between devices  37.3 us (18%)
  matrix products  9.48 us (5%)
  other arithmetic  9.02 us (4%)
  local copies, waits for them, and re-layouts  4.96 us (2%)
    all_to_all x2, blocking collectives, exchange(): return lax.all_to_all(x, axis, 0, 0, tiled=False)  48.1 us
    ppermute x7, starting transfers between devices, swap(): return lax.ppermute(x, 'core', [(0, 1), (1, 0)])  28.5 us
    ppermute x4, starting transfers between devices, z_swap(): return lax.ppermute(x, ('zh', 'zl'), pairs)  20 us
    all_gather x1, blocking collectives, per_device(): lax.all_gather(jnp.concatenate([act, hid_grads], 1), 'zh', axis=0, tiled=...  18.5 us
    ppermute x4, waiting for transfers between devices, collect(): x = pair(x, lax.ppermute(x, 'rep', pairs), bit, axis)  13 us
    ppermute x4, starting transfers between devices, scatter(): return plus(keep, lax.ppermute(send, 'rep', step[1]))  12.6 us
    ppermute x4, waiting for transfers between devices, z_swap(): return lax.ppermute(x, ('zh', 'zl'), pairs)  11.9 us
    ppermute x4, waiting for transfers between devices, scatter(): return plus(keep, lax.ppermute(send, 'rep', step[1]))  11.7 us
  transfers between devices with their start and end apart: 20, of which 11 were waited for; matrix products, arithmetic and copies ran while one was open for 9% of the time, Pallas kernels for 0%

profile of v5, /device:TPU:1, one launch (start us, length us, event | category | flops | bytes accessed | tf_op | source)
XLA Modules:
  0.0 204.8 jit_solution(16611922520207083836)
XLA Ops:
  0.6 0.8 pad_maximum_fusion.15
  1.5 27.9 %all_to_all.15 = bf16[8,64,768]{2,1,0:T(8,128)(2,1)S(1)} all-to-all(bf16[8,64,768]{2,1,0:T(8,128)(2,1)S(1)} %broadcast_in_dim.12), channel_id=1, replica_groups=mesh['row'=8,'zh'=4,'zl'=2,'core'=2,'rep'=4] {'row'}, dimensions={0} | all-to-all | bytes 1572864 | tf_op jit(solution)/shard_map/all_to_all | solution.py:26
  29.5 5.6 %collective-permute-start = (bf16[512,768]{1,0:T(8,128)(2,1)S(1)}, bf16[512,768]{1,0:T(8,128)(2,1)S(1)}, u32[]{:S(2)}, u32[]{:S(2)}) collective-permute-start(bf16[512,768]{1,0:T(8,128)(2,1)S(1)} %bitcast.54), channel_id=1, source_target_pairs={{0,4},{4,0},{1,5},{5,1},{2,6},{6,2},{3,7},{7,3},{8,12},{12,8},{9,1... | collective-permute-start | bytes 2359304 | tf_op jit(solution)/shard_map/ppermute | solution.py:22
  35.1 0.9 constant_dynamic-slice_fusion.2
  36.1 1.9 collective-permute-start.3
  38.0 0.9 constant_dynamic-slice_fusion.4
  38.9 2.4 %collective-permute-start.1 = (bf16[384,768]{1,0:T(8,128)(2,1)S(1)}, bf16[384,768]{1,0:T(8,128)(2,1)}, u32[]{:S(2)}, u32[]{:S(2)}) collective-permute-start(bf16[384,768]{1,0:T(8,128)(2,1)S(1)} %get-tuple-element.13), channel_id=1, source_target_pairs={{0,4},{4,0},{1,5},{5,1},{2,6},{6,2},{3,7},{7,3},{8,12},{12,8},{9,1... | collective-permute-start | bytes 1769480 | tf_op jit(solution)/shard_map/ppermute | solution.py:22
  41.6 2.3 %convolution_convert_fusion.4 = bf16[512,768]{1,0:T(8,128)(2,1)S(1)} fusion(bf16[768,384]{1,0:T(8,128)(2,1)} %collective-permute-done.3, bf16[768,384]{1,0:T(8,128)(2,1)S(1)} %get-tuple-element.14, bf16[512,384]{1,0:T(8,128)(2,1)S(1)} %get-tuple-element.21, bf16[512,384]{1,0:T(8,128)(2,1)S(1)} %get-tuple-element.19), kind=kOutput, calls=%fused_computation.4 | convolution fusion | flops 608305152 | bytes 2752512 | tf_op jit(solution)/shard_map/dot_general | solution.py:16
  43.9 10.7 %collective-permute-start.4 = (bf16[4,64,768]{2,1,0:T(8,128)(2,1)S(1)}, bf16[4,64,768]{2,1,0:T(8,128)(2,1)S(1)}, u32[]{:S(2)}, u32[]{:S(2)}) collective-permute-start(bf16[4,64,768]{2,1,0:T(8,128)(2,1)S(1)} %dynamic-slice_bitcast_fusion.2), channel_id=1, source_target_pairs={{0,56},{8,16},{16,8},{24,32},{32,24},{40,48},{48,40},{56,0},{1,57}... | collective-permute-start | bytes 1179656 | tf_op jit(solution)/shard_map/ppermute | solution.py:64
  54.6 1.8 convolution_convert_fusion.5
  56.5 1.9 collective-permute-start.2
  58.5 5.6 %collective-permute-done.4 = bf16[4,64,768]{2,1,0:T(8,128)(2,1)S(1)} collective-permute-done((bf16[4,64,768]{2,1,0:T(8,128)(2,1)S(1)}, bf16[4,64,768]{2,1,0:T(8,128)(2,1)S(1)}, u32[]{:S(2)}, u32[]{:S(2)}) %collective-permute-start.4) | collective-permute-done | bytes 393248 | tf_op jit(solution)/shard_map/ppermute | solution.py:64
  64.1 0.1 fusion.2
  64.2 4.7 %collective-permute-done.2 = bf16[4,64,768]{2,1,0:T(8,128)(2,1)S(1)} collective-permute-done((bf16[4,64,768]{2,1,0:T(8,128)(2,1)S(1)}, bf16[4,64,768]{2,1,0:T(8,128)(2,1)S(1)}, u32[]{:S(2)}, u32[]{:S(2)}) %collective-permute-start.2) | collective-permute-done | bytes 393248 | tf_op jit(solution)/shard_map/ppermute | solution.py:64
  68.9 0.1 fusion.3
  69.0 20.2 %all_to_all.16 = bf16[4,64,1536]{2,1,0:T(8,128)(2,1)S(1)} all-to-all(bf16[4,64,1536]{2,1,0:T(8,128)(2,1)S(1)} %pad_maximum_fusion.4), channel_id=1, replica_groups=mesh['row'=8,'zh'=4,'zl'=2,'core'=2,'rep'=4] {'zh'}, dimensions={0} | all-to-all | bytes 1572864 | tf_op jit(solution)/shard_map/all_to_all | solution.py:26
  89.2 0.1 add_bitcast_fusion
  89.3 0.1 multiply_convert_fusion
  89.5 18.5 %all_gather.3 = bf16[256,1536]{1,0:T(8,128)(2,1)S(1)} all-gather(bf16[64,1536]{1,0:T(8,128)(2,1)S(1)} %pad_maximum_fusion.14), channel_id=1, replica_groups=mesh['row'=8,'zh'=4,'zl'=2,'core'=2,'rep'=4] {'zh'}, dimensions={0}, use_global_device_ids=true | all-gather | bytes 983040 | tf_op jit(solution)/shard_map/all_gather | solution.py:97
  108.0 4.0 %collective-permute-start.5 = (bf16[256,768]{1,0:T(8,128)(2,1)S(1)}, bf16[256,768]{1,0:T(8,128)(2,1)S(1)}, u32[]{:S(2)}, u32[]{:S(2)}) collective-permute-start(bf16[256,768]{1,0:T(8,128)(2,1)S(1)} %get-tuple-element.17), channel_id=1, source_target_pairs={{0,8},{8,0},{16,24},{24,16},{32,40},{40,32},{48,56},{56,48},{1,9},... | collective-permute-start | bytes 1179656 | tf_op jit(solution)/shard_map/ppermute | solution.py:64
  112.0 3.5 %collective-permute-start.7 = (bf16[256,768]{1,0:T(8,128)(2,1)S(1)}, bf16[256,768]{1,0:T(8,128)(2,1)S(1)}, u32[]{:S(2)}, u32[]{:S(2)}) collective-permute-start(bf16[256,768]{1,0:T(8,128)(2,1)S(1)} %get-tuple-element.16), channel_id=1, source_target_pairs={{0,56},{8,16},{16,8},{24,32},{32,24},{40,48},{48,40},{56,0},{1,57}... | collective-permute-start | bytes 1179656 | tf_op jit(solution)/shard_map/ppermute | solution.py:64
  115.5 1.6 collective-permute-done.5
  117.1 0.3 maximum_select_fusion.2
  117.4 0.8 convolution_convert_fusion.1
  118.3 0.9 dynamic-slice_bitcast_fusion.1
  119.1 3.2 %collective-permute-start.6 = (bf16[384,768]{1,0:T(8,128)(2,1)}, bf16[384,768]{1,0:T(8,128)(2,1)}, u32[]{:S(2)}, u32[]{:S(2)}) collective-permute-start(bf16[384,768]{1,0:T(8,128)(2,1)} %dynamic-slice_bitcast_fusion.1), channel_id=1, source_target_pairs={{0,1},{1,0},{2,3},{3,2},{4,5},{5,4},{6,7},{7,6},{8,9},{9,8},{10,11... | collective-permute-start | bytes 1769480 | tf_op jit(solution)/shard_map/ppermute | solution.py:112
  122.3 0.3 maximum_select_fusion.3
  122.7 0.8 convolution_convert_fusion
  123.6 0.9 dynamic-slice_bitcast_fusion
  124.5 3.8 %collective-permute-start.8 = (bf16[2,2,96,768]{3,2,1,0:T(8,128)(2,1)}, bf16[2,2,96,768]{3,2,1,0:T(8,128)(2,1)}, u32[]{:S(2)}, u32[]{:S(2)}) collective-permute-start(bf16[2,2,96,768]{3,2,1,0:T(8,128)(2,1)} %dynamic-slice_bitcast_fusion), channel_id=1, source_target_pairs={{0,3},{1,2},{2,1},{3,0},{4,7},{5,6},{6,5},{7,4},{8,11},{9,10},{10,... | collective-permute-start | bytes 1769480 | tf_op jit(solution)/shard_map/ppermute | solution.py:112
  128.3 1.7 collective-permute-done.6
  130.1 1.2 fusion.1
  131.3 5.3 %collective-permute-done.8 = bf16[2,2,96,768]{3,2,1,0:T(8,128)(2,1)} collective-permute-done((bf16[2,2,96,768]{3,2,1,0:T(8,128)(2,1)}, bf16[2,2,96,768]{3,2,1,0:T(8,128)(2,1)}, u32[]{:S(2)}, u32[]{:S(2)}) %collective-permute-start.8) | collective-permute-done | bytes 589856 | tf_op jit(solution)/shard_map/ppermute | solution.py:112
  136.6 1.2 fusion
  137.9 1.9 convolution_convert_fusion.2
  139.8 10.7 %collective-permute-start.10 = (bf16[512,384]{1,0:T(8,128)(2,1)S(1)}, bf16[512,384]{1,0:T(8,128)(2,1)S(1)}, u32[]{:S(2)}, u32[]{:S(2)}) collective-permute-start(bf16[512,384]{1,0:T(8,128)(2,1)S(1)} %slice.137), channel_id=1, source_target_pairs={{0,4},{4,0},{1,5},{5,1},{2,6},{6,2},{3,7},{7,3},{8,12},{12,8},{9,1... | collective-permute-start | bytes 1179656 | tf_op jit(solution)/shard_map/ppermute | solution.py:22
  150.6 1.9 collective-permute-start.11
  152.5 1.8 convolution_convert_fusion.3
  154.4 1.9 collective-permute-start.9
  156.4 3.8 %collective-permute-start.15 = (bf16[192,768]{1,0:T(8,128)(2,1)S(1)}, bf16[192,768]{1,0:T(8,128)(2,1)S(1)}, u32[]{:S(2)}, u32[]{:S(2)}) collective-permute-start(bf16[192,768]{1,0:T(8,128)(2,1)S(1)} %dynamic-slice_bitcast_fusion.4), channel_id=1, source_target_pairs={{0,3},{1,2},{2,1},{3,0},{4,7},{5,6},{6,5},{7,4},{8,11},{9,10},{10,... | collective-permute-start | bytes 884744 | tf_op jit(solution)/shard_map/ppermute | solution.py:112
  160.1 1.0 collective-permute-done.11
  161.2 2.7 %collective-permute-start.12 = (bf16[96,768]{1,0:T(8,128)(2,1)S(1)}, bf16[96,768]{1,0:T(8,128)(2,1)S(1)}, u32[]{:S(2)}, u32[]{:S(2)}) collective-permute-start(bf16[96,768]{1,0:T(8,128)(2,1)S(1)} %get-tuple-element.27), channel_id=1, source_target_pairs={{0,4},{4,0},{1,5},{5,1},{2,6},{6,2},{3,7},{7,3},{8,12},{12,8},{9,1... | collective-permute-start | bytes 442376 | tf_op jit(solution)/shard_map/ppermute | solution.py:22
  163.9 3.6 %collective-permute-done.15 = bf16[192,768]{1,0:T(8,128)(2,1)S(1)} collective-permute-done((bf16[192,768]{1,0:T(8,128)(2,1)S(1)}, bf16[192,768]{1,0:T(8,128)(2,1)S(1)}, u32[]{:S(2)}, u32[]{:S(2)}) %collective-permute-start.15) | collective-permute-done | bytes 294944 | tf_op jit(solution)/shard_map/ppermute | solution.py:112
  167.5 0.1 fusion.4
  167.7 3.3 %collective-permute-start.16 = (bf16[1,192,384]{2,1,0:T(8,128)(2,1)S(1)}, bf16[1,192,384]{2,1,0:T(8,128)(2,1)S(1)}, u32[]{:S(2)}, u32[]{:S(2)}) collective-permute-start(bf16[1,192,384]{2,1,0:T(8,128)(2,1)S(1)} %get-tuple-element.25), channel_id=1, source_target_pairs={{0,4},{4,0},{1,5},{5,1},{2,6},{6,2},{3,7},{7,3},{8,12},{12,8},{9,1... | collective-permute-start | bytes 442376 | tf_op jit(solution)/shard_map/ppermute | solution.py:22
  171.0 0.1 add_convert_fusion
  171.1 0.1 add_convert_fusion.1
  171.2 0.7 collective-permute-done.16
  172.0 3.8 %collective-permute-start.17 = (bf16[2,192,384]{2,1,0:T(8,128)(2,1)S(1)}, bf16[2,192,384]{2,1,0:T(8,128)(2,1)S(1)}, u32[]{:S(2)}, u32[]{:S(2)}) collective-permute-start(bf16[2,192,384]{2,1,0:T(8,128)(2,1)S(1)} %maximum_select_fusion.7), channel_id=1, source_target_pairs={{0,3},{1,2},{2,1},{3,0},{4,7},{5,6},{6,5},{7,4},{8,11},{9,10},{10,... | collective-permute-start | bytes 884744 | tf_op jit(solution)/shard_map/ppermute | solution.py:116
  175.7 0.1 maximum_select_fusion.6
  175.8 1.9 collective-permute-start.13
  177.8 1.0 pad_maximum_fusion.5
  178.7 3.5 %all-to-all-start.2 = ((bf16[8,64,768]{2,1,0:T(8,128)(2,1)}), bf16[8,64,768]{2,1,0:T(8,128)(2,1)S(1)}, u32[]{:S(2)}, u32[]{:S(2)}) async-start(bf16[8,64,768]{2,1,0:T(8,128)(2,1)} %bitcast.16), calls=%async_computation.2 | async-start | bytes 1572864 | tf_op jit(solution)/shard_map/all_to_all | solution.py:26
  182.3 1.0 collective-permute-done.17
  183.3 0.2 maximum_select_fusion.5
  183.5 2.4 %collective-permute-start.18 = (bf16[2,384,384]{2,1,0:T(8,128)(2,1)S(1)}, bf16[2,384,384]{2,1,0:T(8,128)(2,1)S(1)}, u32[]{:S(2)}, u32[]{:S(2)}) collective-permute-start(bf16[2,384,384]{2,1,0:T(8,128)(2,1)S(1)} %maximum_select_fusion.5), channel_id=1, source_target_pairs={{0,1},{1,0},{2,3},{3,2},{4,5},{5,4},{6,7},{7,6},{8,9},{9,8},{10,11... | collective-permute-start | bytes 1769480 | tf_op jit(solution)/shard_map/ppermute | solution.py:116
  185.9 0.1 maximum_select_fusion.4
  186.0 3.3 %collective-permute-start.14 = (bf16[192,1536]{1,0:T(8,128)(2,1)S(1)}, bf16[192,1536]{1,0:T(8,128)(2,1)S(1)}, u32[]{:S(2)}, u32[]{:S(2)}) collective-permute-start(bf16[192,1536]{1,0:T(8,128)(2,1)S(1)} %maximum_select_fusion.4), channel_id=1, source_target_pairs={{0,3},{1,2},{2,1},{3,0},{4,7},{5,6},{6,5},{7,4},{8,11},{9,10},{10,... | collective-permute-start | bytes 1769480 | tf_op jit(solution)/shard_map/ppermute | solution.py:116
  189.3 9.7 %collective-permute-done.18 = bf16[2,384,384]{2,1,0:T(8,128)(2,1)S(1)} collective-permute-done((bf16[2,384,384]{2,1,0:T(8,128)(2,1)S(1)}, bf16[2,384,384]{2,1,0:T(8,128)(2,1)S(1)}, u32[]{:S(2)}, u32[]{:S(2)}) %collective-permute-start.18) | collective-permute-done | bytes 589856 | tf_op jit(solution)/shard_map/ppermute | solution.py:116
  199.0 1.4 maximum_select_fusion.1
  200.4 2.2 %collective-permute-done.14 = bf16[192,1536]{1,0:T(8,128)(2,1)S(1)} collective-permute-done((bf16[192,1536]{1,0:T(8,128)(2,1)S(1)}, bf16[192,1536]{1,0:T(8,128)(2,1)S(1)}, u32[]{:S(2)}, u32[]{:S(2)}) %collective-permute-start.14) | collective-permute-done | bytes 589856 | tf_op jit(solution)/shard_map/ppermute | solution.py:116
  202.7 1.4 maximum_select_fusion
  204.0 0.1 fusion.12
  204.2 0.6 fusion.22
  (58 shorter events, 1.0 us)
Async XLA Ops:
  1.5 33.6 %copy-start = (bf16[1536,384]{1,0:T(8,128)(2,1)S(1)}, bf16[1536,384]{1,0:T(8,128)(2,1)}, u32[]{:S(2)}) copy-start(bf16[1536,384]{1,0:T(8,128)(2,1)} %param.6) | copy-start | bytes 3538948
  29.5 11.9 %collective-permute-start = (bf16[512,768]{1,0:T(8,128)(2,1)S(1)}, bf16[512,768]{1,0:T(8,128)(2,1)S(1)}, u32[]{:S(2)}, u32[]{:S(2)}) collective-permute-start(bf16[512,768]{1,0:T(8,128)(2,1)S(1)} %bitcast.54), channel_id=1, source_target_pairs={{0,4},{4,0},{1,5},{5,1},{2,6},{6,2},{3,7},{7,3},{8,12},{12,8},{9,1... | collective-permute-start | bytes 2359304 | tf_op jit(solution)/shard_map/ppermute | solution.py:22
  35.1 2.9 %copy-start.1 = (bf16[384,1536]{1,0:T(8,128)(2,1)S(1)}, bf16[384,1536]{1,0:T(8,128)(2,1)}, u32[]{:S(2)}) copy-start(bf16[384,1536]{1,0:T(8,128)(2,1)} %param.5) | copy-start | bytes 3538948
  36.1 5.5 %copy-start.4 = (bf16[768,384]{1,0:T(8,128)(2,1)}, bf16[768,384]{1,0:T(8,128)(2,1)S(1)}, u32[]{:S(2)}) copy-start(bf16[768,384]{1,0:T(8,128)(2,1)S(1)} %get-tuple-element.14) | copy-start | bytes 1769476
  36.1 5.5 %collective-permute-start.3 = (bf16[768,384]{1,0:T(8,128)(2,1)}, bf16[768,384]{1,0:T(8,128)(2,1)}, u32[]{:S(2)}, u32[]{:S(2)}) collective-permute-start(bf16[768,384]{1,0:T(8,128)(2,1)} %get-tuple-element.15), channel_id=1, source_target_pairs={{0,4},{4,0},{1,5},{5,1},{2,6},{6,2},{3,7},{7,3},{8,12},{12,8},{9,1... | collective-permute-start | bytes 1769480 | tf_op jit(solution)/shard_map/ppermute | solution.py:22
  38.9 15.7 %collective-permute-start.1 = (bf16[384,768]{1,0:T(8,128)(2,1)S(1)}, bf16[384,768]{1,0:T(8,128)(2,1)}, u32[]{:S(2)}, u32[]{:S(2)}) collective-permute-start(bf16[384,768]{1,0:T(8,128)(2,1)S(1)} %get-tuple-element.13), channel_id=1, source_target_pairs={{0,4},{4,0},{1,5},{5,1},{2,6},{6,2},{3,7},{7,3},{8,12},{12,8},{9,1... | collective-permute-start | bytes 1769480 | tf_op jit(solution)/shard_map/ppermute | solution.py:22
  41.4 2.5 %copy-start.12 = (bf16[512,384]{1,0:T(8,128)(2,1)}, bf16[512,384]{1,0:T(8,128)(2,1)S(1)}, u32[]{:S(2)}) copy-start(bf16[512,384]{1,0:T(8,128)(2,1)S(1)} %get-tuple-element.19) | copy-start | bytes 1179652
  41.4 13.2 %copy-start.8 = (bf16[512,384]{1,0:T(8,128)(2,1)}, bf16[512,384]{1,0:T(8,128)(2,1)S(1)}, u32[]{:S(2)}) copy-start(bf16[512,384]{1,0:T(8,128)(2,1)S(1)} %get-tuple-element.18) | copy-start | bytes 1179652
  41.5 2.4 %copy-start.14 = (bf16[512,384]{1,0:T(8,128)(2,1)}, bf16[512,384]{1,0:T(8,128)(2,1)S(1)}, u32[]{:S(2)}) copy-start(bf16[512,384]{1,0:T(8,128)(2,1)S(1)} %get-tuple-element.21) | copy-start | bytes 1179652
  41.5 13.1 %copy-start.10 = (bf16[512,384]{1,0:T(8,128)(2,1)}, bf16[512,384]{1,0:T(8,128)(2,1)S(1)}, u32[]{:S(2)}) copy-start(bf16[512,384]{1,0:T(8,128)(2,1)S(1)} %get-tuple-element.20) | copy-start | bytes 1179652
  41.6 13.1 %copy-start.6 = (bf16[384,768]{1,0:T(8,128)(2,1)S(1)}, bf16[384,768]{1,0:T(8,128)(2,1)}, u32[]{:S(2)}) copy-start(bf16[384,768]{1,0:T(8,128)(2,1)} %get-tuple-element.12) | copy-start | bytes 1769476
  43.9 20.1 %collective-permute-start.4 = (bf16[4,64,768]{2,1,0:T(8,128)(2,1)S(1)}, bf16[4,64,768]{2,1,0:T(8,128)(2,1)S(1)}, u32[]{:S(2)}, u32[]{:S(2)}) collective-permute-start(bf16[4,64,768]{2,1,0:T(8,128)(2,1)S(1)} %dynamic-slice_bitcast_fusion.2), channel_id=1, source_target_pairs={{0,56},{8,16},{16,8},{24,32},{32,24},{40,48},{48,40},{56,0},{1,57}... | collective-permute-start | bytes 1179656 | tf_op jit(solution)/shard_map/ppermute | solution.py:64
  56.5 12.3 %collective-permute-start.2 = (bf16[4,64,768]{2,1,0:T(8,128)(2,1)S(1)}, bf16[4,64,768]{2,1,0:T(8,128)(2,1)S(1)}, u32[]{:S(2)}, u32[]{:S(2)}) collective-permute-start(bf16[4,64,768]{2,1,0:T(8,128)(2,1)S(1)} %dynamic-slice_bitcast_fusion.3), channel_id=1, source_target_pairs={{0,8},{8,0},{16,24},{24,16},{32,40},{40,32},{48,56},{56,48},{1,9},... | collective-permute-start | bytes 1179656 | tf_op jit(solution)/shard_map/ppermute | solution.py:64
  108.0 9.4 %copy-start.13 = (bf16[512,384]{1,0:T(8,128)(2,1)S(1)}, bf16[512,384]{1,0:T(8,128)(2,1)}, u32[]{:S(2)}) copy-start(bf16[512,384]{1,0:T(8,128)(2,1)} %copy-done.12) | copy-start | bytes 1179652
  108.0 9.4 %copy-start.15 = (bf16[512,384]{1,0:T(8,128)(2,1)S(1)}, bf16[512,384]{1,0:T(8,128)(2,1)}, u32[]{:S(2)}) copy-start(bf16[512,384]{1,0:T(8,128)(2,1)} %copy-done.14) | copy-start | bytes 1179652
  108.0 9.1 %collective-permute-start.5 = (bf16[256,768]{1,0:T(8,128)(2,1)S(1)}, bf16[256,768]{1,0:T(8,128)(2,1)S(1)}, u32[]{:S(2)}, u32[]{:S(2)}) collective-permute-start(bf16[256,768]{1,0:T(8,128)(2,1)S(1)} %get-tuple-element.17), channel_id=1, source_target_pairs={{0,8},{8,0},{16,24},{24,16},{32,40},{40,32},{48,56},{56,48},{1,9},... | collective-permute-start | bytes 1179656 | tf_op jit(solution)/shard_map/ppermute | solution.py:64
  112.0 10.3 %collective-permute-start.7 = (bf16[256,768]{1,0:T(8,128)(2,1)S(1)}, bf16[256,768]{1,0:T(8,128)(2,1)S(1)}, u32[]{:S(2)}, u32[]{:S(2)}) collective-permute-start(bf16[256,768]{1,0:T(8,128)(2,1)S(1)} %get-tuple-element.16), channel_id=1, source_target_pairs={{0,56},{8,16},{16,8},{24,32},{32,24},{40,48},{48,40},{56,0},{1,57}... | collective-permute-start | bytes 1179656 | tf_op jit(solution)/shard_map/ppermute | solution.py:64
  118.3 4.4 %copy-start.9 = (bf16[512,384]{1,0:T(8,128)(2,1)S(1)}, bf16[512,384]{1,0:T(8,128)(2,1)}, u32[]{:S(2)}) copy-start(bf16[512,384]{1,0:T(8,128)(2,1)} %copy-done.8) | copy-start | bytes 1179652
  118.3 4.4 %copy-start.11 = (bf16[512,384]{1,0:T(8,128)(2,1)S(1)}, bf16[512,384]{1,0:T(8,128)(2,1)}, u32[]{:S(2)}) copy-start(bf16[512,384]{1,0:T(8,128)(2,1)} %copy-done.10) | copy-start | bytes 1179652
  119.1 10.9 %collective-permute-start.6 = (bf16[384,768]{1,0:T(8,128)(2,1)}, bf16[384,768]{1,0:T(8,128)(2,1)}, u32[]{:S(2)}, u32[]{:S(2)}) collective-permute-start(bf16[384,768]{1,0:T(8,128)(2,1)} %dynamic-slice_bitcast_fusion.1), channel_id=1, source_target_pairs={{0,1},{1,0},{2,3},{3,2},{4,5},{5,4},{6,7},{7,6},{8,9},{9,8},{10,11... | collective-permute-start | bytes 1769480 | tf_op jit(solution)/shard_map/ppermute | solution.py:112
  122.7 0.9 copy-start.2
  124.5 12.1 %collective-permute-start.8 = (bf16[2,2,96,768]{3,2,1,0:T(8,128)(2,1)}, bf16[2,2,96,768]{3,2,1,0:T(8,128)(2,1)}, u32[]{:S(2)}, u32[]{:S(2)}) collective-permute-start(bf16[2,2,96,768]{3,2,1,0:T(8,128)(2,1)} %dynamic-slice_bitcast_fusion), channel_id=1, source_target_pairs={{0,3},{1,2},{2,1},{3,0},{4,7},{5,6},{6,5},{7,4},{8,11},{9,10},{10,... | collective-permute-start | bytes 1769480 | tf_op jit(solution)/shard_map/ppermute | solution.py:112
  131.3 6.6 %copy-start.3 = (bf16[512,768]{1,0:T(8,128)(2,1)S(1)}, bf16[512,768]{1,0:T(8,128)(2,1)}, u32[]{:S(2)}) copy-start(bf16[512,768]{1,0:T(8,128)(2,1)} %copy-done.2) | copy-start | bytes 2359300
  131.3 6.6 %copy-start.7 = (bf16[384,768]{1,0:T(8,128)(2,1)S(1)}, bf16[384,768]{1,0:T(8,128)(2,1)}, u32[]{:S(2)}) copy-start(bf16[384,768]{1,0:T(8,128)(2,1)} %get-tuple-element.12) | copy-start | bytes 1769476
  139.7 12.7 %copy-start.5 = (bf16[768,384]{1,0:T(8,128)(2,1)S(1)}, bf16[768,384]{1,0:T(8,128)(2,1)}, u32[]{:S(2)}) copy-start(bf16[768,384]{1,0:T(8,128)(2,1)} %copy-done.4) | copy-start | bytes 1769476
  139.8 31.1 %collective-permute-start.10 = (bf16[512,384]{1,0:T(8,128)(2,1)S(1)}, bf16[512,384]{1,0:T(8,128)(2,1)S(1)}, u32[]{:S(2)}, u32[]{:S(2)}) collective-permute-start(bf16[512,384]{1,0:T(8,128)(2,1)S(1)} %slice.137), channel_id=1, source_target_pairs={{0,4},{4,0},{1,5},{5,1},{2,6},{6,2},{3,7},{7,3},{8,12},{12,8},{9,1... | collective-permute-start | bytes 1179656 | tf_op jit(solution)/shard_map/ppermute | solution.py:22
  150.6 10.5 %collective-permute-start.11 = (bf16[1,2,96,768]{3,2,1,0:T(8,128)(2,1)S(1)}, bf16[1,2,96,768]{3,2,1,0:T(8,128)(2,1)S(1)}, u32[]{:S(2)}, u32[]{:S(2)}) collective-permute-start(bf16[1,2,96,768]{3,2,1,0:T(8,128)(2,1)S(1)} %constant_dynamic-slice_fusion), channel_id=1, source_target_pairs={{0,1},{1,0},{2,3},{3,2},{4,5},{5,4},{6,7},{7,6},{8,9},{9,8},{10,11... | collective-permute-start | bytes 884744 | tf_op jit(solution)/shard_map/ppermute | solution.py:112
  154.4 16.7 %collective-permute-start.9 = (bf16[512,384]{1,0:T(8,128)(2,1)S(1)}, bf16[512,384]{1,0:T(8,128)(2,1)S(1)}, u32[]{:S(2)}, u32[]{:S(2)}) collective-permute-start(bf16[512,384]{1,0:T(8,128)(2,1)S(1)} %slice.135), channel_id=1, source_target_pairs={{0,4},{4,0},{1,5},{5,1},{2,6},{6,2},{3,7},{7,3},{8,12},{12,8},{9,1... | collective-permute-start | bytes 1179656 | tf_op jit(solution)/shard_map/ppermute | solution.py:22
  156.4 11.2 %collective-permute-start.15 = (bf16[192,768]{1,0:T(8,128)(2,1)S(1)}, bf16[192,768]{1,0:T(8,128)(2,1)S(1)}, u32[]{:S(2)}, u32[]{:S(2)}) collective-permute-start(bf16[192,768]{1,0:T(8,128)(2,1)S(1)} %dynamic-slice_bitcast_fusion.4), channel_id=1, source_target_pairs={{0,3},{1,2},{2,1},{3,0},{4,7},{5,6},{6,5},{7,4},{8,11},{9,10},{10,... | collective-permute-start | bytes 884744 | tf_op jit(solution)/shard_map/ppermute | solution.py:112
  161.2 14.5 %collective-permute-start.12 = (bf16[96,768]{1,0:T(8,128)(2,1)S(1)}, bf16[96,768]{1,0:T(8,128)(2,1)S(1)}, u32[]{:S(2)}, u32[]{:S(2)}) collective-permute-start(bf16[96,768]{1,0:T(8,128)(2,1)S(1)} %get-tuple-element.27), channel_id=1, source_target_pairs={{0,4},{4,0},{1,5},{5,1},{2,6},{6,2},{3,7},{7,3},{8,12},{12,8},{9,1... | collective-permute-start | bytes 442376 | tf_op jit(solution)/shard_map/ppermute | solution.py:22
  167.7 4.3 %collective-permute-start.16 = (bf16[1,192,384]{2,1,0:T(8,128)(2,1)S(1)}, bf16[1,192,384]{2,1,0:T(8,128)(2,1)S(1)}, u32[]{:S(2)}, u32[]{:S(2)}) collective-permute-start(bf16[1,192,384]{2,1,0:T(8,128)(2,1)S(1)} %get-tuple-element.25), channel_id=1, source_target_pairs={{0,4},{4,0},{1,5},{5,1},{2,6},{6,2},{3,7},{7,3},{8,12},{12,8},{9,1... | collective-permute-start | bytes 442376 | tf_op jit(solution)/shard_map/ppermute | solution.py:22
  172.0 11.3 %collective-permute-start.17 = (bf16[2,192,384]{2,1,0:T(8,128)(2,1)S(1)}, bf16[2,192,384]{2,1,0:T(8,128)(2,1)S(1)}, u32[]{:S(2)}, u32[]{:S(2)}) collective-permute-start(bf16[2,192,384]{2,1,0:T(8,128)(2,1)S(1)} %maximum_select_fusion.7), channel_id=1, source_target_pairs={{0,3},{1,2},{2,1},{3,0},{4,7},{5,6},{6,5},{7,4},{8,11},{9,10},{10,... | collective-permute-start | bytes 884744 | tf_op jit(solution)/shard_map/ppermute | solution.py:116
  175.8 10.0 %collective-permute-start.13 = (bf16[96,1536]{1,0:T(8,128)(2,1)S(1)}, bf16[96,1536]{1,0:T(8,128)(2,1)S(1)}, u32[]{:S(2)}, u32[]{:S(2)}) collective-permute-start(bf16[96,1536]{1,0:T(8,128)(2,1)S(1)} %maximum_select_fusion.6), channel_id=1, source_target_pairs={{0,1},{1,0},{2,3},{3,2},{4,5},{5,4},{6,7},{7,6},{8,9},{9,8},{10,11... | collective-permute-start | bytes 884744 | tf_op jit(solution)/shard_map/ppermute | solution.py:116
  178.7 25.3 %all-to-all-start.2 = ((bf16[8,64,768]{2,1,0:T(8,128)(2,1)}), bf16[8,64,768]{2,1,0:T(8,128)(2,1)S(1)}, u32[]{:S(2)}, u32[]{:S(2)}) async-start(bf16[8,64,768]{2,1,0:T(8,128)(2,1)} %bitcast.16), calls=%async_computation.2 | async-start | bytes 1572864 | tf_op jit(solution)/shard_map/all_to_all | solution.py:26
  183.5 15.5 %collective-permute-start.18 = (bf16[2,384,384]{2,1,0:T(8,128)(2,1)S(1)}, bf16[2,384,384]{2,1,0:T(8,128)(2,1)S(1)}, u32[]{:S(2)}, u32[]{:S(2)}) collective-permute-start(bf16[2,384,384]{2,1,0:T(8,128)(2,1)S(1)} %maximum_select_fusion.5), channel_id=1, source_target_pairs={{0,1},{1,0},{2,3},{3,2},{4,5},{5,4},{6,7},{7,6},{8,9},{9,8},{10,11... | collective-permute-start | bytes 1769480 | tf_op jit(solution)/shard_map/ppermute | solution.py:116
  186.0 16.7 %collective-permute-start.14 = (bf16[192,1536]{1,0:T(8,128)(2,1)S(1)}, bf16[192,1536]{1,0:T(8,128)(2,1)S(1)}, u32[]{:S(2)}, u32[]{:S(2)}) collective-permute-start(bf16[192,1536]{1,0:T(8,128)(2,1)S(1)} %maximum_select_fusion.4), channel_id=1, source_target_pairs={{0,3},{1,2},{2,1},{3,0},{4,7},{5,6},{6,5},{7,4},{8,11},{9,10},{10,... | collective-permute-start | bytes 1769480 | tf_op jit(solution)/shard_map/ppermute | solution.py:116

commit v6 on v5

--- a/solution.py
+++ b/solution.py
@@ -5,6 +5,7 @@
 
 bf16 = jnp.bfloat16
 f32 = jnp.float32
+barrier = lax.optimization_barrier
 
 
 def gelu_pullback(hidden, upstream):
@@ -69,26 +70,30 @@
     def plus(a, b):
         return (a.astype(f32) + b.astype(f32)).astype(bf16)
 
-    up_own = lax.dynamic_slice_in_dim(up_weight, mine, half, 1)
+    up_keep = lax.dynamic_slice_in_dim(up_weight, mine, half, 1)
     up_other = swap(lax.dynamic_slice_in_dim(up_weight, theirs, half, 1))
-    down_own = lax.dynamic_slice_in_dim(down_weight, mine, half, 0)
+    down_keep = lax.dynamic_slice_in_dim(down_weight, mine, half, 0)
     down_other = swap(lax.dynamic_slice_in_dim(down_weight, theirs, half, 0))
-    up = jnp.concatenate([up_own, up_other], 0)
-    down = jnp.concatenate([down_own, down_other], 1)
+    up = jnp.concatenate([up_keep, up_other], 0)
+    down = jnp.concatenate([down_keep, down_other], 1)
 
     own = gather(jnp.concatenate([tokens, out_grads], 1), "row")
+    own, up, down = barrier((own, up, down))
     other = swap(own)
     tok = jnp.concatenate([own[:, :width], other[:, :width]], 1)
     og = jnp.concatenate([own[:, width:], other[:, width:]], 1)
     total = tok.shape[0]
     share = total // n_z
 
-    def first_sum(part, pairs):
+    def halves(part):
         part = part.reshape(2, n_zh, share, half)
-        return plus(pick(part, zl), z_swap(pick(part, 1 - zl), pairs))
+        return pick(part, zl), pick(part, 1 - zl)
 
-    hid_half = first_sum(dot(tok, up, (1, 0)), even)
-    ag_half = first_sum(dot(og, down, (1, 1)), odd)
+    hid_keep, hid_send = halves(dot(tok, up, (1, 0)))
+    ag_keep, ag_send = halves(dot(og, down, (1, 1)))
+    hid_send, ag_send = barrier((hid_send, ag_send))
+    hid_half = plus(hid_keep, z_swap(hid_send, even))
+    ag_half = plus(ag_keep, z_swap(ag_send, odd))
     sums = total_of(exchange(jnp.concatenate([hid_half, ag_half], 2), "zh"))
     hidden, act_grads = sums[:, :half], sums[:, half:]
     act = jax.nn.gelu(hidden).astype(bf16)
@@ -103,12 +108,7 @@
 
     act, hg = whole(both[:, :half], even), whole(both[:, half:], odd)
 
-    def split(x, bit):
-        x = x.reshape((2, x.shape[0] // 2) + x.shape[1:])
-        return pick(x, bit), pick(x, 1 - bit)
-
-    def scatter(x, step):
-        keep, send = split(x, step[0])
+    def scatter(keep, send, step):
         return plus(keep, lax.ppermute(send, "rep", step[1]))
 
     def collect(x, steps, axis):
@@ -116,28 +116,43 @@
             x = pair(x, lax.ppermute(x, "rep", pairs), bit, axis)
         return x
 
+    def parts(own, got, bit, axis):
+        own, got = (x.reshape((2, x.shape[0] // 2) + x.shape[1:]) for x in (own, got))
+        return tuple(
+            pair(pick(own, b)[None], pick(got, b)[None], core, 0)
+            if axis == 0
+            else pair(pick(own, b), pick(got, b), core, 1)
+            for b in (bit, 1 - bit)
+        )
+
     high, low = rep // 2, rep % 2
     down_steps = [((rep + 1) // 2 % 2, near), (high, far)]
     up_steps = [(high, far), (low, near)]
-    piece = width // n_rep
-    down_part = scatter(dot(act, og, (0, 0)), down_steps[0])
-    up_part = dot(tok, hg, (0, 0)).reshape(2, n_rep, piece, half)
-    up_part = scatter(jnp.swapaxes(up_part, 0, 1), up_steps[0])
-    down_part, up_part, act, hg = lax.optimization_barrier(
-        (down_part, up_part, act, hg)
+    down_got = swap(dot(act, og[:, width:], (0, 0)))
+    up_got = swap(dot(tok[:, width:], hg, (0, 0)))
+    down_own = dot(act, og[:, :width], (0, 0))
+    up_own = dot(tok[:, :width], hg, (0, 0))
+    down_part = scatter(*parts(down_own, down_got, down_steps[0][0], 0), down_steps[0])
+    up_part = scatter(*parts(up_own, up_got, up_steps[0][0], 1), up_steps[0])
+    down_part, act, hg = barrier((down_part, act, hg))
+    down_part = down_part.reshape(2, 2, -1, width)
+    bit = down_steps[1][0]
+    down_part = scatter(
+        lax.dynamic_index_in_dim(down_part, bit, 1, False),
+        lax.dynamic_index_in_dim(down_part, 1 - bit, 1, False),
+        down_steps[1],
     )
-    down_part = scatter(down_part, down_steps[1])
-    up_part = scatter(up_part, up_steps[1]).reshape(2, piece, half)
-    down_part = pair(down_part[None, :, :width], swap(down_part[None, :, width:]), core, 0)
-    up_part = pair(up_part[0], swap(up_part[1]), core, 1)
+    up_part = up_part.reshape(2, -1, 2 * half)
+    bit = up_steps[1][0]
+    up_part = scatter(pick(up_part, bit), pick(up_part, 1 - bit), up_steps[1])
     down_grads = collect(down_part, down_steps, 1).reshape(2 * half, width)
     up_grads = collect(up_part, up_steps, 0)
 
-    def output(left, weight, dims):
-        part = dot(left, weight, dims)
-        return plus(part[:, :width], swap(part[:, width:]))
-
-    out = jnp.concatenate([output(act, down, (1, 0)), output(hg, up, (1, 1))], 1)
+    block, token = dot(act, down, (1, 0)), dot(hg, up, (1, 1))
+    out = plus(
+        jnp.concatenate([block[:, :width], token[:, :width]], 1),
+        swap(jnp.concatenate([block[:, width:], token[:, width:]], 1)),
+    )
     out = total_of(exchange(out.reshape(n_row, rows, 2 * width), "row")).astype(bf16)
     return (out[:, :width], out[:, width:], up_grads, down_grads)
 

time: 207 us -> 201 us (0.971)
  blocking collectives: 66.5 us -> 35.7 us
  waiting for transfers between devices: 37.3 us -> 59.1 us
  starting transfers between devices: 76.1 us -> 80.9 us
  matrix products: 9.48 us -> 5.39 us
  other arithmetic: 9.02 us -> 12.5 us
    all_to_all x2 -> x1, blocking collectives: 48.1 us -> 19.8 us  [exchange(): return lax.all_to_all(x, axis, 0, 0, tiled=False)]
    all_to_all x1 -> x2, waiting for transfers between devices: 0.01 us -> 10.9 us  [exchange(): return lax.all_to_all(x, axis, 0, 0, tiled=False)]
    all_to_all x1 -> x2, starting transfers between devices: 3.55 us -> 11.2 us  [exchange(): return lax.all_to_all(x, axis, 0, 0, tiled=False)]
    ppermute x4, waiting for transfers between devices: 11.7 us -> 17.4 us  [scatter(): return plus(keep, lax.ppermute(send, 'rep', step[1]))]
    dot_general x6 -> x8, matrix products: 9.48 us -> 5.39 us  [dot(): lax.dot_general(left, right, ((dims[:1], dims[1:]), ((), ())), preferred_...]
    ppermute x7 -> x6, waiting for transfers between devices: 0.76 us -> 3.67 us  [swap(): return lax.ppermute(x, 'core', [(0, 1), (1, 0)])]
    all_gather x1, blocking collectives: 18.5 us -> 15.9 us  [per_device(): lax.all_gather(jnp.concatenate([act, hid_grads], 1), 'zh', axis=0, tiled=...]
    ppermute x4, waiting for transfers between devices: 13 us -> 15.5 us  [collect(): x = pair(x, lax.ppermute(x, 'rep', pairs), bit, axis)]
  transfers between devices with their start and end apart: 20 -> 20, of which waited for: 11 -> 13; matrix products, arithmetic and copies ran while one was open for 9% -> 7% of each run, Pallas kernels for 0% -> 0%
where the time goes in v6:
time: 201 us; the launch traced here: 200 us
  starting transfers between devices  80.9 us (40%)
  waiting for transfers between devices  59.1 us (29%)
  blocking collectives  35.7 us (18%)
  other arithmetic  12.5 us (6%)
  matrix products  5.39 us (3%)
  local copies, waits for them, and re-layouts  4.73 us (2%)
    ppermute x6, starting transfers between devices, swap(): return lax.ppermute(x, 'core', [(0, 1), (1, 0)])  26.3 us
    ppermute x4, starting transfers between devices, z_swap(): return lax.ppermute(x, ('zh', 'zl'), pairs)  21.5 us
    all_to_all x1, blocking collectives, exchange(): return lax.all_to_all(x, axis, 0, 0, tiled=False)  19.8 us
    ppermute x4, waiting for transfers between devices, scatter(): return plus(keep, lax.ppermute(send, 'rep', step[1]))  17.4 us
    all_gather x1, blocking collectives, per_device(): lax.all_gather(jnp.concatenate([act, hid_grads], 1), 'zh', axis=0, tiled=...  15.9 us
    ppermute x4, waiting for transfers between devices, collect(): x = pair(x, lax.ppermute(x, 'rep', pairs), bit, axis)  15.5 us
    ppermute x4, waiting for transfers between devices, z_swap(): return lax.ppermute(x, ('zh', 'zl'), pairs)  11.7 us
    ppermute x4, starting transfers between devices, scatter(): return plus(keep, lax.ppermute(send, 'rep', step[1]))  11.5 us
  transfers between devices with their start and end apart: 20, of which 13 were waited for; matrix products, arithmetic and copies ran while one was open for 7% of the time, Pallas kernels for 0%

profile of v6, /device:TPU:1, one launch (start us, length us, event | category | flops | bytes accessed | tf_op | source)
XLA Modules:
  0.0 199.5 jit_solution(12398635478182875095)
XLA Ops:
  0.6 0.8 pad_maximum_fusion.5
  1.5 0.9 broadcast_in_dim.2
  2.4 7.7 %all-to-all-start = ((bf16[8,64,768]{2,1,0:T(8,128)(2,1)}), bf16[8,64,768]{2,1,0:T(8,128)(2,1)S(1)}, u32[]{:S(2)}, u32[]{:S(2)}) async-start(bf16[8,64,768]{2,1,0:T(8,128)(2,1)} %broadcast_in_dim.2), calls=%async_computation | async-start | bytes 1572864 | tf_op jit(solution)/shard_map/all_to_all | solution.py:27
  10.2 4.8 %collective-permute-start = (bf16[384,768]{1,0:T(8,128)(2,1)S(1)}, bf16[384,768]{1,0:T(8,128)(2,1)S(1)}, u32[]{:S(2)}, u32[]{:S(2)}) collective-permute-start(bf16[384,768]{1,0:T(8,128)(2,1)S(1)} %get-tuple-element.23), channel_id=1, source_target_pairs={{0,4},{4,0},{1,5},{5,1},{2,6},{6,2},{3,7},{7,3},{8,12},{12,8},{9,1... | collective-permute-start | bytes 1769480 | tf_op jit(solution)/shard_map/ppermute | solution.py:23
  15.0 0.1 constant_dynamic-slice_fusion.5
  15.2 1.9 collective-permute-start.1
  17.2 1.9 collective-permute-done.1
  19.1 1.1 pad_maximum_fusion.1
  20.2 10.9 %all-to-all-done = bf16[8,64,768]{2,1,0:T(8,128)(2,1)S(1)} async-done(((bf16[8,64,768]{2,1,0:T(8,128)(2,1)}), bf16[8,64,768]{2,1,0:T(8,128)(2,1)S(1)}, u32[]{:S(2)}, u32[]{:S(2)}) %all-to-all-start) | async-done | bytes 786464 | tf_op jit(solution)/shard_map/all_to_all | solution.py:27
  31.1 5.0 %collective-permute-start.2 = (bf16[512,768]{1,0:T(8,128)(2,1)S(1)}, bf16[512,768]{1,0:T(8,128)(2,1)S(1)}, u32[]{:S(2)}, u32[]{:S(2)}) collective-permute-start(bf16[512,768]{1,0:T(8,128)(2,1)S(1)} %bitcast.55), channel_id=1, source_target_pairs={{0,4},{4,0},{1,5},{5,1},{2,6},{6,2},{3,7},{7,3},{8,12},{12,8},{9,1... | collective-permute-start | bytes 2359304 | tf_op jit(solution)/shard_map/ppermute | solution.py:23
  36.2 1.8 collective-permute-done.2
  38.1 0.8 convolution_convert_fusion.2
  38.9 0.8 convolution_convert_fusion.3
  39.8 1.0 dynamic-slice_bitcast_fusion
  40.7 10.6 %collective-permute-start.4 = (bf16[4,64,768]{2,1,0:T(8,128)(2,1)}, bf16[4,64,768]{2,1,0:T(8,128)(2,1)}, u32[]{:S(2)}, u32[]{:S(2)}) collective-permute-start(bf16[4,64,768]{2,1,0:T(8,128)(2,1)} %get-tuple-element.16), channel_id=1, source_target_pairs={{0,56},{8,16},{16,8},{24,32},{32,24},{40,48},{48,40},{56,0},{1,57}... | collective-permute-start | bytes 1179656 | tf_op jit(solution)/shard_map/ppermute | solution.py:65
  51.4 1.9 collective-permute-start.3
  53.3 7.6 %collective-permute-done.4 = bf16[4,64,768]{2,1,0:T(8,128)(2,1)} collective-permute-done((bf16[4,64,768]{2,1,0:T(8,128)(2,1)}, bf16[4,64,768]{2,1,0:T(8,128)(2,1)}, u32[]{:S(2)}, u32[]{:S(2)}) %collective-permute-start.4) | collective-permute-done | bytes 393248 | tf_op jit(solution)/shard_map/ppermute | solution.py:65
  60.9 1.2 fusion.6
  62.1 1.5 collective-permute-done.3
  63.6 1.1 fusion.7
  64.7 19.8 %all_to_all.15 = bf16[4,64,1536]{2,1,0:T(8,128)(2,1)S(1)} all-to-all(bf16[4,64,1536]{2,1,0:T(8,128)(2,1)S(1)} %pad_maximum_fusion.2), channel_id=1, replica_groups=mesh['row'=8,'zh'=4,'zl'=2,'core'=2,'rep'=4] {'zh'}, dimensions={0} | all-to-all | bytes 1572864 | tf_op jit(solution)/shard_map/all_to_all | solution.py:27
  84.6 0.1 multiply_convert_fusion
  84.8 15.9 %all_gather.3 = bf16[256,1536]{1,0:T(8,128)(2,1)S(1)} all-gather(bf16[64,1536]{1,0:T(8,128)(2,1)S(1)} %pad_maximum_fusion.4), channel_id=1, replica_groups=mesh['row'=8,'zh'=4,'zl'=2,'core'=2,'rep'=4] {'zh'}, dimensions={0}, use_global_device_ids=true | all-gather | bytes 983040 | tf_op jit(solution)/shard_map/all_gather | solution.py:102
  100.8 6.4 %collective-permute-start.5 = (bf16[256,768]{1,0:T(8,128)(2,1)S(1)}, bf16[256,768]{1,0:T(8,128)(2,1)}, u32[]{:S(2)}, u32[]{:S(2)}) collective-permute-start(bf16[256,768]{1,0:T(8,128)(2,1)S(1)} %get-tuple-element.29), channel_id=1, source_target_pairs={{0,8},{8,0},{16,24},{24,16},{32,40},{40,32},{48,56},{56,48},{1,9},... | collective-permute-start | bytes 1179656 | tf_op jit(solution)/shard_map/ppermute | solution.py:65
  107.3 2.6 %collective-permute-start.8 = (bf16[256,768]{1,0:T(8,128)(2,1)S(1)}, bf16[256,768]{1,0:T(8,128)(2,1)S(1)}, u32[]{:S(2)}, u32[]{:S(2)}) collective-permute-start(bf16[256,768]{1,0:T(8,128)(2,1)S(1)} %get-tuple-element.28), channel_id=1, source_target_pairs={{0,56},{8,16},{16,8},{24,32},{32,24},{40,48},{48,40},{56,0},{1,57}... | collective-permute-start | bytes 1179656 | tf_op jit(solution)/shard_map/ppermute | solution.py:65
  109.8 2.6 %collective-permute-done.5 = bf16[256,768]{1,0:T(8,128)(2,1)} collective-permute-done((bf16[256,768]{1,0:T(8,128)(2,1)S(1)}, bf16[256,768]{1,0:T(8,128)(2,1)}, u32[]{:S(2)}, u32[]{:S(2)}) %collective-permute-start.5) | collective-permute-done | bytes 393248 | tf_op jit(solution)/shard_map/ppermute | solution.py:65
  112.4 1.3 maximum_select_fusion.2
  113.8 0.6 convolution_convert_fusion.6
  114.4 9.1 %collective-permute-start.6 = (bf16[768,384]{1,0:T(8,128)(2,1)S(1)}, bf16[768,384]{1,0:T(8,128)(2,1)S(1)}, u32[]{:S(2)}, u32[]{:S(2)}) collective-permute-start(bf16[768,384]{1,0:T(8,128)(2,1)S(1)} %convolution_convert_fusion.6), channel_id=1, source_target_pairs={{0,4},{4,0},{1,5},{5,1},{2,6},{6,2},{3,7},{7,3},{8,12},{12,8},{9,1... | collective-permute-start | bytes 1769480 | tf_op jit(solution)/shard_map/ppermute | solution.py:23
  123.5 0.3 maximum_select_fusion.3
  123.8 0.5 convolution_convert_fusion.4
  124.3 1.9 collective-permute-start.10
  126.2 0.6 convolution_convert_fusion.7
  127.0 0.1 maximum_select_fusion.5
  127.1 4.1 %collective-permute-start.7 = (bf16[2,384,384]{2,1,0:T(8,128)(2,1)S(1)}, bf16[2,384,384]{2,1,0:T(8,128)(2,1)S(1)}, u32[]{:S(2)}, u32[]{:S(2)}) collective-permute-start(bf16[2,384,384]{2,1,0:T(8,128)(2,1)S(1)} %maximum_select_fusion.5), channel_id=1, source_target_pairs={{0,1},{1,0},{2,3},{3,2},{4,5},{5,4},{6,7},{7,6},{8,9},{9,8},{10,11... | collective-permute-start | bytes 1769480 | tf_op jit(solution)/shard_map/ppermute | solution.py:112
  131.2 0.5 convolution_convert_fusion.5
  131.8 0.1 maximum_select_fusion.7
  132.0 2.8 %collective-permute-start.11 = (bf16[192,1536]{1,0:T(8,128)(2,1)S(1)}, bf16[192,1536]{1,0:T(8,128)(2,1)S(1)}, u32[]{:S(2)}, u32[]{:S(2)}) collective-permute-start(bf16[192,1536]{1,0:T(8,128)(2,1)S(1)} %maximum_select_fusion.7), channel_id=1, source_target_pairs={{0,3},{1,2},{2,1},{3,0},{4,7},{5,6},{6,5},{7,4},{8,11},{9,10},{10,... | collective-permute-start | bytes 1769480 | tf_op jit(solution)/shard_map/ppermute | solution.py:112
  134.8 9.7 %collective-permute-done.7 = bf16[2,384,384]{2,1,0:T(8,128)(2,1)S(1)} collective-permute-done((bf16[2,384,384]{2,1,0:T(8,128)(2,1)S(1)}, bf16[2,384,384]{2,1,0:T(8,128)(2,1)S(1)}, u32[]{:S(2)}, u32[]{:S(2)}) %collective-permute-start.7) | collective-permute-done | bytes 589856 | tf_op jit(solution)/shard_map/ppermute | solution.py:112
  144.4 0.2 add_convert_fusion.2
  144.6 0.8 convolution_convert_fusion
  145.5 1.2 copy-done.3
  146.7 0.8 convolution_convert_fusion.1
  147.5 1.6 collective-permute-done.11
  149.2 0.2 add_convert_fusion.1
  149.4 1.9 collective-permute-start.12
  151.5 3.6 %collective-permute-start.9 = (bf16[512,768]{1,0:T(8,128)(2,1)S(1)}, bf16[512,768]{1,0:T(8,128)(2,1)S(1)}, u32[]{:S(2)}, u32[]{:S(2)}) collective-permute-start(bf16[512,768]{1,0:T(8,128)(2,1)S(1)} %pad_maximum_fusion.3), channel_id=1, source_target_pairs={{0,4},{4,0},{1,5},{5,1},{2,6},{6,2},{3,7},{7,3},{8,12},{12,8},{9,1... | collective-permute-start | bytes 2359304 | tf_op jit(solution)/shard_map/ppermute | solution.py:23
  155.1 2.8 %collective-permute-start.15 = (bf16[2,192,384]{2,1,0:T(8,128)(2,1)S(1)}, bf16[2,192,384]{2,1,0:T(8,128)(2,1)S(1)}, u32[]{:S(2)}, u32[]{:S(2)}) collective-permute-start(bf16[2,192,384]{2,1,0:T(8,128)(2,1)S(1)} %dynamic-slice_bitcast_fusion.2), channel_id=1, source_target_pairs={{0,3},{1,2},{2,1},{3,0},{4,7},{5,6},{6,5},{7,4},{8,11},{9,10},{10,... | collective-permute-start | bytes 884744 | tf_op jit(solution)/shard_map/ppermute | solution.py:112
  157.9 0.2 collective-permute-done.12
  158.2 2.8 %collective-permute-start.13 = (bf16[96,1536]{1,0:T(8,128)(2,1)S(1)}, bf16[96,1536]{1,0:T(8,128)(2,1)}, u32[]{:S(2)}, u32[]{:S(2)}) collective-permute-start(bf16[96,1536]{1,0:T(8,128)(2,1)S(1)} %fusion.9), channel_id=1, source_target_pairs={{0,1},{1,0},{2,3},{3,2},{4,5},{5,4},{6,7},{7,6},{8,9},{9,8},{10,11... | collective-permute-start | bytes 884744 | tf_op jit(solution)/shard_map/ppermute | solution.py:116
  161.1 5.8 %collective-permute-done.15 = bf16[2,192,384]{2,1,0:T(8,128)(2,1)S(1)} collective-permute-done((bf16[2,192,384]{2,1,0:T(8,128)(2,1)S(1)}, bf16[2,192,384]{2,1,0:T(8,128)(2,1)S(1)}, u32[]{:S(2)}, u32[]{:S(2)}) %collective-permute-start.15) | collective-permute-done | bytes 294944 | tf_op jit(solution)/shard_map/ppermute | solution.py:112
  167.0 2.8 %collective-permute-start.16 = (bf16[2,192,384]{2,1,0:T(8,128)(2,1)S(1)}, bf16[2,192,384]{2,1,0:T(8,128)(2,1)S(1)}, u32[]{:S(2)}, u32[]{:S(2)}) collective-permute-start(bf16[2,192,384]{2,1,0:T(8,128)(2,1)S(1)} %fusion.8), channel_id=1, source_target_pairs={{0,3},{1,2},{2,1},{3,0},{4,7},{5,6},{6,5},{7,4},{8,11},{9,10},{10,... | collective-permute-start | bytes 884744 | tf_op jit(solution)/shard_map/ppermute | solution.py:116
  169.8 1.1 add_convert_fusion
  170.8 3.5 %all-to-all-start.2 = ((bf16[8,64,768]{2,1,0:T(8,128)(2,1)}), bf16[8,64,768]{2,1,0:T(8,128)(2,1)S(1)}, u32[]{:S(2)}, u32[]{:S(2)}) async-start(bf16[8,64,768]{2,1,0:T(8,128)(2,1)} %bitcast.10), calls=%async_computation.2 | async-start | bytes 1572864 | tf_op jit(solution)/shard_map/all_to_all | solution.py:27
  174.4 3.4 %collective-permute-done.16 = bf16[2,192,384]{2,1,0:T(8,128)(2,1)S(1)} collective-permute-done((bf16[2,192,384]{2,1,0:T(8,128)(2,1)S(1)}, bf16[2,192,384]{2,1,0:T(8,128)(2,1)S(1)}, u32[]{:S(2)}, u32[]{:S(2)}) %collective-permute-start.16) | collective-permute-done | bytes 294944 | tf_op jit(solution)/shard_map/ppermute | solution.py:116
  177.8 0.2 maximum_select_fusion.9
  178.0 1.9 collective-permute-start.17
  180.0 1.2 maximum_select_fusion.8
  181.1 2.8 %collective-permute-start.14 = (bf16[192,1536]{1,0:T(8,128)(2,1)S(1)}, bf16[192,1536]{1,0:T(8,128)(2,1)S(1)}, u32[]{:S(2)}, u32[]{:S(2)}) collective-permute-start(bf16[192,1536]{1,0:T(8,128)(2,1)S(1)} %maximum_select_fusion.8), channel_id=1, source_target_pairs={{0,3},{1,2},{2,1},{3,0},{4,7},{5,6},{6,5},{7,4},{8,11},{9,10},{10,... | collective-permute-start | bytes 1769480 | tf_op jit(solution)/shard_map/ppermute | solution.py:116
  183.9 9.1 %collective-permute-done.17 = bf16[2,384,384]{2,1,0:T(8,128)(2,1)S(1)} collective-permute-done((bf16[2,384,384]{2,1,0:T(8,128)(2,1)S(1)}, bf16[2,384,384]{2,1,0:T(8,128)(2,1)S(1)}, u32[]{:S(2)}, u32[]{:S(2)}) %collective-permute-start.17) | collective-permute-done | bytes 589856 | tf_op jit(solution)/shard_map/ppermute | solution.py:116
  193.1 1.4 maximum_select_fusion.1
  194.4 2.9 %collective-permute-done.14 = bf16[192,1536]{1,0:T(8,128)(2,1)S(1)} collective-permute-done((bf16[192,1536]{1,0:T(8,128)(2,1)S(1)}, bf16[192,1536]{1,0:T(8,128)(2,1)S(1)}, u32[]{:S(2)}, u32[]{:S(2)}) %collective-permute-start.14) | collective-permute-done | bytes 589856 | tf_op jit(solution)/shard_map/ppermute | solution.py:116
  197.4 1.4 maximum_select_fusion
  198.9 0.6 fusion.29
  (36 shorter events, 1.5 us)
Async XLA Ops:
  1.5 8.6 %copy-start = (bf16[384,1536]{1,0:T(8,128)(2,1)S(1)}, bf16[384,1536]{1,0:T(8,128)(2,1)}, u32[]{:S(2)}) copy-start(bf16[384,1536]{1,0:T(8,128)(2,1)} %param.5) | copy-start | bytes 3538948
  2.4 28.7 %all-to-all-start = ((bf16[8,64,768]{2,1,0:T(8,128)(2,1)}), bf16[8,64,768]{2,1,0:T(8,128)(2,1)S(1)}, u32[]{:S(2)}, u32[]{:S(2)}) async-start(bf16[8,64,768]{2,1,0:T(8,128)(2,1)} %broadcast_in_dim.2), calls=%async_computation | async-start | bytes 1572864 | tf_op jit(solution)/shard_map/all_to_all | solution.py:27
  10.1 4.9 %copy-start.1 = (bf16[1536,384]{1,0:T(8,128)(2,1)S(1)}, bf16[1536,384]{1,0:T(8,128)(2,1)}, u32[]{:S(2)}) copy-start(bf16[1536,384]{1,0:T(8,128)(2,1)} %param.6) | copy-start | bytes 3538948
  10.2 6.9 %collective-permute-start = (bf16[384,768]{1,0:T(8,128)(2,1)S(1)}, bf16[384,768]{1,0:T(8,128)(2,1)S(1)}, u32[]{:S(2)}, u32[]{:S(2)}) collective-permute-start(bf16[384,768]{1,0:T(8,128)(2,1)S(1)} %get-tuple-element.23), channel_id=1, source_target_pairs={{0,4},{4,0},{1,5},{5,1},{2,6},{6,2},{3,7},{7,3},{8,12},{12,8},{9,1... | collective-permute-start | bytes 1769480 | tf_op jit(solution)/shard_map/ppermute | solution.py:23
  15.2 3.9 %collective-permute-start.1 = (bf16[768,384]{1,0:T(8,128)(2,1)S(1)}, bf16[768,384]{1,0:T(8,128)(2,1)S(1)}, u32[]{:S(2)}, u32[]{:S(2)}) collective-permute-start(bf16[768,384]{1,0:T(8,128)(2,1)S(1)} %get-tuple-element.21), channel_id=1, source_target_pairs={{0,4},{4,0},{1,5},{5,1},{2,6},{6,2},{3,7},{7,3},{8,12},{12,8},{9,1... | collective-permute-start | bytes 1769480 | tf_op jit(solution)/shard_map/ppermute | solution.py:23
  31.1 6.9 %collective-permute-start.2 = (bf16[512,768]{1,0:T(8,128)(2,1)S(1)}, bf16[512,768]{1,0:T(8,128)(2,1)S(1)}, u32[]{:S(2)}, u32[]{:S(2)}) collective-permute-start(bf16[512,768]{1,0:T(8,128)(2,1)S(1)} %bitcast.55), channel_id=1, source_target_pairs={{0,4},{4,0},{1,5},{5,1},{2,6},{6,2},{3,7},{7,3},{8,12},{12,8},{9,1... | collective-permute-start | bytes 2359304 | tf_op jit(solution)/shard_map/ppermute | solution.py:23
  36.2 1.9 copy-start.2
  38.9 0.9 copy-start.4
  40.7 20.1 %collective-permute-start.4 = (bf16[4,64,768]{2,1,0:T(8,128)(2,1)}, bf16[4,64,768]{2,1,0:T(8,128)(2,1)}, u32[]{:S(2)}, u32[]{:S(2)}) collective-permute-start(bf16[4,64,768]{2,1,0:T(8,128)(2,1)} %get-tuple-element.16), channel_id=1, source_target_pairs={{0,56},{8,16},{16,8},{24,32},{32,24},{40,48},{48,40},{56,0},{1,57}... | collective-permute-start | bytes 1179656 | tf_op jit(solution)/shard_map/ppermute | solution.py:65
  51.4 12.2 %collective-permute-start.3 = (bf16[4,64,768]{2,1,0:T(8,128)(2,1)}, bf16[4,64,768]{2,1,0:T(8,128)(2,1)}, u32[]{:S(2)}, u32[]{:S(2)}) collective-permute-start(bf16[4,64,768]{2,1,0:T(8,128)(2,1)} %get-tuple-element.15), channel_id=1, source_target_pairs={{0,8},{8,0},{16,24},{24,16},{32,40},{40,32},{48,56},{56,48},{1,9},... | collective-permute-start | bytes 1179656 | tf_op jit(solution)/shard_map/ppermute | solution.py:65
  100.8 11.7 %collective-permute-start.5 = (bf16[256,768]{1,0:T(8,128)(2,1)S(1)}, bf16[256,768]{1,0:T(8,128)(2,1)}, u32[]{:S(2)}, u32[]{:S(2)}) collective-permute-start(bf16[256,768]{1,0:T(8,128)(2,1)S(1)} %get-tuple-element.29), channel_id=1, source_target_pairs={{0,8},{8,0},{16,24},{24,16},{32,40},{40,32},{48,56},{56,48},{1,9},... | collective-permute-start | bytes 1179656 | tf_op jit(solution)/shard_map/ppermute | solution.py:65
  107.3 16.2 %collective-permute-start.8 = (bf16[256,768]{1,0:T(8,128)(2,1)S(1)}, bf16[256,768]{1,0:T(8,128)(2,1)S(1)}, u32[]{:S(2)}, u32[]{:S(2)}) collective-permute-start(bf16[256,768]{1,0:T(8,128)(2,1)S(1)} %get-tuple-element.28), channel_id=1, source_target_pairs={{0,56},{8,16},{16,8},{24,32},{32,24},{40,48},{48,40},{56,0},{1,57}... | collective-permute-start | bytes 1179656 | tf_op jit(solution)/shard_map/ppermute | solution.py:65
  114.4 12.5 %collective-permute-start.6 = (bf16[768,384]{1,0:T(8,128)(2,1)S(1)}, bf16[768,384]{1,0:T(8,128)(2,1)S(1)}, u32[]{:S(2)}, u32[]{:S(2)}) collective-permute-start(bf16[768,384]{1,0:T(8,128)(2,1)S(1)} %convolution_convert_fusion.6), channel_id=1, source_target_pairs={{0,4},{4,0},{1,5},{5,1},{2,6},{6,2},{3,7},{7,3},{8,12},{12,8},{9,1... | collective-permute-start | bytes 1769480 | tf_op jit(solution)/shard_map/ppermute | solution.py:23
  124.3 7.5 %collective-permute-start.10 = (bf16[384,768]{1,0:T(8,128)(2,1)S(1)}, bf16[384,768]{1,0:T(8,128)(2,1)S(1)}, u32[]{:S(2)}, u32[]{:S(2)}) collective-permute-start(bf16[384,768]{1,0:T(8,128)(2,1)S(1)} %convolution_convert_fusion.4), channel_id=1, source_target_pairs={{0,4},{4,0},{1,5},{5,1},{2,6},{6,2},{3,7},{7,3},{8,12},{12,8},{9,1... | collective-permute-start | bytes 1769480 | tf_op jit(solution)/shard_map/ppermute | solution.py:23
  127.1 17.3 %collective-permute-start.7 = (bf16[2,384,384]{2,1,0:T(8,128)(2,1)S(1)}, bf16[2,384,384]{2,1,0:T(8,128)(2,1)S(1)}, u32[]{:S(2)}, u32[]{:S(2)}) collective-permute-start(bf16[2,384,384]{2,1,0:T(8,128)(2,1)S(1)} %maximum_select_fusion.5), channel_id=1, source_target_pairs={{0,1},{1,0},{2,3},{3,2},{4,5},{5,4},{6,7},{7,6},{8,9},{9,8},{10,11... | collective-permute-start | bytes 1769480 | tf_op jit(solution)/shard_map/ppermute | solution.py:112
  132.0 17.2 %collective-permute-start.11 = (bf16[192,1536]{1,0:T(8,128)(2,1)S(1)}, bf16[192,1536]{1,0:T(8,128)(2,1)S(1)}, u32[]{:S(2)}, u32[]{:S(2)}) collective-permute-start(bf16[192,1536]{1,0:T(8,128)(2,1)S(1)} %maximum_select_fusion.7), channel_id=1, source_target_pairs={{0,3},{1,2},{2,1},{3,0},{4,7},{5,6},{6,5},{7,4},{8,11},{9,10},{10,... | collective-permute-start | bytes 1769480 | tf_op jit(solution)/shard_map/ppermute | solution.py:112
  145.4 1.3 copy-start.3
  149.4 8.7 %collective-permute-start.12 = (bf16[96,1536]{1,0:T(8,128)(2,1)S(1)}, bf16[96,1536]{1,0:T(8,128)(2,1)S(1)}, u32[]{:S(2)}, u32[]{:S(2)}) collective-permute-start(bf16[96,1536]{1,0:T(8,128)(2,1)S(1)} %dynamic-slice_bitcast_fusion.3), channel_id=1, source_target_pairs={{0,1},{1,0},{2,3},{3,2},{4,5},{5,4},{6,7},{7,6},{8,9},{9,8},{10,11... | collective-permute-start | bytes 884744 | tf_op jit(solution)/shard_map/ppermute | solution.py:112
  151.5 18.2 %collective-permute-start.9 = (bf16[512,768]{1,0:T(8,128)(2,1)S(1)}, bf16[512,768]{1,0:T(8,128)(2,1)S(1)}, u32[]{:S(2)}, u32[]{:S(2)}) collective-permute-start(bf16[512,768]{1,0:T(8,128)(2,1)S(1)} %pad_maximum_fusion.3), channel_id=1, source_target_pairs={{0,4},{4,0},{1,5},{5,1},{2,6},{6,2},{3,7},{7,3},{8,12},{12,8},{9,1... | collective-permute-start | bytes 2359304 | tf_op jit(solution)/shard_map/ppermute | solution.py:23
  155.1 11.7 %collective-permute-start.15 = (bf16[2,192,384]{2,1,0:T(8,128)(2,1)S(1)}, bf16[2,192,384]{2,1,0:T(8,128)(2,1)S(1)}, u32[]{:S(2)}, u32[]{:S(2)}) collective-permute-start(bf16[2,192,384]{2,1,0:T(8,128)(2,1)S(1)} %dynamic-slice_bitcast_fusion.2), channel_id=1, source_target_pairs={{0,3},{1,2},{2,1},{3,0},{4,7},{5,6},{6,5},{7,4},{8,11},{9,10},{10,... | collective-permute-start | bytes 884744 | tf_op jit(solution)/shard_map/ppermute | solution.py:112
  158.2 21.7 %collective-permute-start.13 = (bf16[96,1536]{1,0:T(8,128)(2,1)S(1)}, bf16[96,1536]{1,0:T(8,128)(2,1)}, u32[]{:S(2)}, u32[]{:S(2)}) collective-permute-start(bf16[96,1536]{1,0:T(8,128)(2,1)S(1)} %fusion.9), channel_id=1, source_target_pairs={{0,1},{1,0},{2,3},{3,2},{4,5},{5,4},{6,7},{7,6},{8,9},{9,8},{10,11... | collective-permute-start | bytes 884744 | tf_op jit(solution)/shard_map/ppermute | solution.py:116
  167.0 10.8 %collective-permute-start.16 = (bf16[2,192,384]{2,1,0:T(8,128)(2,1)S(1)}, bf16[2,192,384]{2,1,0:T(8,128)(2,1)S(1)}, u32[]{:S(2)}, u32[]{:S(2)}) collective-permute-start(bf16[2,192,384]{2,1,0:T(8,128)(2,1)S(1)} %fusion.8), channel_id=1, source_target_pairs={{0,3},{1,2},{2,1},{3,0},{4,7},{5,6},{6,5},{7,4},{8,11},{9,10},{10,... | collective-permute-start | bytes 884744 | tf_op jit(solution)/shard_map/ppermute | solution.py:116
  170.8 27.9 %all-to-all-start.2 = ((bf16[8,64,768]{2,1,0:T(8,128)(2,1)}), bf16[8,64,768]{2,1,0:T(8,128)(2,1)S(1)}, u32[]{:S(2)}, u32[]{:S(2)}) async-start(bf16[8,64,768]{2,1,0:T(8,128)(2,1)} %bitcast.10), calls=%async_computation.2 | async-start | bytes 1572864 | tf_op jit(solution)/shard_map/all_to_all | solution.py:27
  178.0 15.0 %collective-permute-start.17 = (bf16[2,384,384]{2,1,0:T(8,128)(2,1)S(1)}, bf16[2,384,384]{2,1,0:T(8,128)(2,1)S(1)}, u32[]{:S(2)}, u32[]{:S(2)}) collective-permute-start(bf16[2,384,384]{2,1,0:T(8,128)(2,1)S(1)} %maximum_select_fusion.9), channel_id=1, source_target_pairs={{0,1},{1,0},{2,3},{3,2},{4,5},{5,4},{6,7},{7,6},{8,9},{9,8},{10,11... | collective-permute-start | bytes 1769480 | tf_op jit(solution)/shard_map/ppermute | solution.py:116
  181.1 16.2 %collective-permute-start.14 = (bf16[192,1536]{1,0:T(8,128)(2,1)S(1)}, bf16[192,1536]{1,0:T(8,128)(2,1)S(1)}, u32[]{:S(2)}, u32[]{:S(2)}) collective-permute-start(bf16[192,1536]{1,0:T(8,128)(2,1)S(1)} %maximum_select_fusion.8), channel_id=1, source_target_pairs={{0,3},{1,2},{2,1},{3,0},{4,7},{5,6},{6,5},{7,4},{8,11},{9,10},{10,... | collective-permute-start | bytes 1769480 | tf_op jit(solution)/shard_map/ppermute | solution.py:116

commit v7 on v6

--- a/solution.py
+++ b/solution.py
@@ -99,61 +99,47 @@
     act = jax.nn.gelu(hidden).astype(bf16)
     hid_grads = gelu_pullback(hidden, act_grads).astype(bf16)
 
-    both = lax.all_gather(
-        jnp.concatenate([act, hid_grads], 1), "zh", axis=0, tiled=True
-    )
+    act_half = lax.all_gather(act, "zh", axis=0, tiled=True)
+    act_half, hid_grads = barrier((act_half, hid_grads))
+    hg_half = gather(hid_grads, "zh")
+    act = pair(act_half, z_swap(act_half, even), zl, 0)
+    hg = pair(hg_half, z_swap(hg_half, odd), zl, 0)
 
-    def whole(part, pairs):
-        return pair(part, z_swap(part, pairs), zl, 0)
+    near_bit, far_bit = (rep + 1) // 2 % 2, rep // 2
+    down_got = swap(dot(act, og[:, width:], (0, 0)))
+    down_own = dot(act, og[:, :width], (0, 0))
+    own_got = [x.reshape(2, half // 2, width) for x in (down_own, down_got)]
 
-    act, hg = whole(both[:, :half], even), whole(both[:, half:], odd)
+    def chosen(bit):
+        return pair(*(pick(x, bit)[None] for x in own_got), core, 0)
 
-    def scatter(keep, send, step):
-        return plus(keep, lax.ppermute(send, "rep", step[1]))
+    down_part = plus(chosen(near_bit), lax.ppermute(chosen(1 - near_bit), "rep", near))
+    down_part = jnp.swapaxes(down_part.reshape(2, 2, -1, width), 0, 1)
+    send, block_act, token_hg = barrier((pick(down_part, 1 - far_bit), act, hg))
+    down_part = plus(pick(down_part, far_bit), lax.ppermute(send, "rep", far))
+    down_part = pair(down_part, lax.ppermute(down_part, "rep", far), far_bit, 1)
+    down_part = pair(down_part, lax.ppermute(down_part, "rep", near), near_bit, 1)
+    down_grads = down_part.reshape(2 * half, width)
 
-    def collect(x, steps, axis):
-        for bit, pairs in steps[::-1]:
-            x = pair(x, lax.ppermute(x, "rep", pairs), bit, axis)
-        return x
-
-    def parts(own, got, bit, axis):
-        own, got = (x.reshape((2, x.shape[0] // 2) + x.shape[1:]) for x in (own, got))
-        return tuple(
-            pair(pick(own, b)[None], pick(got, b)[None], core, 0)
-            if axis == 0
-            else pair(pick(own, b), pick(got, b), core, 1)
-            for b in (bit, 1 - bit)
-        )
-
-    high, low = rep // 2, rep % 2
-    down_steps = [((rep + 1) // 2 % 2, near), (high, far)]
-    up_steps = [(high, far), (low, near)]
-    down_got = swap(dot(act, og[:, width:], (0, 0)))
-    up_got = swap(dot(tok[:, width:], hg, (0, 0)))
-    down_own = dot(act, og[:, :width], (0, 0))
-    up_own = dot(tok[:, :width], hg, (0, 0))
-    down_part = scatter(*parts(down_own, down_got, down_steps[0][0], 0), down_steps[0])
-    up_part = scatter(*parts(up_own, up_got, up_steps[0][0], 1), up_steps[0])
-    down_part, act, hg = barrier((down_part, act, hg))
-    down_part = down_part.reshape(2, 2, -1, width)
-    bit = down_steps[1][0]
-    down_part = scatter(
-        lax.dynamic_index_in_dim(down_part, bit, 1, False),
-        lax.dynamic_index_in_dim(down_part, 1 - bit, 1, False),
-        down_steps[1],
-    )
-    up_part = up_part.reshape(2, -1, 2 * half)
-    bit = up_steps[1][0]
-    up_part = scatter(pick(up_part, bit), pick(up_part, 1 - bit), up_steps[1])
-    down_grads = collect(down_part, down_steps, 1).reshape(2 * half, width)
-    up_grads = collect(up_part, up_steps, 0)
-
-    block, token = dot(act, down, (1, 0)), dot(hg, up, (1, 1))
+    piece = width // n_rep
+    up_part = dot(tok, hg, (0, 0)).reshape(2, n_rep, piece, half)
+    up_part = total_of(exchange(jnp.swapaxes(up_part, 0, 1), "rep")).astype(bf16)
+    block, token = dot(block_act, down, (1, 0)), dot(token_hg, up, (1, 1))
     out = plus(
         jnp.concatenate([block[:, :width], token[:, :width]], 1),
         swap(jnp.concatenate([block[:, width:], token[:, width:]], 1)),
     )
+    up_part, out = barrier((up_part, out))
     out = total_of(exchange(out.reshape(n_row, rows, 2 * width), "row")).astype(bf16)
+    up_part = pair(up_part[0], swap(up_part[1]), core, 1)
+    up_grads = jnp.zeros((n_rep, piece, 2 * half), bf16)
+    for k in range(n_rep):
+        ring = [(i, (i + k) % n_rep) for i in range(n_rep)]
+        got = lax.ppermute(up_part, "rep", ring) if k else up_part
+        source = lax.rem(rep + n_rep - k, n_rep)
+        up_grads = lax.dynamic_update_slice_in_dim(up_grads, got[None], source, 0)
+    up_grads = up_grads.reshape(width, 2 * half)
+
     return (out[:, :width], out[:, width:], up_grads, down_grads)
 
 

time: 201 us -> 214 us (1.065)
  starting transfers between devices: 80.9 us -> 88.3 us
  waiting for transfers between devices: 59.1 us -> 55.7 us
  local copies, waits for them, and re-layouts: 4.73 us -> 7.62 us
  blocking collectives: 35.7 us -> 38 us
  other arithmetic: 12.5 us -> 14.7 us
    ppermute x8 -> x7, waiting for transfers between devices: 32.9 us -> 24.2 us  [the longest x3 11.2 us: per_device(): got = lax.ppermute(up_part, 'rep', ring) if k else up_part]
    all_to_all x2 -> x4, starting transfers between devices: 11.2 us -> 19.4 us  [exchange(): return lax.all_to_all(x, axis, 0, 0, tiled=False)]
    all_to_all x1, blocking collectives: 19.8 us -> 24.8 us  [exchange(): return lax.all_to_all(x, axis, 0, 0, tiled=False)]
    ppermute x4, starting transfers between devices: 21.5 us -> 16.6 us  [z_swap(): return lax.ppermute(x, ('zh', 'zl'), pairs)]
    ppermute x4, waiting for transfers between devices: 11.7 us -> 16.2 us  [z_swap(): return lax.ppermute(x, ('zh', 'zl'), pairs)]
    ppermute x6, starting transfers between devices: 26.3 us -> 30.1 us  [swap(): return lax.ppermute(x, 'core', [(0, 1), (1, 0)])]
    all_gather x1, blocking collectives: 15.9 us -> 13.1 us  [per_device(): act_half = lax.all_gather(act, 'zh', axis=0, tiled=True)]
    convert_element_type x7 -> x5, other arithmetic: 3.95 us -> 5.89 us  [plus(): return (a.astype(f32) + b.astype(f32)).astype(bf16)]
  transfers between devices with their start and end apart: 20 -> 21, of which waited for: 13 -> 13; matrix products, arithmetic and copies ran while one was open for 7% -> 11% of each run, Pallas kernels for 0% -> 0%
where the time goes in v7:
time: 214 us; the launch traced here: 213 us
  starting transfers between devices  88.3 us (41%)
  waiting for transfers between devices  55.7 us (26%)
  blocking collectives  38 us (18%)
  other arithmetic  14.7 us (7%)
  local copies, waits for them, and re-layouts  7.62 us (4%)
  matrix products  7.28 us (3%)
    ppermute x6, starting transfers between devices, swap(): return lax.ppermute(x, 'core', [(0, 1), (1, 0)])  30.1 us
    all_to_all x1, blocking collectives, exchange(): return lax.all_to_all(x, axis, 0, 0, tiled=False)  24.8 us
    all_to_all x4, starting transfers between devices, exchange(): return lax.all_to_all(x, axis, 0, 0, tiled=False)  19.4 us
    ppermute x4, starting transfers between devices, z_swap(): return lax.ppermute(x, ('zh', 'zl'), pairs)  16.6 us
    ppermute x4, waiting for transfers between devices, z_swap(): return lax.ppermute(x, ('zh', 'zl'), pairs)  16.2 us
    all_gather x1, blocking collectives, per_device(): act_half = lax.all_gather(act, 'zh', axis=0, tiled=True)  13.1 us
    all_to_all x4, waiting for transfers between devices, exchange(): return lax.all_to_all(x, axis, 0, 0, tiled=False)  11.8 us
    ppermute x3, waiting for transfers between devices, per_device(): got = lax.ppermute(up_part, 'rep', ring) if k else up_part  11.2 us
  transfers between devices with their start and end apart: 21, of which 13 were waited for; matrix products, arithmetic and copies ran while one was open for 11% of the time, Pallas kernels for 0%

profile of v7, /device:TPU:1, one launch (start us, length us, event | category | flops | bytes accessed | tf_op | source)
XLA Modules:
  0.0 212.9 jit_solution(10634977268479313539)
XLA Ops:
  0.6 0.8 pad_maximum_fusion.7
  1.5 0.9 broadcast_in_dim.12
  2.4 7.7 %all-to-all-start = ((bf16[8,64,768]{2,1,0:T(8,128)(2,1)}), bf16[8,64,768]{2,1,0:T(8,128)(2,1)S(1)}, u32[]{:S(2)}, u32[]{:S(2)}) async-start(bf16[8,64,768]{2,1,0:T(8,128)(2,1)} %broadcast_in_dim.12), calls=%async_computation | async-start | bytes 1572864 | tf_op jit(solution)/shard_map/all_to_all | solution.py:27
  10.2 4.8 %collective-permute-start.1 = (bf16[768,384]{1,0:T(8,128)(2,1)S(1)}, bf16[768,384]{1,0:T(8,128)(2,1)S(1)}, u32[]{:S(2)}, u32[]{:S(2)}) collective-permute-start(bf16[768,384]{1,0:T(8,128)(2,1)S(1)} %get-tuple-element.29), channel_id=1, source_target_pairs={{0,4},{4,0},{1,5},{5,1},{2,6},{6,2},{3,7},{7,3},{8,12},{12,8},{9,1... | collective-permute-start | bytes 1769480 | tf_op jit(solution)/shard_map/ppermute | solution.py:23
  15.2 1.9 collective-permute-start
  17.2 1.9 collective-permute-done
  19.1 1.1 pad_maximum_fusion
  20.2 10.9 %all-to-all-done = bf16[8,64,768]{2,1,0:T(8,128)(2,1)S(1)} async-done(((bf16[8,64,768]{2,1,0:T(8,128)(2,1)}), bf16[8,64,768]{2,1,0:T(8,128)(2,1)S(1)}, u32[]{:S(2)}, u32[]{:S(2)}) %all-to-all-start) | async-done | bytes 786464 | tf_op jit(solution)/shard_map/all_to_all | solution.py:27
  31.1 5.0 %collective-permute-start.2 = (bf16[512,768]{1,0:T(8,128)(2,1)S(1)}, bf16[512,768]{1,0:T(8,128)(2,1)S(1)}, u32[]{:S(2)}, u32[]{:S(2)}) collective-permute-start(bf16[512,768]{1,0:T(8,128)(2,1)S(1)} %bitcast.57), channel_id=1, source_target_pairs={{0,4},{4,0},{1,5},{5,1},{2,6},{6,2},{3,7},{7,3},{8,12},{12,8},{9,1... | collective-permute-start | bytes 2359304 | tf_op jit(solution)/shard_map/ppermute | solution.py:23
  36.2 1.8 collective-permute-done.2
  38.1 0.8 convolution_convert_fusion.4
  39.0 0.8 convolution_convert_fusion.3
  39.9 4.0 %collective-permute-start.3 = (bf16[4,64,768]{2,1,0:T(8,128)(2,1)S(1)}, bf16[4,64,768]{2,1,0:T(8,128)(2,1)}, u32[]{:S(2)}, u32[]{:S(2)}) collective-permute-start(bf16[4,64,768]{2,1,0:T(8,128)(2,1)S(1)} %get-tuple-element.19), channel_id=1, source_target_pairs={{0,8},{8,0},{16,24},{24,16},{32,40},{40,32},{48,56},{56,48},{1,9},... | collective-permute-start | bytes 1179656 | tf_op jit(solution)/shard_map/ppermute | solution.py:65
  43.9 8.8 %collective-permute-start.4 = (bf16[4,64,768]{2,1,0:T(8,128)(2,1)S(1)}, bf16[4,64,768]{2,1,0:T(8,128)(2,1)}, u32[]{:S(2)}, u32[]{:S(2)}) collective-permute-start(bf16[4,64,768]{2,1,0:T(8,128)(2,1)S(1)} %get-tuple-element.20), channel_id=1, source_target_pairs={{0,56},{8,16},{16,8},{24,32},{32,24},{40,48},{48,40},{56,0},{1,57}... | collective-permute-start | bytes 1179656 | tf_op jit(solution)/shard_map/ppermute | solution.py:65
  52.7 0.4 collective-permute-done.3
  53.2 1.2 fusion.4
  54.4 7.3 %collective-permute-done.4 = bf16[4,64,768]{2,1,0:T(8,128)(2,1)} collective-permute-done((bf16[4,64,768]{2,1,0:T(8,128)(2,1)S(1)}, bf16[4,64,768]{2,1,0:T(8,128)(2,1)}, u32[]{:S(2)}, u32[]{:S(2)}) %collective-permute-start.4) | collective-permute-done | bytes 393248 | tf_op jit(solution)/shard_map/ppermute | solution.py:65
  61.7 1.1 fusion.3
  62.9 24.8 %all_to_all.25 = bf16[4,64,1536]{2,1,0:T(8,128)(2,1)S(1)} all-to-all(bf16[4,64,1536]{2,1,0:T(8,128)(2,1)S(1)} %pad_maximum_fusion.3), channel_id=1, replica_groups=mesh['row'=8,'zh'=4,'zl'=2,'core'=2,'rep'=4] {'zh'}, dimensions={0} | all-to-all | bytes 1572864 | tf_op jit(solution)/shard_map/all_to_all | solution.py:27
  87.9 13.1 %all_gather.3 = bf16[256,768]{1,0:T(8,128)(2,1)S(1)} all-gather(bf16[64,768]{1,0:T(8,128)(2,1)S(1)} %get-tuple-element.45), channel_id=1, replica_groups=mesh['row'=8,'zh'=4,'zl'=2,'core'=2,'rep'=4] {'zh'}, dimensions={0}, use_global_device_ids=true | all-gather | bytes 491520 | tf_op jit(solution)/shard_map/all_gather | solution.py:102
  101.1 1.9 collective-permute-start.6
  103.0 0.8 broadcast_in_dim.13
  103.8 4.2 %all-to-all-start.2 = ((bf16[4,64,768]{2,1,0:T(8,128)(2,1)}), bf16[4,64,768]{2,1,0:T(8,128)(2,1)S(1)}, u32[]{:S(2)}, u32[]{:S(2)}) async-start(bf16[4,64,768]{2,1,0:T(8,128)(2,1)} %broadcast_in_dim.13), calls=%async_computation.2 | async-start | bytes 786432 | tf_op jit(solution)/shard_map/all_to_all | solution.py:27
  108.0 1.7 collective-permute-done.6
  109.7 1.3 maximum_select_fusion.2
  111.0 1.4 convolution_convert_fusion.5
  112.5 12.4 %collective-permute-start.7 = (bf16[768,384]{1,0:T(8,128)(2,1)}, bf16[768,384]{1,0:T(8,128)(2,1)}, u32[]{:S(2)}, u32[]{:S(2)}) collective-permute-start(bf16[768,384]{1,0:T(8,128)(2,1)} %convolution_convert_fusion.5), channel_id=1, source_target_pairs={{0,4},{4,0},{1,5},{5,1},{2,6},{6,2},{3,7},{7,3},{8,12},{12,8},{9,1... | collective-permute-start | bytes 1769480 | tf_op jit(solution)/shard_map/ppermute | solution.py:23
  124.9 0.6 convolution_convert_fusion.6
  125.6 1.9 collective-permute-start.5
  127.6 1.1 constant_dynamic-slice_fusion.2
  128.7 0.9 maximum_select_fusion.4
  129.6 3.2 %collective-permute-start.8 = (bf16[2,384,384]{2,1,0:T(8,128)(2,1)}, bf16[2,384,384]{2,1,0:T(8,128)(2,1)}, u32[]{:S(2)}, u32[]{:S(2)}) collective-permute-start(bf16[2,384,384]{2,1,0:T(8,128)(2,1)} %maximum_select_fusion.4), channel_id=1, source_target_pairs={{0,1},{1,0},{2,3},{3,2},{4,5},{5,4},{6,7},{7,6},{8,9},{9,8},{10,11... | collective-permute-start | bytes 1769480 | tf_op jit(solution)/shard_map/ppermute | solution.py:116
  132.9 6.7 %collective-permute-done.5 = bf16[256,768]{1,0:T(8,128)(2,1)} collective-permute-done((bf16[256,768]{1,0:T(8,128)(2,1)S(1)}, bf16[256,768]{1,0:T(8,128)(2,1)}, u32[]{:S(2)}, u32[]{:S(2)}) %collective-permute-start.5) | collective-permute-done | bytes 393248 | tf_op jit(solution)/shard_map/ppermute | solution.py:65
  139.6 1.3 maximum_select_fusion.1
  140.9 2.1 convolution_convert_fusion
  143.0 1.1 copy.13
  144.1 4.0 %all-to-all-start.3 = ((bf16[4,2,96,768]{3,2,1,0:T(8,128)(2,1)}), bf16[4,2,96,768]{3,2,1,0:T(8,128)(2,1)S(1)}, u32[]{:S(2)}, u32[]{:S(2)}) async-start(bf16[4,2,96,768]{3,2,1,0:T(8,128)(2,1)} %bitcast.56), calls=%async_computation.3 | async-start | bytes 2359296 | tf_op jit(solution)/shard_map/all_to_all | solution.py:27
  148.2 1.3 add_convert_fusion.1
  149.5 0.8 dynamic-slice_bitcast_fusion.2
  150.2 0.8 convolution_convert_fusion.2
  151.1 0.2 copy-done.10
  151.4 1.0 copy-done.3
  152.4 0.8 convolution_convert_fusion.1
  153.3 0.9 pad_maximum_fusion.4
  154.2 3.0 %collective-permute-start.9 = (bf16[512,768]{1,0:T(8,128)(2,1)}, bf16[512,768]{1,0:T(8,128)(2,1)}, u32[]{:S(2)}, u32[]{:S(2)}) collective-permute-start(bf16[512,768]{1,0:T(8,128)(2,1)} %pad_maximum_fusion.4), channel_id=1, source_target_pairs={{0,4},{4,0},{1,5},{5,1},{2,6},{6,2},{3,7},{7,3},{8,12},{12,8},{9,1... | collective-permute-start | bytes 2359304 | tf_op jit(solution)/shard_map/ppermute | solution.py:23
  157.2 4.9 %collective-permute-start.14 = (bf16[2,192,384]{2,1,0:T(8,128)(2,1)}, bf16[2,192,384]{2,1,0:T(8,128)(2,1)S(1)}, u32[]{:S(2)}, u32[]{:S(2)}) collective-permute-start(bf16[2,192,384]{2,1,0:T(8,128)(2,1)} %dynamic-slice_bitcast_fusion.2), channel_id=1, source_target_pairs={{0,3},{1,2},{2,1},{3,0},{4,7},{5,6},{6,5},{7,4},{8,11},{9,10},{10,... | collective-permute-start | bytes 884744 | tf_op jit(solution)/shard_map/ppermute | solution.py:119
  162.1 9.5 %collective-permute-done.14 = bf16[2,192,384]{2,1,0:T(8,128)(2,1)S(1)} collective-permute-done((bf16[2,192,384]{2,1,0:T(8,128)(2,1)}, bf16[2,192,384]{2,1,0:T(8,128)(2,1)S(1)}, u32[]{:S(2)}, u32[]{:S(2)}) %collective-permute-start.14) | collective-permute-done | bytes 294944 | tf_op jit(solution)/shard_map/ppermute | solution.py:119
  171.6 2.5 %collective-permute-start.15 = (bf16[2,192,384]{2,1,0:T(8,128)(2,1)S(1)}, bf16[2,192,384]{2,1,0:T(8,128)(2,1)S(1)}, u32[]{:S(2)}, u32[]{:S(2)}) collective-permute-start(bf16[2,192,384]{2,1,0:T(8,128)(2,1)S(1)} %fusion.5), channel_id=1, source_target_pairs={{0,3},{1,2},{2,1},{3,0},{4,7},{5,6},{6,5},{7,4},{8,11},{9,10},{10,... | collective-permute-start | bytes 884744 | tf_op jit(solution)/shard_map/ppermute | solution.py:120
  174.1 0.1 fusion.6
  174.3 2.2 %add_convert_fusion = bf16[512,768]{1,0:T(8,128)(2,1)} fusion(bf16[512,768]{1,0:T(8,128)(2,1)} %collective-permute-done.9, bf16[512,384]{1,0:T(8,128)(2,1)S(1)} %get-tuple-element.34, bf16[512,384]{1,0:T(8,128)(2,1)S(1)} %get-tuple-element.32), kind=kLoop, calls=%fused_computation | loop fusion | flops 2752512 | bytes 2359296 | tf_op jit(solution)/shard_map/convert_element_type | solution.py:71
  176.5 3.0 %collective-permute-start.10 = (bf16[96,768]{1,0:T(8,128)(2,1)S(1)}, bf16[96,768]{1,0:T(8,128)(2,1)S(1)}, u32[]{:S(2)}, u32[]{:S(2)}) collective-permute-start(bf16[96,768]{1,0:T(8,128)(2,1)S(1)} %get-tuple-element.47), channel_id=1, source_target_pairs={{0,4},{4,0},{1,5},{5,1},{2,6},{6,2},{3,7},{7,3},{8,12},{12,8},{9,1... | collective-permute-start | bytes 442376 | tf_op jit(solution)/shard_map/ppermute | solution.py:23
  179.5 3.4 %collective-permute-done.15 = bf16[2,192,384]{2,1,0:T(8,128)(2,1)S(1)} collective-permute-done((bf16[2,192,384]{2,1,0:T(8,128)(2,1)S(1)}, bf16[2,192,384]{2,1,0:T(8,128)(2,1)S(1)}, u32[]{:S(2)}, u32[]{:S(2)}) %collective-permute-start.15) | collective-permute-done | bytes 294944 | tf_op jit(solution)/shard_map/ppermute | solution.py:120
  182.9 0.2 maximum_select_fusion.5
  183.1 1.9 collective-permute-start.16
  185.1 3.6 %all-to-all-start.4 = ((bf16[8,64,768]{2,1,0:T(8,128)(2,1)}), bf16[8,64,768]{2,1,0:T(8,128)(2,1)S(1)}, u32[]{:S(2)}, u32[]{:S(2)}) async-start(bf16[8,64,768]{2,1,0:T(8,128)(2,1)} %bitcast.16), calls=%async_computation.4 | async-start | bytes 1572864 | tf_op jit(solution)/shard_map/all_to_all | solution.py:27
  188.7 3.4 %collective-permute-start.11 = (bf16[96,1536]{1,0:T(8,128)(2,1)S(1)}, bf16[96,1536]{1,0:T(8,128)(2,1)S(1)}, u32[]{:S(2)}, u32[]{:S(2)}) collective-permute-start(bf16[96,1536]{1,0:T(8,128)(2,1)S(1)} %maximum_select_fusion.7), channel_id=1, source_target_pairs={{0,1},{1,2},{2,3},{3,0},{4,5},{5,6},{6,7},{7,4},{8,9},{9,10},{10,1... | collective-permute-start | bytes 884744 | tf_op jit(solution)/shard_map/ppermute | solution.py:138
  192.1 1.9 collective-permute-start.12
  194.0 4.3 %collective-permute-start.13 = (bf16[96,1536]{1,0:T(8,128)(2,1)S(1)}, bf16[96,1536]{1,0:T(8,128)(2,1)S(1)}, u32[]{:S(2)}, u32[]{:S(2)}) collective-permute-start(bf16[96,1536]{1,0:T(8,128)(2,1)S(1)} %maximum_select_fusion.7), channel_id=1, source_target_pairs={{0,3},{1,0},{2,1},{3,2},{4,7},{5,4},{6,5},{7,6},{8,11},{9,8},{10,9... | collective-permute-start | bytes 884744 | tf_op jit(solution)/shard_map/ppermute | solution.py:138
  198.6 1.4 maximum_select_fusion
  199.9 3.0 %collective-permute-done.11 = bf16[96,1536]{1,0:T(8,128)(2,1)S(1)} collective-permute-done((bf16[96,1536]{1,0:T(8,128)(2,1)S(1)}, bf16[96,1536]{1,0:T(8,128)(2,1)S(1)}, u32[]{:S(2)}, u32[]{:S(2)}) %collective-permute-start.11) | collective-permute-done | bytes 294944 | tf_op jit(solution)/shard_map/ppermute | solution.py:138
  203.0 7.6 %collective-permute-done.12 = bf16[96,1536]{1,0:T(8,128)(2,1)S(1)} collective-permute-done((bf16[96,1536]{1,0:T(8,128)(2,1)S(1)}, bf16[96,1536]{1,0:T(8,128)(2,1)S(1)}, u32[]{:S(2)}, u32[]{:S(2)}) %collective-permute-start.12) | collective-permute-done | bytes 294944 | tf_op jit(solution)/shard_map/ppermute | solution.py:138
  210.6 0.6 collective-permute-done.13
  211.3 0.8 all-to-all-done.4
  212.2 0.7 fusion.25
  (57 shorter events, 1.9 us)
Async XLA Ops:
  1.5 8.6 %copy-start = (bf16[1536,384]{1,0:T(8,128)(2,1)S(1)}, bf16[1536,384]{1,0:T(8,128)(2,1)}, u32[]{:S(2)}) copy-start(bf16[1536,384]{1,0:T(8,128)(2,1)} %param.6) | copy-start | bytes 3538948
  2.4 28.7 %all-to-all-start = ((bf16[8,64,768]{2,1,0:T(8,128)(2,1)}), bf16[8,64,768]{2,1,0:T(8,128)(2,1)S(1)}, u32[]{:S(2)}, u32[]{:S(2)}) async-start(bf16[8,64,768]{2,1,0:T(8,128)(2,1)} %broadcast_in_dim.12), calls=%async_computation | async-start | bytes 1572864 | tf_op jit(solution)/shard_map/all_to_all | solution.py:27
  10.1 5.0 %copy-start.1 = (bf16[384,1536]{1,0:T(8,128)(2,1)S(1)}, bf16[384,1536]{1,0:T(8,128)(2,1)}, u32[]{:S(2)}) copy-start(bf16[384,1536]{1,0:T(8,128)(2,1)} %param.5) | copy-start | bytes 3538948
  10.2 6.9 %collective-permute-start.1 = (bf16[768,384]{1,0:T(8,128)(2,1)S(1)}, bf16[768,384]{1,0:T(8,128)(2,1)S(1)}, u32[]{:S(2)}, u32[]{:S(2)}) collective-permute-start(bf16[768,384]{1,0:T(8,128)(2,1)S(1)} %get-tuple-element.29), channel_id=1, source_target_pairs={{0,4},{4,0},{1,5},{5,1},{2,6},{6,2},{3,7},{7,3},{8,12},{12,8},{9,1... | collective-permute-start | bytes 1769480 | tf_op jit(solution)/shard_map/ppermute | solution.py:23
  15.2 3.9 %collective-permute-start = (bf16[384,768]{1,0:T(8,128)(2,1)S(1)}, bf16[384,768]{1,0:T(8,128)(2,1)S(1)}, u32[]{:S(2)}, u32[]{:S(2)}) collective-permute-start(bf16[384,768]{1,0:T(8,128)(2,1)S(1)} %get-tuple-element.31), channel_id=1, source_target_pairs={{0,4},{4,0},{1,5},{5,1},{2,6},{6,2},{3,7},{7,3},{8,12},{12,8},{9,1... | collective-permute-start | bytes 1769480 | tf_op jit(solution)/shard_map/ppermute | solution.py:23
  31.1 6.9 %collective-permute-start.2 = (bf16[512,768]{1,0:T(8,128)(2,1)S(1)}, bf16[512,768]{1,0:T(8,128)(2,1)S(1)}, u32[]{:S(2)}, u32[]{:S(2)}) collective-permute-start(bf16[512,768]{1,0:T(8,128)(2,1)S(1)} %bitcast.57), channel_id=1, source_target_pairs={{0,4},{4,0},{1,5},{5,1},{2,6},{6,2},{3,7},{7,3},{8,12},{12,8},{9,1... | collective-permute-start | bytes 2359304 | tf_op jit(solution)/shard_map/ppermute | solution.py:23
  36.2 2.7 %copy-start.12 = (bf16[512,384]{1,0:T(8,128)(2,1)}, bf16[512,384]{1,0:T(8,128)(2,1)S(1)}, u32[]{:S(2)}) copy-start(bf16[512,384]{1,0:T(8,128)(2,1)S(1)} %get-tuple-element.37) | copy-start | bytes 1179652
  36.2 1.9 copy-start.2
  38.0 0.9 copy-start.7
  38.1 0.9 copy-start.14
  38.9 0.9 copy-start.11
  39.9 13.2 %collective-permute-start.3 = (bf16[4,64,768]{2,1,0:T(8,128)(2,1)S(1)}, bf16[4,64,768]{2,1,0:T(8,128)(2,1)}, u32[]{:S(2)}, u32[]{:S(2)}) collective-permute-start(bf16[4,64,768]{2,1,0:T(8,128)(2,1)S(1)} %get-tuple-element.19), channel_id=1, source_target_pairs={{0,8},{8,0},{16,24},{24,16},{32,40},{40,32},{48,56},{56,48},{1,9},... | collective-permute-start | bytes 1179656 | tf_op jit(solution)/shard_map/ppermute | solution.py:65
  43.9 17.8 %collective-permute-start.4 = (bf16[4,64,768]{2,1,0:T(8,128)(2,1)S(1)}, bf16[4,64,768]{2,1,0:T(8,128)(2,1)}, u32[]{:S(2)}, u32[]{:S(2)}) collective-permute-start(bf16[4,64,768]{2,1,0:T(8,128)(2,1)S(1)} %get-tuple-element.20), channel_id=1, source_target_pairs={{0,56},{8,16},{16,8},{24,32},{32,24},{40,48},{48,40},{56,0},{1,57}... | collective-permute-start | bytes 1179656 | tf_op jit(solution)/shard_map/ppermute | solution.py:65
  101.1 8.6 %collective-permute-start.6 = (bf16[256,768]{1,0:T(8,128)(2,1)S(1)}, bf16[256,768]{1,0:T(8,128)(2,1)}, u32[]{:S(2)}, u32[]{:S(2)}) collective-permute-start(bf16[256,768]{1,0:T(8,128)(2,1)S(1)} %all_gather.3), channel_id=1, source_target_pairs={{0,8},{8,0},{16,24},{24,16},{32,40},{40,32},{48,56},{56,48},{1,9},... | collective-permute-start | bytes 1179656 | tf_op jit(solution)/shard_map/ppermute | solution.py:65
  103.8 21.8 %all-to-all-start.2 = ((bf16[4,64,768]{2,1,0:T(8,128)(2,1)}), bf16[4,64,768]{2,1,0:T(8,128)(2,1)S(1)}, u32[]{:S(2)}, u32[]{:S(2)}) async-start(bf16[4,64,768]{2,1,0:T(8,128)(2,1)} %broadcast_in_dim.13), calls=%async_computation.2 | async-start | bytes 786432 | tf_op jit(solution)/shard_map/all_to_all | solution.py:27
  108.0 3.0 %copy-start.8 = (bf16[512,768]{1,0:T(8,128)(2,1)S(1)}, bf16[512,768]{1,0:T(8,128)(2,1)}, u32[]{:S(2)}) copy-start(bf16[512,768]{1,0:T(8,128)(2,1)} %copy-done.7) | copy-start | bytes 2359300
  111.0 18.6 %copy-start.5 = (bf16[512,768]{1,0:T(8,128)(2,1)}, bf16[512,768]{1,0:T(8,128)(2,1)S(1)}, u32[]{:S(2)}) copy-start(bf16[512,768]{1,0:T(8,128)(2,1)S(1)} %maximum_select_fusion.2) | copy-start | bytes 2359300
  112.5 15.1 %collective-permute-start.7 = (bf16[768,384]{1,0:T(8,128)(2,1)}, bf16[768,384]{1,0:T(8,128)(2,1)}, u32[]{:S(2)}, u32[]{:S(2)}) collective-permute-start(bf16[768,384]{1,0:T(8,128)(2,1)} %convolution_convert_fusion.5), channel_id=1, source_target_pairs={{0,4},{4,0},{1,5},{5,1},{2,6},{6,2},{3,7},{7,3},{8,12},{12,8},{9,1... | collective-permute-start | bytes 1769480 | tf_op jit(solution)/shard_map/ppermute | solution.py:23
  125.6 13.9 %collective-permute-start.5 = (bf16[256,768]{1,0:T(8,128)(2,1)S(1)}, bf16[256,768]{1,0:T(8,128)(2,1)}, u32[]{:S(2)}, u32[]{:S(2)}) collective-permute-start(bf16[256,768]{1,0:T(8,128)(2,1)S(1)} %bitcast.62), channel_id=1, source_target_pairs={{0,56},{8,16},{16,8},{24,32},{32,24},{40,48},{48,40},{56,0},{1,57}... | collective-permute-start | bytes 1179656 | tf_op jit(solution)/shard_map/ppermute | solution.py:65
  129.6 11.3 %copy-start.13 = (bf16[512,384]{1,0:T(8,128)(2,1)S(1)}, bf16[512,384]{1,0:T(8,128)(2,1)}, u32[]{:S(2)}) copy-start(bf16[512,384]{1,0:T(8,128)(2,1)} %copy-done.12) | copy-start | bytes 1179652
  129.6 18.5 %collective-permute-start.8 = (bf16[2,384,384]{2,1,0:T(8,128)(2,1)}, bf16[2,384,384]{2,1,0:T(8,128)(2,1)}, u32[]{:S(2)}, u32[]{:S(2)}) collective-permute-start(bf16[2,384,384]{2,1,0:T(8,128)(2,1)} %maximum_select_fusion.4), channel_id=1, source_target_pairs={{0,1},{1,0},{2,3},{3,2},{4,5},{5,4},{6,7},{7,6},{8,9},{9,8},{10,11... | collective-permute-start | bytes 1769480 | tf_op jit(solution)/shard_map/ppermute | solution.py:116
  140.9 2.1 copy-start.9
  144.1 30.0 %all-to-all-start.3 = ((bf16[4,2,96,768]{3,2,1,0:T(8,128)(2,1)}), bf16[4,2,96,768]{3,2,1,0:T(8,128)(2,1)S(1)}, u32[]{:S(2)}, u32[]{:S(2)}) async-start(bf16[4,2,96,768]{3,2,1,0:T(8,128)(2,1)} %bitcast.56), calls=%async_computation.3 | async-start | bytes 2359296 | tf_op jit(solution)/shard_map/all_to_all | solution.py:27
  148.2 2.1 copy-start.6
  150.2 1.1 copy-start.10
  151.0 1.3 copy-start.3
  154.2 20.0 %collective-permute-start.9 = (bf16[512,768]{1,0:T(8,128)(2,1)}, bf16[512,768]{1,0:T(8,128)(2,1)}, u32[]{:S(2)}, u32[]{:S(2)}) collective-permute-start(bf16[512,768]{1,0:T(8,128)(2,1)} %pad_maximum_fusion.4), channel_id=1, source_target_pairs={{0,4},{4,0},{1,5},{5,1},{2,6},{6,2},{3,7},{7,3},{8,12},{12,8},{9,1... | collective-permute-start | bytes 2359304 | tf_op jit(solution)/shard_map/ppermute | solution.py:23
  157.2 14.3 %collective-permute-start.14 = (bf16[2,192,384]{2,1,0:T(8,128)(2,1)}, bf16[2,192,384]{2,1,0:T(8,128)(2,1)S(1)}, u32[]{:S(2)}, u32[]{:S(2)}) collective-permute-start(bf16[2,192,384]{2,1,0:T(8,128)(2,1)} %dynamic-slice_bitcast_fusion.2), channel_id=1, source_target_pairs={{0,3},{1,2},{2,1},{3,0},{4,7},{5,6},{6,5},{7,4},{8,11},{9,10},{10,... | collective-permute-start | bytes 884744 | tf_op jit(solution)/shard_map/ppermute | solution.py:119
  171.6 11.3 %collective-permute-start.15 = (bf16[2,192,384]{2,1,0:T(8,128)(2,1)S(1)}, bf16[2,192,384]{2,1,0:T(8,128)(2,1)S(1)}, u32[]{:S(2)}, u32[]{:S(2)}) collective-permute-start(bf16[2,192,384]{2,1,0:T(8,128)(2,1)S(1)} %fusion.5), channel_id=1, source_target_pairs={{0,3},{1,2},{2,1},{3,0},{4,7},{5,6},{6,5},{7,4},{8,11},{9,10},{10,... | collective-permute-start | bytes 884744 | tf_op jit(solution)/shard_map/ppermute | solution.py:120
  176.5 12.1 %collective-permute-start.10 = (bf16[96,768]{1,0:T(8,128)(2,1)S(1)}, bf16[96,768]{1,0:T(8,128)(2,1)S(1)}, u32[]{:S(2)}, u32[]{:S(2)}) collective-permute-start(bf16[96,768]{1,0:T(8,128)(2,1)S(1)} %get-tuple-element.47), channel_id=1, source_target_pairs={{0,4},{4,0},{1,5},{5,1},{2,6},{6,2},{3,7},{7,3},{8,12},{12,8},{9,1... | collective-permute-start | bytes 442376 | tf_op jit(solution)/shard_map/ppermute | solution.py:23
  183.1 15.5 %collective-permute-start.16 = (bf16[2,384,384]{2,1,0:T(8,128)(2,1)S(1)}, bf16[2,384,384]{2,1,0:T(8,128)(2,1)S(1)}, u32[]{:S(2)}, u32[]{:S(2)}) collective-permute-start(bf16[2,384,384]{2,1,0:T(8,128)(2,1)S(1)} %maximum_select_fusion.5), channel_id=1, source_target_pairs={{0,1},{1,0},{2,3},{3,2},{4,5},{5,4},{6,7},{7,6},{8,9},{9,8},{10,11... | collective-permute-start | bytes 1769480 | tf_op jit(solution)/shard_map/ppermute | solution.py:121
  185.1 27.1 %all-to-all-start.4 = ((bf16[8,64,768]{2,1,0:T(8,128)(2,1)}), bf16[8,64,768]{2,1,0:T(8,128)(2,1)S(1)}, u32[]{:S(2)}, u32[]{:S(2)}) async-start(bf16[8,64,768]{2,1,0:T(8,128)(2,1)} %bitcast.16), calls=%async_computation.4 | async-start | bytes 1572864 | tf_op jit(solution)/shard_map/all_to_all | solution.py:27
  188.7 14.3 %collective-permute-start.11 = (bf16[96,1536]{1,0:T(8,128)(2,1)S(1)}, bf16[96,1536]{1,0:T(8,128)(2,1)S(1)}, u32[]{:S(2)}, u32[]{:S(2)}) collective-permute-start(bf16[96,1536]{1,0:T(8,128)(2,1)S(1)} %maximum_select_fusion.7), channel_id=1, source_target_pairs={{0,1},{1,2},{2,3},{3,0},{4,5},{5,6},{6,7},{7,4},{8,9},{9,10},{10,1... | collective-permute-start | bytes 884744 | tf_op jit(solution)/shard_map/ppermute | solution.py:138
  192.1 18.5 %collective-permute-start.12 = (bf16[96,1536]{1,0:T(8,128)(2,1)S(1)}, bf16[96,1536]{1,0:T(8,128)(2,1)S(1)}, u32[]{:S(2)}, u32[]{:S(2)}) collective-permute-start(bf16[96,1536]{1,0:T(8,128)(2,1)S(1)} %maximum_select_fusion.7), channel_id=1, source_target_pairs={{0,2},{1,3},{2,0},{3,1},{4,6},{5,7},{6,4},{7,5},{8,10},{9,11},{10,... | collective-permute-start | bytes 884744 | tf_op jit(solution)/shard_map/ppermute | solution.py:138
  194.0 17.2 %collective-permute-start.13 = (bf16[96,1536]{1,0:T(8,128)(2,1)S(1)}, bf16[96,1536]{1,0:T(8,128)(2,1)S(1)}, u32[]{:S(2)}, u32[]{:S(2)}) collective-permute-start(bf16[96,1536]{1,0:T(8,128)(2,1)S(1)} %maximum_select_fusion.7), channel_id=1, source_target_pairs={{0,3},{1,0},{2,1},{3,2},{4,7},{5,4},{6,5},{7,6},{8,11},{9,8},{10,9... | collective-permute-start | bytes 884744 | tf_op jit(solution)/shard_map/ppermute | solution.py:138
  211.3 1.6 copy-start.4

commit v8 on v6

--- a/solution.py
+++ b/solution.py
@@ -108,45 +108,31 @@
 
     act, hg = whole(both[:, :half], even), whole(both[:, half:], odd)
 
-    def scatter(keep, send, step):
-        return plus(keep, lax.ppermute(send, "rep", step[1]))
+    def scatter(x, axis, bit, pairs):
+        def at(place):
+            return lax.dynamic_index_in_dim(x, place, axis, False)
+
+        return plus(at(bit), lax.ppermute(at(1 - bit), "rep", pairs))
 
     def collect(x, steps, axis):
-        for bit, pairs in steps[::-1]:
+        for bit, pairs in steps:
             x = pair(x, lax.ppermute(x, "rep", pairs), bit, axis)
         return x
 
-    def parts(own, got, bit, axis):
-        own, got = (x.reshape((2, x.shape[0] // 2) + x.shape[1:]) for x in (own, got))
-        return tuple(
-            pair(pick(own, b)[None], pick(got, b)[None], core, 0)
-            if axis == 0
-            else pair(pick(own, b), pick(got, b), core, 1)
-            for b in (bit, 1 - bit)
-        )
-
-    high, low = rep // 2, rep % 2
-    down_steps = [((rep + 1) // 2 % 2, near), (high, far)]
-    up_steps = [(high, far), (low, near)]
-    down_got = swap(dot(act, og[:, width:], (0, 0)))
-    up_got = swap(dot(tok[:, width:], hg, (0, 0)))
-    down_own = dot(act, og[:, :width], (0, 0))
-    up_own = dot(tok[:, :width], hg, (0, 0))
-    down_part = scatter(*parts(down_own, down_got, down_steps[0][0], 0), down_steps[0])
-    up_part = scatter(*parts(up_own, up_got, up_steps[0][0], 1), up_steps[0])
+    turn, high, low = (rep + 1) // 2 % 2, rep // 2, rep % 2
+    down_part = dot(act, og, (0, 0)).reshape(2, 2, -1, 2 * width)
+    down_part = scatter(down_part, 0, turn, near)
+    up_part = dot(tok, hg, (0, 0)).reshape(2, 2, 2, -1, half)
+    up_part = scatter(up_part, 1, high, far)
+    down_part = scatter(down_part, 0, high, far)
     down_part, act, hg = barrier((down_part, act, hg))
-    down_part = down_part.reshape(2, 2, -1, width)
-    bit = down_steps[1][0]
-    down_part = scatter(
-        lax.dynamic_index_in_dim(down_part, bit, 1, False),
-        lax.dynamic_index_in_dim(down_part, 1 - bit, 1, False),
-        down_steps[1],
-    )
-    up_part = up_part.reshape(2, -1, 2 * half)
-    bit = up_steps[1][0]
-    up_part = scatter(pick(up_part, bit), pick(up_part, 1 - bit), up_steps[1])
-    down_grads = collect(down_part, down_steps, 1).reshape(2 * half, width)
-    up_grads = collect(up_part, up_steps, 0)
+    up_part = scatter(up_part, 1, low, near)
+    down_own, down_got = down_part[:, :width], swap(down_part[:, width:])
+    down_part = pair(down_own[None], down_got[None], core, 0)
+    down_part = collect(down_part, [(high, far), (turn, near)], 1)
+    down_grads = down_part.reshape(2 * half, width)
+    up_part = pair(up_part[0], swap(up_part[1]), core, 1)
+    up_grads = collect(up_part, [(low, near), (high, far)], 0)
 
     block, token = dot(act, down, (1, 0)), dot(hg, up, (1, 1))
     out = plus(

time: 201 us -> 196 us (0.975)
  waiting for transfers between devices: 59.1 us -> 47.1 us
  starting transfers between devices: 80.9 us -> 84.1 us
  local copies, waits for them, and re-layouts: 4.73 us -> 7.46 us
    ppermute x4, waiting for transfers between devices: 17.4 us -> 5.78 us  [scatter(): return plus(at(bit), lax.ppermute(at(1 - bit), 'rep', pairs))]
    ppermute x4, starting transfers between devices: 10.3 us -> 12.9 us  [collect(): x = pair(x, lax.ppermute(x, 'rep', pairs), bit, axis)]
    ppermute x4, waiting for transfers between devices: 15.5 us -> 13.3 us  [collect(): x = pair(x, lax.ppermute(x, 'rep', pairs), bit, axis)]
    dot_general x8 -> x6, matrix products: 5.39 us -> 4.79 us  [dot(): lax.dot_general(left, right, ((dims[:1], dims[1:]), ((), ())), preferred_...]
  transfers between devices with their start and end apart: 20 -> 20, of which waited for: 13 -> 12; matrix products, arithmetic and copies ran while one was open for 7% -> 8% of each run, Pallas kernels for 0% -> 0%
where the time goes in v8:
time: 196 us; the launch traced here: 194 us
  starting transfers between devices  84.1 us (43%)
  waiting for transfers between devices  47.1 us (24%)
  blocking collectives  36.8 us (19%)
  other arithmetic  12.5 us (6%)
  local copies, waits for them, and re-layouts  7.46 us (4%)
  matrix products  4.79 us (2%)
    ppermute x6, starting transfers between devices, swap(): return lax.ppermute(x, 'core', [(0, 1), (1, 0)])  26.8 us
    ppermute x4, starting transfers between devices, z_swap(): return lax.ppermute(x, ('zh', 'zl'), pairs)  20.2 us
    all_to_all x1, blocking collectives, exchange(): return lax.all_to_all(x, axis, 0, 0, tiled=False)  19.8 us
    all_gather x1, blocking collectives, per_device(): lax.all_gather(jnp.concatenate([act, hid_grads], 1), 'zh', axis=0, tiled=...  17 us
    ppermute x4, waiting for transfers between devices, collect(): x = pair(x, lax.ppermute(x, 'rep', pairs), bit, axis)  13.3 us
    ppermute x4, starting transfers between devices, scatter(): return plus(at(bit), lax.ppermute(at(1 - bit), 'rep', pairs))  13.1 us
    ppermute x4, starting transfers between devices, collect(): x = pair(x, lax.ppermute(x, 'rep', pairs), bit, axis)  12.9 us
    ppermute x4, waiting for transfers between devices, z_swap(): return lax.ppermute(x, ('zh', 'zl'), pairs)  12.3 us
  transfers between devices with their start and end apart: 20, of which 12 were waited for; matrix products, arithmetic and copies ran while one was open for 8% of the time, Pallas kernels for 0%

profile of v8, /device:TPU:1, one launch (start us, length us, event | category | flops | bytes accessed | tf_op | source)
XLA Modules:
  0.0 194.0 jit_solution(1226754941722556561)
XLA Ops:
  0.6 0.8 pad_maximum_fusion.11
  1.5 0.9 broadcast_in_dim.12
  2.4 7.7 %all-to-all-start = ((bf16[8,64,768]{2,1,0:T(8,128)(2,1)}), bf16[8,64,768]{2,1,0:T(8,128)(2,1)S(1)}, u32[]{:S(2)}, u32[]{:S(2)}) async-start(bf16[8,64,768]{2,1,0:T(8,128)(2,1)} %broadcast_in_dim.12), calls=%async_computation | async-start | bytes 1572864 | tf_op jit(solution)/shard_map/all_to_all | solution.py:27
  10.2 4.8 %collective-permute-start = (bf16[384,768]{1,0:T(8,128)(2,1)S(1)}, bf16[384,768]{1,0:T(8,128)(2,1)S(1)}, u32[]{:S(2)}, u32[]{:S(2)}) collective-permute-start(bf16[384,768]{1,0:T(8,128)(2,1)S(1)} %get-tuple-element.25), channel_id=1, source_target_pairs={{0,4},{4,0},{1,5},{5,1},{2,6},{6,2},{3,7},{7,3},{8,12},{12,8},{9,1... | collective-permute-start | bytes 1769480 | tf_op jit(solution)/shard_map/ppermute | solution.py:23
  15.0 0.1 constant_dynamic-slice_fusion.3
  15.2 1.9 collective-permute-start.1
  17.2 1.9 collective-permute-done.1
  19.1 0.1 pad_maximum_fusion.1
  19.2 11.9 %all-to-all-done = bf16[8,64,768]{2,1,0:T(8,128)(2,1)S(1)} async-done(((bf16[8,64,768]{2,1,0:T(8,128)(2,1)}), bf16[8,64,768]{2,1,0:T(8,128)(2,1)S(1)}, u32[]{:S(2)}, u32[]{:S(2)}) %all-to-all-start) | async-done | bytes 786464 | tf_op jit(solution)/shard_map/all_to_all | solution.py:27
  31.1 5.0 %collective-permute-start.2 = (bf16[512,768]{1,0:T(8,128)(2,1)S(1)}, bf16[512,768]{1,0:T(8,128)(2,1)}, u32[]{:S(2)}, u32[]{:S(2)}) collective-permute-start(bf16[512,768]{1,0:T(8,128)(2,1)S(1)} %bitcast.59), channel_id=1, source_target_pairs={{0,4},{4,0},{1,5},{5,1},{2,6},{6,2},{3,7},{7,3},{8,12},{12,8},{9,1... | collective-permute-start | bytes 2359304 | tf_op jit(solution)/shard_map/ppermute | solution.py:23
  36.2 1.9 collective-permute-done.2
  38.1 1.2 fusion.22
  39.3 0.8 convolution_convert_fusion.4
  40.2 0.8 convolution_convert_fusion.5
  41.0 1.0 dynamic-slice_bitcast_fusion.1
  42.0 10.6 %collective-permute-start.4 = (bf16[4,64,768]{2,1,0:T(8,128)(2,1)}, bf16[4,64,768]{2,1,0:T(8,128)(2,1)}, u32[]{:S(2)}, u32[]{:S(2)}) collective-permute-start(bf16[4,64,768]{2,1,0:T(8,128)(2,1)} %get-tuple-element.16), channel_id=1, source_target_pairs={{0,56},{8,16},{16,8},{24,32},{32,24},{40,48},{48,40},{56,0},{1,57}... | collective-permute-start | bytes 1179656 | tf_op jit(solution)/shard_map/ppermute | solution.py:65
  52.6 1.9 collective-permute-start.3
  54.6 7.6 %collective-permute-done.4 = bf16[4,64,768]{2,1,0:T(8,128)(2,1)} collective-permute-done((bf16[4,64,768]{2,1,0:T(8,128)(2,1)}, bf16[4,64,768]{2,1,0:T(8,128)(2,1)}, u32[]{:S(2)}, u32[]{:S(2)}) %collective-permute-start.4) | collective-permute-done | bytes 393248 | tf_op jit(solution)/shard_map/ppermute | solution.py:65
  62.1 1.2 fusion.2
  63.3 1.5 collective-permute-done.3
  64.9 1.1 fusion.3
  66.0 19.8 %all_to_all.15 = bf16[4,64,1536]{2,1,0:T(8,128)(2,1)S(1)} all-to-all(bf16[4,64,1536]{2,1,0:T(8,128)(2,1)S(1)} %pad_maximum_fusion.4), channel_id=1, replica_groups=mesh['row'=8,'zh'=4,'zl'=2,'core'=2,'rep'=4] {'zh'}, dimensions={0} | all-to-all | bytes 1572864 | tf_op jit(solution)/shard_map/all_to_all | solution.py:27
  85.8 0.1 add_bitcast_fusion
  85.9 0.1 multiply_convert_fusion
  86.1 17.0 %all_gather.3 = bf16[256,1536]{1,0:T(8,128)(2,1)S(1)} all-gather(bf16[64,1536]{1,0:T(8,128)(2,1)S(1)} %pad_maximum_fusion.10), channel_id=1, replica_groups=mesh['row'=8,'zh'=4,'zl'=2,'core'=2,'rep'=4] {'zh'}, dimensions={0}, use_global_device_ids=true | all-gather | bytes 983040 | tf_op jit(solution)/shard_map/all_gather | solution.py:102
  103.1 5.5 %collective-permute-start.5 = (bf16[256,768]{1,0:T(8,128)(2,1)S(1)}, bf16[256,768]{1,0:T(8,128)(2,1)}, u32[]{:S(2)}, u32[]{:S(2)}) collective-permute-start(bf16[256,768]{1,0:T(8,128)(2,1)S(1)} %get-tuple-element.31), channel_id=1, source_target_pairs={{0,8},{8,0},{16,24},{24,16},{32,40},{40,32},{48,56},{56,48},{1,9},... | collective-permute-start | bytes 1179656 | tf_op jit(solution)/shard_map/ppermute | solution.py:65
  108.7 2.1 %collective-permute-start.8 = (bf16[256,768]{1,0:T(8,128)(2,1)S(1)}, bf16[256,768]{1,0:T(8,128)(2,1)S(1)}, u32[]{:S(2)}, u32[]{:S(2)}) collective-permute-start(bf16[256,768]{1,0:T(8,128)(2,1)S(1)} %get-tuple-element.30), channel_id=1, source_target_pairs={{0,56},{8,16},{16,8},{24,32},{32,24},{40,48},{48,40},{56,0},{1,57}... | collective-permute-start | bytes 1179656 | tf_op jit(solution)/shard_map/ppermute | solution.py:65
  110.8 3.2 %collective-permute-done.5 = bf16[256,768]{1,0:T(8,128)(2,1)} collective-permute-done((bf16[256,768]{1,0:T(8,128)(2,1)S(1)}, bf16[256,768]{1,0:T(8,128)(2,1)}, u32[]{:S(2)}, u32[]{:S(2)}) %collective-permute-start.5) | collective-permute-done | bytes 393248 | tf_op jit(solution)/shard_map/ppermute | solution.py:65
  114.0 1.4 maximum_select_fusion.2
  115.4 0.8 convolution_convert_fusion.1
  116.3 0.8 dynamic-slice_bitcast_fusion
  117.1 2.9 %collective-permute-start.6 = (bf16[2,192,768]{2,1,0:T(8,128)(2,1)}, bf16[2,192,768]{2,1,0:T(8,128)(2,1)}, u32[]{:S(2)}, u32[]{:S(2)}) collective-permute-start(bf16[2,192,768]{2,1,0:T(8,128)(2,1)} %dynamic-slice_bitcast_fusion), channel_id=1, source_target_pairs={{0,1},{1,0},{2,3},{3,2},{4,5},{5,4},{6,7},{7,6},{8,9},{9,8},{10,11... | collective-permute-start | bytes 1769480 | tf_op jit(solution)/shard_map/ppermute | solution.py:115
  120.1 0.3 maximum_select_fusion.3
  120.5 0.8 convolution_convert_fusion
  121.4 0.9 copy.15
  122.3 3.9 %collective-permute-start.10 = (bf16[2,2,96,768]{3,2,0,1:T(8,128)(2,1)}, bf16[2,2,96,768]{3,2,0,1:T(8,128)(2,1)S(1)}, u32[]{:S(2)}, u32[]{:S(2)}) collective-permute-start(bf16[2,2,96,768]{3,2,0,1:T(8,128)(2,1)} %bitcast.58), channel_id=1, source_target_pairs={{0,3},{1,2},{2,1},{3,0},{4,7},{5,6},{6,5},{7,4},{8,11},{9,10},{10,... | collective-permute-start | bytes 1769480 | tf_op jit(solution)/shard_map/ppermute | solution.py:115
  126.2 1.9 collective-permute-done.6
  128.1 1.4 fusion.1
  129.5 4.3 %collective-permute-start.7 = (bf16[192,768]{1,0:T(8,128)(2,1)S(1)}, bf16[192,768]{1,0:T(8,128)(2,1)S(1)}, u32[]{:S(2)}, u32[]{:S(2)}) collective-permute-start(bf16[192,768]{1,0:T(8,128)(2,1)S(1)} %dynamic-slice_bitcast_fusion.4), channel_id=1, source_target_pairs={{0,3},{1,2},{2,1},{3,0},{4,7},{5,6},{6,5},{7,4},{8,11},{9,10},{10,... | collective-permute-start | bytes 884744 | tf_op jit(solution)/shard_map/ppermute | solution.py:115
  133.8 0.6 collective-permute-done.10
  134.3 0.1 fusion
  134.5 2.1 %collective-permute-start.11 = (bf16[2,96,768]{2,1,0:T(8,128)(2,1)S(1)}, bf16[2,96,768]{2,1,0:T(8,128)(2,1)S(1)}, u32[]{:S(2)}, u32[]{:S(2)}) collective-permute-start(bf16[2,96,768]{2,1,0:T(8,128)(2,1)S(1)} %dynamic-slice_bitcast_fusion.3), channel_id=1, source_target_pairs={{0,1},{1,0},{2,3},{3,2},{4,5},{5,4},{6,7},{7,6},{8,9},{9,8},{10,11... | collective-permute-start | bytes 884744 | tf_op jit(solution)/shard_map/ppermute | solution.py:115
  136.6 3.3 %collective-permute-done.7 = bf16[192,768]{1,0:T(8,128)(2,1)S(1)} collective-permute-done((bf16[192,768]{1,0:T(8,128)(2,1)S(1)}, bf16[192,768]{1,0:T(8,128)(2,1)S(1)}, u32[]{:S(2)}, u32[]{:S(2)}) %collective-permute-start.7) | collective-permute-done | bytes 294944 | tf_op jit(solution)/shard_map/ppermute | solution.py:115
  140.0 0.8 convolution_convert_fusion.2
  140.9 1.0 copy-done.4
  141.9 0.8 convolution_convert_fusion.3
  142.9 10.4 %collective-permute-start.9 = (bf16[512,768]{1,0:T(8,128)(2,1)S(1)}, bf16[512,768]{1,0:T(8,128)(2,1)S(1)}, u32[]{:S(2)}, u32[]{:S(2)}) collective-permute-start(bf16[512,768]{1,0:T(8,128)(2,1)S(1)} %pad_maximum_fusion.5), channel_id=1, source_target_pairs={{0,4},{4,0},{1,5},{5,1},{2,6},{6,2},{3,7},{7,3},{8,12},{12,8},{9,1... | collective-permute-start | bytes 2359304 | tf_op jit(solution)/shard_map/ppermute | solution.py:23
  153.4 2.8 %collective-permute-start.12 = (bf16[96,768]{1,0:T(8,128)(2,1)S(1)}, bf16[96,768]{1,0:T(8,128)(2,1)S(1)}, u32[]{:S(2)}, u32[]{:S(2)}) collective-permute-start(bf16[96,768]{1,0:T(8,128)(2,1)S(1)} %get-tuple-element.41), channel_id=1, source_target_pairs={{0,4},{4,0},{1,5},{5,1},{2,6},{6,2},{3,7},{7,3},{8,12},{12,8},{9,1... | collective-permute-start | bytes 442376 | tf_op jit(solution)/shard_map/ppermute | solution.py:23
  156.2 1.9 collective-permute-start.15
  158.2 2.4 %collective-permute-start.13 = (bf16[96,1536]{1,0:T(8,128)(2,1)S(1)}, bf16[96,1536]{1,0:T(8,128)(2,1)}, u32[]{:S(2)}, u32[]{:S(2)}) collective-permute-start(bf16[96,1536]{1,0:T(8,128)(2,1)S(1)} %maximum_select_fusion.6), channel_id=1, source_target_pairs={{0,1},{1,0},{2,3},{3,2},{4,5},{5,4},{6,7},{7,6},{8,9},{9,8},{10,11... | collective-permute-start | bytes 884744 | tf_op jit(solution)/shard_map/ppermute | solution.py:119
  160.7 4.3 %collective-permute-start.16 = (bf16[2,192,384]{2,1,0:T(8,128)(2,1)S(1)}, bf16[2,192,384]{2,1,0:T(8,128)(2,1)S(1)}, u32[]{:S(2)}, u32[]{:S(2)}) collective-permute-start(bf16[2,192,384]{2,1,0:T(8,128)(2,1)S(1)} %maximum_select_fusion.7), channel_id=1, source_target_pairs={{0,3},{1,2},{2,1},{3,0},{4,7},{5,6},{6,5},{7,4},{8,11},{9,10},{10,... | collective-permute-start | bytes 884744 | tf_op jit(solution)/shard_map/ppermute | solution.py:119
  165.0 1.1 add_convert_fusion
  166.1 3.5 %all-to-all-start.2 = ((bf16[8,64,768]{2,1,0:T(8,128)(2,1)}), bf16[8,64,768]{2,1,0:T(8,128)(2,1)S(1)}, u32[]{:S(2)}, u32[]{:S(2)}) async-start(bf16[8,64,768]{2,1,0:T(8,128)(2,1)} %bitcast.13), calls=%async_computation.2 | async-start | bytes 1572864 | tf_op jit(solution)/shard_map/all_to_all | solution.py:27
  169.6 2.5 %collective-permute-done.16 = bf16[2,192,384]{2,1,0:T(8,128)(2,1)S(1)} collective-permute-done((bf16[2,192,384]{2,1,0:T(8,128)(2,1)S(1)}, bf16[2,192,384]{2,1,0:T(8,128)(2,1)S(1)}, u32[]{:S(2)}, u32[]{:S(2)}) %collective-permute-start.16) | collective-permute-done | bytes 294944 | tf_op jit(solution)/shard_map/ppermute | solution.py:119
  172.1 0.2 maximum_select_fusion.5
  172.3 1.9 collective-permute-start.17
  174.2 1.2 maximum_select_fusion.4
  175.4 4.3 %collective-permute-start.14 = (bf16[192,1536]{1,0:T(8,128)(2,1)S(1)}, bf16[192,1536]{1,0:T(8,128)(2,1)S(1)}, u32[]{:S(2)}, u32[]{:S(2)}) collective-permute-start(bf16[192,1536]{1,0:T(8,128)(2,1)S(1)} %maximum_select_fusion.4), channel_id=1, source_target_pairs={{0,3},{1,2},{2,1},{3,0},{4,7},{5,6},{6,5},{7,4},{8,11},{9,10},{10,... | collective-permute-start | bytes 1769480 | tf_op jit(solution)/shard_map/ppermute | solution.py:119
  179.7 8.2 %collective-permute-done.17 = bf16[2,384,384]{2,1,0:T(8,128)(2,1)S(1)} collective-permute-done((bf16[2,384,384]{2,1,0:T(8,128)(2,1)S(1)}, bf16[2,384,384]{2,1,0:T(8,128)(2,1)S(1)}, u32[]{:S(2)}, u32[]{:S(2)}) %collective-permute-start.17) | collective-permute-done | bytes 589856 | tf_op jit(solution)/shard_map/ppermute | solution.py:119
  187.9 1.4 maximum_select_fusion.1
  189.3 2.6 %collective-permute-done.14 = bf16[192,1536]{1,0:T(8,128)(2,1)S(1)} collective-permute-done((bf16[192,1536]{1,0:T(8,128)(2,1)S(1)}, bf16[192,1536]{1,0:T(8,128)(2,1)S(1)}, u32[]{:S(2)}, u32[]{:S(2)}) %collective-permute-start.14) | collective-permute-done | bytes 589856 | tf_op jit(solution)/shard_map/ppermute | solution.py:119
  191.9 1.4 maximum_select_fusion
  193.3 0.1 fusion.13
  193.4 0.6 fusion.23
  (53 shorter events, 1.4 us)
Async XLA Ops:
  1.5 8.6 %copy-start = (bf16[384,1536]{1,0:T(8,128)(2,1)S(1)}, bf16[384,1536]{1,0:T(8,128)(2,1)}, u32[]{:S(2)}) copy-start(bf16[384,1536]{1,0:T(8,128)(2,1)} %param.5) | copy-start | bytes 3538948
  2.4 28.7 %all-to-all-start = ((bf16[8,64,768]{2,1,0:T(8,128)(2,1)}), bf16[8,64,768]{2,1,0:T(8,128)(2,1)S(1)}, u32[]{:S(2)}, u32[]{:S(2)}) async-start(bf16[8,64,768]{2,1,0:T(8,128)(2,1)} %broadcast_in_dim.12), calls=%async_computation | async-start | bytes 1572864 | tf_op jit(solution)/shard_map/all_to_all | solution.py:27
  10.1 4.9 %copy-start.1 = (bf16[1536,384]{1,0:T(8,128)(2,1)S(1)}, bf16[1536,384]{1,0:T(8,128)(2,1)}, u32[]{:S(2)}) copy-start(bf16[1536,384]{1,0:T(8,128)(2,1)} %param.6) | copy-start | bytes 3538948
  10.2 6.9 %collective-permute-start = (bf16[384,768]{1,0:T(8,128)(2,1)S(1)}, bf16[384,768]{1,0:T(8,128)(2,1)S(1)}, u32[]{:S(2)}, u32[]{:S(2)}) collective-permute-start(bf16[384,768]{1,0:T(8,128)(2,1)S(1)} %get-tuple-element.25), channel_id=1, source_target_pairs={{0,4},{4,0},{1,5},{5,1},{2,6},{6,2},{3,7},{7,3},{8,12},{12,8},{9,1... | collective-permute-start | bytes 1769480 | tf_op jit(solution)/shard_map/ppermute | solution.py:23
  15.2 3.9 %collective-permute-start.1 = (bf16[768,384]{1,0:T(8,128)(2,1)S(1)}, bf16[768,384]{1,0:T(8,128)(2,1)S(1)}, u32[]{:S(2)}, u32[]{:S(2)}) collective-permute-start(bf16[768,384]{1,0:T(8,128)(2,1)S(1)} %get-tuple-element.23), channel_id=1, source_target_pairs={{0,4},{4,0},{1,5},{5,1},{2,6},{6,2},{3,7},{7,3},{8,12},{12,8},{9,1... | collective-permute-start | bytes 1769480 | tf_op jit(solution)/shard_map/ppermute | solution.py:23
  31.1 7.0 %collective-permute-start.2 = (bf16[512,768]{1,0:T(8,128)(2,1)S(1)}, bf16[512,768]{1,0:T(8,128)(2,1)}, u32[]{:S(2)}, u32[]{:S(2)}) collective-permute-start(bf16[512,768]{1,0:T(8,128)(2,1)S(1)} %bitcast.59), channel_id=1, source_target_pairs={{0,4},{4,0},{1,5},{5,1},{2,6},{6,2},{3,7},{7,3},{8,12},{12,8},{9,1... | collective-permute-start | bytes 2359304 | tf_op jit(solution)/shard_map/ppermute | solution.py:23
  36.2 4.0 %copy-start.10 = (bf16[512,384]{1,0:T(8,128)(2,1)}, bf16[512,384]{1,0:T(8,128)(2,1)S(1)}, u32[]{:S(2)}) copy-start(bf16[512,384]{1,0:T(8,128)(2,1)S(1)} %get-tuple-element.32) | copy-start | bytes 1179652
  39.3 0.9 copy-start.12
  39.3 0.9 copy-start.8
  40.2 0.9 copy-start.7
  42.0 20.1 %collective-permute-start.4 = (bf16[4,64,768]{2,1,0:T(8,128)(2,1)}, bf16[4,64,768]{2,1,0:T(8,128)(2,1)}, u32[]{:S(2)}, u32[]{:S(2)}) collective-permute-start(bf16[4,64,768]{2,1,0:T(8,128)(2,1)} %get-tuple-element.16), channel_id=1, source_target_pairs={{0,56},{8,16},{16,8},{24,32},{32,24},{40,48},{48,40},{56,0},{1,57}... | collective-permute-start | bytes 1179656 | tf_op jit(solution)/shard_map/ppermute | solution.py:65
  52.6 12.2 %collective-permute-start.3 = (bf16[4,64,768]{2,1,0:T(8,128)(2,1)}, bf16[4,64,768]{2,1,0:T(8,128)(2,1)}, u32[]{:S(2)}, u32[]{:S(2)}) collective-permute-start(bf16[4,64,768]{2,1,0:T(8,128)(2,1)} %get-tuple-element.15), channel_id=1, source_target_pairs={{0,8},{8,0},{16,24},{24,16},{32,40},{40,32},{48,56},{56,48},{1,9},... | collective-permute-start | bytes 1179656 | tf_op jit(solution)/shard_map/ppermute | solution.py:65
  103.1 10.9 %collective-permute-start.5 = (bf16[256,768]{1,0:T(8,128)(2,1)S(1)}, bf16[256,768]{1,0:T(8,128)(2,1)}, u32[]{:S(2)}, u32[]{:S(2)}) collective-permute-start(bf16[256,768]{1,0:T(8,128)(2,1)S(1)} %get-tuple-element.31), channel_id=1, source_target_pairs={{0,8},{8,0},{16,24},{24,16},{32,40},{40,32},{48,56},{56,48},{1,9},... | collective-permute-start | bytes 1179656 | tf_op jit(solution)/shard_map/ppermute | solution.py:65
  108.7 6.7 %copy-start.11 = (bf16[512,384]{1,0:T(8,128)(2,1)S(1)}, bf16[512,384]{1,0:T(8,128)(2,1)}, u32[]{:S(2)}) copy-start(bf16[512,384]{1,0:T(8,128)(2,1)} %copy-done.10) | copy-start | bytes 1179652
  108.7 6.7 %copy-start.13 = (bf16[512,384]{1,0:T(8,128)(2,1)S(1)}, bf16[512,384]{1,0:T(8,128)(2,1)}, u32[]{:S(2)}) copy-start(bf16[512,384]{1,0:T(8,128)(2,1)} %copy-done.12) | copy-start | bytes 1179652
  108.7 11.4 %collective-permute-start.8 = (bf16[256,768]{1,0:T(8,128)(2,1)S(1)}, bf16[256,768]{1,0:T(8,128)(2,1)S(1)}, u32[]{:S(2)}, u32[]{:S(2)}) collective-permute-start(bf16[256,768]{1,0:T(8,128)(2,1)S(1)} %get-tuple-element.30), channel_id=1, source_target_pairs={{0,56},{8,16},{16,8},{24,32},{32,24},{40,48},{48,40},{56,0},{1,57}... | collective-permute-start | bytes 1179656 | tf_op jit(solution)/shard_map/ppermute | solution.py:65
  115.4 0.9 copy-start.3
  116.3 3.8 %copy-start.2 = (bf16[768,768]{1,0:T(8,128)(2,1)}, bf16[768,768]{1,0:T(8,128)(2,1)S(1)}, u32[]{:S(2)}) copy-start(bf16[768,768]{1,0:T(8,128)(2,1)S(1)} %convolution_convert_fusion.1) | copy-start | bytes 3538948
  116.3 4.2 %copy-start.9 = (bf16[512,384]{1,0:T(8,128)(2,1)S(1)}, bf16[512,384]{1,0:T(8,128)(2,1)}, u32[]{:S(2)}) copy-start(bf16[512,384]{1,0:T(8,128)(2,1)} %copy-done.8) | copy-start | bytes 1179652
  117.1 10.9 %collective-permute-start.6 = (bf16[2,192,768]{2,1,0:T(8,128)(2,1)}, bf16[2,192,768]{2,1,0:T(8,128)(2,1)}, u32[]{:S(2)}, u32[]{:S(2)}) collective-permute-start(bf16[2,192,768]{2,1,0:T(8,128)(2,1)} %dynamic-slice_bitcast_fusion), channel_id=1, source_target_pairs={{0,1},{1,0},{2,3},{3,2},{4,5},{5,4},{6,7},{7,6},{8,9},{9,8},{10,11... | collective-permute-start | bytes 1769480 | tf_op jit(solution)/shard_map/ppermute | solution.py:115
  120.4 0.9 copy-start.5
  122.3 12.0 %collective-permute-start.10 = (bf16[2,2,96,768]{3,2,0,1:T(8,128)(2,1)}, bf16[2,2,96,768]{3,2,0,1:T(8,128)(2,1)S(1)}, u32[]{:S(2)}, u32[]{:S(2)}) collective-permute-start(bf16[2,2,96,768]{3,2,0,1:T(8,128)(2,1)} %bitcast.58), channel_id=1, source_target_pairs={{0,3},{1,2},{2,1},{3,0},{4,7},{5,6},{6,5},{7,4},{8,11},{9,10},{10,... | collective-permute-start | bytes 1769480 | tf_op jit(solution)/shard_map/ppermute | solution.py:115
  129.5 10.4 %collective-permute-start.7 = (bf16[192,768]{1,0:T(8,128)(2,1)S(1)}, bf16[192,768]{1,0:T(8,128)(2,1)S(1)}, u32[]{:S(2)}, u32[]{:S(2)}) collective-permute-start(bf16[192,768]{1,0:T(8,128)(2,1)S(1)} %dynamic-slice_bitcast_fusion.4), channel_id=1, source_target_pairs={{0,3},{1,2},{2,1},{3,0},{4,7},{5,6},{6,5},{7,4},{8,11},{9,10},{10,... | collective-permute-start | bytes 884744 | tf_op jit(solution)/shard_map/ppermute | solution.py:115
  134.5 5.5 %copy-start.6 = (bf16[512,768]{1,0:T(8,128)(2,1)S(1)}, bf16[512,768]{1,0:T(8,128)(2,1)}, u32[]{:S(2)}) copy-start(bf16[512,768]{1,0:T(8,128)(2,1)} %copy-done.5) | copy-start | bytes 2359300
  134.5 18.7 %collective-permute-start.11 = (bf16[2,96,768]{2,1,0:T(8,128)(2,1)S(1)}, bf16[2,96,768]{2,1,0:T(8,128)(2,1)S(1)}, u32[]{:S(2)}, u32[]{:S(2)}) collective-permute-start(bf16[2,96,768]{2,1,0:T(8,128)(2,1)S(1)} %dynamic-slice_bitcast_fusion.3), channel_id=1, source_target_pairs={{0,1},{1,0},{2,3},{3,2},{4,5},{5,4},{6,7},{7,6},{8,9},{9,8},{10,11... | collective-permute-start | bytes 884744 | tf_op jit(solution)/shard_map/ppermute | solution.py:115
  140.8 1.1 copy-start.4
  142.9 22.1 %collective-permute-start.9 = (bf16[512,768]{1,0:T(8,128)(2,1)S(1)}, bf16[512,768]{1,0:T(8,128)(2,1)S(1)}, u32[]{:S(2)}, u32[]{:S(2)}) collective-permute-start(bf16[512,768]{1,0:T(8,128)(2,1)S(1)} %pad_maximum_fusion.5), channel_id=1, source_target_pairs={{0,4},{4,0},{1,5},{5,1},{2,6},{6,2},{3,7},{7,3},{8,12},{12,8},{9,1... | collective-permute-start | bytes 2359304 | tf_op jit(solution)/shard_map/ppermute | solution.py:23
  153.4 4.7 %collective-permute-start.12 = (bf16[96,768]{1,0:T(8,128)(2,1)S(1)}, bf16[96,768]{1,0:T(8,128)(2,1)S(1)}, u32[]{:S(2)}, u32[]{:S(2)}) collective-permute-start(bf16[96,768]{1,0:T(8,128)(2,1)S(1)} %get-tuple-element.41), channel_id=1, source_target_pairs={{0,4},{4,0},{1,5},{5,1},{2,6},{6,2},{3,7},{7,3},{8,12},{12,8},{9,1... | collective-permute-start | bytes 442376 | tf_op jit(solution)/shard_map/ppermute | solution.py:23
  156.2 4.4 %collective-permute-start.15 = (bf16[192,384]{1,0:T(8,128)(2,1)S(1)}, bf16[192,384]{1,0:T(8,128)(2,1)S(1)}, u32[]{:S(2)}, u32[]{:S(2)}) collective-permute-start(bf16[192,384]{1,0:T(8,128)(2,1)S(1)} %get-tuple-element.39), channel_id=1, source_target_pairs={{0,4},{4,0},{1,5},{5,1},{2,6},{6,2},{3,7},{7,3},{8,12},{12,8},{9,1... | collective-permute-start | bytes 442376 | tf_op jit(solution)/shard_map/ppermute | solution.py:23
  158.2 16.0 %collective-permute-start.13 = (bf16[96,1536]{1,0:T(8,128)(2,1)S(1)}, bf16[96,1536]{1,0:T(8,128)(2,1)}, u32[]{:S(2)}, u32[]{:S(2)}) collective-permute-start(bf16[96,1536]{1,0:T(8,128)(2,1)S(1)} %maximum_select_fusion.6), channel_id=1, source_target_pairs={{0,1},{1,0},{2,3},{3,2},{4,5},{5,4},{6,7},{7,6},{8,9},{9,8},{10,11... | collective-permute-start | bytes 884744 | tf_op jit(solution)/shard_map/ppermute | solution.py:119
  160.7 11.4 %collective-permute-start.16 = (bf16[2,192,384]{2,1,0:T(8,128)(2,1)S(1)}, bf16[2,192,384]{2,1,0:T(8,128)(2,1)S(1)}, u32[]{:S(2)}, u32[]{:S(2)}) collective-permute-start(bf16[2,192,384]{2,1,0:T(8,128)(2,1)S(1)} %maximum_select_fusion.7), channel_id=1, source_target_pairs={{0,3},{1,2},{2,1},{3,0},{4,7},{5,6},{6,5},{7,4},{8,11},{9,10},{10,... | collective-permute-start | bytes 884744 | tf_op jit(solution)/shard_map/ppermute | solution.py:119
  166.1 27.2 %all-to-all-start.2 = ((bf16[8,64,768]{2,1,0:T(8,128)(2,1)}), bf16[8,64,768]{2,1,0:T(8,128)(2,1)S(1)}, u32[]{:S(2)}, u32[]{:S(2)}) async-start(bf16[8,64,768]{2,1,0:T(8,128)(2,1)} %bitcast.13), calls=%async_computation.2 | async-start | bytes 1572864 | tf_op jit(solution)/shard_map/all_to_all | solution.py:27
  172.3 15.6 %collective-permute-start.17 = (bf16[2,384,384]{2,1,0:T(8,128)(2,1)S(1)}, bf16[2,384,384]{2,1,0:T(8,128)(2,1)S(1)}, u32[]{:S(2)}, u32[]{:S(2)}) collective-permute-start(bf16[2,384,384]{2,1,0:T(8,128)(2,1)S(1)} %maximum_select_fusion.5), channel_id=1, source_target_pairs={{0,1},{1,0},{2,3},{3,2},{4,5},{5,4},{6,7},{7,6},{8,9},{9,8},{10,11... | collective-permute-start | bytes 1769480 | tf_op jit(solution)/shard_map/ppermute | solution.py:119
  175.4 16.5 %collective-permute-start.14 = (bf16[192,1536]{1,0:T(8,128)(2,1)S(1)}, bf16[192,1536]{1,0:T(8,128)(2,1)S(1)}, u32[]{:S(2)}, u32[]{:S(2)}) collective-permute-start(bf16[192,1536]{1,0:T(8,128)(2,1)S(1)} %maximum_select_fusion.4), channel_id=1, source_target_pairs={{0,3},{1,2},{2,1},{3,0},{4,7},{5,6},{6,5},{7,4},{8,11},{9,10},{10,... | collective-permute-start | bytes 1769480 | tf_op jit(solution)/shard_map/ppermute | solution.py:119

commit v9 on v8

--- a/solution.py
+++ b/solution.py
@@ -80,21 +80,31 @@
     own = gather(jnp.concatenate([tokens, out_grads], 1), "row")
     own, up, down = barrier((own, up, down))
     other = swap(own)
-    tok = jnp.concatenate([own[:, :width], other[:, :width]], 1)
-    og = jnp.concatenate([own[:, width:], other[:, width:]], 1)
-    total = tok.shape[0]
-    share = total // n_z
+    total = own.shape[0]
+    same, share = total // 2, total // n_z
 
-    def halves(part):
-        part = part.reshape(2, n_zh, share, half)
-        return pick(part, zl), pick(part, 1 - zl)
+    def columns_of(x, place):
+        x = pick(x.reshape(2, same, 2 * width), place)
+        return x[:, :width], x[:, width:]
 
-    hid_keep, hid_send = halves(dot(tok, up, (1, 0)))
-    ag_keep, ag_send = halves(dot(og, down, (1, 1)))
-    hid_send, ag_send = barrier((hid_send, ag_send))
-    hid_half = plus(hid_keep, z_swap(hid_send, even))
-    ag_half = plus(ag_keep, z_swap(ag_send, odd))
-    sums = total_of(exchange(jnp.concatenate([hid_half, ag_half], 2), "zh"))
+    def rows_of(place):
+        (t0, g0), (t1, g1) = columns_of(own, place), columns_of(other, place)
+        return jnp.concatenate([t0, t1], 1), jnp.concatenate([g0, g1], 1)
+
+    tok_send, og_send = rows_of(1 - zl)
+    tok_keep, og_keep = rows_of(zl)
+
+    hid_send = dot(tok_send, up, (1, 0))
+    ag_send = dot(og_send, down, (1, 1))
+    hid_send, ag_send, tok_keep, og_keep = barrier(
+        (hid_send, ag_send, tok_keep, og_keep)
+    )
+    tok = jnp.concatenate([tok_keep, tok_send], 0)
+    og = jnp.concatenate([og_keep, og_send], 0)
+    hid_half = plus(dot(tok_keep, up, (1, 0)), z_swap(hid_send, even))
+    ag_half = plus(dot(og_keep, down, (1, 1)), z_swap(ag_send, odd))
+    halves = jnp.concatenate([hid_half, ag_half], 1).reshape(n_zh, share, 2 * half)
+    sums = total_of(exchange(halves, "zh"))
     hidden, act_grads = sums[:, :half], sums[:, half:]
     act = jax.nn.gelu(hidden).astype(bf16)
     hid_grads = gelu_pullback(hidden, act_grads).astype(bf16)
@@ -103,10 +113,10 @@
         jnp.concatenate([act, hid_grads], 1), "zh", axis=0, tiled=True
     )
 
-    def whole(part, pairs):
-        return pair(part, z_swap(part, pairs), zl, 0)
-
-    act, hg = whole(both[:, :half], even), whole(both[:, half:], odd)
+    act_half, hg_half = both[:, :half], both[:, half:]
+    act_got, hg_got = z_swap(act_half, even), z_swap(hg_half, odd)
+    act = jnp.concatenate([act_half, act_got], 0)
+    hg = jnp.concatenate([hg_half, hg_got], 0)
 
     def scatter(x, axis, bit, pairs):
         def at(place):
@@ -122,10 +132,14 @@
     turn, high, low = (rep + 1) // 2 % 2, rep // 2, rep % 2
     down_part = dot(act, og, (0, 0)).reshape(2, 2, -1, 2 * width)
     down_part = scatter(down_part, 0, turn, near)
-    up_part = dot(tok, hg, (0, 0)).reshape(2, 2, 2, -1, half)
-    up_part = scatter(up_part, 1, high, far)
+    cut = width // 2
+    order = [tok[:, i * cut : (i + 1) * cut] for i in (0, 2, 1, 3)]
+    up_part = dot(jnp.concatenate(order, 1), hg, (0, 0)).reshape(2, width, half)
+    up_part = scatter(up_part, 0, high, far).reshape(2, 2, -1, half)
     down_part = scatter(down_part, 0, high, far)
-    down_part, act, hg = barrier((down_part, act, hg))
+    down_part, act_half, act_got, hg_half, hg_got = barrier(
+        (down_part, act_half, act_got, hg_half, hg_got)
+    )
     up_part = scatter(up_part, 1, low, near)
     down_own, down_got = down_part[:, :width], swap(down_part[:, width:])
     down_part = pair(down_own[None], down_got[None], core, 0)
@@ -134,11 +148,15 @@
     up_part = pair(up_part[0], swap(up_part[1]), core, 1)
     up_grads = collect(up_part, [(low, near), (high, far)], 0)
 
-    block, token = dot(act, down, (1, 0)), dot(hg, up, (1, 1))
-    out = plus(
-        jnp.concatenate([block[:, :width], token[:, :width]], 1),
-        swap(jnp.concatenate([block[:, width:], token[:, width:]], 1)),
-    )
+    act, hg = pair(act_half, act_got, zl, 0), pair(hg_half, hg_got, zl, 0)
+
+    def output(columns):
+        block = dot(act, down[:, columns], (1, 0))
+        token = dot(hg, up[columns], (1, 1))
+        return jnp.concatenate([block, token], 1)
+
+    send = output(slice(width, None))
+    out = plus(output(slice(width)), swap(send))
     out = total_of(exchange(out.reshape(n_row, rows, 2 * width), "row")).astype(bf16)
     return (out[:, :width], out[:, width:], up_grads, down_grads)
 

time: 196 us -> 196 us (level)
  matrix products: 4.79 us -> 9.77 us
  other arithmetic: 12.5 us -> 7.67 us
  waiting for transfers between devices: 47.1 us -> 43.4 us
  local copies, waits for them, and re-layouts: 7.46 us -> 10.2 us
    dot_general x6 -> x10, matrix products: 4.79 us -> 9.77 us  [dot(): lax.dot_general(left, right, ((dims[:1], dims[1:]), ((), ())), preferred_...]
    select_n x8 -> x6, other arithmetic: 5.96 us -> 3.2 us  [pair(): jnp.where(place == 0, jnp.concatenate([own, other], axis), jnp.concatenat...]
    ppermute x4, waiting for transfers between devices: 5.78 us -> 3.42 us  [scatter(): return plus(at(bit), lax.ppermute(at(1 - bit), 'rep', pairs))]
    convert_element_type x7 -> x5, other arithmetic: 5.07 us -> 2.87 us  [plus(): return (a.astype(f32) + b.astype(f32)).astype(bf16)]
    ppermute x6, starting transfers between devices: 26.8 us -> 28.8 us  [swap(): return lax.ppermute(x, 'core', [(0, 1), (1, 0)])]
  transfers between devices with their start and end apart: 20 -> 20, of which waited for: 12 -> 12; matrix products, arithmetic and copies ran while one was open for 8% -> 9% of each run, Pallas kernels for 0% -> 0%
where the time goes in v9:
time: 196 us; the launch traced here: 194 us
  starting transfers between devices  85.2 us (43%)
  waiting for transfers between devices  43.4 us (22%)
  blocking collectives  36.8 us (19%)
  local copies, waits for them, and re-layouts  10.2 us (5%)
  matrix products  9.77 us (5%)
  other arithmetic  7.67 us (4%)
    ppermute x6, starting transfers between devices, swap(): return lax.ppermute(x, 'core', [(0, 1), (1, 0)])  28.8 us
    ppermute x4, starting transfers between devices, z_swap(): return lax.ppermute(x, ('zh', 'zl'), pairs)  20.1 us
    all_to_all x1, blocking collectives, exchange(): return lax.all_to_all(x, axis, 0, 0, tiled=False)  19.8 us
    all_gather x1, blocking collectives, per_device(): lax.all_gather(jnp.concatenate([act, hid_grads], 1), 'zh', axis=0, tiled=...  17 us
    ppermute x4, starting transfers between devices, scatter(): return plus(at(bit), lax.ppermute(at(1 - bit), 'rep', pairs))  13.2 us
    ppermute x4, waiting for transfers between devices, collect(): x = pair(x, lax.ppermute(x, 'rep', pairs), bit, axis)  12.7 us
    ppermute x4, starting transfers between devices, collect(): x = pair(x, lax.ppermute(x, 'rep', pairs), bit, axis)  11.9 us
    all_to_all x2, waiting for transfers between devices, exchange(): return lax.all_to_all(x, axis, 0, 0, tiled=False)  11.9 us
  transfers between devices with their start and end apart: 20, of which 12 were waited for; matrix products, arithmetic and copies ran while one was open for 9% of the time, Pallas kernels for 0%

profile of v9, /device:TPU:1, one launch (start us, length us, event | category | flops | bytes accessed | tf_op | source)
XLA Modules:
  0.0 194.3 jit_solution(16191259371628610524)
XLA Ops:
  0.6 0.8 pad_maximum_fusion.7
  1.5 0.9 broadcast_in_dim.12
  2.4 7.7 %all-to-all-start = ((bf16[8,64,768]{2,1,0:T(8,128)(2,1)}), bf16[8,64,768]{2,1,0:T(8,128)(2,1)S(1)}, u32[]{:S(2)}, u32[]{:S(2)}) async-start(bf16[8,64,768]{2,1,0:T(8,128)(2,1)} %broadcast_in_dim.12), calls=%async_computation | async-start | bytes 1572864 | tf_op jit(solution)/shard_map/all_to_all | solution.py:27
  10.2 4.8 %collective-permute-start = (bf16[384,768]{1,0:T(8,128)(2,1)S(1)}, bf16[384,768]{1,0:T(8,128)(2,1)S(1)}, u32[]{:S(2)}, u32[]{:S(2)}) collective-permute-start(bf16[384,768]{1,0:T(8,128)(2,1)S(1)} %get-tuple-element.31), channel_id=1, source_target_pairs={{0,4},{4,0},{1,5},{5,1},{2,6},{6,2},{3,7},{7,3},{8,12},{12,8},{9,1... | collective-permute-start | bytes 1769480 | tf_op jit(solution)/shard_map/ppermute | solution.py:23
  15.0 0.1 constant_dynamic-slice_fusion.1
  15.2 1.9 collective-permute-start.1
  17.2 1.9 collective-permute-done.1
  19.2 11.9 %all-to-all-done = bf16[8,64,768]{2,1,0:T(8,128)(2,1)S(1)} async-done(((bf16[8,64,768]{2,1,0:T(8,128)(2,1)}), bf16[8,64,768]{2,1,0:T(8,128)(2,1)S(1)}, u32[]{:S(2)}, u32[]{:S(2)}) %all-to-all-start) | async-done | bytes 786464 | tf_op jit(solution)/shard_map/all_to_all | solution.py:27
  31.1 5.0 %collective-permute-start.2 = (bf16[512,768]{1,0:T(8,128)(2,1)S(1)}, bf16[512,768]{1,0:T(8,128)(2,1)}, u32[]{:S(2)}, u32[]{:S(2)}) collective-permute-start(bf16[512,768]{1,0:T(8,128)(2,1)S(1)} %bitcast.55), channel_id=1, source_target_pairs={{0,4},{4,0},{1,5},{5,1},{2,6},{6,2},{3,7},{7,3},{8,12},{12,8},{9,1... | collective-permute-start | bytes 2359304 | tf_op jit(solution)/shard_map/ppermute | solution.py:23
  36.3 1.8 collective-permute-done.2
  38.1 1.2 dynamic-slice_bitcast_fusion.2
  39.5 0.5 convolution_convert_fusion.9
  40.0 0.5 convolution_convert_fusion.8
  40.6 10.6 %collective-permute-start.4 = (bf16[256,768]{1,0:T(8,128)(2,1)S(1)}, bf16[256,768]{1,0:T(8,128)(2,1)S(1)}, u32[]{:S(2)}, u32[]{:S(2)}) collective-permute-start(bf16[256,768]{1,0:T(8,128)(2,1)S(1)} %convolution_convert_fusion.8), channel_id=1, source_target_pairs={{0,56},{8,16},{16,8},{24,32},{32,24},{40,48},{48,40},{56,0},{1,57}... | collective-permute-start | bytes 1179656 | tf_op jit(solution)/shard_map/ppermute | solution.py:65
  51.2 1.9 collective-permute-start.3
  53.1 7.2 %collective-permute-done.4 = bf16[256,768]{1,0:T(8,128)(2,1)S(1)} collective-permute-done((bf16[256,768]{1,0:T(8,128)(2,1)S(1)}, bf16[256,768]{1,0:T(8,128)(2,1)S(1)}, u32[]{:S(2)}, u32[]{:S(2)}) %collective-permute-start.4) | collective-permute-done | bytes 393248 | tf_op jit(solution)/shard_map/ppermute | solution.py:65
  60.4 0.5 add_convert_fusion.1
  60.9 2.2 %collective-permute-done.3 = bf16[256,768]{1,0:T(8,128)(2,1)S(1)} collective-permute-done((bf16[256,768]{1,0:T(8,128)(2,1)S(1)}, bf16[256,768]{1,0:T(8,128)(2,1)S(1)}, u32[]{:S(2)}, u32[]{:S(2)}) %collective-permute-start.3) | collective-permute-done | bytes 393248 | tf_op jit(solution)/shard_map/ppermute | solution.py:65
  63.1 0.5 add_convert_fusion.2
  63.6 19.8 %all_to_all.15 = bf16[4,64,1536]{2,1,0:T(8,128)(2,1)S(1)} all-to-all(bf16[4,64,1536]{2,1,0:T(8,128)(2,1)S(1)} %bitcast.54), channel_id=1, replica_groups=mesh['row'=8,'zh'=4,'zl'=2,'core'=2,'rep'=4] {'zh'}, dimensions={0} | all-to-all | bytes 1572864 | tf_op jit(solution)/shard_map/all_to_all | solution.py:27
  83.5 0.1 multiply_convert_fusion
  83.7 17.0 %all_gather.3 = bf16[256,1536]{1,0:T(8,128)(2,1)S(1)} all-gather(bf16[64,1536]{1,0:T(8,128)(2,1)S(1)} %pad_maximum_fusion.6), channel_id=1, replica_groups=mesh['row'=8,'zh'=4,'zl'=2,'core'=2,'rep'=4] {'zh'}, dimensions={0}, use_global_device_ids=true | all-gather | bytes 983040 | tf_op jit(solution)/shard_map/all_gather | solution.py:112
  100.7 0.9 fusion.51
  101.6 5.2 %collective-permute-start.5 = (bf16[256,768]{1,0:T(8,128)(2,1)}, bf16[256,768]{1,0:T(8,128)(2,1)}, u32[]{:S(2)}, u32[]{:S(2)}) collective-permute-start(bf16[256,768]{1,0:T(8,128)(2,1)} %get-tuple-element.23), channel_id=1, source_target_pairs={{0,8},{8,0},{16,24},{24,16},{32,40},{40,32},{48,56},{56,48},{1,9},... | collective-permute-start | bytes 1179656 | tf_op jit(solution)/shard_map/ppermute | solution.py:65
  107.0 0.9 copy-done.6
  107.9 2.3 %collective-permute-start.8 = (bf16[256,768]{1,0:T(8,128)(2,1)S(1)}, bf16[256,768]{1,0:T(8,128)(2,1)S(1)}, u32[]{:S(2)}, u32[]{:S(2)}) collective-permute-start(bf16[256,768]{1,0:T(8,128)(2,1)S(1)} %copy-done.6), channel_id=1, source_target_pairs={{0,56},{8,16},{16,8},{24,32},{32,24},{40,48},{48,40},{56,0},{1,57}... | collective-permute-start | bytes 1179656 | tf_op jit(solution)/shard_map/ppermute | solution.py:65
  110.2 2.1 %collective-permute-done.5 = bf16[256,768]{1,0:T(8,128)(2,1)} collective-permute-done((bf16[256,768]{1,0:T(8,128)(2,1)}, bf16[256,768]{1,0:T(8,128)(2,1)}, u32[]{:S(2)}, u32[]{:S(2)}) %collective-permute-start.5) | collective-permute-done | bytes 393248 | tf_op jit(solution)/shard_map/ppermute | solution.py:65
  112.3 1.9 convolution_convert_fusion.1
  114.3 0.9 dynamic-slice_bitcast_fusion.1
  115.2 2.8 %collective-permute-start.6 = (bf16[2,192,768]{2,1,0:T(8,128)(2,1)}, bf16[2,192,768]{2,1,0:T(8,128)(2,1)}, u32[]{:S(2)}, u32[]{:S(2)}) collective-permute-start(bf16[2,192,768]{2,1,0:T(8,128)(2,1)} %dynamic-slice_bitcast_fusion.1), channel_id=1, source_target_pairs={{0,1},{1,0},{2,3},{3,2},{4,5},{5,4},{6,7},{7,6},{8,9},{9,8},{10,11... | collective-permute-start | bytes 1769480 | tf_op jit(solution)/shard_map/ppermute | solution.py:125
  117.9 0.2 fusion.50
  118.2 0.7 copy-done.12
  119.0 1.1 convolution_convert_fusion
  120.1 1.0 copy-done.4
  121.1 0.8 dynamic-slice_bitcast_fusion
  121.9 4.0 %collective-permute-start.10 = (bf16[384,768]{1,0:T(8,128)(2,1)}, bf16[384,768]{1,0:T(8,128)(2,1)}, u32[]{:S(2)}, u32[]{:S(2)}) collective-permute-start(bf16[384,768]{1,0:T(8,128)(2,1)} %dynamic-slice_bitcast_fusion), channel_id=1, source_target_pairs={{0,3},{1,2},{2,1},{3,0},{4,7},{5,6},{6,5},{7,4},{8,11},{9,10},{10,... | collective-permute-start | bytes 1769480 | tf_op jit(solution)/shard_map/ppermute | solution.py:125
  126.0 0.1 collective-permute-done.6
  126.1 1.3 fusion.3
  127.4 4.3 %collective-permute-start.7 = (bf16[192,768]{1,0:T(8,128)(2,1)S(1)}, bf16[192,768]{1,0:T(8,128)(2,1)S(1)}, u32[]{:S(2)}, u32[]{:S(2)}) collective-permute-start(bf16[192,768]{1,0:T(8,128)(2,1)S(1)} %dynamic-slice_bitcast_fusion.7), channel_id=1, source_target_pairs={{0,3},{1,2},{2,1},{3,0},{4,7},{5,6},{6,5},{7,4},{8,11},{9,10},{10,... | collective-permute-start | bytes 884744 | tf_op jit(solution)/shard_map/ppermute | solution.py:125
  131.7 2.3 %collective-permute-done.10 = bf16[384,768]{1,0:T(8,128)(2,1)} collective-permute-done((bf16[384,768]{1,0:T(8,128)(2,1)}, bf16[384,768]{1,0:T(8,128)(2,1)}, u32[]{:S(2)}, u32[]{:S(2)}) %collective-permute-start.10) | collective-permute-done | bytes 589856 | tf_op jit(solution)/shard_map/ppermute | solution.py:125
  134.1 1.2 fusion.2
  135.3 2.2 %collective-permute-start.11 = (bf16[2,96,768]{2,1,0:T(8,128)(2,1)S(1)}, bf16[2,96,768]{2,1,0:T(8,128)(2,1)S(1)}, u32[]{:S(2)}, u32[]{:S(2)}) collective-permute-start(bf16[2,96,768]{2,1,0:T(8,128)(2,1)S(1)} %dynamic-slice_bitcast_fusion.6), channel_id=1, source_target_pairs={{0,1},{1,0},{2,3},{3,2},{4,5},{5,4},{6,7},{7,6},{8,9},{9,8},{10,11... | collective-permute-start | bytes 884744 | tf_op jit(solution)/shard_map/ppermute | solution.py:125
  137.5 1.0 collective-permute-done.7
  138.6 0.5 convolution_convert_fusion.2
  139.1 1.9 convolution_convert_fusion.3
  141.0 11.1 %collective-permute-start.9 = (bf16[512,768]{0,1:T(8,128)(2,1)S(1)}, bf16[512,768]{0,1:T(8,128)(2,1)S(1)}, u32[]{:S(2)}, u32[]{:S(2)}) collective-permute-start(bf16[512,768]{0,1:T(8,128)(2,1)S(1)} %pad_maximum_fusion.3), channel_id=1, source_target_pairs={{0,4},{4,0},{1,5},{5,1},{2,6},{6,2},{3,7},{7,3},{8,12},{12,8},{9,1... | collective-permute-start | bytes 2359304 | tf_op jit(solution)/shard_map/ppermute | solution.py:23
  152.3 4.0 %collective-permute-start.12 = (bf16[96,768]{1,0:T(8,128)(2,1)S(1)}, bf16[96,768]{1,0:T(8,128)(2,1)S(1)}, u32[]{:S(2)}, u32[]{:S(2)}) collective-permute-start(bf16[96,768]{1,0:T(8,128)(2,1)S(1)} %get-tuple-element.55), channel_id=1, source_target_pairs={{0,4},{4,0},{1,5},{5,1},{2,6},{6,2},{3,7},{7,3},{8,12},{12,8},{9,1... | collective-permute-start | bytes 442376 | tf_op jit(solution)/shard_map/ppermute | solution.py:23
  156.3 1.9 collective-permute-start.15
  158.3 0.5 convolution_convert_fusion.4
  158.8 1.9 convolution_convert_fusion.5
  160.8 2.0 %collective-permute-start.13 = (bf16[96,1536]{1,0:T(8,128)(2,1)S(1)}, bf16[96,1536]{1,0:T(8,128)(2,1)S(1)}, u32[]{:S(2)}, u32[]{:S(2)}) collective-permute-start(bf16[96,1536]{1,0:T(8,128)(2,1)S(1)} %maximum_select_fusion.6), channel_id=1, source_target_pairs={{0,1},{1,0},{2,3},{3,2},{4,5},{5,4},{6,7},{7,6},{8,9},{9,8},{10,11... | collective-permute-start | bytes 884744 | tf_op jit(solution)/shard_map/ppermute | solution.py:129
  162.8 4.0 %collective-permute-start.16 = (bf16[2,192,384]{2,1,0:T(8,128)(2,1)S(1)}, bf16[2,192,384]{2,1,0:T(8,128)(2,1)S(1)}, u32[]{:S(2)}, u32[]{:S(2)}) collective-permute-start(bf16[2,192,384]{2,1,0:T(8,128)(2,1)S(1)} %maximum_select_fusion.7), channel_id=1, source_target_pairs={{0,3},{1,2},{2,1},{3,0},{4,7},{5,6},{6,5},{7,4},{8,11},{9,10},{10,... | collective-permute-start | bytes 884744 | tf_op jit(solution)/shard_map/ppermute | solution.py:129
  166.8 0.2 add_convert_fusion
  167.1 1.2 copy.9
  168.2 3.5 %all-to-all-start.2 = ((bf16[8,64,768]{2,1,0:T(8,128)(2,1)}), bf16[8,64,768]{2,1,0:T(8,128)(2,1)S(1)}, u32[]{:S(2)}, u32[]{:S(2)}) async-start(bf16[8,64,768]{2,1,0:T(8,128)(2,1)} %bitcast.14), calls=%async_computation.2 | async-start | bytes 1572864 | tf_op jit(solution)/shard_map/all_to_all | solution.py:27
  171.8 2.1 %collective-permute-done.16 = bf16[2,192,384]{2,1,0:T(8,128)(2,1)S(1)} collective-permute-done((bf16[2,192,384]{2,1,0:T(8,128)(2,1)S(1)}, bf16[2,192,384]{2,1,0:T(8,128)(2,1)S(1)}, u32[]{:S(2)}, u32[]{:S(2)}) %collective-permute-start.16) | collective-permute-done | bytes 294944 | tf_op jit(solution)/shard_map/ppermute | solution.py:129
  173.9 0.2 maximum_select_fusion.5
  174.1 1.9 collective-permute-start.17
  176.2 4.0 %collective-permute-start.14 = (bf16[192,1536]{1,0:T(8,128)(2,1)S(1)}, bf16[192,1536]{1,0:T(8,128)(2,1)S(1)}, u32[]{:S(2)}, u32[]{:S(2)}) collective-permute-start(bf16[192,1536]{1,0:T(8,128)(2,1)S(1)} %maximum_select_fusion.4), channel_id=1, source_target_pairs={{0,3},{1,2},{2,1},{3,0},{4,7},{5,6},{6,5},{7,4},{8,11},{9,10},{10,... | collective-permute-start | bytes 1769480 | tf_op jit(solution)/shard_map/ppermute | solution.py:129
  180.2 9.2 %collective-permute-done.17 = bf16[2,384,384]{2,1,0:T(8,128)(2,1)S(1)} collective-permute-done((bf16[2,384,384]{2,1,0:T(8,128)(2,1)S(1)}, bf16[2,384,384]{2,1,0:T(8,128)(2,1)S(1)}, u32[]{:S(2)}, u32[]{:S(2)}) %collective-permute-start.17) | collective-permute-done | bytes 589856 | tf_op jit(solution)/shard_map/ppermute | solution.py:129
  189.5 1.4 maximum_select_fusion.1
  190.8 1.4 collective-permute-done.14
  192.2 1.4 maximum_select_fusion
  193.7 0.6 fusion.56
  (56 shorter events, 1.6 us)
Async XLA Ops:
  1.5 8.6 %copy-start = (bf16[384,1536]{1,0:T(8,128)(2,1)S(1)}, bf16[384,1536]{1,0:T(8,128)(2,1)}, u32[]{:S(2)}) copy-start(bf16[384,1536]{1,0:T(8,128)(2,1)} %param.5) | copy-start | bytes 3538948
  2.4 28.7 %all-to-all-start = ((bf16[8,64,768]{2,1,0:T(8,128)(2,1)}), bf16[8,64,768]{2,1,0:T(8,128)(2,1)S(1)}, u32[]{:S(2)}, u32[]{:S(2)}) async-start(bf16[8,64,768]{2,1,0:T(8,128)(2,1)} %broadcast_in_dim.12), calls=%async_computation | async-start | bytes 1572864 | tf_op jit(solution)/shard_map/all_to_all | solution.py:27
  10.1 4.9 %copy-start.1 = (bf16[1536,384]{1,0:T(8,128)(2,1)S(1)}, bf16[1536,384]{1,0:T(8,128)(2,1)}, u32[]{:S(2)}) copy-start(bf16[1536,384]{1,0:T(8,128)(2,1)} %param.6) | copy-start | bytes 3538948
  10.2 6.9 %collective-permute-start = (bf16[384,768]{1,0:T(8,128)(2,1)S(1)}, bf16[384,768]{1,0:T(8,128)(2,1)S(1)}, u32[]{:S(2)}, u32[]{:S(2)}) collective-permute-start(bf16[384,768]{1,0:T(8,128)(2,1)S(1)} %get-tuple-element.31), channel_id=1, source_target_pairs={{0,4},{4,0},{1,5},{5,1},{2,6},{6,2},{3,7},{7,3},{8,12},{12,8},{9,1... | collective-permute-start | bytes 1769480 | tf_op jit(solution)/shard_map/ppermute | solution.py:23
  15.2 3.9 %collective-permute-start.1 = (bf16[768,384]{1,0:T(8,128)(2,1)S(1)}, bf16[768,384]{1,0:T(8,128)(2,1)S(1)}, u32[]{:S(2)}, u32[]{:S(2)}) collective-permute-start(bf16[768,384]{1,0:T(8,128)(2,1)S(1)} %get-tuple-element.29), channel_id=1, source_target_pairs={{0,4},{4,0},{1,5},{5,1},{2,6},{6,2},{3,7},{7,3},{8,12},{12,8},{9,1... | collective-permute-start | bytes 1769480 | tf_op jit(solution)/shard_map/ppermute | solution.py:23
  31.1 7.0 %collective-permute-start.2 = (bf16[512,768]{1,0:T(8,128)(2,1)S(1)}, bf16[512,768]{1,0:T(8,128)(2,1)}, u32[]{:S(2)}, u32[]{:S(2)}) collective-permute-start(bf16[512,768]{1,0:T(8,128)(2,1)S(1)} %bitcast.55), channel_id=1, source_target_pairs={{0,4},{4,0},{1,5},{5,1},{2,6},{6,2},{3,7},{7,3},{8,12},{12,8},{9,1... | collective-permute-start | bytes 2359304 | tf_op jit(solution)/shard_map/ppermute | solution.py:23
  36.2 3.7 %copy-start.8 = (bf16[256,384]{1,0:T(8,128)(2,1)}, bf16[256,384]{1,0:T(8,128)(2,1)S(1)}, u32[]{:S(2)}) copy-start(bf16[256,384]{1,0:T(8,128)(2,1)S(1)} %get-tuple-element.61) | copy-start | bytes 589828
  39.4 0.7 copy-start.10
  40.6 19.8 %collective-permute-start.4 = (bf16[256,768]{1,0:T(8,128)(2,1)S(1)}, bf16[256,768]{1,0:T(8,128)(2,1)S(1)}, u32[]{:S(2)}, u32[]{:S(2)}) collective-permute-start(bf16[256,768]{1,0:T(8,128)(2,1)S(1)} %convolution_convert_fusion.8), channel_id=1, source_target_pairs={{0,56},{8,16},{16,8},{24,32},{32,24},{40,48},{48,40},{56,0},{1,57}... | collective-permute-start | bytes 1179656 | tf_op jit(solution)/shard_map/ppermute | solution.py:65
  51.2 11.9 %collective-permute-start.3 = (bf16[256,768]{1,0:T(8,128)(2,1)S(1)}, bf16[256,768]{1,0:T(8,128)(2,1)S(1)}, u32[]{:S(2)}, u32[]{:S(2)}) collective-permute-start(bf16[256,768]{1,0:T(8,128)(2,1)S(1)} %convolution_convert_fusion.9), channel_id=1, source_target_pairs={{0,8},{8,0},{16,24},{24,16},{32,40},{40,32},{48,56},{56,48},{1,9},... | collective-permute-start | bytes 1179656 | tf_op jit(solution)/shard_map/ppermute | solution.py:65
  101.6 10.7 %collective-permute-start.5 = (bf16[256,768]{1,0:T(8,128)(2,1)}, bf16[256,768]{1,0:T(8,128)(2,1)}, u32[]{:S(2)}, u32[]{:S(2)}) collective-permute-start(bf16[256,768]{1,0:T(8,128)(2,1)} %get-tuple-element.23), channel_id=1, source_target_pairs={{0,8},{8,0},{16,24},{24,16},{32,40},{40,32},{48,56},{56,48},{1,9},... | collective-permute-start | bytes 1179656 | tf_op jit(solution)/shard_map/ppermute | solution.py:65
  106.9 1.0 copy-start.6
  106.9 5.4 %copy-start.9 = (bf16[256,384]{1,0:T(8,128)(2,1)S(1)}, bf16[256,384]{1,0:T(8,128)(2,1)}, u32[]{:S(2)}) copy-start(bf16[256,384]{1,0:T(8,128)(2,1)} %copy-done.8) | copy-start | bytes 589828
  106.9 5.4 %copy-start.11 = (bf16[256,384]{1,0:T(8,128)(2,1)S(1)}, bf16[256,384]{1,0:T(8,128)(2,1)}, u32[]{:S(2)}) copy-start(bf16[256,384]{1,0:T(8,128)(2,1)} %copy-done.10) | copy-start | bytes 589828
  107.9 10.3 %collective-permute-start.8 = (bf16[256,768]{1,0:T(8,128)(2,1)S(1)}, bf16[256,768]{1,0:T(8,128)(2,1)S(1)}, u32[]{:S(2)}, u32[]{:S(2)}) collective-permute-start(bf16[256,768]{1,0:T(8,128)(2,1)S(1)} %copy-done.6), channel_id=1, source_target_pairs={{0,56},{8,16},{16,8},{24,32},{32,24},{40,48},{48,40},{56,0},{1,57}... | collective-permute-start | bytes 1179656 | tf_op jit(solution)/shard_map/ppermute | solution.py:65
  114.2 3.9 %copy-start.2 = (bf16[768,768]{1,0:T(8,128)(2,1)}, bf16[768,768]{1,0:T(8,128)(2,1)S(1)}, u32[]{:S(2)}) copy-start(bf16[768,768]{1,0:T(8,128)(2,1)S(1)} %convolution_convert_fusion.1) | copy-start | bytes 3538948
  115.2 10.9 %collective-permute-start.6 = (bf16[2,192,768]{2,1,0:T(8,128)(2,1)}, bf16[2,192,768]{2,1,0:T(8,128)(2,1)}, u32[]{:S(2)}, u32[]{:S(2)}) collective-permute-start(bf16[2,192,768]{2,1,0:T(8,128)(2,1)} %dynamic-slice_bitcast_fusion.1), channel_id=1, source_target_pairs={{0,1},{1,0},{2,3},{3,2},{4,5},{5,4},{6,7},{7,6},{8,9},{9,8},{10,11... | collective-permute-start | bytes 1769480 | tf_op jit(solution)/shard_map/ppermute | solution.py:125
  118.2 0.7 copy-start.12
  120.1 1.0 copy-start.4
  120.1 6.0 %copy-start.3 = (bf16[768,768]{1,0:T(8,128)(2,1)S(1)}, bf16[768,768]{1,0:T(8,128)(2,1)}, u32[]{:S(2)}) copy-start(bf16[768,768]{1,0:T(8,128)(2,1)} %copy-done.2) | copy-start | bytes 3538948
  121.9 12.1 %collective-permute-start.10 = (bf16[384,768]{1,0:T(8,128)(2,1)}, bf16[384,768]{1,0:T(8,128)(2,1)}, u32[]{:S(2)}, u32[]{:S(2)}) collective-permute-start(bf16[384,768]{1,0:T(8,128)(2,1)} %dynamic-slice_bitcast_fusion), channel_id=1, source_target_pairs={{0,3},{1,2},{2,1},{3,0},{4,7},{5,6},{6,5},{7,4},{8,11},{9,10},{10,... | collective-permute-start | bytes 1769480 | tf_op jit(solution)/shard_map/ppermute | solution.py:125
  126.0 8.1 %copy-start.5 = (bf16[768,768]{1,0:T(8,128)(2,1)S(1)}, bf16[768,768]{1,0:T(8,128)(2,1)}, u32[]{:S(2)}) copy-start(bf16[768,768]{1,0:T(8,128)(2,1)} %copy-done.4) | copy-start | bytes 3538948
  127.4 11.1 %collective-permute-start.7 = (bf16[192,768]{1,0:T(8,128)(2,1)S(1)}, bf16[192,768]{1,0:T(8,128)(2,1)S(1)}, u32[]{:S(2)}, u32[]{:S(2)}) collective-permute-start(bf16[192,768]{1,0:T(8,128)(2,1)S(1)} %dynamic-slice_bitcast_fusion.7), channel_id=1, source_target_pairs={{0,3},{1,2},{2,1},{3,0},{4,7},{5,6},{6,5},{7,4},{8,11},{9,10},{10,... | collective-permute-start | bytes 884744 | tf_op jit(solution)/shard_map/ppermute | solution.py:125
  135.3 3.3 %copy-start.7 = (bf16[256,768]{1,0:T(8,128)(2,1)S(1)}, bf16[256,768]{1,0:T(8,128)(2,1)}, u32[]{:S(2)}) copy-start(bf16[256,768]{1,0:T(8,128)(2,1)} %get-tuple-element.25) | copy-start | bytes 1179652
  135.3 3.3 %copy-start.13 = (bf16[256,768]{1,0:T(8,128)(2,1)S(1)}, bf16[256,768]{1,0:T(8,128)(2,1)}, u32[]{:S(2)}) copy-start(bf16[256,768]{1,0:T(8,128)(2,1)} %copy-done.12) | copy-start | bytes 1179652
  135.3 16.8 %collective-permute-start.11 = (bf16[2,96,768]{2,1,0:T(8,128)(2,1)S(1)}, bf16[2,96,768]{2,1,0:T(8,128)(2,1)S(1)}, u32[]{:S(2)}, u32[]{:S(2)}) collective-permute-start(bf16[2,96,768]{2,1,0:T(8,128)(2,1)S(1)} %dynamic-slice_bitcast_fusion.6), channel_id=1, source_target_pairs={{0,1},{1,0},{2,3},{3,2},{4,5},{5,4},{6,7},{7,6},{8,9},{9,8},{10,11... | collective-permute-start | bytes 884744 | tf_op jit(solution)/shard_map/ppermute | solution.py:125
  141.0 25.8 %collective-permute-start.9 = (bf16[512,768]{0,1:T(8,128)(2,1)S(1)}, bf16[512,768]{0,1:T(8,128)(2,1)S(1)}, u32[]{:S(2)}, u32[]{:S(2)}) collective-permute-start(bf16[512,768]{0,1:T(8,128)(2,1)S(1)} %pad_maximum_fusion.3), channel_id=1, source_target_pairs={{0,4},{4,0},{1,5},{5,1},{2,6},{6,2},{3,7},{7,3},{8,12},{12,8},{9,1... | collective-permute-start | bytes 2359304 | tf_op jit(solution)/shard_map/ppermute | solution.py:23
  152.3 8.4 %collective-permute-start.12 = (bf16[96,768]{1,0:T(8,128)(2,1)S(1)}, bf16[96,768]{1,0:T(8,128)(2,1)S(1)}, u32[]{:S(2)}, u32[]{:S(2)}) collective-permute-start(bf16[96,768]{1,0:T(8,128)(2,1)S(1)} %get-tuple-element.55), channel_id=1, source_target_pairs={{0,4},{4,0},{1,5},{5,1},{2,6},{6,2},{3,7},{7,3},{8,12},{12,8},{9,1... | collective-permute-start | bytes 442376 | tf_op jit(solution)/shard_map/ppermute | solution.py:23
  156.3 6.4 %collective-permute-start.15 = (bf16[192,384]{1,0:T(8,128)(2,1)S(1)}, bf16[192,384]{1,0:T(8,128)(2,1)S(1)}, u32[]{:S(2)}, u32[]{:S(2)}) collective-permute-start(bf16[192,384]{1,0:T(8,128)(2,1)S(1)} %get-tuple-element.53), channel_id=1, source_target_pairs={{0,4},{4,0},{1,5},{5,1},{2,6},{6,2},{3,7},{7,3},{8,12},{12,8},{9,1... | collective-permute-start | bytes 442376 | tf_op jit(solution)/shard_map/ppermute | solution.py:23
  160.8 15.3 %collective-permute-start.13 = (bf16[96,1536]{1,0:T(8,128)(2,1)S(1)}, bf16[96,1536]{1,0:T(8,128)(2,1)S(1)}, u32[]{:S(2)}, u32[]{:S(2)}) collective-permute-start(bf16[96,1536]{1,0:T(8,128)(2,1)S(1)} %maximum_select_fusion.6), channel_id=1, source_target_pairs={{0,1},{1,0},{2,3},{3,2},{4,5},{5,4},{6,7},{7,6},{8,9},{9,8},{10,11... | collective-permute-start | bytes 884744 | tf_op jit(solution)/shard_map/ppermute | solution.py:129
  162.8 11.1 %collective-permute-start.16 = (bf16[2,192,384]{2,1,0:T(8,128)(2,1)S(1)}, bf16[2,192,384]{2,1,0:T(8,128)(2,1)S(1)}, u32[]{:S(2)}, u32[]{:S(2)}) collective-permute-start(bf16[2,192,384]{2,1,0:T(8,128)(2,1)S(1)} %maximum_select_fusion.7), channel_id=1, source_target_pairs={{0,3},{1,2},{2,1},{3,0},{4,7},{5,6},{6,5},{7,4},{8,11},{9,10},{10,... | collective-permute-start | bytes 884744 | tf_op jit(solution)/shard_map/ppermute | solution.py:129
  168.2 25.4 %all-to-all-start.2 = ((bf16[8,64,768]{2,1,0:T(8,128)(2,1)}), bf16[8,64,768]{2,1,0:T(8,128)(2,1)S(1)}, u32[]{:S(2)}, u32[]{:S(2)}) async-start(bf16[8,64,768]{2,1,0:T(8,128)(2,1)} %bitcast.14), calls=%async_computation.2 | async-start | bytes 1572864 | tf_op jit(solution)/shard_map/all_to_all | solution.py:27
  174.1 15.3 %collective-permute-start.17 = (bf16[2,384,384]{2,1,0:T(8,128)(2,1)S(1)}, bf16[2,384,384]{2,1,0:T(8,128)(2,1)S(1)}, u32[]{:S(2)}, u32[]{:S(2)}) collective-permute-start(bf16[2,384,384]{2,1,0:T(8,128)(2,1)S(1)} %maximum_select_fusion.5), channel_id=1, source_target_pairs={{0,1},{1,0},{2,3},{3,2},{4,5},{5,4},{6,7},{7,6},{8,9},{9,8},{10,11... | collective-permute-start | bytes 1769480 | tf_op jit(solution)/shard_map/ppermute | solution.py:129
  176.2 16.0 %collective-permute-start.14 = (bf16[192,1536]{1,0:T(8,128)(2,1)S(1)}, bf16[192,1536]{1,0:T(8,128)(2,1)S(1)}, u32[]{:S(2)}, u32[]{:S(2)}) collective-permute-start(bf16[192,1536]{1,0:T(8,128)(2,1)S(1)} %maximum_select_fusion.4), channel_id=1, source_target_pairs={{0,3},{1,2},{2,1},{3,0},{4,7},{5,6},{6,5},{7,4},{8,11},{9,10},{10,... | collective-permute-start | bytes 1769480 | tf_op jit(solution)/shard_map/ppermute | solution.py:129

commit v10 on v9

--- a/solution.py
+++ b/solution.py
@@ -124,29 +124,24 @@
 
         return plus(at(bit), lax.ppermute(at(1 - bit), "rep", pairs))
 
-    def collect(x, steps, axis):
-        for bit, pairs in steps:
-            x = pair(x, lax.ppermute(x, "rep", pairs), bit, axis)
-        return x
-
-    turn, high, low = (rep + 1) // 2 % 2, rep // 2, rep % 2
-    down_part = dot(act, og, (0, 0)).reshape(2, 2, -1, 2 * width)
+    turn, high = (rep + 1) // 2 % 2, rep // 2
+    down_part = dot(act, og, (0, 0)).reshape(2, half // 2, 2 * width)
     down_part = scatter(down_part, 0, turn, near)
+    down_part, act_half, act_got, hg_half, hg_got = barrier(
+        (down_part, act_half, act_got, hg_half, hg_got)
+    )
     cut = width // 2
     order = [tok[:, i * cut : (i + 1) * cut] for i in (0, 2, 1, 3)]
     up_part = dot(jnp.concatenate(order, 1), hg, (0, 0)).reshape(2, width, half)
-    up_part = scatter(up_part, 0, high, far).reshape(2, 2, -1, half)
-    down_part = scatter(down_part, 0, high, far)
-    down_part, act_half, act_got, hg_half, hg_got = barrier(
-        (down_part, act_half, act_got, hg_half, hg_got)
-    )
-    up_part = scatter(up_part, 1, low, near)
+    up_part = scatter(up_part, 0, high, far)
+    down_part = plus(down_part, lax.ppermute(down_part, "rep", far))
+    up_part = plus(up_part, lax.ppermute(up_part, "rep", near))
     down_own, down_got = down_part[:, :width], swap(down_part[:, width:])
     down_part = pair(down_own[None], down_got[None], core, 0)
-    down_part = collect(down_part, [(high, far), (turn, near)], 1)
+    down_part = pair(down_part, lax.ppermute(down_part, "rep", near), turn, 1)
     down_grads = down_part.reshape(2 * half, width)
-    up_part = pair(up_part[0], swap(up_part[1]), core, 1)
-    up_grads = collect(up_part, [(low, near), (high, far)], 0)
+    up_part = pair(up_part[:cut], swap(up_part[cut:]), core, 1)
+    up_grads = pair(up_part, lax.ppermute(up_part, "rep", far), high, 0)
 
     act, hg = pair(act_half, act_got, zl, 0), pair(hg_half, hg_got, zl, 0)
 

time: 196 us -> 189 us (0.964)
  waiting for transfers between devices: 43.4 us -> 49.6 us
  starting transfers between devices: 85.2 us -> 79.4 us
  local copies, waits for them, and re-layouts: 10.2 us -> 6.56 us
  other arithmetic: 7.67 us -> 5.46 us
    ppermute x4 -> x2, starting transfers between devices: 13.2 us -> 6.42 us  [scatter(): return plus(at(bit), lax.ppermute(at(1 - bit), 'rep', pairs))]
    ppermute x4 -> x2, waiting for transfers between devices: 3.42 us -> 7.32 us  [scatter(): return plus(at(bit), lax.ppermute(at(1 - bit), 'rep', pairs))]
    all_to_all x2, waiting for transfers between devices: 11.9 us -> 14.1 us  [exchange(): return lax.all_to_all(x, axis, 0, 0, tiled=False)]
    convert_element_type x5, other arithmetic: 2.87 us -> 0.85 us  [plus(): return (a.astype(f32) + b.astype(f32)).astype(bf16)]
  transfers between devices with their start and end apart: 20 -> 18, of which waited for: 12 -> 11; matrix products, arithmetic and copies ran while one was open for 9% -> 8% of each run, Pallas kernels for 0% -> 0%
where the time goes in v10:
time: 189 us; the launch traced here: 188 us
  starting transfers between devices  79.4 us (42%)
  waiting for transfers between devices  49.6 us (26%)
  blocking collectives  35.7 us (19%)
  matrix products  9.9 us (5%)
  local copies, waits for them, and re-layouts  6.56 us (3%)
  other arithmetic  5.46 us (3%)
    ppermute x6, starting transfers between devices, swap(): return lax.ppermute(x, 'core', [(0, 1), (1, 0)])  28.3 us
    ppermute x4, starting transfers between devices, z_swap(): return lax.ppermute(x, ('zh', 'zl'), pairs)  21.5 us
    all_to_all x1, blocking collectives, exchange(): return lax.all_to_all(x, axis, 0, 0, tiled=False)  19.8 us
    all_gather x1, blocking collectives, per_device(): lax.all_gather(jnp.concatenate([act, hid_grads], 1), 'zh', axis=0, tiled=...  15.9 us
    all_to_all x2, waiting for transfers between devices, exchange(): return lax.all_to_all(x, axis, 0, 0, tiled=False)  14.1 us
    ppermute x4, waiting for transfers between devices, z_swap(): return lax.ppermute(x, ('zh', 'zl'), pairs)  12.3 us
    all_to_all x2, starting transfers between devices, exchange(): return lax.all_to_all(x, axis, 0, 0, tiled=False)  11.2 us
    ppermute x1, waiting for transfers between devices, per_device(): down_part = pair(down_part, lax.ppermute(down_part, 'rep', near), turn, 1)  10.4 us
  transfers between devices with their start and end apart: 18, of which 11 were waited for; matrix products, arithmetic and copies ran while one was open for 8% of the time, Pallas kernels for 0%

profile of v10, /device:TPU:1, one launch (start us, length us, event | category | flops | bytes accessed | tf_op | source)
XLA Modules:
  0.0 187.8 jit_solution(10671484625601641330)
XLA Ops:
  0.6 0.8 pad_maximum_fusion.7
  1.5 0.9 broadcast_in_dim.12
  2.4 7.7 %all-to-all-start = ((bf16[8,64,768]{2,1,0:T(8,128)(2,1)}), bf16[8,64,768]{2,1,0:T(8,128)(2,1)S(1)}, u32[]{:S(2)}, u32[]{:S(2)}) async-start(bf16[8,64,768]{2,1,0:T(8,128)(2,1)} %broadcast_in_dim.12), calls=%async_computation | async-start | bytes 1572864 | tf_op jit(solution)/shard_map/all_to_all | solution.py:27
  10.2 4.8 %collective-permute-start = (bf16[384,768]{1,0:T(8,128)(2,1)S(1)}, bf16[384,768]{1,0:T(8,128)(2,1)S(1)}, u32[]{:S(2)}, u32[]{:S(2)}) collective-permute-start(bf16[384,768]{1,0:T(8,128)(2,1)S(1)} %get-tuple-element.31), channel_id=1, source_target_pairs={{0,4},{4,0},{1,5},{5,1},{2,6},{6,2},{3,7},{7,3},{8,12},{12,8},{9,1... | collective-permute-start | bytes 1769480 | tf_op jit(solution)/shard_map/ppermute | solution.py:23
  15.0 0.1 constant_dynamic-slice_fusion.1
  15.2 1.9 %collective-permute-start.1 = (bf16[768,384]{1,0:T(8,128)(2,1)S(1)}, bf16[768,384]{1,0:T(8,128)(2,1)S(1)}, u32[]{:S(2)}, u32[]{:S(2)}) collective-permute-start(bf16[768,384]{1,0:T(8,128)(2,1)S(1)} %get-tuple-element.29), channel_id=1, source_target_pairs={{0,4},{4,0},{1,5},{5,1},{2,6},{6,2},{3,7},{7,3},{8,12},{12,8},{9,1... | collective-permute-start | bytes 1769480 | tf_op jit(solution)/shard_map/ppermute | solution.py:23
  17.2 1.9 collective-permute-done.1
  19.1 0.1 pad_maximum_fusion.1
  19.2 11.9 %all-to-all-done = bf16[8,64,768]{2,1,0:T(8,128)(2,1)S(1)} async-done(((bf16[8,64,768]{2,1,0:T(8,128)(2,1)}), bf16[8,64,768]{2,1,0:T(8,128)(2,1)S(1)}, u32[]{:S(2)}, u32[]{:S(2)}) %all-to-all-start) | async-done | bytes 786464 | tf_op jit(solution)/shard_map/all_to_all | solution.py:27
  31.1 5.0 %collective-permute-start.2 = (bf16[512,768]{1,0:T(8,128)(2,1)S(1)}, bf16[512,768]{1,0:T(8,128)(2,1)}, u32[]{:S(2)}, u32[]{:S(2)}) collective-permute-start(bf16[512,768]{1,0:T(8,128)(2,1)S(1)} %bitcast.40), channel_id=1, source_target_pairs={{0,4},{4,0},{1,5},{5,1},{2,6},{6,2},{3,7},{7,3},{8,12},{12,8},{9,1... | collective-permute-start | bytes 2359304 | tf_op jit(solution)/shard_map/ppermute | solution.py:23
  36.3 1.8 collective-permute-done.2
  38.1 1.2 dynamic-slice_bitcast_fusion.2
  39.5 0.5 convolution_convert_fusion.9
  40.0 0.1 copy-done.4
  40.0 0.5 convolution_convert_fusion.8
  40.6 10.6 %collective-permute-start.4 = (bf16[256,768]{1,0:T(8,128)(2,1)S(1)}, bf16[256,768]{1,0:T(8,128)(2,1)S(1)}, u32[]{:S(2)}, u32[]{:S(2)}) collective-permute-start(bf16[256,768]{1,0:T(8,128)(2,1)S(1)} %convolution_convert_fusion.8), channel_id=1, source_target_pairs={{0,56},{8,16},{16,8},{24,32},{32,24},{40,48},{48,40},{56,0},{1,57}... | collective-permute-start | bytes 1179656 | tf_op jit(solution)/shard_map/ppermute | solution.py:65
  51.2 1.9 %collective-permute-start.3 = (bf16[256,768]{1,0:T(8,128)(2,1)S(1)}, bf16[256,768]{1,0:T(8,128)(2,1)S(1)}, u32[]{:S(2)}, u32[]{:S(2)}) collective-permute-start(bf16[256,768]{1,0:T(8,128)(2,1)S(1)} %convolution_convert_fusion.9), channel_id=1, source_target_pairs={{0,8},{8,0},{16,24},{24,16},{32,40},{40,32},{48,56},{56,48},{1,9},... | collective-permute-start | bytes 1179656 | tf_op jit(solution)/shard_map/ppermute | solution.py:65
  53.1 7.2 %collective-permute-done.4 = bf16[256,768]{1,0:T(8,128)(2,1)S(1)} collective-permute-done((bf16[256,768]{1,0:T(8,128)(2,1)S(1)}, bf16[256,768]{1,0:T(8,128)(2,1)S(1)}, u32[]{:S(2)}, u32[]{:S(2)}) %collective-permute-start.4) | collective-permute-done | bytes 393248 | tf_op jit(solution)/shard_map/ppermute | solution.py:65
  60.4 0.5 add_convert_fusion.3
  60.9 2.2 %collective-permute-done.3 = bf16[256,768]{1,0:T(8,128)(2,1)S(1)} collective-permute-done((bf16[256,768]{1,0:T(8,128)(2,1)S(1)}, bf16[256,768]{1,0:T(8,128)(2,1)S(1)}, u32[]{:S(2)}, u32[]{:S(2)}) %collective-permute-start.3) | collective-permute-done | bytes 393248 | tf_op jit(solution)/shard_map/ppermute | solution.py:65
  63.1 0.5 add_convert_fusion.4
  63.6 19.8 %all_to_all.15 = bf16[4,64,1536]{2,1,0:T(8,128)(2,1)S(1)} all-to-all(bf16[4,64,1536]{2,1,0:T(8,128)(2,1)S(1)} %bitcast.39), channel_id=1, replica_groups=mesh['row'=8,'zh'=4,'zl'=2,'core'=2,'rep'=4] {'zh'}, dimensions={0} | all-to-all | bytes 1572864 | tf_op jit(solution)/shard_map/all_to_all | solution.py:27
  83.4 0.1 add_bitcast_fusion
  83.5 0.1 multiply_convert_fusion
  83.7 15.9 %all_gather.3 = bf16[256,1536]{1,0:T(8,128)(2,1)S(1)} all-gather(bf16[64,1536]{1,0:T(8,128)(2,1)S(1)} %pad_maximum_fusion.6), channel_id=1, replica_groups=mesh['row'=8,'zh'=4,'zl'=2,'core'=2,'rep'=4] {'zh'}, dimensions={0}, use_global_device_ids=true | all-gather | bytes 983040 | tf_op jit(solution)/shard_map/all_gather | solution.py:112
  99.6 0.9 fusion.49
  100.5 6.4 %collective-permute-start.5 = (bf16[256,768]{1,0:T(8,128)(2,1)}, bf16[256,768]{1,0:T(8,128)(2,1)}, u32[]{:S(2)}, u32[]{:S(2)}) collective-permute-start(bf16[256,768]{1,0:T(8,128)(2,1)} %get-tuple-element.23), channel_id=1, source_target_pairs={{0,8},{8,0},{16,24},{24,16},{32,40},{40,32},{48,56},{56,48},{1,9},... | collective-permute-start | bytes 1179656 | tf_op jit(solution)/shard_map/ppermute | solution.py:65
  107.0 2.5 %collective-permute-start.7 = (bf16[256,768]{1,0:T(8,128)(2,1)}, bf16[256,768]{1,0:T(8,128)(2,1)S(1)}, u32[]{:S(2)}, u32[]{:S(2)}) collective-permute-start(bf16[256,768]{1,0:T(8,128)(2,1)} %get-tuple-element.25), channel_id=1, source_target_pairs={{0,56},{8,16},{16,8},{24,32},{32,24},{40,48},{48,40},{56,0},{1,57}... | collective-permute-start | bytes 1179656 | tf_op jit(solution)/shard_map/ppermute | solution.py:65
  109.5 2.9 %collective-permute-done.5 = bf16[256,768]{1,0:T(8,128)(2,1)} collective-permute-done((bf16[256,768]{1,0:T(8,128)(2,1)}, bf16[256,768]{1,0:T(8,128)(2,1)}, u32[]{:S(2)}, u32[]{:S(2)}) %collective-permute-start.5) | collective-permute-done | bytes 393248 | tf_op jit(solution)/shard_map/ppermute | solution.py:65
  112.4 2.0 %convolution_convert_fusion.1 = bf16[768,768]{1,0:T(8,128)(2,1)S(1)} fusion(bf16[256,768]{1,0:T(8,128)(2,1)} %collective-permute-done.5, bf16[256,768]{1,0:T(8,128)(2,1)} %get-tuple-element.23, bf16[256,384]{1,0:T(8,128)(2,1)} %copy-done.4, bf16[256,384]{1,0:T(8,128)(2,1)} %copy-done.3, bf16[256,768]{1,0:T(8,128)(2,1)S(1)} %pad_maximum_fusion.5), kind=kOutput, calls=%fused_computation.2 | convolution fusion | flops 608501760 | bytes 2752512 | tf_op jit(solution)/shard_map/dot_general | solution.py:17
  114.5 3.1 %collective-permute-start.6 = (bf16[384,768]{1,0:T(8,128)(2,1)S(1)}, bf16[384,768]{1,0:T(8,128)(2,1)S(1)}, u32[]{:S(2)}, u32[]{:S(2)}) collective-permute-start(bf16[384,768]{1,0:T(8,128)(2,1)S(1)} %dynamic-slice_bitcast_fusion.1), channel_id=1, source_target_pairs={{0,1},{1,0},{2,3},{3,2},{4,5},{5,4},{6,7},{7,6},{8,9},{9,8},{10,11... | collective-permute-start | bytes 1769480 | tf_op jit(solution)/shard_map/ppermute | solution.py:125
  117.7 0.2 fusion.48
  118.0 0.7 copy-done.2
  118.7 1.1 convolution_convert_fusion
  119.9 3.3 %collective-permute-start.9 = (bf16[384,768]{1,0:T(8,128)(2,1)S(1)}, bf16[384,768]{1,0:T(8,128)(2,1)S(1)}, u32[]{:S(2)}, u32[]{:S(2)}) collective-permute-start(bf16[384,768]{1,0:T(8,128)(2,1)S(1)} %dynamic-slice_bitcast_fusion), channel_id=1, source_target_pairs={{0,3},{1,2},{2,1},{3,0},{4,7},{5,6},{6,5},{7,4},{8,11},{9,10},{10,... | collective-permute-start | bytes 1769480 | tf_op jit(solution)/shard_map/ppermute | solution.py:125
  123.2 2.0 %collective-permute-done.6 = bf16[384,768]{1,0:T(8,128)(2,1)S(1)} collective-permute-done((bf16[384,768]{1,0:T(8,128)(2,1)S(1)}, bf16[384,768]{1,0:T(8,128)(2,1)S(1)}, u32[]{:S(2)}, u32[]{:S(2)}) %collective-permute-start.6) | collective-permute-done | bytes 589856 | tf_op jit(solution)/shard_map/ppermute | solution.py:125
  125.1 0.2 fusion.3
  125.3 0.5 convolution_convert_fusion.2
  125.8 0.5 convolution_convert_fusion.4
  126.3 5.4 %collective-permute-done.9 = bf16[384,768]{1,0:T(8,128)(2,1)S(1)} collective-permute-done((bf16[384,768]{1,0:T(8,128)(2,1)S(1)}, bf16[384,768]{1,0:T(8,128)(2,1)S(1)}, u32[]{:S(2)}, u32[]{:S(2)}) %collective-permute-start.9) | collective-permute-done | bytes 589856 | tf_op jit(solution)/shard_map/ppermute | solution.py:125
  131.7 0.2 fusion.2
  131.9 1.9 %collective-permute-start.10 = (bf16[384,768]{1,0:T(8,128)(2,1)S(1)}, bf16[384,768]{1,0:T(8,128)(2,1)S(1)}, u32[]{:S(2)}, u32[]{:S(2)}) collective-permute-start(bf16[384,768]{1,0:T(8,128)(2,1)S(1)} %fusion.2), channel_id=1, source_target_pairs={{0,1},{1,0},{2,3},{3,2},{4,5},{5,4},{6,7},{7,6},{8,9},{9,8},{10,11... | collective-permute-start | bytes 1769480 | tf_op jit(solution)/shard_map/ppermute | solution.py:138
  133.8 3.8 %collective-permute-start.13 = (bf16[384,768]{1,0:T(8,128)(2,1)S(1)}, bf16[384,768]{1,0:T(8,128)(2,1)S(1)}, u32[]{:S(2)}, u32[]{:S(2)}) collective-permute-start(bf16[384,768]{1,0:T(8,128)(2,1)S(1)} %fusion.3), channel_id=1, source_target_pairs={{0,3},{1,2},{2,1},{3,0},{4,7},{5,6},{6,5},{7,4},{8,11},{9,10},{10,... | collective-permute-start | bytes 1769480 | tf_op jit(solution)/shard_map/ppermute | solution.py:137
  137.6 1.9 convolution_convert_fusion.3
  139.5 1.9 %convolution_convert_fusion.5 = bf16[512,384]{0,1:T(8,128)(2,1)S(1)} fusion(bf16[768,768]{1,0:T(8,128)(2,1)S(1)} %pad_maximum_fusion.1, bf16[256,768]{1,0:T(8,128)(2,1)} %collective-permute-done.5, bf16[256,768]{1,0:T(8,128)(2,1)} %get-tuple-element.23, pred[]{:T(512)S(6)} %eq.16), kind=kOutput, calls=%fused_computation.6 | convolution fusion | flops 305725440 | bytes 1769473 | tf_op jit(solution)/shard_map/dot_general | solution.py:17
  141.5 12.2 %collective-permute-start.8 = (bf16[512,768]{0,1:T(8,128)(2,1)S(1)}, bf16[512,768]{0,1:T(8,128)(2,1)S(1)}, u32[]{:S(2)}, u32[]{:S(2)}) collective-permute-start(bf16[512,768]{0,1:T(8,128)(2,1)S(1)} %pad_maximum_fusion.3), channel_id=1, source_target_pairs={{0,4},{4,0},{1,5},{5,1},{2,6},{6,2},{3,7},{7,3},{8,12},{12,8},{9,1... | collective-permute-start | bytes 2359304 | tf_op jit(solution)/shard_map/ppermute | solution.py:23
  153.7 0.1 add_convert_fusion.2
  153.9 1.9 %collective-permute-start.11 = (bf16[192,768]{1,0:T(8,128)(2,1)S(1)}, bf16[192,768]{1,0:T(8,128)(2,1)S(1)}, u32[]{:S(2)}, u32[]{:S(2)}) collective-permute-start(bf16[192,768]{1,0:T(8,128)(2,1)S(1)} %get-tuple-element.45), channel_id=1, source_target_pairs={{0,4},{4,0},{1,5},{5,1},{2,6},{6,2},{3,7},{7,3},{8,12},{12,8},{9,1... | collective-permute-start | bytes 884744 | tf_op jit(solution)/shard_map/ppermute | solution.py:23
  155.8 0.2 add_convert_fusion.1
  156.0 2.4 %collective-permute-start.14 = (bf16[384,384]{1,0:T(8,128)(2,1)S(1)}, bf16[384,384]{1,0:T(8,128)(2,1)S(1)}, u32[]{:S(2)}, u32[]{:S(2)}) collective-permute-start(bf16[384,384]{1,0:T(8,128)(2,1)S(1)} %get-tuple-element.43), channel_id=1, source_target_pairs={{0,4},{4,0},{1,5},{5,1},{2,6},{6,2},{3,7},{7,3},{8,12},{12,8},{9,1... | collective-permute-start | bytes 884744 | tf_op jit(solution)/shard_map/ppermute | solution.py:23
  158.5 0.2 add_convert_fusion
  158.7 1.2 copy.9
  159.9 3.5 %all-to-all-start.2 = ((bf16[8,64,768]{2,1,0:T(8,128)(2,1)}), bf16[8,64,768]{2,1,0:T(8,128)(2,1)S(1)}, u32[]{:S(2)}, u32[]{:S(2)}) async-start(bf16[8,64,768]{2,1,0:T(8,128)(2,1)} %bitcast.12), calls=%async_computation.2 | async-start | bytes 1572864 | tf_op jit(solution)/shard_map/all_to_all | solution.py:27
  163.4 0.1 maximum_select_fusion.5
  163.6 1.9 %collective-permute-start.15 = (bf16[2,384,384]{2,1,0:T(8,128)(2,1)S(1)}, bf16[2,384,384]{2,1,0:T(8,128)(2,1)S(1)}, u32[]{:S(2)}, u32[]{:S(2)}) collective-permute-start(bf16[2,384,384]{2,1,0:T(8,128)(2,1)S(1)} %maximum_select_fusion.5), channel_id=1, source_target_pairs={{0,1},{1,0},{2,3},{3,2},{4,5},{5,4},{6,7},{7,6},{8,9},{9,8},{10,11... | collective-permute-start | bytes 1769480 | tf_op jit(solution)/shard_map/ppermute | solution.py:141
  165.5 0.1 maximum_select_fusion.4
  165.6 4.3 %collective-permute-start.12 = (bf16[192,1536]{1,0:T(8,128)(2,1)S(1)}, bf16[192,1536]{1,0:T(8,128)(2,1)S(1)}, u32[]{:S(2)}, u32[]{:S(2)}) collective-permute-start(bf16[192,1536]{1,0:T(8,128)(2,1)S(1)} %maximum_select_fusion.4), channel_id=1, source_target_pairs={{0,3},{1,2},{2,1},{3,0},{4,7},{5,6},{6,5},{7,4},{8,11},{9,10},{10,... | collective-permute-start | bytes 1769480 | tf_op jit(solution)/shard_map/ppermute | solution.py:144
  170.0 10.4 %collective-permute-done.15 = bf16[2,384,384]{2,1,0:T(8,128)(2,1)S(1)} collective-permute-done((bf16[2,384,384]{2,1,0:T(8,128)(2,1)S(1)}, bf16[2,384,384]{2,1,0:T(8,128)(2,1)S(1)}, u32[]{:S(2)}, u32[]{:S(2)}) %collective-permute-start.15) | collective-permute-done | bytes 589856 | tf_op jit(solution)/shard_map/ppermute | solution.py:141
  180.4 1.4 maximum_select_fusion.1
  181.8 1.7 collective-permute-done.12
  183.5 1.4 maximum_select_fusion
  184.8 2.2 %all-to-all-done.2 = bf16[8,64,768]{2,1,0:T(8,128)(2,1)S(1)} async-done(((bf16[8,64,768]{2,1,0:T(8,128)(2,1)}), bf16[8,64,768]{2,1,0:T(8,128)(2,1)S(1)}, u32[]{:S(2)}, u32[]{:S(2)}) %all-to-all-start.2) | async-done | bytes 786464 | tf_op jit(solution)/shard_map/all_to_all | solution.py:27
  187.0 0.1 fusion.39
  187.1 0.6 fusion.55
  (30 shorter events, 0.9 us)
Async XLA Ops:
  1.5 8.6 %copy-start = (bf16[384,1536]{1,0:T(8,128)(2,1)S(1)}, bf16[384,1536]{1,0:T(8,128)(2,1)}, u32[]{:S(2)}) copy-start(bf16[384,1536]{1,0:T(8,128)(2,1)} %param.5) | copy-start | bytes 3538948
  2.4 28.7 %all-to-all-start = ((bf16[8,64,768]{2,1,0:T(8,128)(2,1)}), bf16[8,64,768]{2,1,0:T(8,128)(2,1)S(1)}, u32[]{:S(2)}, u32[]{:S(2)}) async-start(bf16[8,64,768]{2,1,0:T(8,128)(2,1)} %broadcast_in_dim.12), calls=%async_computation | async-start | bytes 1572864 | tf_op jit(solution)/shard_map/all_to_all | solution.py:27
  10.1 4.9 %copy-start.1 = (bf16[1536,384]{1,0:T(8,128)(2,1)S(1)}, bf16[1536,384]{1,0:T(8,128)(2,1)}, u32[]{:S(2)}) copy-start(bf16[1536,384]{1,0:T(8,128)(2,1)} %param.6) | copy-start | bytes 3538948
  10.2 6.9 %collective-permute-start = (bf16[384,768]{1,0:T(8,128)(2,1)S(1)}, bf16[384,768]{1,0:T(8,128)(2,1)S(1)}, u32[]{:S(2)}, u32[]{:S(2)}) collective-permute-start(bf16[384,768]{1,0:T(8,128)(2,1)S(1)} %get-tuple-element.31), channel_id=1, source_target_pairs={{0,4},{4,0},{1,5},{5,1},{2,6},{6,2},{3,7},{7,3},{8,12},{12,8},{9,1... | collective-permute-start | bytes 1769480 | tf_op jit(solution)/shard_map/ppermute | solution.py:23
  15.2 3.9 %collective-permute-start.1 = (bf16[768,384]{1,0:T(8,128)(2,1)S(1)}, bf16[768,384]{1,0:T(8,128)(2,1)S(1)}, u32[]{:S(2)}, u32[]{:S(2)}) collective-permute-start(bf16[768,384]{1,0:T(8,128)(2,1)S(1)} %get-tuple-element.29), channel_id=1, source_target_pairs={{0,4},{4,0},{1,5},{5,1},{2,6},{6,2},{3,7},{7,3},{8,12},{12,8},{9,1... | collective-permute-start | bytes 1769480 | tf_op jit(solution)/shard_map/ppermute | solution.py:23
  31.1 7.0 %collective-permute-start.2 = (bf16[512,768]{1,0:T(8,128)(2,1)S(1)}, bf16[512,768]{1,0:T(8,128)(2,1)}, u32[]{:S(2)}, u32[]{:S(2)}) collective-permute-start(bf16[512,768]{1,0:T(8,128)(2,1)S(1)} %bitcast.40), channel_id=1, source_target_pairs={{0,4},{4,0},{1,5},{5,1},{2,6},{6,2},{3,7},{7,3},{8,12},{12,8},{9,1... | collective-permute-start | bytes 2359304 | tf_op jit(solution)/shard_map/ppermute | solution.py:23
  36.2 3.7 %copy-start.3 = (bf16[256,384]{1,0:T(8,128)(2,1)}, bf16[256,384]{1,0:T(8,128)(2,1)S(1)}, u32[]{:S(2)}) copy-start(bf16[256,384]{1,0:T(8,128)(2,1)S(1)} %get-tuple-element.61) | copy-start | bytes 589828
  39.4 0.7 copy-start.4
  40.6 19.8 %collective-permute-start.4 = (bf16[256,768]{1,0:T(8,128)(2,1)S(1)}, bf16[256,768]{1,0:T(8,128)(2,1)S(1)}, u32[]{:S(2)}, u32[]{:S(2)}) collective-permute-start(bf16[256,768]{1,0:T(8,128)(2,1)S(1)} %convolution_convert_fusion.8), channel_id=1, source_target_pairs={{0,56},{8,16},{16,8},{24,32},{32,24},{40,48},{48,40},{56,0},{1,57}... | collective-permute-start | bytes 1179656 | tf_op jit(solution)/shard_map/ppermute | solution.py:65
  51.2 11.9 %collective-permute-start.3 = (bf16[256,768]{1,0:T(8,128)(2,1)S(1)}, bf16[256,768]{1,0:T(8,128)(2,1)S(1)}, u32[]{:S(2)}, u32[]{:S(2)}) collective-permute-start(bf16[256,768]{1,0:T(8,128)(2,1)S(1)} %convolution_convert_fusion.9), channel_id=1, source_target_pairs={{0,8},{8,0},{16,24},{24,16},{32,40},{40,32},{48,56},{56,48},{1,9},... | collective-permute-start | bytes 1179656 | tf_op jit(solution)/shard_map/ppermute | solution.py:65
  100.5 11.9 %collective-permute-start.5 = (bf16[256,768]{1,0:T(8,128)(2,1)}, bf16[256,768]{1,0:T(8,128)(2,1)}, u32[]{:S(2)}, u32[]{:S(2)}) collective-permute-start(bf16[256,768]{1,0:T(8,128)(2,1)} %get-tuple-element.23), channel_id=1, source_target_pairs={{0,8},{8,0},{16,24},{24,16},{32,40},{40,32},{48,56},{56,48},{1,9},... | collective-permute-start | bytes 1179656 | tf_op jit(solution)/shard_map/ppermute | solution.py:65
  107.0 11.0 %collective-permute-start.7 = (bf16[256,768]{1,0:T(8,128)(2,1)}, bf16[256,768]{1,0:T(8,128)(2,1)S(1)}, u32[]{:S(2)}, u32[]{:S(2)}) collective-permute-start(bf16[256,768]{1,0:T(8,128)(2,1)} %get-tuple-element.25), channel_id=1, source_target_pairs={{0,56},{8,16},{16,8},{24,32},{32,24},{40,48},{48,40},{56,0},{1,57}... | collective-permute-start | bytes 1179656 | tf_op jit(solution)/shard_map/ppermute | solution.py:65
  114.5 10.6 %collective-permute-start.6 = (bf16[384,768]{1,0:T(8,128)(2,1)S(1)}, bf16[384,768]{1,0:T(8,128)(2,1)S(1)}, u32[]{:S(2)}, u32[]{:S(2)}) collective-permute-start(bf16[384,768]{1,0:T(8,128)(2,1)S(1)} %dynamic-slice_bitcast_fusion.1), channel_id=1, source_target_pairs={{0,1},{1,0},{2,3},{3,2},{4,5},{5,4},{6,7},{7,6},{8,9},{9,8},{10,11... | collective-permute-start | bytes 1769480 | tf_op jit(solution)/shard_map/ppermute | solution.py:125
  117.7 1.0 copy-start.2
  119.9 11.8 %collective-permute-start.9 = (bf16[384,768]{1,0:T(8,128)(2,1)S(1)}, bf16[384,768]{1,0:T(8,128)(2,1)S(1)}, u32[]{:S(2)}, u32[]{:S(2)}) collective-permute-start(bf16[384,768]{1,0:T(8,128)(2,1)S(1)} %dynamic-slice_bitcast_fusion), channel_id=1, source_target_pairs={{0,3},{1,2},{2,1},{3,0},{4,7},{5,6},{6,5},{7,4},{8,11},{9,10},{10,... | collective-permute-start | bytes 1769480 | tf_op jit(solution)/shard_map/ppermute | solution.py:125
  131.9 21.8 %collective-permute-start.10 = (bf16[384,768]{1,0:T(8,128)(2,1)S(1)}, bf16[384,768]{1,0:T(8,128)(2,1)S(1)}, u32[]{:S(2)}, u32[]{:S(2)}) collective-permute-start(bf16[384,768]{1,0:T(8,128)(2,1)S(1)} %fusion.2), channel_id=1, source_target_pairs={{0,1},{1,0},{2,3},{3,2},{4,5},{5,4},{6,7},{7,6},{8,9},{9,8},{10,11... | collective-permute-start | bytes 1769480 | tf_op jit(solution)/shard_map/ppermute | solution.py:138
  133.8 22.0 %collective-permute-start.13 = (bf16[384,768]{1,0:T(8,128)(2,1)S(1)}, bf16[384,768]{1,0:T(8,128)(2,1)S(1)}, u32[]{:S(2)}, u32[]{:S(2)}) collective-permute-start(bf16[384,768]{1,0:T(8,128)(2,1)S(1)} %fusion.3), channel_id=1, source_target_pairs={{0,3},{1,2},{2,1},{3,0},{4,7},{5,6},{6,5},{7,4},{8,11},{9,10},{10,... | collective-permute-start | bytes 1769480 | tf_op jit(solution)/shard_map/ppermute | solution.py:137
  141.5 17.0 %collective-permute-start.8 = (bf16[512,768]{0,1:T(8,128)(2,1)S(1)}, bf16[512,768]{0,1:T(8,128)(2,1)S(1)}, u32[]{:S(2)}, u32[]{:S(2)}) collective-permute-start(bf16[512,768]{0,1:T(8,128)(2,1)S(1)} %pad_maximum_fusion.3), channel_id=1, source_target_pairs={{0,4},{4,0},{1,5},{5,1},{2,6},{6,2},{3,7},{7,3},{8,12},{12,8},{9,1... | collective-permute-start | bytes 2359304 | tf_op jit(solution)/shard_map/ppermute | solution.py:23
  153.9 11.6 %collective-permute-start.11 = (bf16[192,768]{1,0:T(8,128)(2,1)S(1)}, bf16[192,768]{1,0:T(8,128)(2,1)S(1)}, u32[]{:S(2)}, u32[]{:S(2)}) collective-permute-start(bf16[192,768]{1,0:T(8,128)(2,1)S(1)} %get-tuple-element.45), channel_id=1, source_target_pairs={{0,4},{4,0},{1,5},{5,1},{2,6},{6,2},{3,7},{7,3},{8,12},{12,8},{9,1... | collective-permute-start | bytes 884744 | tf_op jit(solution)/shard_map/ppermute | solution.py:23
  156.0 7.4 %collective-permute-start.14 = (bf16[384,384]{1,0:T(8,128)(2,1)S(1)}, bf16[384,384]{1,0:T(8,128)(2,1)S(1)}, u32[]{:S(2)}, u32[]{:S(2)}) collective-permute-start(bf16[384,384]{1,0:T(8,128)(2,1)S(1)} %get-tuple-element.43), channel_id=1, source_target_pairs={{0,4},{4,0},{1,5},{5,1},{2,6},{6,2},{3,7},{7,3},{8,12},{12,8},{9,1... | collective-permute-start | bytes 884744 | tf_op jit(solution)/shard_map/ppermute | solution.py:23
  159.9 27.1 %all-to-all-start.2 = ((bf16[8,64,768]{2,1,0:T(8,128)(2,1)}), bf16[8,64,768]{2,1,0:T(8,128)(2,1)S(1)}, u32[]{:S(2)}, u32[]{:S(2)}) async-start(bf16[8,64,768]{2,1,0:T(8,128)(2,1)} %bitcast.12), calls=%async_computation.2 | async-start | bytes 1572864 | tf_op jit(solution)/shard_map/all_to_all | solution.py:27
  163.6 16.8 %collective-permute-start.15 = (bf16[2,384,384]{2,1,0:T(8,128)(2,1)S(1)}, bf16[2,384,384]{2,1,0:T(8,128)(2,1)S(1)}, u32[]{:S(2)}, u32[]{:S(2)}) collective-permute-start(bf16[2,384,384]{2,1,0:T(8,128)(2,1)S(1)} %maximum_select_fusion.5), channel_id=1, source_target_pairs={{0,1},{1,0},{2,3},{3,2},{4,5},{5,4},{6,7},{7,6},{8,9},{9,8},{10,11... | collective-permute-start | bytes 1769480 | tf_op jit(solution)/shard_map/ppermute | solution.py:141
  165.6 17.8 %collective-permute-start.12 = (bf16[192,1536]{1,0:T(8,128)(2,1)S(1)}, bf16[192,1536]{1,0:T(8,128)(2,1)S(1)}, u32[]{:S(2)}, u32[]{:S(2)}) collective-permute-start(bf16[192,1536]{1,0:T(8,128)(2,1)S(1)} %maximum_select_fusion.4), channel_id=1, source_target_pairs={{0,3},{1,2},{2,1},{3,0},{4,7},{5,6},{6,5},{7,4},{8,11},{9,10},{10,... | collective-permute-start | bytes 1769480 | tf_op jit(solution)/shard_map/ppermute | solution.py:144

commit v11 on v10

--- a/solution.py
+++ b/solution.py
@@ -126,14 +126,26 @@
 
     turn, high = (rep + 1) // 2 % 2, rep // 2
     down_part = dot(act, og, (0, 0)).reshape(2, half // 2, 2 * width)
+    cut = width // 2
+    order = [tok[:, i * cut : (i + 1) * cut] for i in (0, 2, 1, 3)]
+    up_part = dot(jnp.concatenate(order, 1), hg, (0, 0)).reshape(2, width, half)
     down_part = scatter(down_part, 0, turn, near)
     down_part, act_half, act_got, hg_half, hg_got = barrier(
         (down_part, act_half, act_got, hg_half, hg_got)
     )
-    cut = width // 2
-    order = [tok[:, i * cut : (i + 1) * cut] for i in (0, 2, 1, 3)]
-    up_part = dot(jnp.concatenate(order, 1), hg, (0, 0)).reshape(2, width, half)
-    up_part = scatter(up_part, 0, high, far)
+    act, hg = pair(act_half, act_got, zl, 0), pair(hg_half, hg_got, zl, 0)
+
+    def output(columns):
+        block = dot(act, down[:, columns], (1, 0))
+        token = dot(hg, up[columns], (1, 1))
+        return jnp.concatenate([block, token], 1)
+
+    send = output(slice(width, None))
+    up_keep, up_got = pick(up_part, high), lax.ppermute(
+        pick(up_part, 1 - high), "rep", far
+    )
+    up_got, send, keep = barrier((up_got, send, output(slice(width))))
+    up_part = plus(up_keep, up_got)
     down_part = plus(down_part, lax.ppermute(down_part, "rep", far))
     up_part = plus(up_part, lax.ppermute(up_part, "rep", near))
     down_own, down_got = down_part[:, :width], swap(down_part[:, width:])
@@ -143,15 +155,7 @@
     up_part = pair(up_part[:cut], swap(up_part[cut:]), core, 1)
     up_grads = pair(up_part, lax.ppermute(up_part, "rep", far), high, 0)
 
-    act, hg = pair(act_half, act_got, zl, 0), pair(hg_half, hg_got, zl, 0)
-
-    def output(columns):
-        block = dot(act, down[:, columns], (1, 0))
-        token = dot(hg, up[columns], (1, 1))
-        return jnp.concatenate([block, token], 1)
-
-    send = output(slice(width, None))
-    out = plus(output(slice(width)), swap(send))
+    out = plus(keep, swap(send))
     out = total_of(exchange(out.reshape(n_row, rows, 2 * width), "row")).astype(bf16)
     return (out[:, :width], out[:, width:], up_grads, down_grads)
 

time: 189 us -> 194 us (1.026)
  blocking collectives: 35.7 us -> 41.7 us
    all_to_all x1, blocking collectives: 19.8 us -> 24.8 us  [exchange(): return lax.all_to_all(x, axis, 0, 0, tiled=False)]
    ppermute x0 -> x1, starting transfers between devices: none -> 3.99 us  [per_device(): lax.ppermute(pick(up_part, 1 - high), 'rep', far)]
    ppermute x4, starting transfers between devices: 21.5 us -> 18.6 us  [z_swap(): return lax.ppermute(x, ('zh', 'zl'), pairs)]
    ppermute x2 -> x1, waiting for transfers between devices: 7.32 us -> 4.96 us  [scatter(): return plus(at(bit), lax.ppermute(at(1 - bit), 'rep', pairs))]
    ppermute x2 -> x1, starting transfers between devices: 6.42 us -> 5.06 us  [scatter(): return plus(at(bit), lax.ppermute(at(1 - bit), 'rep', pairs))]
where the time goes in v11:
time: 194 us; the launch traced here: 193 us
  starting transfers between devices  77.8 us (40%)
  waiting for transfers between devices  50.2 us (26%)
  blocking collectives  41.7 us (21%)
  matrix products  9.93 us (5%)
  local copies, waits for them, and re-layouts  6.47 us (3%)
  other arithmetic  5.5 us (3%)
    ppermute x6, starting transfers between devices, swap(): return lax.ppermute(x, 'core', [(0, 1), (1, 0)])  27.3 us
    all_to_all x1, blocking collectives, exchange(): return lax.all_to_all(x, axis, 0, 0, tiled=False)  24.8 us
    ppermute x4, starting transfers between devices, z_swap(): return lax.ppermute(x, ('zh', 'zl'), pairs)  18.6 us
    all_gather x1, blocking collectives, per_device(): lax.all_gather(jnp.concatenate([act, hid_grads], 1), 'zh', axis=0, tiled=...  16.9 us
    all_to_all x2, waiting for transfers between devices, exchange(): return lax.all_to_all(x, axis, 0, 0, tiled=False)  13.6 us
    ppermute x4, waiting for transfers between devices, z_swap(): return lax.ppermute(x, ('zh', 'zl'), pairs)  12.9 us
    ppermute x1, waiting for transfers between devices, per_device(): down_part = pair(down_part, lax.ppermute(down_part, 'rep', near), turn, 1)  11.6 us
    all_to_all x2, starting transfers between devices, exchange(): return lax.all_to_all(x, axis, 0, 0, tiled=False)  11.2 us
  transfers between devices with their start and end apart: 18, of which 11 were waited for; matrix products, arithmetic and copies ran while one was open for 8% of the time, Pallas kernels for 0%

profile of v11, /device:TPU:1, one launch (start us, length us, event | category | flops | bytes accessed | tf_op | source)
XLA Modules:
  0.0 192.9 jit_solution(10580466994606386432)
XLA Ops:
  0.6 0.8 pad_maximum_fusion.8
  1.5 0.9 broadcast_in_dim.12
  2.4 7.7 %all-to-all-start = ((bf16[8,64,768]{2,1,0:T(8,128)(2,1)}), bf16[8,64,768]{2,1,0:T(8,128)(2,1)S(1)}, u32[]{:S(2)}, u32[]{:S(2)}) async-start(bf16[8,64,768]{2,1,0:T(8,128)(2,1)} %broadcast_in_dim.12), calls=%async_computation | async-start | bytes 1572864 | tf_op jit(solution)/shard_map/all_to_all | solution.py:27
  10.1 0.1 constant_dynamic-slice_fusion.1
  10.2 4.8 %collective-permute-start.1 = (bf16[768,384]{1,0:T(8,128)(2,1)S(1)}, bf16[768,384]{1,0:T(8,128)(2,1)S(1)}, u32[]{:S(2)}, u32[]{:S(2)}) collective-permute-start(bf16[768,384]{1,0:T(8,128)(2,1)S(1)} %get-tuple-element.35), channel_id=1, source_target_pairs={{0,4},{4,0},{1,5},{5,1},{2,6},{6,2},{3,7},{7,3},{8,12},{12,8},{9,1... | collective-permute-start | bytes 1769480 | tf_op jit(solution)/shard_map/ppermute | solution.py:23
  15.1 0.1 constant_dynamic-slice_fusion.3
  15.2 1.9 collective-permute-start
  17.1 0.1 pad_maximum_fusion.1
  17.2 1.9 collective-permute-done
  19.1 11.9 %all-to-all-done = bf16[8,64,768]{2,1,0:T(8,128)(2,1)S(1)} async-done(((bf16[8,64,768]{2,1,0:T(8,128)(2,1)}), bf16[8,64,768]{2,1,0:T(8,128)(2,1)S(1)}, u32[]{:S(2)}, u32[]{:S(2)}) %all-to-all-start) | async-done | bytes 786464 | tf_op jit(solution)/shard_map/all_to_all | solution.py:27
  31.1 5.0 %collective-permute-start.2 = (bf16[512,768]{1,0:T(8,128)(2,1)S(1)}, bf16[512,768]{1,0:T(8,128)(2,1)}, u32[]{:S(2)}, u32[]{:S(2)}) collective-permute-start(bf16[512,768]{1,0:T(8,128)(2,1)S(1)} %bitcast.40), channel_id=1, source_target_pairs={{0,4},{4,0},{1,5},{5,1},{2,6},{6,2},{3,7},{7,3},{8,12},{12,8},{9,1... | collective-permute-start | bytes 2359304 | tf_op jit(solution)/shard_map/ppermute | solution.py:23
  36.3 1.8 collective-permute-done.2
  38.1 1.2 dynamic-slice_bitcast_fusion.2
  39.5 0.5 convolution_convert_fusion.8
  40.0 0.5 convolution_convert_fusion.9
  40.5 4.0 %collective-permute-start.3 = (bf16[256,768]{1,0:T(8,128)(2,1)S(1)}, bf16[256,768]{1,0:T(8,128)(2,1)S(1)}, u32[]{:S(2)}, u32[]{:S(2)}) collective-permute-start(bf16[256,768]{1,0:T(8,128)(2,1)S(1)} %convolution_convert_fusion.9), channel_id=1, source_target_pairs={{0,8},{8,0},{16,24},{24,16},{32,40},{40,32},{48,56},{56,48},{1,9},... | collective-permute-start | bytes 1179656 | tf_op jit(solution)/shard_map/ppermute | solution.py:65
  44.4 8.8 %collective-permute-start.4 = (bf16[256,768]{1,0:T(8,128)(2,1)S(1)}, bf16[256,768]{1,0:T(8,128)(2,1)S(1)}, u32[]{:S(2)}, u32[]{:S(2)}) collective-permute-start(bf16[256,768]{1,0:T(8,128)(2,1)S(1)} %convolution_convert_fusion.8), channel_id=1, source_target_pairs={{0,56},{8,16},{16,8},{24,32},{32,24},{40,48},{48,40},{56,0},{1,57}... | collective-permute-start | bytes 1179656 | tf_op jit(solution)/shard_map/ppermute | solution.py:65
  53.3 0.3 collective-permute-done.3
  53.6 0.5 add_convert_fusion.4
  54.1 8.1 %collective-permute-done.4 = bf16[256,768]{1,0:T(8,128)(2,1)S(1)} collective-permute-done((bf16[256,768]{1,0:T(8,128)(2,1)S(1)}, bf16[256,768]{1,0:T(8,128)(2,1)S(1)}, u32[]{:S(2)}, u32[]{:S(2)}) %collective-permute-start.4) | collective-permute-done | bytes 393248 | tf_op jit(solution)/shard_map/ppermute | solution.py:65
  62.1 0.5 add_convert_fusion.3
  62.7 24.8 %all_to_all.15 = bf16[4,64,1536]{2,1,0:T(8,128)(2,1)S(1)} all-to-all(bf16[4,64,1536]{2,1,0:T(8,128)(2,1)S(1)} %bitcast.39), channel_id=1, replica_groups=mesh['row'=8,'zh'=4,'zl'=2,'core'=2,'rep'=4] {'zh'}, dimensions={0} | all-to-all | bytes 1572864 | tf_op jit(solution)/shard_map/all_to_all | solution.py:27
  87.6 0.1 add_bitcast_fusion
  87.6 0.1 multiply_convert_fusion
  87.8 16.9 %all_gather.3 = bf16[256,1536]{1,0:T(8,128)(2,1)S(1)} all-gather(bf16[64,1536]{1,0:T(8,128)(2,1)S(1)} %pad_maximum_fusion.7), channel_id=1, replica_groups=mesh['row'=8,'zh'=4,'zl'=2,'core'=2,'rep'=4] {'zh'}, dimensions={0}, use_global_device_ids=true | all-gather | bytes 983040 | tf_op jit(solution)/shard_map/all_gather | solution.py:112
  104.7 0.9 fusion.48
  105.7 1.9 collective-permute-start.7
  107.6 3.9 %collective-permute-start.5 = (bf16[256,768]{1,0:T(8,128)(2,1)}, bf16[256,768]{1,0:T(8,128)(2,1)S(1)}, u32[]{:S(2)}, u32[]{:S(2)}) collective-permute-start(bf16[256,768]{1,0:T(8,128)(2,1)} %get-tuple-element.28), channel_id=1, source_target_pairs={{0,56},{8,16},{16,8},{24,32},{32,24},{40,48},{48,40},{56,0},{1,57}... | collective-permute-start | bytes 1179656 | tf_op jit(solution)/shard_map/ppermute | solution.py:65
  111.5 4.6 %collective-permute-done.7 = bf16[256,768]{1,0:T(8,128)(2,1)} collective-permute-done((bf16[256,768]{1,0:T(8,128)(2,1)}, bf16[256,768]{1,0:T(8,128)(2,1)}, u32[]{:S(2)}, u32[]{:S(2)}) %collective-permute-start.7) | collective-permute-done | bytes 393248 | tf_op jit(solution)/shard_map/ppermute | solution.py:65
  116.1 2.0 %convolution_convert_fusion = bf16[768,768]{1,0:T(8,128)(2,1)S(1)} fusion(bf16[256,768]{1,0:T(8,128)(2,1)} %collective-permute-done.7, bf16[256,768]{1,0:T(8,128)(2,1)} %get-tuple-element.26, bf16[256,384]{1,0:T(8,128)(2,1)} %copy-done.4, bf16[256,384]{1,0:T(8,128)(2,1)} %copy-done.3, bf16[256,768]{1,0:T(8,128)(2,1)S(1)} %pad_maximum_fusion.6), kind=kOutput, calls=%fused_computation.1 | convolution fusion | flops 608501760 | bytes 2752512 | tf_op jit(solution)/shard_map/dot_general | solution.py:17
  118.2 5.1 %collective-permute-start.8 = (bf16[384,768]{1,0:T(8,128)(2,1)S(1)}, bf16[384,768]{1,0:T(8,128)(2,1)S(1)}, u32[]{:S(2)}, u32[]{:S(2)}) collective-permute-start(bf16[384,768]{1,0:T(8,128)(2,1)S(1)} %dynamic-slice_bitcast_fusion), channel_id=1, source_target_pairs={{0,1},{1,0},{2,3},{3,2},{4,5},{5,4},{6,7},{7,6},{8,9},{9,8},{10,11... | collective-permute-start | bytes 1769480 | tf_op jit(solution)/shard_map/ppermute | solution.py:125
  123.3 0.2 fusion.49
  123.6 0.7 copy-done.2
  124.3 1.1 convolution_convert_fusion.1
  125.5 4.0 %collective-permute-start.6 = (bf16[384,768]{1,0:T(8,128)(2,1)S(1)}, bf16[384,768]{1,0:T(8,128)(2,1)S(1)}, u32[]{:S(2)}, u32[]{:S(2)}) collective-permute-start(bf16[384,768]{1,0:T(8,128)(2,1)S(1)} %dynamic-slice_bitcast_fusion.1), channel_id=1, source_target_pairs={{0,3},{1,2},{2,1},{3,0},{4,7},{5,6},{6,5},{7,4},{8,11},{9,10},{10,... | collective-permute-start | bytes 1769480 | tf_op jit(solution)/shard_map/ppermute | solution.py:144
  129.5 5.0 %collective-permute-done.8 = bf16[384,768]{1,0:T(8,128)(2,1)S(1)} collective-permute-done((bf16[384,768]{1,0:T(8,128)(2,1)S(1)}, bf16[384,768]{1,0:T(8,128)(2,1)S(1)}, u32[]{:S(2)}, u32[]{:S(2)}) %collective-permute-start.8) | collective-permute-done | bytes 589856 | tf_op jit(solution)/shard_map/ppermute | solution.py:125
  134.4 0.2 fusion.3
  134.6 1.9 convolution_convert_fusion.3
  136.5 1.9 convolution_convert_fusion.5
  138.4 4.1 %collective-permute-start.13 = (bf16[384,768]{1,0:T(8,128)(2,1)S(1)}, bf16[384,768]{1,0:T(8,128)(2,1)S(1)}, u32[]{:S(2)}, u32[]{:S(2)}) collective-permute-start(bf16[384,768]{1,0:T(8,128)(2,1)S(1)} %fusion.3), channel_id=1, source_target_pairs={{0,3},{1,2},{2,1},{3,0},{4,7},{5,6},{6,5},{7,4},{8,11},{9,10},{10,... | collective-permute-start | bytes 1769480 | tf_op jit(solution)/shard_map/ppermute | solution.py:149
  142.5 0.5 convolution_convert_fusion.2
  143.0 0.5 convolution_convert_fusion.4
  143.7 0.2 fusion.2
  143.8 2.5 %collective-permute-start.10 = (bf16[384,768]{1,0:T(8,128)(2,1)S(1)}, bf16[384,768]{1,0:T(8,128)(2,1)S(1)}, u32[]{:S(2)}, u32[]{:S(2)}) collective-permute-start(bf16[384,768]{1,0:T(8,128)(2,1)S(1)} %fusion.2), channel_id=1, source_target_pairs={{0,1},{1,0},{2,3},{3,2},{4,5},{5,4},{6,7},{7,6},{8,9},{9,8},{10,11... | collective-permute-start | bytes 1769480 | tf_op jit(solution)/shard_map/ppermute | solution.py:150
  146.3 5.7 %collective-permute-start.9 = (bf16[512,768]{0,1:T(8,128)(2,1)S(1)}, bf16[512,768]{0,1:T(8,128)(2,1)S(1)}, u32[]{:S(2)}, u32[]{:S(2)}) collective-permute-start(bf16[512,768]{0,1:T(8,128)(2,1)S(1)} %pad_maximum_fusion.3), channel_id=1, source_target_pairs={{0,4},{4,0},{1,5},{5,1},{2,6},{6,2},{3,7},{7,3},{8,12},{12,8},{9,1... | collective-permute-start | bytes 2359304 | tf_op jit(solution)/shard_map/ppermute | solution.py:23
  152.0 1.2 collective-permute-done.13
  153.2 0.1 add_convert_fusion.1
  153.4 5.9 %collective-permute-start.14 = (bf16[384,384]{1,0:T(8,128)(2,1)S(1)}, bf16[384,384]{1,0:T(8,128)(2,1)S(1)}, u32[]{:S(2)}, u32[]{:S(2)}) collective-permute-start(bf16[384,384]{1,0:T(8,128)(2,1)S(1)} %get-tuple-element.49), channel_id=1, source_target_pairs={{0,4},{4,0},{1,5},{5,1},{2,6},{6,2},{3,7},{7,3},{8,12},{12,8},{9,1... | collective-permute-start | bytes 884744 | tf_op jit(solution)/shard_map/ppermute | solution.py:23
  159.4 0.2 add_convert_fusion.2
  159.6 4.0 %collective-permute-start.11 = (bf16[192,768]{1,0:T(8,128)(2,1)S(1)}, bf16[192,768]{1,0:T(8,128)(2,1)S(1)}, u32[]{:S(2)}, u32[]{:S(2)}) collective-permute-start(bf16[192,768]{1,0:T(8,128)(2,1)S(1)} %get-tuple-element.51), channel_id=1, source_target_pairs={{0,4},{4,0},{1,5},{5,1},{2,6},{6,2},{3,7},{7,3},{8,12},{12,8},{9,1... | collective-permute-start | bytes 884744 | tf_op jit(solution)/shard_map/ppermute | solution.py:23
  163.6 0.2 add_convert_fusion
  163.8 1.2 copy.9
  165.0 3.5 %all-to-all-start.2 = ((bf16[8,64,768]{2,1,0:T(8,128)(2,1)}), bf16[8,64,768]{2,1,0:T(8,128)(2,1)S(1)}, u32[]{:S(2)}, u32[]{:S(2)}) async-start(bf16[8,64,768]{2,1,0:T(8,128)(2,1)} %bitcast.14), calls=%async_computation.2 | async-start | bytes 1572864 | tf_op jit(solution)/shard_map/all_to_all | solution.py:27
  168.6 0.1 maximum_select_fusion.5
  168.7 2.5 %collective-permute-start.15 = (bf16[2,384,384]{2,1,0:T(8,128)(2,1)S(1)}, bf16[2,384,384]{2,1,0:T(8,128)(2,1)S(1)}, u32[]{:S(2)}, u32[]{:S(2)}) collective-permute-start(bf16[2,384,384]{2,1,0:T(8,128)(2,1)S(1)} %maximum_select_fusion.5), channel_id=1, source_target_pairs={{0,1},{1,0},{2,3},{3,2},{4,5},{5,4},{6,7},{7,6},{8,9},{9,8},{10,11... | collective-permute-start | bytes 1769480 | tf_op jit(solution)/shard_map/ppermute | solution.py:153
  171.2 0.1 maximum_select_fusion.4
  171.3 2.5 %collective-permute-start.12 = (bf16[192,1536]{1,0:T(8,128)(2,1)S(1)}, bf16[192,1536]{1,0:T(8,128)(2,1)S(1)}, u32[]{:S(2)}, u32[]{:S(2)}) collective-permute-start(bf16[192,1536]{1,0:T(8,128)(2,1)S(1)} %maximum_select_fusion.4), channel_id=1, source_target_pairs={{0,3},{1,2},{2,1},{3,0},{4,7},{5,6},{6,5},{7,4},{8,11},{9,10},{10,... | collective-permute-start | bytes 1769480 | tf_op jit(solution)/shard_map/ppermute | solution.py:156
  173.9 11.6 %collective-permute-done.15 = bf16[2,384,384]{2,1,0:T(8,128)(2,1)S(1)} collective-permute-done((bf16[2,384,384]{2,1,0:T(8,128)(2,1)S(1)}, bf16[2,384,384]{2,1,0:T(8,128)(2,1)S(1)}, u32[]{:S(2)}, u32[]{:S(2)}) %collective-permute-start.15) | collective-permute-done | bytes 589856 | tf_op jit(solution)/shard_map/ppermute | solution.py:153
  185.5 1.4 maximum_select_fusion.1
  186.9 2.2 %collective-permute-done.12 = bf16[192,1536]{1,0:T(8,128)(2,1)S(1)} collective-permute-done((bf16[192,1536]{1,0:T(8,128)(2,1)S(1)}, bf16[192,1536]{1,0:T(8,128)(2,1)S(1)}, u32[]{:S(2)}, u32[]{:S(2)}) %collective-permute-start.12) | collective-permute-done | bytes 589856 | tf_op jit(solution)/shard_map/ppermute | solution.py:156
  189.1 1.4 maximum_select_fusion
  190.4 1.7 all-to-all-done.2
  192.1 0.1 fusion.39
  192.2 0.6 fusion.55
  (31 shorter events, 0.8 us)
Async XLA Ops:
  1.5 8.6 %copy-start = (bf16[1536,384]{1,0:T(8,128)(2,1)S(1)}, bf16[1536,384]{1,0:T(8,128)(2,1)}, u32[]{:S(2)}) copy-start(bf16[1536,384]{1,0:T(8,128)(2,1)} %param.6) | copy-start | bytes 3538948
  2.4 28.7 %all-to-all-start = ((bf16[8,64,768]{2,1,0:T(8,128)(2,1)}), bf16[8,64,768]{2,1,0:T(8,128)(2,1)S(1)}, u32[]{:S(2)}, u32[]{:S(2)}) async-start(bf16[8,64,768]{2,1,0:T(8,128)(2,1)} %broadcast_in_dim.12), calls=%async_computation | async-start | bytes 1572864 | tf_op jit(solution)/shard_map/all_to_all | solution.py:27
  10.1 5.0 %copy-start.1 = (bf16[384,1536]{1,0:T(8,128)(2,1)S(1)}, bf16[384,1536]{1,0:T(8,128)(2,1)}, u32[]{:S(2)}) copy-start(bf16[384,1536]{1,0:T(8,128)(2,1)} %param.5) | copy-start | bytes 3538948
  10.2 6.9 %collective-permute-start.1 = (bf16[768,384]{1,0:T(8,128)(2,1)S(1)}, bf16[768,384]{1,0:T(8,128)(2,1)S(1)}, u32[]{:S(2)}, u32[]{:S(2)}) collective-permute-start(bf16[768,384]{1,0:T(8,128)(2,1)S(1)} %get-tuple-element.35), channel_id=1, source_target_pairs={{0,4},{4,0},{1,5},{5,1},{2,6},{6,2},{3,7},{7,3},{8,12},{12,8},{9,1... | collective-permute-start | bytes 1769480 | tf_op jit(solution)/shard_map/ppermute | solution.py:23
  15.2 3.9 %collective-permute-start = (bf16[384,768]{1,0:T(8,128)(2,1)S(1)}, bf16[384,768]{1,0:T(8,128)(2,1)S(1)}, u32[]{:S(2)}, u32[]{:S(2)}) collective-permute-start(bf16[384,768]{1,0:T(8,128)(2,1)S(1)} %get-tuple-element.37), channel_id=1, source_target_pairs={{0,4},{4,0},{1,5},{5,1},{2,6},{6,2},{3,7},{7,3},{8,12},{12,8},{9,1... | collective-permute-start | bytes 1769480 | tf_op jit(solution)/shard_map/ppermute | solution.py:23
  31.1 7.0 %collective-permute-start.2 = (bf16[512,768]{1,0:T(8,128)(2,1)S(1)}, bf16[512,768]{1,0:T(8,128)(2,1)}, u32[]{:S(2)}, u32[]{:S(2)}) collective-permute-start(bf16[512,768]{1,0:T(8,128)(2,1)S(1)} %bitcast.40), channel_id=1, source_target_pairs={{0,4},{4,0},{1,5},{5,1},{2,6},{6,2},{3,7},{7,3},{8,12},{12,8},{9,1... | collective-permute-start | bytes 2359304 | tf_op jit(solution)/shard_map/ppermute | solution.py:23
  36.2 4.2 %copy-start.3 = (bf16[256,384]{1,0:T(8,128)(2,1)}, bf16[256,384]{1,0:T(8,128)(2,1)S(1)}, u32[]{:S(2)}) copy-start(bf16[256,384]{1,0:T(8,128)(2,1)S(1)} %get-tuple-element.67) | copy-start | bytes 589828
  39.4 1.1 copy-start.4
  40.5 13.1 %collective-permute-start.3 = (bf16[256,768]{1,0:T(8,128)(2,1)S(1)}, bf16[256,768]{1,0:T(8,128)(2,1)S(1)}, u32[]{:S(2)}, u32[]{:S(2)}) collective-permute-start(bf16[256,768]{1,0:T(8,128)(2,1)S(1)} %convolution_convert_fusion.9), channel_id=1, source_target_pairs={{0,8},{8,0},{16,24},{24,16},{32,40},{40,32},{48,56},{56,48},{1,9},... | collective-permute-start | bytes 1179656 | tf_op jit(solution)/shard_map/ppermute | solution.py:65
  44.4 17.7 %collective-permute-start.4 = (bf16[256,768]{1,0:T(8,128)(2,1)S(1)}, bf16[256,768]{1,0:T(8,128)(2,1)S(1)}, u32[]{:S(2)}, u32[]{:S(2)}) collective-permute-start(bf16[256,768]{1,0:T(8,128)(2,1)S(1)} %convolution_convert_fusion.8), channel_id=1, source_target_pairs={{0,56},{8,16},{16,8},{24,32},{32,24},{40,48},{48,40},{56,0},{1,57}... | collective-permute-start | bytes 1179656 | tf_op jit(solution)/shard_map/ppermute | solution.py:65
  105.7 10.4 %collective-permute-start.7 = (bf16[256,768]{1,0:T(8,128)(2,1)}, bf16[256,768]{1,0:T(8,128)(2,1)}, u32[]{:S(2)}, u32[]{:S(2)}) collective-permute-start(bf16[256,768]{1,0:T(8,128)(2,1)} %get-tuple-element.26), channel_id=1, source_target_pairs={{0,8},{8,0},{16,24},{24,16},{32,40},{40,32},{48,56},{56,48},{1,9},... | collective-permute-start | bytes 1179656 | tf_op jit(solution)/shard_map/ppermute | solution.py:65
  107.6 15.9 %collective-permute-start.5 = (bf16[256,768]{1,0:T(8,128)(2,1)}, bf16[256,768]{1,0:T(8,128)(2,1)S(1)}, u32[]{:S(2)}, u32[]{:S(2)}) collective-permute-start(bf16[256,768]{1,0:T(8,128)(2,1)} %get-tuple-element.28), channel_id=1, source_target_pairs={{0,56},{8,16},{16,8},{24,32},{32,24},{40,48},{48,40},{56,0},{1,57}... | collective-permute-start | bytes 1179656 | tf_op jit(solution)/shard_map/ppermute | solution.py:65
  118.2 16.3 %collective-permute-start.8 = (bf16[384,768]{1,0:T(8,128)(2,1)S(1)}, bf16[384,768]{1,0:T(8,128)(2,1)S(1)}, u32[]{:S(2)}, u32[]{:S(2)}) collective-permute-start(bf16[384,768]{1,0:T(8,128)(2,1)S(1)} %dynamic-slice_bitcast_fusion), channel_id=1, source_target_pairs={{0,1},{1,0},{2,3},{3,2},{4,5},{5,4},{6,7},{7,6},{8,9},{9,8},{10,11... | collective-permute-start | bytes 1769480 | tf_op jit(solution)/shard_map/ppermute | solution.py:125
  123.3 1.0 copy-start.2
  125.5 18.2 %collective-permute-start.6 = (bf16[384,768]{1,0:T(8,128)(2,1)S(1)}, bf16[384,768]{1,0:T(8,128)(2,1)S(1)}, u32[]{:S(2)}, u32[]{:S(2)}) collective-permute-start(bf16[384,768]{1,0:T(8,128)(2,1)S(1)} %dynamic-slice_bitcast_fusion.1), channel_id=1, source_target_pairs={{0,3},{1,2},{2,1},{3,0},{4,7},{5,6},{6,5},{7,4},{8,11},{9,10},{10,... | collective-permute-start | bytes 1769480 | tf_op jit(solution)/shard_map/ppermute | solution.py:144
  138.4 14.9 %collective-permute-start.13 = (bf16[384,768]{1,0:T(8,128)(2,1)S(1)}, bf16[384,768]{1,0:T(8,128)(2,1)S(1)}, u32[]{:S(2)}, u32[]{:S(2)}) collective-permute-start(bf16[384,768]{1,0:T(8,128)(2,1)S(1)} %fusion.3), channel_id=1, source_target_pairs={{0,3},{1,2},{2,1},{3,0},{4,7},{5,6},{6,5},{7,4},{8,11},{9,10},{10,... | collective-permute-start | bytes 1769480 | tf_op jit(solution)/shard_map/ppermute | solution.py:149
  143.8 15.5 %collective-permute-start.10 = (bf16[384,768]{1,0:T(8,128)(2,1)S(1)}, bf16[384,768]{1,0:T(8,128)(2,1)S(1)}, u32[]{:S(2)}, u32[]{:S(2)}) collective-permute-start(bf16[384,768]{1,0:T(8,128)(2,1)S(1)} %fusion.2), channel_id=1, source_target_pairs={{0,1},{1,0},{2,3},{3,2},{4,5},{5,4},{6,7},{7,6},{8,9},{9,8},{10,11... | collective-permute-start | bytes 1769480 | tf_op jit(solution)/shard_map/ppermute | solution.py:150
  146.3 17.3 %collective-permute-start.9 = (bf16[512,768]{0,1:T(8,128)(2,1)S(1)}, bf16[512,768]{0,1:T(8,128)(2,1)S(1)}, u32[]{:S(2)}, u32[]{:S(2)}) collective-permute-start(bf16[512,768]{0,1:T(8,128)(2,1)S(1)} %pad_maximum_fusion.3), channel_id=1, source_target_pairs={{0,4},{4,0},{1,5},{5,1},{2,6},{6,2},{3,7},{7,3},{8,12},{12,8},{9,1... | collective-permute-start | bytes 2359304 | tf_op jit(solution)/shard_map/ppermute | solution.py:23
  153.4 15.1 %collective-permute-start.14 = (bf16[384,384]{1,0:T(8,128)(2,1)S(1)}, bf16[384,384]{1,0:T(8,128)(2,1)S(1)}, u32[]{:S(2)}, u32[]{:S(2)}) collective-permute-start(bf16[384,384]{1,0:T(8,128)(2,1)S(1)} %get-tuple-element.49), channel_id=1, source_target_pairs={{0,4},{4,0},{1,5},{5,1},{2,6},{6,2},{3,7},{7,3},{8,12},{12,8},{9,1... | collective-permute-start | bytes 884744 | tf_op jit(solution)/shard_map/ppermute | solution.py:23
  159.6 11.6 %collective-permute-start.11 = (bf16[192,768]{1,0:T(8,128)(2,1)S(1)}, bf16[192,768]{1,0:T(8,128)(2,1)S(1)}, u32[]{:S(2)}, u32[]{:S(2)}) collective-permute-start(bf16[192,768]{1,0:T(8,128)(2,1)S(1)} %get-tuple-element.51), channel_id=1, source_target_pairs={{0,4},{4,0},{1,5},{5,1},{2,6},{6,2},{3,7},{7,3},{8,12},{12,8},{9,1... | collective-permute-start | bytes 884744 | tf_op jit(solution)/shard_map/ppermute | solution.py:23
  165.0 27.1 %all-to-all-start.2 = ((bf16[8,64,768]{2,1,0:T(8,128)(2,1)}), bf16[8,64,768]{2,1,0:T(8,128)(2,1)S(1)}, u32[]{:S(2)}, u32[]{:S(2)}) async-start(bf16[8,64,768]{2,1,0:T(8,128)(2,1)} %bitcast.14), calls=%async_computation.2 | async-start | bytes 1572864 | tf_op jit(solution)/shard_map/all_to_all | solution.py:27
  168.7 16.8 %collective-permute-start.15 = (bf16[2,384,384]{2,1,0:T(8,128)(2,1)S(1)}, bf16[2,384,384]{2,1,0:T(8,128)(2,1)S(1)}, u32[]{:S(2)}, u32[]{:S(2)}) collective-permute-start(bf16[2,384,384]{2,1,0:T(8,128)(2,1)S(1)} %maximum_select_fusion.5), channel_id=1, source_target_pairs={{0,1},{1,0},{2,3},{3,2},{4,5},{5,4},{6,7},{7,6},{8,9},{9,8},{10,11... | collective-permute-start | bytes 1769480 | tf_op jit(solution)/shard_map/ppermute | solution.py:153
  171.3 17.7 %collective-permute-start.12 = (bf16[192,1536]{1,0:T(8,128)(2,1)S(1)}, bf16[192,1536]{1,0:T(8,128)(2,1)S(1)}, u32[]{:S(2)}, u32[]{:S(2)}) collective-permute-start(bf16[192,1536]{1,0:T(8,128)(2,1)S(1)} %maximum_select_fusion.4), channel_id=1, source_target_pairs={{0,3},{1,2},{2,1},{3,0},{4,7},{5,6},{6,5},{7,4},{8,11},{9,10},{10,... | collective-permute-start | bytes 1769480 | tf_op jit(solution)/shard_map/ppermute | solution.py:156

commit v12 on v10

--- a/solution.py
+++ b/solution.py
@@ -133,11 +133,13 @@
     cut = width // 2
     order = [tok[:, i * cut : (i + 1) * cut] for i in (0, 2, 1, 3)]
     up_part = dot(jnp.concatenate(order, 1), hg, (0, 0)).reshape(2, width, half)
-    up_part = scatter(up_part, 0, high, far)
+    up_got = lax.ppermute(pick(up_part, 1 - high), "rep", far)
+    down_own, down_got = down_part[:, :width], swap(down_part[:, width:])
+    down_got, up_got = barrier((down_got, up_got))
+    up_part = plus(pick(up_part, high), up_got)
+    down_part = pair(down_own[None], down_got[None], core, 0)
     down_part = plus(down_part, lax.ppermute(down_part, "rep", far))
     up_part = plus(up_part, lax.ppermute(up_part, "rep", near))
-    down_own, down_got = down_part[:, :width], swap(down_part[:, width:])
-    down_part = pair(down_own[None], down_got[None], core, 0)
     down_part = pair(down_part, lax.ppermute(down_part, "rep", near), turn, 1)
     down_grads = down_part.reshape(2 * half, width)
     up_part = pair(up_part[:cut], swap(up_part[cut:]), core, 1)

time: 189 us -> 191 us (1.011)
    ppermute x1, waiting for transfers between devices: 0.01 us -> 6.72 us  [per_device(): up_part = plus(up_part, lax.ppermute(up_part, 'rep', near))]
    ppermute x2 -> x1, waiting for transfers between devices: 7.32 us -> 1.95 us  [scatter(): return plus(at(bit), lax.ppermute(at(1 - bit), 'rep', pairs))]
    ppermute x2 -> x1, starting transfers between devices: 6.42 us -> 3.11 us  [scatter(): return plus(at(bit), lax.ppermute(at(1 - bit), 'rep', pairs))]
    ppermute x0 -> x1, starting transfers between devices: none -> 3.3 us  [per_device(): up_got = lax.ppermute(pick(up_part, 1 - high), 'rep', far)]
    all_to_all x2, waiting for transfers between devices: 14.1 us -> 11.9 us  [exchange(): return lax.all_to_all(x, axis, 0, 0, tiled=False)]
    ppermute x1, waiting for transfers between devices: 1.68 us -> 3.82 us  [per_device(): up_grads = pair(up_part, lax.ppermute(up_part, 'rep', far), high, 0)]
  transfers between devices with their start and end apart: 18 -> 18, of which waited for: 11 -> 10; matrix products, arithmetic and copies ran while one was open for 8% -> 9% of each run, Pallas kernels for 0% -> 0%
where the time goes in v12:
time: 191 us; the launch traced here: 190 us
  starting transfers between devices  80.3 us (42%)
  waiting for transfers between devices  49.1 us (26%)
  blocking collectives  35.7 us (19%)
  matrix products  9.9 us (5%)
  local copies, waits for them, and re-layouts  7.27 us (4%)
  other arithmetic  6.53 us (3%)
    ppermute x6, starting transfers between devices, swap(): return lax.ppermute(x, 'core', [(0, 1), (1, 0)])  27.1 us
    ppermute x4, starting transfers between devices, z_swap(): return lax.ppermute(x, ('zh', 'zl'), pairs)  21.5 us
    all_to_all x1, blocking collectives, exchange(): return lax.all_to_all(x, axis, 0, 0, tiled=False)  19.8 us
    all_gather x1, blocking collectives, per_device(): lax.all_gather(jnp.concatenate([act, hid_grads], 1), 'zh', axis=0, tiled=...  15.9 us
    ppermute x4, waiting for transfers between devices, z_swap(): return lax.ppermute(x, ('zh', 'zl'), pairs)  12.3 us
    all_to_all x2, waiting for transfers between devices, exchange(): return lax.all_to_all(x, axis, 0, 0, tiled=False)  11.9 us
    all_to_all x2, starting transfers between devices, exchange(): return lax.all_to_all(x, axis, 0, 0, tiled=False)  11.2 us
    dot_general x10, matrix products, dot(): lax.dot_general(left, right, ((dims[:1], dims[1:]), ((), ())), preferred_...  9.9 us
  transfers between devices with their start and end apart: 18, of which 10 were waited for; matrix products, arithmetic and copies ran while one was open for 9% of the time, Pallas kernels for 0%

profile of v12, /device:TPU:1, one launch (start us, length us, event | category | flops | bytes accessed | tf_op | source)
XLA Modules:
  0.0 190.0 jit_solution(16171105316914635544)
XLA Ops:
  0.6 0.8 pad_maximum_fusion.7
  1.5 0.9 broadcast_in_dim.12
  2.4 7.7 %all-to-all-start = ((bf16[8,64,768]{2,1,0:T(8,128)(2,1)}), bf16[8,64,768]{2,1,0:T(8,128)(2,1)S(1)}, u32[]{:S(2)}, u32[]{:S(2)}) async-start(bf16[8,64,768]{2,1,0:T(8,128)(2,1)} %broadcast_in_dim.12), calls=%async_computation | async-start | bytes 1572864 | tf_op jit(solution)/shard_map/all_to_all | solution.py:27
  10.2 4.8 %collective-permute-start = (bf16[384,768]{1,0:T(8,128)(2,1)S(1)}, bf16[384,768]{1,0:T(8,128)(2,1)S(1)}, u32[]{:S(2)}, u32[]{:S(2)}) collective-permute-start(bf16[384,768]{1,0:T(8,128)(2,1)S(1)} %get-tuple-element.35), channel_id=1, source_target_pairs={{0,4},{4,0},{1,5},{5,1},{2,6},{6,2},{3,7},{7,3},{8,12},{12,8},{9,1... | collective-permute-start | bytes 1769480 | tf_op jit(solution)/shard_map/ppermute | solution.py:23
  15.0 0.1 constant_dynamic-slice_fusion.1
  15.2 1.9 %collective-permute-start.1 = (bf16[768,384]{1,0:T(8,128)(2,1)S(1)}, bf16[768,384]{1,0:T(8,128)(2,1)S(1)}, u32[]{:S(2)}, u32[]{:S(2)}) collective-permute-start(bf16[768,384]{1,0:T(8,128)(2,1)S(1)} %get-tuple-element.33), channel_id=1, source_target_pairs={{0,4},{4,0},{1,5},{5,1},{2,6},{6,2},{3,7},{7,3},{8,12},{12,8},{9,1... | collective-permute-start | bytes 1769480 | tf_op jit(solution)/shard_map/ppermute | solution.py:23
  17.2 1.9 collective-permute-done.1
  19.1 0.1 pad_maximum_fusion.1
  19.2 11.9 %all-to-all-done = bf16[8,64,768]{2,1,0:T(8,128)(2,1)S(1)} async-done(((bf16[8,64,768]{2,1,0:T(8,128)(2,1)}), bf16[8,64,768]{2,1,0:T(8,128)(2,1)S(1)}, u32[]{:S(2)}, u32[]{:S(2)}) %all-to-all-start) | async-done | bytes 786464 | tf_op jit(solution)/shard_map/all_to_all | solution.py:27
  31.1 5.0 %collective-permute-start.2 = (bf16[512,768]{1,0:T(8,128)(2,1)S(1)}, bf16[512,768]{1,0:T(8,128)(2,1)}, u32[]{:S(2)}, u32[]{:S(2)}) collective-permute-start(bf16[512,768]{1,0:T(8,128)(2,1)S(1)} %bitcast.40), channel_id=1, source_target_pairs={{0,4},{4,0},{1,5},{5,1},{2,6},{6,2},{3,7},{7,3},{8,12},{12,8},{9,1... | collective-permute-start | bytes 2359304 | tf_op jit(solution)/shard_map/ppermute | solution.py:23
  36.3 1.8 collective-permute-done.2
  38.1 1.2 dynamic-slice_bitcast_fusion.2
  39.5 0.5 convolution_convert_fusion.9
  40.0 0.1 copy-done.4
  40.0 0.5 convolution_convert_fusion.8
  40.6 10.6 %collective-permute-start.4 = (bf16[256,768]{1,0:T(8,128)(2,1)S(1)}, bf16[256,768]{1,0:T(8,128)(2,1)S(1)}, u32[]{:S(2)}, u32[]{:S(2)}) collective-permute-start(bf16[256,768]{1,0:T(8,128)(2,1)S(1)} %convolution_convert_fusion.8), channel_id=1, source_target_pairs={{0,56},{8,16},{16,8},{24,32},{32,24},{40,48},{48,40},{56,0},{1,57}... | collective-permute-start | bytes 1179656 | tf_op jit(solution)/shard_map/ppermute | solution.py:65
  51.2 1.9 %collective-permute-start.3 = (bf16[256,768]{1,0:T(8,128)(2,1)S(1)}, bf16[256,768]{1,0:T(8,128)(2,1)S(1)}, u32[]{:S(2)}, u32[]{:S(2)}) collective-permute-start(bf16[256,768]{1,0:T(8,128)(2,1)S(1)} %convolution_convert_fusion.9), channel_id=1, source_target_pairs={{0,8},{8,0},{16,24},{24,16},{32,40},{40,32},{48,56},{56,48},{1,9},... | collective-permute-start | bytes 1179656 | tf_op jit(solution)/shard_map/ppermute | solution.py:65
  53.1 7.2 %collective-permute-done.4 = bf16[256,768]{1,0:T(8,128)(2,1)S(1)} collective-permute-done((bf16[256,768]{1,0:T(8,128)(2,1)S(1)}, bf16[256,768]{1,0:T(8,128)(2,1)S(1)}, u32[]{:S(2)}, u32[]{:S(2)}) %collective-permute-start.4) | collective-permute-done | bytes 393248 | tf_op jit(solution)/shard_map/ppermute | solution.py:65
  60.4 0.5 add_convert_fusion.3
  60.9 2.2 %collective-permute-done.3 = bf16[256,768]{1,0:T(8,128)(2,1)S(1)} collective-permute-done((bf16[256,768]{1,0:T(8,128)(2,1)S(1)}, bf16[256,768]{1,0:T(8,128)(2,1)S(1)}, u32[]{:S(2)}, u32[]{:S(2)}) %collective-permute-start.3) | collective-permute-done | bytes 393248 | tf_op jit(solution)/shard_map/ppermute | solution.py:65
  63.1 0.5 add_convert_fusion.4
  63.6 19.8 %all_to_all.15 = bf16[4,64,1536]{2,1,0:T(8,128)(2,1)S(1)} all-to-all(bf16[4,64,1536]{2,1,0:T(8,128)(2,1)S(1)} %bitcast.39), channel_id=1, replica_groups=mesh['row'=8,'zh'=4,'zl'=2,'core'=2,'rep'=4] {'zh'}, dimensions={0} | all-to-all | bytes 1572864 | tf_op jit(solution)/shard_map/all_to_all | solution.py:27
  83.4 0.1 add_bitcast_fusion
  83.5 0.1 multiply_convert_fusion
  83.7 15.9 %all_gather.3 = bf16[256,1536]{1,0:T(8,128)(2,1)S(1)} all-gather(bf16[64,1536]{1,0:T(8,128)(2,1)S(1)} %pad_maximum_fusion.6), channel_id=1, replica_groups=mesh['row'=8,'zh'=4,'zl'=2,'core'=2,'rep'=4] {'zh'}, dimensions={0}, use_global_device_ids=true | all-gather | bytes 983040 | tf_op jit(solution)/shard_map/all_gather | solution.py:112
  99.6 0.9 fusion.49
  100.5 6.4 %collective-permute-start.5 = (bf16[256,768]{1,0:T(8,128)(2,1)}, bf16[256,768]{1,0:T(8,128)(2,1)}, u32[]{:S(2)}, u32[]{:S(2)}) collective-permute-start(bf16[256,768]{1,0:T(8,128)(2,1)} %get-tuple-element.25), channel_id=1, source_target_pairs={{0,8},{8,0},{16,24},{24,16},{32,40},{40,32},{48,56},{56,48},{1,9},... | collective-permute-start | bytes 1179656 | tf_op jit(solution)/shard_map/ppermute | solution.py:65
  107.0 2.5 %collective-permute-start.7 = (bf16[256,768]{1,0:T(8,128)(2,1)}, bf16[256,768]{1,0:T(8,128)(2,1)S(1)}, u32[]{:S(2)}, u32[]{:S(2)}) collective-permute-start(bf16[256,768]{1,0:T(8,128)(2,1)} %get-tuple-element.27), channel_id=1, source_target_pairs={{0,56},{8,16},{16,8},{24,32},{32,24},{40,48},{48,40},{56,0},{1,57}... | collective-permute-start | bytes 1179656 | tf_op jit(solution)/shard_map/ppermute | solution.py:65
  109.6 2.9 %collective-permute-done.5 = bf16[256,768]{1,0:T(8,128)(2,1)} collective-permute-done((bf16[256,768]{1,0:T(8,128)(2,1)}, bf16[256,768]{1,0:T(8,128)(2,1)}, u32[]{:S(2)}, u32[]{:S(2)}) %collective-permute-start.5) | collective-permute-done | bytes 393248 | tf_op jit(solution)/shard_map/ppermute | solution.py:65
  112.4 2.0 %convolution_convert_fusion.1 = bf16[768,768]{1,0:T(8,128)(2,1)S(1)} fusion(bf16[256,768]{1,0:T(8,128)(2,1)} %collective-permute-done.5, bf16[256,768]{1,0:T(8,128)(2,1)} %get-tuple-element.25, bf16[256,384]{1,0:T(8,128)(2,1)} %copy-done.4, bf16[256,384]{1,0:T(8,128)(2,1)} %copy-done.3, bf16[256,768]{1,0:T(8,128)(2,1)S(1)} %pad_maximum_fusion.5), kind=kOutput, calls=%fused_computation.2 | convolution fusion | flops 608501760 | bytes 2752512 | tf_op jit(solution)/shard_map/dot_general | solution.py:17
  114.5 3.1 %collective-permute-start.6 = (bf16[384,768]{1,0:T(8,128)(2,1)S(1)}, bf16[384,768]{1,0:T(8,128)(2,1)S(1)}, u32[]{:S(2)}, u32[]{:S(2)}) collective-permute-start(bf16[384,768]{1,0:T(8,128)(2,1)S(1)} %dynamic-slice_bitcast_fusion.1), channel_id=1, source_target_pairs={{0,1},{1,0},{2,3},{3,2},{4,5},{5,4},{6,7},{7,6},{8,9},{9,8},{10,11... | collective-permute-start | bytes 1769480 | tf_op jit(solution)/shard_map/ppermute | solution.py:125
  117.7 0.2 fusion.48
  118.0 0.7 copy-done.2
  118.7 1.1 convolution_convert_fusion
  119.9 3.3 %collective-permute-start.10 = (bf16[384,768]{1,0:T(8,128)(2,1)S(1)}, bf16[384,768]{1,0:T(8,128)(2,1)S(1)}, u32[]{:S(2)}, u32[]{:S(2)}) collective-permute-start(bf16[384,768]{1,0:T(8,128)(2,1)S(1)} %dynamic-slice_bitcast_fusion), channel_id=1, source_target_pairs={{0,3},{1,2},{2,1},{3,0},{4,7},{5,6},{6,5},{7,4},{8,11},{9,10},{10,... | collective-permute-start | bytes 1769480 | tf_op jit(solution)/shard_map/ppermute | solution.py:136
  123.2 2.0 %collective-permute-done.6 = bf16[384,768]{1,0:T(8,128)(2,1)S(1)} collective-permute-done((bf16[384,768]{1,0:T(8,128)(2,1)S(1)}, bf16[384,768]{1,0:T(8,128)(2,1)S(1)}, u32[]{:S(2)}, u32[]{:S(2)}) %collective-permute-start.6) | collective-permute-done | bytes 589856 | tf_op jit(solution)/shard_map/ppermute | solution.py:125
  125.1 0.2 fusion.3
  125.4 10.2 %collective-permute-start.9 = (bf16[384,384]{1,0:T(8,128)(2,1)S(1)}, bf16[384,384]{1,0:T(8,128)(2,1)S(1)}, u32[]{:S(2)}, u32[]{:S(2)}) collective-permute-start(bf16[384,384]{1,0:T(8,128)(2,1)S(1)} %get-tuple-element.47), channel_id=1, source_target_pairs={{0,4},{4,0},{1,5},{5,1},{2,6},{6,2},{3,7},{7,3},{8,12},{12,8},{9,1... | collective-permute-start | bytes 884744 | tf_op jit(solution)/shard_map/ppermute | solution.py:23
  135.6 0.5 convolution_convert_fusion.2
  136.1 1.9 convolution_convert_fusion.3
  138.1 1.9 %collective-permute-start.8 = (bf16[512,768]{0,1:T(8,128)(2,1)S(1)}, bf16[512,768]{0,1:T(8,128)(2,1)S(1)}, u32[]{:S(2)}, u32[]{:S(2)}) collective-permute-start(bf16[512,768]{0,1:T(8,128)(2,1)S(1)} %pad_maximum_fusion.3), channel_id=1, source_target_pairs={{0,4},{4,0},{1,5},{5,1},{2,6},{6,2},{3,7},{7,3},{8,12},{12,8},{9,1... | collective-permute-start | bytes 2359304 | tf_op jit(solution)/shard_map/ppermute | solution.py:23
  140.0 0.2 fusion.2
  140.2 3.1 %collective-permute-start.11 = (bf16[384,768]{1,0:T(8,128)(2,1)S(1)}, bf16[384,768]{1,0:T(8,128)(2,1)S(1)}, u32[]{:S(2)}, u32[]{:S(2)}) collective-permute-start(bf16[384,768]{1,0:T(8,128)(2,1)S(1)} %fusion.2), channel_id=1, source_target_pairs={{0,1},{1,0},{2,3},{3,2},{4,5},{5,4},{6,7},{7,6},{8,9},{9,8},{10,11... | collective-permute-start | bytes 1769480 | tf_op jit(solution)/shard_map/ppermute | solution.py:142
  143.3 0.5 convolution_convert_fusion.4
  143.8 1.9 convolution_convert_fusion.5
  145.7 0.1 maximum_select_fusion.5
  145.8 3.9 %collective-permute-start.14 = (bf16[2,384,384]{2,1,0:T(8,128)(2,1)S(1)}, bf16[2,384,384]{2,1,0:T(8,128)(2,1)S(1)}, u32[]{:S(2)}, u32[]{:S(2)}) collective-permute-start(bf16[2,384,384]{2,1,0:T(8,128)(2,1)S(1)} %maximum_select_fusion.5), channel_id=1, source_target_pairs={{0,3},{1,2},{2,1},{3,0},{4,7},{5,6},{6,5},{7,4},{8,11},{9,10},{10,... | collective-permute-start | bytes 1769480 | tf_op jit(solution)/shard_map/ppermute | solution.py:141
  149.7 6.7 %collective-permute-done.11 = bf16[384,768]{1,0:T(8,128)(2,1)S(1)} collective-permute-done((bf16[384,768]{1,0:T(8,128)(2,1)S(1)}, bf16[384,768]{1,0:T(8,128)(2,1)S(1)}, u32[]{:S(2)}, u32[]{:S(2)}) %collective-permute-start.11) | collective-permute-done | bytes 589856 | tf_op jit(solution)/shard_map/ppermute | solution.py:142
  156.5 0.1 add_convert_fusion.2
  156.6 0.8 fusion.50
  157.4 3.2 %collective-permute-start.12 = (bf16[192,768]{1,0:T(8,128)(2,1)}, bf16[192,768]{1,0:T(8,128)(2,1)}, u32[]{:S(2)}, u32[]{:S(2)}) collective-permute-start(bf16[192,768]{1,0:T(8,128)(2,1)} %get-tuple-element.49), channel_id=1, source_target_pairs={{0,4},{4,0},{1,5},{5,1},{2,6},{6,2},{3,7},{7,3},{8,12},{12,8},{9,1... | collective-permute-start | bytes 884744 | tf_op jit(solution)/shard_map/ppermute | solution.py:23
  160.6 0.2 add_convert_fusion
  160.9 1.2 copy.9
  162.0 3.5 %all-to-all-start.2 = ((bf16[8,64,768]{2,1,0:T(8,128)(2,1)}), bf16[8,64,768]{2,1,0:T(8,128)(2,1)S(1)}, u32[]{:S(2)}, u32[]{:S(2)}) async-start(bf16[8,64,768]{2,1,0:T(8,128)(2,1)} %bitcast.12), calls=%async_computation.2 | async-start | bytes 1572864 | tf_op jit(solution)/shard_map/all_to_all | solution.py:27
  165.6 0.2 add_convert_fusion.1
  165.8 3.1 %collective-permute-start.15 = (bf16[2,384,384]{2,1,0:T(8,128)(2,1)S(1)}, bf16[2,384,384]{2,1,0:T(8,128)(2,1)S(1)}, u32[]{:S(2)}, u32[]{:S(2)}) collective-permute-start(bf16[2,384,384]{2,1,0:T(8,128)(2,1)S(1)} %add_convert_fusion.1), channel_id=1, source_target_pairs={{0,1},{1,0},{2,3},{3,2},{4,5},{5,4},{6,7},{7,6},{8,9},{9,8},{10,11... | collective-permute-start | bytes 1769480 | tf_op jit(solution)/shard_map/ppermute | solution.py:143
  168.9 1.2 maximum_select_fusion.4
  170.1 3.9 %collective-permute-start.13 = (bf16[192,1536]{1,0:T(8,128)(2,1)S(1)}, bf16[192,1536]{1,0:T(8,128)(2,1)S(1)}, u32[]{:S(2)}, u32[]{:S(2)}) collective-permute-start(bf16[192,1536]{1,0:T(8,128)(2,1)S(1)} %maximum_select_fusion.4), channel_id=1, source_target_pairs={{0,3},{1,2},{2,1},{3,0},{4,7},{5,6},{6,5},{7,4},{8,11},{9,10},{10,... | collective-permute-start | bytes 1769480 | tf_op jit(solution)/shard_map/ppermute | solution.py:146
  174.0 8.6 %collective-permute-done.15 = bf16[2,384,384]{2,1,0:T(8,128)(2,1)S(1)} collective-permute-done((bf16[2,384,384]{2,1,0:T(8,128)(2,1)S(1)}, bf16[2,384,384]{2,1,0:T(8,128)(2,1)S(1)}, u32[]{:S(2)}, u32[]{:S(2)}) %collective-permute-start.15) | collective-permute-done | bytes 589856 | tf_op jit(solution)/shard_map/ppermute | solution.py:143
  182.6 1.4 maximum_select_fusion.1
  184.0 3.8 %collective-permute-done.13 = bf16[192,1536]{1,0:T(8,128)(2,1)S(1)} collective-permute-done((bf16[192,1536]{1,0:T(8,128)(2,1)S(1)}, bf16[192,1536]{1,0:T(8,128)(2,1)S(1)}, u32[]{:S(2)}, u32[]{:S(2)}) %collective-permute-start.13) | collective-permute-done | bytes 589856 | tf_op jit(solution)/shard_map/ppermute | solution.py:146
  187.8 1.4 maximum_select_fusion
  189.2 0.1 fusion.39
  189.3 0.6 fusion.55
  (30 shorter events, 0.8 us)
Async XLA Ops:
  1.5 8.6 %copy-start = (bf16[384,1536]{1,0:T(8,128)(2,1)S(1)}, bf16[384,1536]{1,0:T(8,128)(2,1)}, u32[]{:S(2)}) copy-start(bf16[384,1536]{1,0:T(8,128)(2,1)} %param.5) | copy-start | bytes 3538948
  2.4 28.7 %all-to-all-start = ((bf16[8,64,768]{2,1,0:T(8,128)(2,1)}), bf16[8,64,768]{2,1,0:T(8,128)(2,1)S(1)}, u32[]{:S(2)}, u32[]{:S(2)}) async-start(bf16[8,64,768]{2,1,0:T(8,128)(2,1)} %broadcast_in_dim.12), calls=%async_computation | async-start | bytes 1572864 | tf_op jit(solution)/shard_map/all_to_all | solution.py:27
  10.1 4.9 %copy-start.1 = (bf16[1536,384]{1,0:T(8,128)(2,1)S(1)}, bf16[1536,384]{1,0:T(8,128)(2,1)}, u32[]{:S(2)}) copy-start(bf16[1536,384]{1,0:T(8,128)(2,1)} %param.6) | copy-start | bytes 3538948
  10.2 6.9 %collective-permute-start = (bf16[384,768]{1,0:T(8,128)(2,1)S(1)}, bf16[384,768]{1,0:T(8,128)(2,1)S(1)}, u32[]{:S(2)}, u32[]{:S(2)}) collective-permute-start(bf16[384,768]{1,0:T(8,128)(2,1)S(1)} %get-tuple-element.35), channel_id=1, source_target_pairs={{0,4},{4,0},{1,5},{5,1},{2,6},{6,2},{3,7},{7,3},{8,12},{12,8},{9,1... | collective-permute-start | bytes 1769480 | tf_op jit(solution)/shard_map/ppermute | solution.py:23
  15.2 3.9 %collective-permute-start.1 = (bf16[768,384]{1,0:T(8,128)(2,1)S(1)}, bf16[768,384]{1,0:T(8,128)(2,1)S(1)}, u32[]{:S(2)}, u32[]{:S(2)}) collective-permute-start(bf16[768,384]{1,0:T(8,128)(2,1)S(1)} %get-tuple-element.33), channel_id=1, source_target_pairs={{0,4},{4,0},{1,5},{5,1},{2,6},{6,2},{3,7},{7,3},{8,12},{12,8},{9,1... | collective-permute-start | bytes 1769480 | tf_op jit(solution)/shard_map/ppermute | solution.py:23
  31.1 7.0 %collective-permute-start.2 = (bf16[512,768]{1,0:T(8,128)(2,1)S(1)}, bf16[512,768]{1,0:T(8,128)(2,1)}, u32[]{:S(2)}, u32[]{:S(2)}) collective-permute-start(bf16[512,768]{1,0:T(8,128)(2,1)S(1)} %bitcast.40), channel_id=1, source_target_pairs={{0,4},{4,0},{1,5},{5,1},{2,6},{6,2},{3,7},{7,3},{8,12},{12,8},{9,1... | collective-permute-start | bytes 2359304 | tf_op jit(solution)/shard_map/ppermute | solution.py:23
  36.2 3.7 %copy-start.3 = (bf16[256,384]{1,0:T(8,128)(2,1)}, bf16[256,384]{1,0:T(8,128)(2,1)S(1)}, u32[]{:S(2)}) copy-start(bf16[256,384]{1,0:T(8,128)(2,1)S(1)} %get-tuple-element.65) | copy-start | bytes 589828
  39.4 0.7 copy-start.4
  40.6 19.8 %collective-permute-start.4 = (bf16[256,768]{1,0:T(8,128)(2,1)S(1)}, bf16[256,768]{1,0:T(8,128)(2,1)S(1)}, u32[]{:S(2)}, u32[]{:S(2)}) collective-permute-start(bf16[256,768]{1,0:T(8,128)(2,1)S(1)} %convolution_convert_fusion.8), channel_id=1, source_target_pairs={{0,56},{8,16},{16,8},{24,32},{32,24},{40,48},{48,40},{56,0},{1,57}... | collective-permute-start | bytes 1179656 | tf_op jit(solution)/shard_map/ppermute | solution.py:65
  51.2 11.9 %collective-permute-start.3 = (bf16[256,768]{1,0:T(8,128)(2,1)S(1)}, bf16[256,768]{1,0:T(8,128)(2,1)S(1)}, u32[]{:S(2)}, u32[]{:S(2)}) collective-permute-start(bf16[256,768]{1,0:T(8,128)(2,1)S(1)} %convolution_convert_fusion.9), channel_id=1, source_target_pairs={{0,8},{8,0},{16,24},{24,16},{32,40},{40,32},{48,56},{56,48},{1,9},... | collective-permute-start | bytes 1179656 | tf_op jit(solution)/shard_map/ppermute | solution.py:65
  100.5 11.9 %collective-permute-start.5 = (bf16[256,768]{1,0:T(8,128)(2,1)}, bf16[256,768]{1,0:T(8,128)(2,1)}, u32[]{:S(2)}, u32[]{:S(2)}) collective-permute-start(bf16[256,768]{1,0:T(8,128)(2,1)} %get-tuple-element.25), channel_id=1, source_target_pairs={{0,8},{8,0},{16,24},{24,16},{32,40},{40,32},{48,56},{56,48},{1,9},... | collective-permute-start | bytes 1179656 | tf_op jit(solution)/shard_map/ppermute | solution.py:65
  107.0 11.0 %collective-permute-start.7 = (bf16[256,768]{1,0:T(8,128)(2,1)}, bf16[256,768]{1,0:T(8,128)(2,1)S(1)}, u32[]{:S(2)}, u32[]{:S(2)}) collective-permute-start(bf16[256,768]{1,0:T(8,128)(2,1)} %get-tuple-element.27), channel_id=1, source_target_pairs={{0,56},{8,16},{16,8},{24,32},{32,24},{40,48},{48,40},{56,0},{1,57}... | collective-permute-start | bytes 1179656 | tf_op jit(solution)/shard_map/ppermute | solution.py:65
  114.5 10.6 %collective-permute-start.6 = (bf16[384,768]{1,0:T(8,128)(2,1)S(1)}, bf16[384,768]{1,0:T(8,128)(2,1)S(1)}, u32[]{:S(2)}, u32[]{:S(2)}) collective-permute-start(bf16[384,768]{1,0:T(8,128)(2,1)S(1)} %dynamic-slice_bitcast_fusion.1), channel_id=1, source_target_pairs={{0,1},{1,0},{2,3},{3,2},{4,5},{5,4},{6,7},{7,6},{8,9},{9,8},{10,11... | collective-permute-start | bytes 1769480 | tf_op jit(solution)/shard_map/ppermute | solution.py:125
  117.7 1.0 copy-start.2
  119.9 20.1 %collective-permute-start.10 = (bf16[384,768]{1,0:T(8,128)(2,1)S(1)}, bf16[384,768]{1,0:T(8,128)(2,1)S(1)}, u32[]{:S(2)}, u32[]{:S(2)}) collective-permute-start(bf16[384,768]{1,0:T(8,128)(2,1)S(1)} %dynamic-slice_bitcast_fusion), channel_id=1, source_target_pairs={{0,3},{1,2},{2,1},{3,0},{4,7},{5,6},{6,5},{7,4},{8,11},{9,10},{10,... | collective-permute-start | bytes 1769480 | tf_op jit(solution)/shard_map/ppermute | solution.py:136
  125.4 14.6 %collective-permute-start.9 = (bf16[384,384]{1,0:T(8,128)(2,1)S(1)}, bf16[384,384]{1,0:T(8,128)(2,1)S(1)}, u32[]{:S(2)}, u32[]{:S(2)}) collective-permute-start(bf16[384,384]{1,0:T(8,128)(2,1)S(1)} %get-tuple-element.47), channel_id=1, source_target_pairs={{0,4},{4,0},{1,5},{5,1},{2,6},{6,2},{3,7},{7,3},{8,12},{12,8},{9,1... | collective-permute-start | bytes 884744 | tf_op jit(solution)/shard_map/ppermute | solution.py:23
  138.1 22.6 %collective-permute-start.8 = (bf16[512,768]{0,1:T(8,128)(2,1)S(1)}, bf16[512,768]{0,1:T(8,128)(2,1)S(1)}, u32[]{:S(2)}, u32[]{:S(2)}) collective-permute-start(bf16[512,768]{0,1:T(8,128)(2,1)S(1)} %pad_maximum_fusion.3), channel_id=1, source_target_pairs={{0,4},{4,0},{1,5},{5,1},{2,6},{6,2},{3,7},{7,3},{8,12},{12,8},{9,1... | collective-permute-start | bytes 2359304 | tf_op jit(solution)/shard_map/ppermute | solution.py:23
  140.2 16.3 %collective-permute-start.11 = (bf16[384,768]{1,0:T(8,128)(2,1)S(1)}, bf16[384,768]{1,0:T(8,128)(2,1)S(1)}, u32[]{:S(2)}, u32[]{:S(2)}) collective-permute-start(bf16[384,768]{1,0:T(8,128)(2,1)S(1)} %fusion.2), channel_id=1, source_target_pairs={{0,1},{1,0},{2,3},{3,2},{4,5},{5,4},{6,7},{7,6},{8,9},{9,8},{10,11... | collective-permute-start | bytes 1769480 | tf_op jit(solution)/shard_map/ppermute | solution.py:142
  145.8 19.8 %collective-permute-start.14 = (bf16[2,384,384]{2,1,0:T(8,128)(2,1)S(1)}, bf16[2,384,384]{2,1,0:T(8,128)(2,1)S(1)}, u32[]{:S(2)}, u32[]{:S(2)}) collective-permute-start(bf16[2,384,384]{2,1,0:T(8,128)(2,1)S(1)} %maximum_select_fusion.5), channel_id=1, source_target_pairs={{0,3},{1,2},{2,1},{3,0},{4,7},{5,6},{6,5},{7,4},{8,11},{9,10},{10,... | collective-permute-start | bytes 1769480 | tf_op jit(solution)/shard_map/ppermute | solution.py:141
  157.4 11.5 %collective-permute-start.12 = (bf16[192,768]{1,0:T(8,128)(2,1)}, bf16[192,768]{1,0:T(8,128)(2,1)}, u32[]{:S(2)}, u32[]{:S(2)}) collective-permute-start(bf16[192,768]{1,0:T(8,128)(2,1)} %get-tuple-element.49), channel_id=1, source_target_pairs={{0,4},{4,0},{1,5},{5,1},{2,6},{6,2},{3,7},{7,3},{8,12},{12,8},{9,1... | collective-permute-start | bytes 884744 | tf_op jit(solution)/shard_map/ppermute | solution.py:23
  162.0 27.2 %all-to-all-start.2 = ((bf16[8,64,768]{2,1,0:T(8,128)(2,1)}), bf16[8,64,768]{2,1,0:T(8,128)(2,1)S(1)}, u32[]{:S(2)}, u32[]{:S(2)}) async-start(bf16[8,64,768]{2,1,0:T(8,128)(2,1)} %bitcast.12), calls=%async_computation.2 | async-start | bytes 1572864 | tf_op jit(solution)/shard_map/all_to_all | solution.py:27
  165.8 16.8 %collective-permute-start.15 = (bf16[2,384,384]{2,1,0:T(8,128)(2,1)S(1)}, bf16[2,384,384]{2,1,0:T(8,128)(2,1)S(1)}, u32[]{:S(2)}, u32[]{:S(2)}) collective-permute-start(bf16[2,384,384]{2,1,0:T(8,128)(2,1)S(1)} %add_convert_fusion.1), channel_id=1, source_target_pairs={{0,1},{1,0},{2,3},{3,2},{4,5},{5,4},{6,7},{7,6},{8,9},{9,8},{10,11... | collective-permute-start | bytes 1769480 | tf_op jit(solution)/shard_map/ppermute | solution.py:143
  170.1 17.7 %collective-permute-start.13 = (bf16[192,1536]{1,0:T(8,128)(2,1)S(1)}, bf16[192,1536]{1,0:T(8,128)(2,1)S(1)}, u32[]{:S(2)}, u32[]{:S(2)}) collective-permute-start(bf16[192,1536]{1,0:T(8,128)(2,1)S(1)} %maximum_select_fusion.4), channel_id=1, source_target_pairs={{0,3},{1,2},{2,1},{3,0},{4,7},{5,6},{6,5},{7,4},{8,11},{9,10},{10,... | collective-permute-start | bytes 1769480 | tf_op jit(solution)/shard_map/ppermute | solution.py:146

commit v13 on v11

--- a/solution.py
+++ b/solution.py
@@ -126,13 +126,15 @@
 
     turn, high = (rep + 1) // 2 % 2, rep // 2
     down_part = dot(act, og, (0, 0)).reshape(2, half // 2, 2 * width)
-    cut = width // 2
-    order = [tok[:, i * cut : (i + 1) * cut] for i in (0, 2, 1, 3)]
-    up_part = dot(jnp.concatenate(order, 1), hg, (0, 0)).reshape(2, width, half)
     down_part = scatter(down_part, 0, turn, near)
     down_part, act_half, act_got, hg_half, hg_got = barrier(
         (down_part, act_half, act_got, hg_half, hg_got)
     )
+    cut = width // 2
+    order = [tok[:, i * cut : (i + 1) * cut] for i in (0, 2, 1, 3)]
+    up_part = dot(jnp.concatenate(order, 1), hg, (0, 0)).reshape(2, width, half)
+    up_got = lax.ppermute(pick(up_part, 1 - high), "rep", far)
+
     act, hg = pair(act_half, act_got, zl, 0), pair(hg_half, hg_got, zl, 0)
 
     def output(columns):
@@ -141,11 +143,8 @@
         return jnp.concatenate([block, token], 1)
 
     send = output(slice(width, None))
-    up_keep, up_got = pick(up_part, high), lax.ppermute(
-        pick(up_part, 1 - high), "rep", far
-    )
-    up_got, send, keep = barrier((up_got, send, output(slice(width))))
-    up_part = plus(up_keep, up_got)
+    up_got, send = barrier((up_got, send))
+    up_part = plus(pick(up_part, high), up_got)
     down_part = plus(down_part, lax.ppermute(down_part, "rep", far))
     up_part = plus(up_part, lax.ppermute(up_part, "rep", near))
     down_own, down_got = down_part[:, :width], swap(down_part[:, width:])
@@ -155,7 +154,7 @@
     up_part = pair(up_part[:cut], swap(up_part[cut:]), core, 1)
     up_grads = pair(up_part, lax.ppermute(up_part, "rep", far), high, 0)
 
-    out = plus(keep, swap(send))
+    out = plus(output(slice(width)), swap(send))
     out = total_of(exchange(out.reshape(n_row, rows, 2 * width), "row")).astype(bf16)
     return (out[:, :width], out[:, width:], up_grads, down_grads)
 

time: 194 us -> 188 us (0.969)
  blocking collectives: 41.7 us -> 35.7 us
  starting transfers between devices: 77.8 us -> 80.8 us
  waiting for transfers between devices: 50.2 us -> 47.7 us
    all_to_all x1, blocking collectives: 24.8 us -> 19.8 us  [exchange(): return lax.all_to_all(x, axis, 0, 0, tiled=False)]
    ppermute x1, waiting for transfers between devices: 0.01 us -> 3.94 us  [per_device(): up_got = lax.ppermute(pick(up_part, 1 - high), 'rep', far)]
    ppermute x1, waiting for transfers between devices: 4.96 us -> 1.95 us  [scatter(): return plus(at(bit), lax.ppermute(at(1 - bit), 'rep', pairs))]
    ppermute x4, starting transfers between devices: 18.6 us -> 21.5 us  [z_swap(): return lax.ppermute(x, ('zh', 'zl'), pairs)]
    ppermute x1, starting transfers between devices: 2.53 us -> 4.53 us  [per_device(): up_grads = pair(up_part, lax.ppermute(up_part, 'rep', far), high, 0)]
    ppermute x6, starting transfers between devices: 27.3 us -> 29.3 us  [swap(): return lax.ppermute(x, 'core', [(0, 1), (1, 0)])]
    ppermute x1, starting transfers between devices: 5.06 us -> 3.11 us  [scatter(): return plus(at(bit), lax.ppermute(at(1 - bit), 'rep', pairs))]
where the time goes in v13:
time: 188 us; the launch traced here: 187 us
  starting transfers between devices  80.8 us (43%)
  waiting for transfers between devices  47.7 us (25%)
  blocking collectives  35.7 us (19%)
  matrix products  9.92 us (5%)
  local copies, waits for them, and re-layouts  6.56 us (3%)
  other arithmetic  5.43 us (3%)
    ppermute x6, starting transfers between devices, swap(): return lax.ppermute(x, 'core', [(0, 1), (1, 0)])  29.3 us
    ppermute x4, starting transfers between devices, z_swap(): return lax.ppermute(x, ('zh', 'zl'), pairs)  21.5 us
    all_to_all x1, blocking collectives, exchange(): return lax.all_to_all(x, axis, 0, 0, tiled=False)  19.8 us
    all_gather x1, blocking collectives, per_device(): lax.all_gather(jnp.concatenate([act, hid_grads], 1), 'zh', axis=0, tiled=...  15.9 us
    all_to_all x2, waiting for transfers between devices, exchange(): return lax.all_to_all(x, axis, 0, 0, tiled=False)  14 us
    ppermute x4, waiting for transfers between devices, z_swap(): return lax.ppermute(x, ('zh', 'zl'), pairs)  12.3 us
    all_to_all x2, starting transfers between devices, exchange(): return lax.all_to_all(x, axis, 0, 0, tiled=False)  11.2 us
    ppermute x1, waiting for transfers between devices, per_device(): down_part = pair(down_part, lax.ppermute(down_part, 'rep', near), turn, 1)  10 us
  transfers between devices with their start and end apart: 18, of which 11 were waited for; matrix products, arithmetic and copies ran while one was open for 8% of the time, Pallas kernels for 0%

profile of v13, /device:TPU:1, one launch (start us, length us, event | category | flops | bytes accessed | tf_op | source)
XLA Modules:
  0.0 187.3 jit_solution(8378592728255415107)
XLA Ops:
  0.6 0.8 pad_maximum_fusion.7
  1.5 0.9 broadcast_in_dim.12
  2.4 7.7 %all-to-all-start = ((bf16[8,64,768]{2,1,0:T(8,128)(2,1)}), bf16[8,64,768]{2,1,0:T(8,128)(2,1)S(1)}, u32[]{:S(2)}, u32[]{:S(2)}) async-start(bf16[8,64,768]{2,1,0:T(8,128)(2,1)} %broadcast_in_dim.12), calls=%async_computation | async-start | bytes 1572864 | tf_op jit(solution)/shard_map/all_to_all | solution.py:27
  10.2 4.8 %collective-permute-start = (bf16[384,768]{1,0:T(8,128)(2,1)S(1)}, bf16[384,768]{1,0:T(8,128)(2,1)S(1)}, u32[]{:S(2)}, u32[]{:S(2)}) collective-permute-start(bf16[384,768]{1,0:T(8,128)(2,1)S(1)} %get-tuple-element.35), channel_id=1, source_target_pairs={{0,4},{4,0},{1,5},{5,1},{2,6},{6,2},{3,7},{7,3},{8,12},{12,8},{9,1... | collective-permute-start | bytes 1769480 | tf_op jit(solution)/shard_map/ppermute | solution.py:23
  15.0 0.1 constant_dynamic-slice_fusion.1
  15.2 1.9 %collective-permute-start.1 = (bf16[768,384]{1,0:T(8,128)(2,1)S(1)}, bf16[768,384]{1,0:T(8,128)(2,1)S(1)}, u32[]{:S(2)}, u32[]{:S(2)}) collective-permute-start(bf16[768,384]{1,0:T(8,128)(2,1)S(1)} %get-tuple-element.33), channel_id=1, source_target_pairs={{0,4},{4,0},{1,5},{5,1},{2,6},{6,2},{3,7},{7,3},{8,12},{12,8},{9,1... | collective-permute-start | bytes 1769480 | tf_op jit(solution)/shard_map/ppermute | solution.py:23
  17.2 1.9 collective-permute-done.1
  19.1 0.1 pad_maximum_fusion.1
  19.2 11.9 %all-to-all-done = bf16[8,64,768]{2,1,0:T(8,128)(2,1)S(1)} async-done(((bf16[8,64,768]{2,1,0:T(8,128)(2,1)}), bf16[8,64,768]{2,1,0:T(8,128)(2,1)S(1)}, u32[]{:S(2)}, u32[]{:S(2)}) %all-to-all-start) | async-done | bytes 786464 | tf_op jit(solution)/shard_map/all_to_all | solution.py:27
  31.1 5.0 %collective-permute-start.2 = (bf16[512,768]{1,0:T(8,128)(2,1)S(1)}, bf16[512,768]{1,0:T(8,128)(2,1)}, u32[]{:S(2)}, u32[]{:S(2)}) collective-permute-start(bf16[512,768]{1,0:T(8,128)(2,1)S(1)} %bitcast.40), channel_id=1, source_target_pairs={{0,4},{4,0},{1,5},{5,1},{2,6},{6,2},{3,7},{7,3},{8,12},{12,8},{9,1... | collective-permute-start | bytes 2359304 | tf_op jit(solution)/shard_map/ppermute | solution.py:23
  36.3 1.8 collective-permute-done.2
  38.1 1.2 dynamic-slice_bitcast_fusion.2
  39.5 0.5 convolution_convert_fusion.9
  40.0 0.1 copy-done.4
  40.0 0.5 convolution_convert_fusion.8
  40.6 10.6 %collective-permute-start.4 = (bf16[256,768]{1,0:T(8,128)(2,1)S(1)}, bf16[256,768]{1,0:T(8,128)(2,1)S(1)}, u32[]{:S(2)}, u32[]{:S(2)}) collective-permute-start(bf16[256,768]{1,0:T(8,128)(2,1)S(1)} %convolution_convert_fusion.8), channel_id=1, source_target_pairs={{0,56},{8,16},{16,8},{24,32},{32,24},{40,48},{48,40},{56,0},{1,57}... | collective-permute-start | bytes 1179656 | tf_op jit(solution)/shard_map/ppermute | solution.py:65
  51.2 1.9 %collective-permute-start.3 = (bf16[256,768]{1,0:T(8,128)(2,1)S(1)}, bf16[256,768]{1,0:T(8,128)(2,1)S(1)}, u32[]{:S(2)}, u32[]{:S(2)}) collective-permute-start(bf16[256,768]{1,0:T(8,128)(2,1)S(1)} %convolution_convert_fusion.9), channel_id=1, source_target_pairs={{0,8},{8,0},{16,24},{24,16},{32,40},{40,32},{48,56},{56,48},{1,9},... | collective-permute-start | bytes 1179656 | tf_op jit(solution)/shard_map/ppermute | solution.py:65
  53.1 7.2 %collective-permute-done.4 = bf16[256,768]{1,0:T(8,128)(2,1)S(1)} collective-permute-done((bf16[256,768]{1,0:T(8,128)(2,1)S(1)}, bf16[256,768]{1,0:T(8,128)(2,1)S(1)}, u32[]{:S(2)}, u32[]{:S(2)}) %collective-permute-start.4) | collective-permute-done | bytes 393248 | tf_op jit(solution)/shard_map/ppermute | solution.py:65
  60.4 0.5 add_convert_fusion.3
  60.9 2.2 %collective-permute-done.3 = bf16[256,768]{1,0:T(8,128)(2,1)S(1)} collective-permute-done((bf16[256,768]{1,0:T(8,128)(2,1)S(1)}, bf16[256,768]{1,0:T(8,128)(2,1)S(1)}, u32[]{:S(2)}, u32[]{:S(2)}) %collective-permute-start.3) | collective-permute-done | bytes 393248 | tf_op jit(solution)/shard_map/ppermute | solution.py:65
  63.1 0.5 add_convert_fusion.4
  63.6 19.8 %all_to_all.15 = bf16[4,64,1536]{2,1,0:T(8,128)(2,1)S(1)} all-to-all(bf16[4,64,1536]{2,1,0:T(8,128)(2,1)S(1)} %bitcast.39), channel_id=1, replica_groups=mesh['row'=8,'zh'=4,'zl'=2,'core'=2,'rep'=4] {'zh'}, dimensions={0} | all-to-all | bytes 1572864 | tf_op jit(solution)/shard_map/all_to_all | solution.py:27
  83.4 0.1 add_bitcast_fusion
  83.5 0.1 multiply_convert_fusion
  83.7 15.9 %all_gather.3 = bf16[256,1536]{1,0:T(8,128)(2,1)S(1)} all-gather(bf16[64,1536]{1,0:T(8,128)(2,1)S(1)} %pad_maximum_fusion.6), channel_id=1, replica_groups=mesh['row'=8,'zh'=4,'zl'=2,'core'=2,'rep'=4] {'zh'}, dimensions={0}, use_global_device_ids=true | all-gather | bytes 983040 | tf_op jit(solution)/shard_map/all_gather | solution.py:112
  99.6 0.9 fusion.48
  100.5 6.4 %collective-permute-start.5 = (bf16[256,768]{1,0:T(8,128)(2,1)}, bf16[256,768]{1,0:T(8,128)(2,1)}, u32[]{:S(2)}, u32[]{:S(2)}) collective-permute-start(bf16[256,768]{1,0:T(8,128)(2,1)} %get-tuple-element.25), channel_id=1, source_target_pairs={{0,8},{8,0},{16,24},{24,16},{32,40},{40,32},{48,56},{56,48},{1,9},... | collective-permute-start | bytes 1179656 | tf_op jit(solution)/shard_map/ppermute | solution.py:65
  107.0 2.5 %collective-permute-start.7 = (bf16[256,768]{1,0:T(8,128)(2,1)}, bf16[256,768]{1,0:T(8,128)(2,1)S(1)}, u32[]{:S(2)}, u32[]{:S(2)}) collective-permute-start(bf16[256,768]{1,0:T(8,128)(2,1)} %get-tuple-element.27), channel_id=1, source_target_pairs={{0,56},{8,16},{16,8},{24,32},{32,24},{40,48},{48,40},{56,0},{1,57}... | collective-permute-start | bytes 1179656 | tf_op jit(solution)/shard_map/ppermute | solution.py:65
  109.5 2.9 %collective-permute-done.5 = bf16[256,768]{1,0:T(8,128)(2,1)} collective-permute-done((bf16[256,768]{1,0:T(8,128)(2,1)}, bf16[256,768]{1,0:T(8,128)(2,1)}, u32[]{:S(2)}, u32[]{:S(2)}) %collective-permute-start.5) | collective-permute-done | bytes 393248 | tf_op jit(solution)/shard_map/ppermute | solution.py:65
  112.4 2.0 %convolution_convert_fusion.1 = bf16[768,768]{1,0:T(8,128)(2,1)S(1)} fusion(bf16[256,768]{1,0:T(8,128)(2,1)} %collective-permute-done.5, bf16[256,768]{1,0:T(8,128)(2,1)} %get-tuple-element.25, bf16[256,384]{1,0:T(8,128)(2,1)} %copy-done.4, bf16[256,384]{1,0:T(8,128)(2,1)} %copy-done.3, bf16[256,768]{1,0:T(8,128)(2,1)S(1)} %pad_maximum_fusion.5), kind=kOutput, calls=%fused_computation.2 | convolution fusion | flops 608501760 | bytes 2752512 | tf_op jit(solution)/shard_map/dot_general | solution.py:17
  114.5 3.1 %collective-permute-start.6 = (bf16[384,768]{1,0:T(8,128)(2,1)S(1)}, bf16[384,768]{1,0:T(8,128)(2,1)S(1)}, u32[]{:S(2)}, u32[]{:S(2)}) collective-permute-start(bf16[384,768]{1,0:T(8,128)(2,1)S(1)} %dynamic-slice_bitcast_fusion.1), channel_id=1, source_target_pairs={{0,1},{1,0},{2,3},{3,2},{4,5},{5,4},{6,7},{7,6},{8,9},{9,8},{10,11... | collective-permute-start | bytes 1769480 | tf_op jit(solution)/shard_map/ppermute | solution.py:125
  117.7 0.2 fusion.49
  118.0 0.7 copy-done.2
  118.7 1.1 convolution_convert_fusion
  119.9 3.3 %collective-permute-start.8 = (bf16[384,768]{1,0:T(8,128)(2,1)S(1)}, bf16[384,768]{1,0:T(8,128)(2,1)S(1)}, u32[]{:S(2)}, u32[]{:S(2)}) collective-permute-start(bf16[384,768]{1,0:T(8,128)(2,1)S(1)} %dynamic-slice_bitcast_fusion), channel_id=1, source_target_pairs={{0,3},{1,2},{2,1},{3,0},{4,7},{5,6},{6,5},{7,4},{8,11},{9,10},{10,... | collective-permute-start | bytes 1769480 | tf_op jit(solution)/shard_map/ppermute | solution.py:136
  123.2 2.0 %collective-permute-done.6 = bf16[384,768]{1,0:T(8,128)(2,1)S(1)} collective-permute-done((bf16[384,768]{1,0:T(8,128)(2,1)S(1)}, bf16[384,768]{1,0:T(8,128)(2,1)S(1)}, u32[]{:S(2)}, u32[]{:S(2)}) %collective-permute-start.6) | collective-permute-done | bytes 589856 | tf_op jit(solution)/shard_map/ppermute | solution.py:125
  125.1 0.2 fusion.3
  125.3 0.5 convolution_convert_fusion.2
  125.8 1.9 %convolution_convert_fusion.3 = bf16[512,384]{0,1:T(8,128)(2,1)S(1)} fusion(bf16[768,768]{1,0:T(8,128)(2,1)S(1)} %pad_maximum_fusion.1, bf16[256,768]{1,0:T(8,128)(2,1)} %collective-permute-done.5, bf16[256,768]{1,0:T(8,128)(2,1)} %get-tuple-element.25, pred[]{:T(512)S(6)} %eq.16), kind=kOutput, calls=%fused_computation.4 | convolution fusion | flops 305725440 | bytes 1769473 | tf_op jit(solution)/shard_map/dot_general | solution.py:17
  127.8 3.9 %collective-permute-done.8 = bf16[384,768]{1,0:T(8,128)(2,1)S(1)} collective-permute-done((bf16[384,768]{1,0:T(8,128)(2,1)S(1)}, bf16[384,768]{1,0:T(8,128)(2,1)S(1)}, u32[]{:S(2)}, u32[]{:S(2)}) %collective-permute-start.8) | collective-permute-done | bytes 589856 | tf_op jit(solution)/shard_map/ppermute | solution.py:136
  131.7 0.2 fusion.2
  131.9 1.9 %collective-permute-start.10 = (bf16[384,768]{1,0:T(8,128)(2,1)S(1)}, bf16[384,768]{1,0:T(8,128)(2,1)S(1)}, u32[]{:S(2)}, u32[]{:S(2)}) collective-permute-start(bf16[384,768]{1,0:T(8,128)(2,1)S(1)} %fusion.2), channel_id=1, source_target_pairs={{0,1},{1,0},{2,3},{3,2},{4,5},{5,4},{6,7},{7,6},{8,9},{9,8},{10,11... | collective-permute-start | bytes 1769480 | tf_op jit(solution)/shard_map/ppermute | solution.py:149
  133.8 3.8 %collective-permute-start.13 = (bf16[384,768]{1,0:T(8,128)(2,1)S(1)}, bf16[384,768]{1,0:T(8,128)(2,1)S(1)}, u32[]{:S(2)}, u32[]{:S(2)}) collective-permute-start(bf16[384,768]{1,0:T(8,128)(2,1)S(1)} %fusion.3), channel_id=1, source_target_pairs={{0,3},{1,2},{2,1},{3,0},{4,7},{5,6},{6,5},{7,4},{8,11},{9,10},{10,... | collective-permute-start | bytes 1769480 | tf_op jit(solution)/shard_map/ppermute | solution.py:148
  137.6 0.5 convolution_convert_fusion.4
  138.1 1.9 %convolution_convert_fusion.5 = bf16[512,384]{0,1:T(8,128)(2,1)S(1)} fusion(bf16[768,768]{1,0:T(8,128)(2,1)S(1)} %pad_maximum_fusion.1, bf16[256,768]{1,0:T(8,128)(2,1)} %collective-permute-done.5, bf16[256,768]{1,0:T(8,128)(2,1)} %get-tuple-element.25, pred[]{:T(512)S(6)} %eq.16), kind=kOutput, calls=%fused_computation.6 | convolution fusion | flops 305725440 | bytes 1769473 | tf_op jit(solution)/shard_map/dot_general | solution.py:17
  140.0 12.2 %collective-permute-start.9 = (bf16[512,768]{0,1:T(8,128)(2,1)S(1)}, bf16[512,768]{0,1:T(8,128)(2,1)S(1)}, u32[]{:S(2)}, u32[]{:S(2)}) collective-permute-start(bf16[512,768]{0,1:T(8,128)(2,1)S(1)} %pad_maximum_fusion.3), channel_id=1, source_target_pairs={{0,4},{4,0},{1,5},{5,1},{2,6},{6,2},{3,7},{7,3},{8,12},{12,8},{9,1... | collective-permute-start | bytes 2359304 | tf_op jit(solution)/shard_map/ppermute | solution.py:23
  152.3 0.1 add_convert_fusion.2
  152.5 2.1 %collective-permute-start.11 = (bf16[192,768]{1,0:T(8,128)(2,1)S(1)}, bf16[192,768]{1,0:T(8,128)(2,1)S(1)}, u32[]{:S(2)}, u32[]{:S(2)}) collective-permute-start(bf16[192,768]{1,0:T(8,128)(2,1)S(1)} %get-tuple-element.49), channel_id=1, source_target_pairs={{0,4},{4,0},{1,5},{5,1},{2,6},{6,2},{3,7},{7,3},{8,12},{12,8},{9,1... | collective-permute-start | bytes 884744 | tf_op jit(solution)/shard_map/ppermute | solution.py:23
  154.6 0.1 add_convert_fusion.1
  154.8 3.3 %collective-permute-start.14 = (bf16[384,384]{1,0:T(8,128)(2,1)S(1)}, bf16[384,384]{1,0:T(8,128)(2,1)S(1)}, u32[]{:S(2)}, u32[]{:S(2)}) collective-permute-start(bf16[384,384]{1,0:T(8,128)(2,1)S(1)} %get-tuple-element.47), channel_id=1, source_target_pairs={{0,4},{4,0},{1,5},{5,1},{2,6},{6,2},{3,7},{7,3},{8,12},{12,8},{9,1... | collective-permute-start | bytes 884744 | tf_op jit(solution)/shard_map/ppermute | solution.py:23
  158.1 0.2 add_convert_fusion
  158.3 1.2 copy.9
  159.4 3.5 %all-to-all-start.2 = ((bf16[8,64,768]{2,1,0:T(8,128)(2,1)}), bf16[8,64,768]{2,1,0:T(8,128)(2,1)S(1)}, u32[]{:S(2)}, u32[]{:S(2)}) async-start(bf16[8,64,768]{2,1,0:T(8,128)(2,1)} %bitcast.14), calls=%async_computation.2 | async-start | bytes 1572864 | tf_op jit(solution)/shard_map/all_to_all | solution.py:27
  163.0 0.1 maximum_select_fusion.5
  163.1 2.1 %collective-permute-start.15 = (bf16[2,384,384]{2,1,0:T(8,128)(2,1)S(1)}, bf16[2,384,384]{2,1,0:T(8,128)(2,1)S(1)}, u32[]{:S(2)}, u32[]{:S(2)}) collective-permute-start(bf16[2,384,384]{2,1,0:T(8,128)(2,1)S(1)} %maximum_select_fusion.5), channel_id=1, source_target_pairs={{0,1},{1,0},{2,3},{3,2},{4,5},{5,4},{6,7},{7,6},{8,9},{9,8},{10,11... | collective-permute-start | bytes 1769480 | tf_op jit(solution)/shard_map/ppermute | solution.py:152
  165.2 0.1 maximum_select_fusion.4
  165.4 4.5 %collective-permute-start.12 = (bf16[192,1536]{1,0:T(8,128)(2,1)S(1)}, bf16[192,1536]{1,0:T(8,128)(2,1)S(1)}, u32[]{:S(2)}, u32[]{:S(2)}) collective-permute-start(bf16[192,1536]{1,0:T(8,128)(2,1)S(1)} %maximum_select_fusion.4), channel_id=1, source_target_pairs={{0,3},{1,2},{2,1},{3,0},{4,7},{5,6},{6,5},{7,4},{8,11},{9,10},{10,... | collective-permute-start | bytes 1769480 | tf_op jit(solution)/shard_map/ppermute | solution.py:155
  169.9 10.0 %collective-permute-done.15 = bf16[2,384,384]{2,1,0:T(8,128)(2,1)S(1)} collective-permute-done((bf16[2,384,384]{2,1,0:T(8,128)(2,1)S(1)}, bf16[2,384,384]{2,1,0:T(8,128)(2,1)S(1)}, u32[]{:S(2)}, u32[]{:S(2)}) %collective-permute-start.15) | collective-permute-done | bytes 589856 | tf_op jit(solution)/shard_map/ppermute | solution.py:152
  180.0 1.4 maximum_select_fusion.1
  181.3 1.8 collective-permute-done.12
  183.1 1.4 maximum_select_fusion
  184.5 2.1 %all-to-all-done.2 = bf16[8,64,768]{2,1,0:T(8,128)(2,1)S(1)} async-done(((bf16[8,64,768]{2,1,0:T(8,128)(2,1)}), bf16[8,64,768]{2,1,0:T(8,128)(2,1)S(1)}, u32[]{:S(2)}, u32[]{:S(2)}) %all-to-all-start.2) | async-done | bytes 786464 | tf_op jit(solution)/shard_map/all_to_all | solution.py:27
  186.6 0.1 fusion.39
  186.7 0.6 fusion.55
  (30 shorter events, 0.9 us)
Async XLA Ops:
  1.5 8.6 %copy-start = (bf16[384,1536]{1,0:T(8,128)(2,1)S(1)}, bf16[384,1536]{1,0:T(8,128)(2,1)}, u32[]{:S(2)}) copy-start(bf16[384,1536]{1,0:T(8,128)(2,1)} %param.5) | copy-start | bytes 3538948
  2.4 28.7 %all-to-all-start = ((bf16[8,64,768]{2,1,0:T(8,128)(2,1)}), bf16[8,64,768]{2,1,0:T(8,128)(2,1)S(1)}, u32[]{:S(2)}, u32[]{:S(2)}) async-start(bf16[8,64,768]{2,1,0:T(8,128)(2,1)} %broadcast_in_dim.12), calls=%async_computation | async-start | bytes 1572864 | tf_op jit(solution)/shard_map/all_to_all | solution.py:27
  10.1 4.9 %copy-start.1 = (bf16[1536,384]{1,0:T(8,128)(2,1)S(1)}, bf16[1536,384]{1,0:T(8,128)(2,1)}, u32[]{:S(2)}) copy-start(bf16[1536,384]{1,0:T(8,128)(2,1)} %param.6) | copy-start | bytes 3538948
  10.2 6.9 %collective-permute-start = (bf16[384,768]{1,0:T(8,128)(2,1)S(1)}, bf16[384,768]{1,0:T(8,128)(2,1)S(1)}, u32[]{:S(2)}, u32[]{:S(2)}) collective-permute-start(bf16[384,768]{1,0:T(8,128)(2,1)S(1)} %get-tuple-element.35), channel_id=1, source_target_pairs={{0,4},{4,0},{1,5},{5,1},{2,6},{6,2},{3,7},{7,3},{8,12},{12,8},{9,1... | collective-permute-start | bytes 1769480 | tf_op jit(solution)/shard_map/ppermute | solution.py:23
  15.2 3.9 %collective-permute-start.1 = (bf16[768,384]{1,0:T(8,128)(2,1)S(1)}, bf16[768,384]{1,0:T(8,128)(2,1)S(1)}, u32[]{:S(2)}, u32[]{:S(2)}) collective-permute-start(bf16[768,384]{1,0:T(8,128)(2,1)S(1)} %get-tuple-element.33), channel_id=1, source_target_pairs={{0,4},{4,0},{1,5},{5,1},{2,6},{6,2},{3,7},{7,3},{8,12},{12,8},{9,1... | collective-permute-start | bytes 1769480 | tf_op jit(solution)/shard_map/ppermute | solution.py:23
  31.1 7.0 %collective-permute-start.2 = (bf16[512,768]{1,0:T(8,128)(2,1)S(1)}, bf16[512,768]{1,0:T(8,128)(2,1)}, u32[]{:S(2)}, u32[]{:S(2)}) collective-permute-start(bf16[512,768]{1,0:T(8,128)(2,1)S(1)} %bitcast.40), channel_id=1, source_target_pairs={{0,4},{4,0},{1,5},{5,1},{2,6},{6,2},{3,7},{7,3},{8,12},{12,8},{9,1... | collective-permute-start | bytes 2359304 | tf_op jit(solution)/shard_map/ppermute | solution.py:23
  36.2 3.7 %copy-start.3 = (bf16[256,384]{1,0:T(8,128)(2,1)}, bf16[256,384]{1,0:T(8,128)(2,1)S(1)}, u32[]{:S(2)}) copy-start(bf16[256,384]{1,0:T(8,128)(2,1)S(1)} %get-tuple-element.65) | copy-start | bytes 589828
  39.4 0.7 copy-start.4
  40.6 19.8 %collective-permute-start.4 = (bf16[256,768]{1,0:T(8,128)(2,1)S(1)}, bf16[256,768]{1,0:T(8,128)(2,1)S(1)}, u32[]{:S(2)}, u32[]{:S(2)}) collective-permute-start(bf16[256,768]{1,0:T(8,128)(2,1)S(1)} %convolution_convert_fusion.8), channel_id=1, source_target_pairs={{0,56},{8,16},{16,8},{24,32},{32,24},{40,48},{48,40},{56,0},{1,57}... | collective-permute-start | bytes 1179656 | tf_op jit(solution)/shard_map/ppermute | solution.py:65
  51.2 11.9 %collective-permute-start.3 = (bf16[256,768]{1,0:T(8,128)(2,1)S(1)}, bf16[256,768]{1,0:T(8,128)(2,1)S(1)}, u32[]{:S(2)}, u32[]{:S(2)}) collective-permute-start(bf16[256,768]{1,0:T(8,128)(2,1)S(1)} %convolution_convert_fusion.9), channel_id=1, source_target_pairs={{0,8},{8,0},{16,24},{24,16},{32,40},{40,32},{48,56},{56,48},{1,9},... | collective-permute-start | bytes 1179656 | tf_op jit(solution)/shard_map/ppermute | solution.py:65
  100.5 11.9 %collective-permute-start.5 = (bf16[256,768]{1,0:T(8,128)(2,1)}, bf16[256,768]{1,0:T(8,128)(2,1)}, u32[]{:S(2)}, u32[]{:S(2)}) collective-permute-start(bf16[256,768]{1,0:T(8,128)(2,1)} %get-tuple-element.25), channel_id=1, source_target_pairs={{0,8},{8,0},{16,24},{24,16},{32,40},{40,32},{48,56},{56,48},{1,9},... | collective-permute-start | bytes 1179656 | tf_op jit(solution)/shard_map/ppermute | solution.py:65
  107.0 11.0 %collective-permute-start.7 = (bf16[256,768]{1,0:T(8,128)(2,1)}, bf16[256,768]{1,0:T(8,128)(2,1)S(1)}, u32[]{:S(2)}, u32[]{:S(2)}) collective-permute-start(bf16[256,768]{1,0:T(8,128)(2,1)} %get-tuple-element.27), channel_id=1, source_target_pairs={{0,56},{8,16},{16,8},{24,32},{32,24},{40,48},{48,40},{56,0},{1,57}... | collective-permute-start | bytes 1179656 | tf_op jit(solution)/shard_map/ppermute | solution.py:65
  114.5 10.6 %collective-permute-start.6 = (bf16[384,768]{1,0:T(8,128)(2,1)S(1)}, bf16[384,768]{1,0:T(8,128)(2,1)S(1)}, u32[]{:S(2)}, u32[]{:S(2)}) collective-permute-start(bf16[384,768]{1,0:T(8,128)(2,1)S(1)} %dynamic-slice_bitcast_fusion.1), channel_id=1, source_target_pairs={{0,1},{1,0},{2,3},{3,2},{4,5},{5,4},{6,7},{7,6},{8,9},{9,8},{10,11... | collective-permute-start | bytes 1769480 | tf_op jit(solution)/shard_map/ppermute | solution.py:125
  117.7 1.0 copy-start.2
  119.9 11.8 %collective-permute-start.8 = (bf16[384,768]{1,0:T(8,128)(2,1)S(1)}, bf16[384,768]{1,0:T(8,128)(2,1)S(1)}, u32[]{:S(2)}, u32[]{:S(2)}) collective-permute-start(bf16[384,768]{1,0:T(8,128)(2,1)S(1)} %dynamic-slice_bitcast_fusion), channel_id=1, source_target_pairs={{0,3},{1,2},{2,1},{3,0},{4,7},{5,6},{6,5},{7,4},{8,11},{9,10},{10,... | collective-permute-start | bytes 1769480 | tf_op jit(solution)/shard_map/ppermute | solution.py:136
  131.9 20.4 %collective-permute-start.10 = (bf16[384,768]{1,0:T(8,128)(2,1)S(1)}, bf16[384,768]{1,0:T(8,128)(2,1)S(1)}, u32[]{:S(2)}, u32[]{:S(2)}) collective-permute-start(bf16[384,768]{1,0:T(8,128)(2,1)S(1)} %fusion.2), channel_id=1, source_target_pairs={{0,1},{1,0},{2,3},{3,2},{4,5},{5,4},{6,7},{7,6},{8,9},{9,8},{10,11... | collective-permute-start | bytes 1769480 | tf_op jit(solution)/shard_map/ppermute | solution.py:149
  133.8 20.8 %collective-permute-start.13 = (bf16[384,768]{1,0:T(8,128)(2,1)S(1)}, bf16[384,768]{1,0:T(8,128)(2,1)S(1)}, u32[]{:S(2)}, u32[]{:S(2)}) collective-permute-start(bf16[384,768]{1,0:T(8,128)(2,1)S(1)} %fusion.3), channel_id=1, source_target_pairs={{0,3},{1,2},{2,1},{3,0},{4,7},{5,6},{6,5},{7,4},{8,11},{9,10},{10,... | collective-permute-start | bytes 1769480 | tf_op jit(solution)/shard_map/ppermute | solution.py:148
  140.0 18.0 %collective-permute-start.9 = (bf16[512,768]{0,1:T(8,128)(2,1)S(1)}, bf16[512,768]{0,1:T(8,128)(2,1)S(1)}, u32[]{:S(2)}, u32[]{:S(2)}) collective-permute-start(bf16[512,768]{0,1:T(8,128)(2,1)S(1)} %pad_maximum_fusion.3), channel_id=1, source_target_pairs={{0,4},{4,0},{1,5},{5,1},{2,6},{6,2},{3,7},{7,3},{8,12},{12,8},{9,1... | collective-permute-start | bytes 2359304 | tf_op jit(solution)/shard_map/ppermute | solution.py:23
  152.5 12.8 %collective-permute-start.11 = (bf16[192,768]{1,0:T(8,128)(2,1)S(1)}, bf16[192,768]{1,0:T(8,128)(2,1)S(1)}, u32[]{:S(2)}, u32[]{:S(2)}) collective-permute-start(bf16[192,768]{1,0:T(8,128)(2,1)S(1)} %get-tuple-element.49), channel_id=1, source_target_pairs={{0,4},{4,0},{1,5},{5,1},{2,6},{6,2},{3,7},{7,3},{8,12},{12,8},{9,1... | collective-permute-start | bytes 884744 | tf_op jit(solution)/shard_map/ppermute | solution.py:23
  154.8 8.2 %collective-permute-start.14 = (bf16[384,384]{1,0:T(8,128)(2,1)S(1)}, bf16[384,384]{1,0:T(8,128)(2,1)S(1)}, u32[]{:S(2)}, u32[]{:S(2)}) collective-permute-start(bf16[384,384]{1,0:T(8,128)(2,1)S(1)} %get-tuple-element.47), channel_id=1, source_target_pairs={{0,4},{4,0},{1,5},{5,1},{2,6},{6,2},{3,7},{7,3},{8,12},{12,8},{9,1... | collective-permute-start | bytes 884744 | tf_op jit(solution)/shard_map/ppermute | solution.py:23
  159.4 27.1 %all-to-all-start.2 = ((bf16[8,64,768]{2,1,0:T(8,128)(2,1)}), bf16[8,64,768]{2,1,0:T(8,128)(2,1)S(1)}, u32[]{:S(2)}, u32[]{:S(2)}) async-start(bf16[8,64,768]{2,1,0:T(8,128)(2,1)} %bitcast.14), calls=%async_computation.2 | async-start | bytes 1572864 | tf_op jit(solution)/shard_map/all_to_all | solution.py:27
  163.1 16.8 %collective-permute-start.15 = (bf16[2,384,384]{2,1,0:T(8,128)(2,1)S(1)}, bf16[2,384,384]{2,1,0:T(8,128)(2,1)S(1)}, u32[]{:S(2)}, u32[]{:S(2)}) collective-permute-start(bf16[2,384,384]{2,1,0:T(8,128)(2,1)S(1)} %maximum_select_fusion.5), channel_id=1, source_target_pairs={{0,1},{1,0},{2,3},{3,2},{4,5},{5,4},{6,7},{7,6},{8,9},{9,8},{10,11... | collective-permute-start | bytes 1769480 | tf_op jit(solution)/shard_map/ppermute | solution.py:152
  165.4 17.7 %collective-permute-start.12 = (bf16[192,1536]{1,0:T(8,128)(2,1)S(1)}, bf16[192,1536]{1,0:T(8,128)(2,1)S(1)}, u32[]{:S(2)}, u32[]{:S(2)}) collective-permute-start(bf16[192,1536]{1,0:T(8,128)(2,1)S(1)} %maximum_select_fusion.4), channel_id=1, source_target_pairs={{0,3},{1,2},{2,1},{3,0},{4,7},{5,6},{6,5},{7,4},{8,11},{9,10},{10,... | collective-permute-start | bytes 1769480 | tf_op jit(solution)/shard_map/ppermute | solution.py:155

commit v14 on v13

--- a/solution.py
+++ b/solution.py
@@ -77,7 +77,9 @@
     up = jnp.concatenate([up_keep, up_other], 0)
     down = jnp.concatenate([down_keep, down_other], 1)
 
-    own = gather(jnp.concatenate([tokens, out_grads], 1), "row")
+    own = lax.all_gather(
+        jnp.concatenate([tokens, out_grads], 1), "row", axis=0, tiled=True
+    )
     own, up, down = barrier((own, up, down))
     other = swap(own)
     total = own.shape[0]

time: 188 us -> 192 us (1.021)
  blocking collectives: 35.7 us -> 57.7 us
  waiting for transfers between devices: 47.7 us -> 33 us
  starting transfers between devices: 80.8 us -> 77.4 us
    all_gather x0 -> x1, blocking collectives: none -> 20.7 us  [per_device(): lax.all_gather(jnp.concatenate([tokens, out_grads], 1), 'row', axis=0, ti...]
    all_to_all x2 -> x1, waiting for transfers between devices: 14 us -> 1.53 us  [exchange(): return lax.all_to_all(x, axis, 0, 0, tiled=False)]
    ppermute x6, starting transfers between devices: 29.3 us -> 36 us  [swap(): return lax.ppermute(x, 'core', [(0, 1), (1, 0)])]
    all_to_all x2 -> x1, starting transfers between devices: 11.2 us -> 4.9 us  [exchange(): return lax.all_to_all(x, axis, 0, 0, tiled=False)]
    ppermute x4, starting transfers between devices: 21.5 us -> 16.1 us  [z_swap(): return lax.ppermute(x, ('zh', 'zl'), pairs)]
  transfers between devices with their start and end apart: 18 -> 17, of which waited for: 11 -> 9; matrix products, arithmetic and copies ran while one was open for 8% -> 7% of each run, Pallas kernels for 0% -> 0%
where the time goes in v14:
time: 192 us; the launch traced here: 191 us
  starting transfers between devices  77.4 us (40%)
  blocking collectives  57.7 us (30%)
  waiting for transfers between devices  33 us (17%)
  matrix products  9.92 us (5%)
  local copies, waits for them, and re-layouts  6.96 us (4%)
  other arithmetic  4.6 us (2%)
    ppermute x6, starting transfers between devices, swap(): return lax.ppermute(x, 'core', [(0, 1), (1, 0)])  36 us
    all_gather x1, blocking collectives, per_device(): lax.all_gather(jnp.concatenate([tokens, out_grads], 1), 'row', axis=0, ti...  20.7 us
    all_to_all x1, blocking collectives, exchange(): return lax.all_to_all(x, axis, 0, 0, tiled=False)  19.7 us
    all_gather x1, blocking collectives, per_device(): lax.all_gather(jnp.concatenate([act, hid_grads], 1), 'zh', axis=0, tiled=...  17.4 us
    ppermute x4, starting transfers between devices, z_swap(): return lax.ppermute(x, ('zh', 'zl'), pairs)  16.1 us
    ppermute x4, waiting for transfers between devices, z_swap(): return lax.ppermute(x, ('zh', 'zl'), pairs)  12.6 us
    dot_general x10, matrix products, dot(): lax.dot_general(left, right, ((dims[:1], dims[1:]), ((), ())), preferred_...  9.92 us
    ppermute x1, waiting for transfers between devices, per_device(): down_part = pair(down_part, lax.ppermute(down_part, 'rep', near), turn, 1)  9.06 us
  transfers between devices with their start and end apart: 17, of which 9 were waited for; matrix products, arithmetic and copies ran while one was open for 7% of the time, Pallas kernels for 0%

profile of v14, /device:TPU:1, one launch (start us, length us, event | category | flops | bytes accessed | tf_op | source)
XLA Modules:
  0.0 190.9 jit_solution(17892778323515224798)
XLA Ops:
  0.6 1.4 constant_dynamic-slice_fusion.3
  2.1 8.8 %collective-permute-start = (bf16[384,768]{1,0:T(8,128)(2,1)S(1)}, bf16[384,768]{1,0:T(8,128)(2,1)S(1)}, u32[]{:S(2)}, u32[]{:S(2)}) collective-permute-start(bf16[384,768]{1,0:T(8,128)(2,1)S(1)} %get-tuple-element.35), channel_id=1, source_target_pairs={{0,4},{4,0},{1,5},{5,1},{2,6},{6,2},{3,7},{7,3},{8,12},{12,8},{9,1... | collective-permute-start | bytes 1769480 | tf_op jit(solution)/shard_map/ppermute | solution.py:23
  10.9 0.1 constant_dynamic-slice_fusion.1
  11.0 1.9 %collective-permute-start.1 = (bf16[768,384]{1,0:T(8,128)(2,1)S(1)}, bf16[768,384]{1,0:T(8,128)(2,1)S(1)}, u32[]{:S(2)}, u32[]{:S(2)}) collective-permute-start(bf16[768,384]{1,0:T(8,128)(2,1)S(1)} %get-tuple-element.33), channel_id=1, source_target_pairs={{0,4},{4,0},{1,5},{5,1},{2,6},{6,2},{3,7},{7,3},{8,12},{12,8},{9,1... | collective-permute-start | bytes 1769480 | tf_op jit(solution)/shard_map/ppermute | solution.py:23
  13.0 20.7 %all_gather.6 = bf16[512,768]{1,0:T(8,128)(2,1)S(1)} all-gather(bf16[64,768]{1,0:T(8,128)(2,1)S(1)} %pad_maximum_fusion.7), channel_id=1, replica_groups=mesh['row'=8,'zh'=4,'zl'=2,'core'=2,'rep'=4] {'row'}, dimensions={0}, use_global_device_ids=true | all-gather | bytes 884736 | tf_op jit(solution)/shard_map/all_gather | solution.py:80
  33.7 0.1 pad_maximum_fusion
  33.8 0.1 pad_maximum_fusion.1
  33.9 7.8 %collective-permute-start.2 = (bf16[512,768]{1,0:T(8,128)(2,1)S(1)}, bf16[512,768]{1,0:T(8,128)(2,1)}, u32[]{:S(2)}, u32[]{:S(2)}) collective-permute-start(bf16[512,768]{1,0:T(8,128)(2,1)S(1)} %all_gather.6), channel_id=1, source_target_pairs={{0,4},{4,0},{1,5},{5,1},{2,6},{6,2},{3,7},{7,3},{8,12},{12,8},{9,1... | collective-permute-start | bytes 2359304 | tf_op jit(solution)/shard_map/ppermute | solution.py:23
  41.8 0.1 fusion.51
  41.9 1.8 collective-permute-done.2
  43.7 1.2 dynamic-slice_bitcast_fusion.2
  44.9 0.1 fusion.52
  45.1 0.5 convolution_convert_fusion.9
  45.5 0.1 copy-done.3
  45.6 0.5 convolution_convert_fusion.8
  46.1 7.0 %collective-permute-start.4 = (bf16[256,768]{1,0:T(8,128)(2,1)S(1)}, bf16[256,768]{1,0:T(8,128)(2,1)S(1)}, u32[]{:S(2)}, u32[]{:S(2)}) collective-permute-start(bf16[256,768]{1,0:T(8,128)(2,1)S(1)} %convolution_convert_fusion.8), channel_id=1, source_target_pairs={{0,56},{8,16},{16,8},{24,32},{32,24},{40,48},{48,40},{56,0},{1,57}... | collective-permute-start | bytes 1179656 | tf_op jit(solution)/shard_map/ppermute | solution.py:65
  53.2 1.9 %collective-permute-start.3 = (bf16[256,768]{1,0:T(8,128)(2,1)S(1)}, bf16[256,768]{1,0:T(8,128)(2,1)S(1)}, u32[]{:S(2)}, u32[]{:S(2)}) collective-permute-start(bf16[256,768]{1,0:T(8,128)(2,1)S(1)} %convolution_convert_fusion.9), channel_id=1, source_target_pairs={{0,8},{8,0},{16,24},{24,16},{32,40},{40,32},{48,56},{56,48},{1,9},... | collective-permute-start | bytes 1179656 | tf_op jit(solution)/shard_map/ppermute | solution.py:65
  55.1 7.2 %collective-permute-done.4 = bf16[256,768]{1,0:T(8,128)(2,1)S(1)} collective-permute-done((bf16[256,768]{1,0:T(8,128)(2,1)S(1)}, bf16[256,768]{1,0:T(8,128)(2,1)S(1)}, u32[]{:S(2)}, u32[]{:S(2)}) %collective-permute-start.4) | collective-permute-done | bytes 393248 | tf_op jit(solution)/shard_map/ppermute | solution.py:65
  62.3 0.5 add_convert_fusion.3
  62.8 2.2 %collective-permute-done.3 = bf16[256,768]{1,0:T(8,128)(2,1)S(1)} collective-permute-done((bf16[256,768]{1,0:T(8,128)(2,1)S(1)}, bf16[256,768]{1,0:T(8,128)(2,1)S(1)}, u32[]{:S(2)}, u32[]{:S(2)}) %collective-permute-start.3) | collective-permute-done | bytes 393248 | tf_op jit(solution)/shard_map/ppermute | solution.py:65
  65.0 0.5 add_convert_fusion.4
  65.6 19.7 %all_to_all.10 = bf16[4,64,1536]{2,1,0:T(8,128)(2,1)S(1)} all-to-all(bf16[4,64,1536]{2,1,0:T(8,128)(2,1)S(1)} %bitcast.38), channel_id=1, replica_groups=mesh['row'=8,'zh'=4,'zl'=2,'core'=2,'rep'=4] {'zh'}, dimensions={0} | all-to-all | bytes 1572864 | tf_op jit(solution)/shard_map/all_to_all | solution.py:27
  85.3 0.1 add_bitcast_fusion
  85.4 0.1 multiply_convert_fusion
  85.6 17.4 %all_gather.7 = bf16[256,1536]{1,0:T(8,128)(2,1)S(1)} all-gather(bf16[64,1536]{1,0:T(8,128)(2,1)S(1)} %pad_maximum_fusion.6), channel_id=1, replica_groups=mesh['row'=8,'zh'=4,'zl'=2,'core'=2,'rep'=4] {'zh'}, dimensions={0}, use_global_device_ids=true | all-gather | bytes 983040 | tf_op jit(solution)/shard_map/all_gather | solution.py:114
  102.9 0.9 fusion.48
  103.8 4.9 %collective-permute-start.5 = (bf16[256,768]{1,0:T(8,128)(2,1)}, bf16[256,768]{1,0:T(8,128)(2,1)}, u32[]{:S(2)}, u32[]{:S(2)}) collective-permute-start(bf16[256,768]{1,0:T(8,128)(2,1)} %get-tuple-element.25), channel_id=1, source_target_pairs={{0,8},{8,0},{16,24},{24,16},{32,40},{40,32},{48,56},{56,48},{1,9},... | collective-permute-start | bytes 1179656 | tf_op jit(solution)/shard_map/ppermute | solution.py:65
  108.8 2.3 %collective-permute-start.7 = (bf16[256,768]{1,0:T(8,128)(2,1)}, bf16[256,768]{1,0:T(8,128)(2,1)S(1)}, u32[]{:S(2)}, u32[]{:S(2)}) collective-permute-start(bf16[256,768]{1,0:T(8,128)(2,1)} %get-tuple-element.27), channel_id=1, source_target_pairs={{0,56},{8,16},{16,8},{24,32},{32,24},{40,48},{48,40},{56,0},{1,57}... | collective-permute-start | bytes 1179656 | tf_op jit(solution)/shard_map/ppermute | solution.py:65
  111.1 3.1 %collective-permute-done.5 = bf16[256,768]{1,0:T(8,128)(2,1)} collective-permute-done((bf16[256,768]{1,0:T(8,128)(2,1)}, bf16[256,768]{1,0:T(8,128)(2,1)}, u32[]{:S(2)}, u32[]{:S(2)}) %collective-permute-start.5) | collective-permute-done | bytes 393248 | tf_op jit(solution)/shard_map/ppermute | solution.py:65
  114.2 2.0 %convolution_convert_fusion.1 = bf16[768,768]{1,0:T(8,128)(2,1)S(1)} fusion(bf16[256,768]{1,0:T(8,128)(2,1)} %collective-permute-done.5, bf16[256,768]{1,0:T(8,128)(2,1)} %get-tuple-element.25, bf16[256,384]{1,0:T(8,128)(2,1)} %copy-done.3, bf16[256,384]{1,0:T(8,128)(2,1)} %copy-done.2, bf16[256,768]{1,0:T(8,128)(2,1)S(1)} %pad_maximum_fusion.5), kind=kOutput, calls=%fused_computation.2 | convolution fusion | flops 608501760 | bytes 2752512 | tf_op jit(solution)/shard_map/dot_general | solution.py:17
  116.3 3.4 %collective-permute-start.6 = (bf16[384,768]{1,0:T(8,128)(2,1)S(1)}, bf16[384,768]{1,0:T(8,128)(2,1)S(1)}, u32[]{:S(2)}, u32[]{:S(2)}) collective-permute-start(bf16[384,768]{1,0:T(8,128)(2,1)S(1)} %dynamic-slice_bitcast_fusion.1), channel_id=1, source_target_pairs={{0,1},{1,0},{2,3},{3,2},{4,5},{5,4},{6,7},{7,6},{8,9},{9,8},{10,11... | collective-permute-start | bytes 1769480 | tf_op jit(solution)/shard_map/ppermute | solution.py:127
  119.7 0.2 fusion.49
  120.0 0.7 copy-done.1
  120.7 1.1 convolution_convert_fusion
  121.9 3.9 %collective-permute-start.8 = (bf16[384,768]{1,0:T(8,128)(2,1)S(1)}, bf16[384,768]{1,0:T(8,128)(2,1)S(1)}, u32[]{:S(2)}, u32[]{:S(2)}) collective-permute-start(bf16[384,768]{1,0:T(8,128)(2,1)S(1)} %dynamic-slice_bitcast_fusion), channel_id=1, source_target_pairs={{0,3},{1,2},{2,1},{3,0},{4,7},{5,6},{6,5},{7,4},{8,11},{9,10},{10,... | collective-permute-start | bytes 1769480 | tf_op jit(solution)/shard_map/ppermute | solution.py:138
  125.8 1.1 collective-permute-done.6
  126.9 0.2 fusion.3
  127.1 0.5 convolution_convert_fusion.2
  127.6 1.9 convolution_convert_fusion.3
  129.6 4.2 %collective-permute-done.8 = bf16[384,768]{1,0:T(8,128)(2,1)S(1)} collective-permute-done((bf16[384,768]{1,0:T(8,128)(2,1)S(1)}, bf16[384,768]{1,0:T(8,128)(2,1)S(1)}, u32[]{:S(2)}, u32[]{:S(2)}) %collective-permute-start.8) | collective-permute-done | bytes 589856 | tf_op jit(solution)/shard_map/ppermute | solution.py:138
  133.7 0.2 fusion.2
  133.9 1.9 %collective-permute-start.10 = (bf16[384,768]{1,0:T(8,128)(2,1)S(1)}, bf16[384,768]{1,0:T(8,128)(2,1)S(1)}, u32[]{:S(2)}, u32[]{:S(2)}) collective-permute-start(bf16[384,768]{1,0:T(8,128)(2,1)S(1)} %fusion.2), channel_id=1, source_target_pairs={{0,1},{1,0},{2,3},{3,2},{4,5},{5,4},{6,7},{7,6},{8,9},{9,8},{10,11... | collective-permute-start | bytes 1769480 | tf_op jit(solution)/shard_map/ppermute | solution.py:151
  135.8 3.9 %collective-permute-start.13 = (bf16[384,768]{1,0:T(8,128)(2,1)S(1)}, bf16[384,768]{1,0:T(8,128)(2,1)S(1)}, u32[]{:S(2)}, u32[]{:S(2)}) collective-permute-start(bf16[384,768]{1,0:T(8,128)(2,1)S(1)} %fusion.3), channel_id=1, source_target_pairs={{0,3},{1,2},{2,1},{3,0},{4,7},{5,6},{6,5},{7,4},{8,11},{9,10},{10,... | collective-permute-start | bytes 1769480 | tf_op jit(solution)/shard_map/ppermute | solution.py:150
  139.8 0.5 convolution_convert_fusion.4
  140.3 1.9 convolution_convert_fusion.5
  142.2 11.6 %collective-permute-start.9 = (bf16[512,768]{0,1:T(8,128)(2,1)S(1)}, bf16[512,768]{0,1:T(8,128)(2,1)S(1)}, u32[]{:S(2)}, u32[]{:S(2)}) collective-permute-start(bf16[512,768]{0,1:T(8,128)(2,1)S(1)} %pad_maximum_fusion.3), channel_id=1, source_target_pairs={{0,4},{4,0},{1,5},{5,1},{2,6},{6,2},{3,7},{7,3},{8,12},{12,8},{9,1... | collective-permute-start | bytes 2359304 | tf_op jit(solution)/shard_map/ppermute | solution.py:23
  153.8 0.1 add_convert_fusion.2
  154.0 3.0 %collective-permute-start.11 = (bf16[192,768]{1,0:T(8,128)(2,1)S(1)}, bf16[192,768]{1,0:T(8,128)(2,1)S(1)}, u32[]{:S(2)}, u32[]{:S(2)}) collective-permute-start(bf16[192,768]{1,0:T(8,128)(2,1)S(1)} %get-tuple-element.49), channel_id=1, source_target_pairs={{0,4},{4,0},{1,5},{5,1},{2,6},{6,2},{3,7},{7,3},{8,12},{12,8},{9,1... | collective-permute-start | bytes 884744 | tf_op jit(solution)/shard_map/ppermute | solution.py:23
  157.0 0.1 add_convert_fusion.1
  157.2 2.9 %collective-permute-start.14 = (bf16[384,384]{1,0:T(8,128)(2,1)S(1)}, bf16[384,384]{1,0:T(8,128)(2,1)S(1)}, u32[]{:S(2)}, u32[]{:S(2)}) collective-permute-start(bf16[384,384]{1,0:T(8,128)(2,1)S(1)} %get-tuple-element.47), channel_id=1, source_target_pairs={{0,4},{4,0},{1,5},{5,1},{2,6},{6,2},{3,7},{7,3},{8,12},{12,8},{9,1... | collective-permute-start | bytes 884744 | tf_op jit(solution)/shard_map/ppermute | solution.py:23
  160.2 0.2 add_convert_fusion
  160.4 1.2 copy.9
  161.6 4.9 %all-to-all-start.1 = ((bf16[8,64,768]{2,1,0:T(8,128)(2,1)}), bf16[8,64,768]{2,1,0:T(8,128)(2,1)S(1)}, u32[]{:S(2)}, u32[]{:S(2)}) async-start(bf16[8,64,768]{2,1,0:T(8,128)(2,1)} %bitcast.13), calls=%async_computation.1 | async-start | bytes 1572864 | tf_op jit(solution)/shard_map/all_to_all | solution.py:27
  166.5 0.1 maximum_select_fusion.5
  166.6 3.0 %collective-permute-start.15 = (bf16[2,384,384]{2,1,0:T(8,128)(2,1)S(1)}, bf16[2,384,384]{2,1,0:T(8,128)(2,1)S(1)}, u32[]{:S(2)}, u32[]{:S(2)}) collective-permute-start(bf16[2,384,384]{2,1,0:T(8,128)(2,1)S(1)} %maximum_select_fusion.5), channel_id=1, source_target_pairs={{0,1},{1,0},{2,3},{3,2},{4,5},{5,4},{6,7},{7,6},{8,9},{9,8},{10,11... | collective-permute-start | bytes 1769480 | tf_op jit(solution)/shard_map/ppermute | solution.py:154
  169.6 0.1 maximum_select_fusion.4
  169.8 4.2 %collective-permute-start.12 = (bf16[192,1536]{1,0:T(8,128)(2,1)S(1)}, bf16[192,1536]{1,0:T(8,128)(2,1)S(1)}, u32[]{:S(2)}, u32[]{:S(2)}) collective-permute-start(bf16[192,1536]{1,0:T(8,128)(2,1)S(1)} %maximum_select_fusion.4), channel_id=1, source_target_pairs={{0,3},{1,2},{2,1},{3,0},{4,7},{5,6},{6,5},{7,4},{8,11},{9,10},{10,... | collective-permute-start | bytes 1769480 | tf_op jit(solution)/shard_map/ppermute | solution.py:157
  174.0 9.1 %collective-permute-done.15 = bf16[2,384,384]{2,1,0:T(8,128)(2,1)S(1)} collective-permute-done((bf16[2,384,384]{2,1,0:T(8,128)(2,1)S(1)}, bf16[2,384,384]{2,1,0:T(8,128)(2,1)S(1)}, u32[]{:S(2)}, u32[]{:S(2)}) %collective-permute-start.15) | collective-permute-done | bytes 589856 | tf_op jit(solution)/shard_map/ppermute | solution.py:154
  183.1 1.4 maximum_select_fusion.1
  184.5 2.7 %collective-permute-done.12 = bf16[192,1536]{1,0:T(8,128)(2,1)S(1)} collective-permute-done((bf16[192,1536]{1,0:T(8,128)(2,1)S(1)}, bf16[192,1536]{1,0:T(8,128)(2,1)S(1)}, u32[]{:S(2)}, u32[]{:S(2)}) %collective-permute-start.12) | collective-permute-done | bytes 589856 | tf_op jit(solution)/shard_map/ppermute | solution.py:157
  187.2 1.4 maximum_select_fusion
  188.6 1.5 all-to-all-done.1
  190.1 0.1 fusion.39
  190.2 0.6 fusion.55
  (30 shorter events, 0.6 us)
Async XLA Ops:
  0.6 10.3 %copy-start = (bf16[1536,384]{1,0:T(8,128)(2,1)S(1)}, bf16[1536,384]{1,0:T(8,128)(2,1)}, u32[]{:S(2)}) copy-start(bf16[1536,384]{1,0:T(8,128)(2,1)} %param.6) | copy-start | bytes 3538948
  2.1 10.9 %copy-start.4 = (bf16[64,384]{1,0:T(8,128)(2,1)S(1)}, bf16[64,384]{1,0:T(8,128)(2,1)}, u32[]{:S(2)}) copy-start(bf16[64,384]{1,0:T(8,128)(2,1)} %param.7) | copy-start | bytes 147460
  2.1 10.9 %copy-start.5 = (bf16[64,384]{1,0:T(8,128)(2,1)S(1)}, bf16[64,384]{1,0:T(8,128)(2,1)}, u32[]{:S(2)}) copy-start(bf16[64,384]{1,0:T(8,128)(2,1)} %param.4) | copy-start | bytes 147460
  2.1 31.6 %collective-permute-start = (bf16[384,768]{1,0:T(8,128)(2,1)S(1)}, bf16[384,768]{1,0:T(8,128)(2,1)S(1)}, u32[]{:S(2)}, u32[]{:S(2)}) collective-permute-start(bf16[384,768]{1,0:T(8,128)(2,1)S(1)} %get-tuple-element.35), channel_id=1, source_target_pairs={{0,4},{4,0},{1,5},{5,1},{2,6},{6,2},{3,7},{7,3},{8,12},{12,8},{9,1... | collective-permute-start | bytes 1769480 | tf_op jit(solution)/shard_map/ppermute | solution.py:23
  11.0 22.7 %collective-permute-start.1 = (bf16[768,384]{1,0:T(8,128)(2,1)S(1)}, bf16[768,384]{1,0:T(8,128)(2,1)S(1)}, u32[]{:S(2)}, u32[]{:S(2)}) collective-permute-start(bf16[768,384]{1,0:T(8,128)(2,1)S(1)} %get-tuple-element.33), channel_id=1, source_target_pairs={{0,4},{4,0},{1,5},{5,1},{2,6},{6,2},{3,7},{7,3},{8,12},{12,8},{9,1... | collective-permute-start | bytes 1769480 | tf_op jit(solution)/shard_map/ppermute | solution.py:23
  33.9 9.8 %collective-permute-start.2 = (bf16[512,768]{1,0:T(8,128)(2,1)S(1)}, bf16[512,768]{1,0:T(8,128)(2,1)}, u32[]{:S(2)}, u32[]{:S(2)}) collective-permute-start(bf16[512,768]{1,0:T(8,128)(2,1)S(1)} %all_gather.6), channel_id=1, source_target_pairs={{0,4},{4,0},{1,5},{5,1},{2,6},{6,2},{3,7},{7,3},{8,12},{12,8},{9,1... | collective-permute-start | bytes 2359304 | tf_op jit(solution)/shard_map/ppermute | solution.py:23
  41.8 3.7 %copy-start.2 = (bf16[256,384]{1,0:T(8,128)(2,1)}, bf16[256,384]{1,0:T(8,128)(2,1)S(1)}, u32[]{:S(2)}) copy-start(bf16[256,384]{1,0:T(8,128)(2,1)S(1)} %get-tuple-element.65) | copy-start | bytes 589828
  45.0 0.7 copy-start.3
  46.1 16.2 %collective-permute-start.4 = (bf16[256,768]{1,0:T(8,128)(2,1)S(1)}, bf16[256,768]{1,0:T(8,128)(2,1)S(1)}, u32[]{:S(2)}, u32[]{:S(2)}) collective-permute-start(bf16[256,768]{1,0:T(8,128)(2,1)S(1)} %convolution_convert_fusion.8), channel_id=1, source_target_pairs={{0,56},{8,16},{16,8},{24,32},{32,24},{40,48},{48,40},{56,0},{1,57}... | collective-permute-start | bytes 1179656 | tf_op jit(solution)/shard_map/ppermute | solution.py:65
  53.2 11.9 %collective-permute-start.3 = (bf16[256,768]{1,0:T(8,128)(2,1)S(1)}, bf16[256,768]{1,0:T(8,128)(2,1)S(1)}, u32[]{:S(2)}, u32[]{:S(2)}) collective-permute-start(bf16[256,768]{1,0:T(8,128)(2,1)S(1)} %convolution_convert_fusion.9), channel_id=1, source_target_pairs={{0,8},{8,0},{16,24},{24,16},{32,40},{40,32},{48,56},{56,48},{1,9},... | collective-permute-start | bytes 1179656 | tf_op jit(solution)/shard_map/ppermute | solution.py:65
  103.8 10.3 %collective-permute-start.5 = (bf16[256,768]{1,0:T(8,128)(2,1)}, bf16[256,768]{1,0:T(8,128)(2,1)}, u32[]{:S(2)}, u32[]{:S(2)}) collective-permute-start(bf16[256,768]{1,0:T(8,128)(2,1)} %get-tuple-element.25), channel_id=1, source_target_pairs={{0,8},{8,0},{16,24},{24,16},{32,40},{40,32},{48,56},{56,48},{1,9},... | collective-permute-start | bytes 1179656 | tf_op jit(solution)/shard_map/ppermute | solution.py:65
  108.8 11.2 %collective-permute-start.7 = (bf16[256,768]{1,0:T(8,128)(2,1)}, bf16[256,768]{1,0:T(8,128)(2,1)S(1)}, u32[]{:S(2)}, u32[]{:S(2)}) collective-permute-start(bf16[256,768]{1,0:T(8,128)(2,1)} %get-tuple-element.27), channel_id=1, source_target_pairs={{0,56},{8,16},{16,8},{24,32},{32,24},{40,48},{48,40},{56,0},{1,57}... | collective-permute-start | bytes 1179656 | tf_op jit(solution)/shard_map/ppermute | solution.py:65
  116.3 10.6 %collective-permute-start.6 = (bf16[384,768]{1,0:T(8,128)(2,1)S(1)}, bf16[384,768]{1,0:T(8,128)(2,1)S(1)}, u32[]{:S(2)}, u32[]{:S(2)}) collective-permute-start(bf16[384,768]{1,0:T(8,128)(2,1)S(1)} %dynamic-slice_bitcast_fusion.1), channel_id=1, source_target_pairs={{0,1},{1,0},{2,3},{3,2},{4,5},{5,4},{6,7},{7,6},{8,9},{9,8},{10,11... | collective-permute-start | bytes 1769480 | tf_op jit(solution)/shard_map/ppermute | solution.py:127
  119.7 1.0 copy-start.1
  121.9 11.8 %collective-permute-start.8 = (bf16[384,768]{1,0:T(8,128)(2,1)S(1)}, bf16[384,768]{1,0:T(8,128)(2,1)S(1)}, u32[]{:S(2)}, u32[]{:S(2)}) collective-permute-start(bf16[384,768]{1,0:T(8,128)(2,1)S(1)} %dynamic-slice_bitcast_fusion), channel_id=1, source_target_pairs={{0,3},{1,2},{2,1},{3,0},{4,7},{5,6},{6,5},{7,4},{8,11},{9,10},{10,... | collective-permute-start | bytes 1769480 | tf_op jit(solution)/shard_map/ppermute | solution.py:138
  133.9 19.9 %collective-permute-start.10 = (bf16[384,768]{1,0:T(8,128)(2,1)S(1)}, bf16[384,768]{1,0:T(8,128)(2,1)S(1)}, u32[]{:S(2)}, u32[]{:S(2)}) collective-permute-start(bf16[384,768]{1,0:T(8,128)(2,1)S(1)} %fusion.2), channel_id=1, source_target_pairs={{0,1},{1,0},{2,3},{3,2},{4,5},{5,4},{6,7},{7,6},{8,9},{9,8},{10,11... | collective-permute-start | bytes 1769480 | tf_op jit(solution)/shard_map/ppermute | solution.py:151
  135.8 21.2 %collective-permute-start.13 = (bf16[384,768]{1,0:T(8,128)(2,1)S(1)}, bf16[384,768]{1,0:T(8,128)(2,1)S(1)}, u32[]{:S(2)}, u32[]{:S(2)}) collective-permute-start(bf16[384,768]{1,0:T(8,128)(2,1)S(1)} %fusion.3), channel_id=1, source_target_pairs={{0,3},{1,2},{2,1},{3,0},{4,7},{5,6},{6,5},{7,4},{8,11},{9,10},{10,... | collective-permute-start | bytes 1769480 | tf_op jit(solution)/shard_map/ppermute | solution.py:150
  142.2 18.0 %collective-permute-start.9 = (bf16[512,768]{0,1:T(8,128)(2,1)S(1)}, bf16[512,768]{0,1:T(8,128)(2,1)S(1)}, u32[]{:S(2)}, u32[]{:S(2)}) collective-permute-start(bf16[512,768]{0,1:T(8,128)(2,1)S(1)} %pad_maximum_fusion.3), channel_id=1, source_target_pairs={{0,4},{4,0},{1,5},{5,1},{2,6},{6,2},{3,7},{7,3},{8,12},{12,8},{9,1... | collective-permute-start | bytes 2359304 | tf_op jit(solution)/shard_map/ppermute | solution.py:23
  154.0 15.6 %collective-permute-start.11 = (bf16[192,768]{1,0:T(8,128)(2,1)S(1)}, bf16[192,768]{1,0:T(8,128)(2,1)S(1)}, u32[]{:S(2)}, u32[]{:S(2)}) collective-permute-start(bf16[192,768]{1,0:T(8,128)(2,1)S(1)} %get-tuple-element.49), channel_id=1, source_target_pairs={{0,4},{4,0},{1,5},{5,1},{2,6},{6,2},{3,7},{7,3},{8,12},{12,8},{9,1... | collective-permute-start | bytes 884744 | tf_op jit(solution)/shard_map/ppermute | solution.py:23
  157.2 9.2 %collective-permute-start.14 = (bf16[384,384]{1,0:T(8,128)(2,1)S(1)}, bf16[384,384]{1,0:T(8,128)(2,1)S(1)}, u32[]{:S(2)}, u32[]{:S(2)}) collective-permute-start(bf16[384,384]{1,0:T(8,128)(2,1)S(1)} %get-tuple-element.47), channel_id=1, source_target_pairs={{0,4},{4,0},{1,5},{5,1},{2,6},{6,2},{3,7},{7,3},{8,12},{12,8},{9,1... | collective-permute-start | bytes 884744 | tf_op jit(solution)/shard_map/ppermute | solution.py:23
  161.6 28.5 %all-to-all-start.1 = ((bf16[8,64,768]{2,1,0:T(8,128)(2,1)}), bf16[8,64,768]{2,1,0:T(8,128)(2,1)S(1)}, u32[]{:S(2)}, u32[]{:S(2)}) async-start(bf16[8,64,768]{2,1,0:T(8,128)(2,1)} %bitcast.13), calls=%async_computation.1 | async-start | bytes 1572864 | tf_op jit(solution)/shard_map/all_to_all | solution.py:27
  166.6 16.5 %collective-permute-start.15 = (bf16[2,384,384]{2,1,0:T(8,128)(2,1)S(1)}, bf16[2,384,384]{2,1,0:T(8,128)(2,1)S(1)}, u32[]{:S(2)}, u32[]{:S(2)}) collective-permute-start(bf16[2,384,384]{2,1,0:T(8,128)(2,1)S(1)} %maximum_select_fusion.5), channel_id=1, source_target_pairs={{0,1},{1,0},{2,3},{3,2},{4,5},{5,4},{6,7},{7,6},{8,9},{9,8},{10,11... | collective-permute-start | bytes 1769480 | tf_op jit(solution)/shard_map/ppermute | solution.py:154
  169.8 17.4 %collective-permute-start.12 = (bf16[192,1536]{1,0:T(8,128)(2,1)S(1)}, bf16[192,1536]{1,0:T(8,128)(2,1)S(1)}, u32[]{:S(2)}, u32[]{:S(2)}) collective-permute-start(bf16[192,1536]{1,0:T(8,128)(2,1)S(1)} %maximum_select_fusion.4), channel_id=1, source_target_pairs={{0,3},{1,2},{2,1},{3,0},{4,7},{5,6},{6,5},{7,4},{8,11},{9,10},{10,... | collective-permute-start | bytes 1769480 | tf_op jit(solution)/shard_map/ppermute | solution.py:157
